TPU v7x, 32 devices: a whole 2x2x4 slice. The times are simulated.
32 devices in a mesh: fsdp: 4 (over z), ctx: 2 (over x), tp: 4 (over y, core).
Axes of the slice: x: 2, y: 2, z: 4, core: 2. Of those that a mesh axis runs over, the one named last changes fastest.
Arguments:
- tokens: bfloat16 [4, 2048, 1536], P('fsdp', 'ctx'), may hold values from -6 to 6
- prefix_len: int32 [4], P('fsdp'), may hold values from 204 to 1024
- positions: int32 [4, 2048], P('fsdp', 'ctx'), may hold values from 0 to 3071, as said below
- gain_attend: bfloat16 [1536], P('fsdp'), may hold values from 0.5 to 1.5
- w_query: bfloat16 [1536, 1536], P('fsdp', 'tp'), may hold values from -0.15625 to 0.15625
- w_key: bfloat16 [1536, 768], P('fsdp', 'tp'), may hold values from -0.15625 to 0.15625
- w_value: bfloat16 [1536, 768], P('fsdp', 'tp'), may hold values from -0.15625 to 0.15625
- w_project: bfloat16 [1536, 1536], P('tp', 'fsdp'), may hold values from -2.5 to 2.5
- gain_feed: bfloat16 [1536], P('fsdp'), may hold values from 0.5 to 1.5
- w_gate: bfloat16 [1536, 4096], P('fsdp', 'tp'), may hold values from -0.15625 to 0.15625
- w_up: bfloat16 [1536, 4096], P('fsdp', 'tp'), may hold values from -0.15625 to 0.15625
- w_down: bfloat16 [4096, 1536], P('tp', 'fsdp'), may hold values from -0.09375 to 0.09375
- cotangent: bfloat16 [4, 2048, 1536], P('fsdp', 'ctx'), may hold values from -6 to 6
Outputs:
- layer_output: bfloat16 [4, 2048, 1536], P('fsdp', 'ctx')
- tokens_grad: bfloat16 [4, 2048, 1536], P('fsdp', 'ctx')
- attend_grad: float32 [1536], P('fsdp')
- query_grad: float32 [1536, 1536], P('fsdp', 'tp')
- key_grad: float32 [1536, 768], P('fsdp', 'tp')
- value_grad: float32 [1536, 768], P('fsdp', 'tp')
- project_grad: float32 [1536, 1536], P('tp', 'fsdp')
- feed_grad: float32 [1536], P('fsdp')
- gate_grad: float32 [1536, 4096], P('fsdp', 'tp')
- up_grad: float32 [1536, 4096], P('fsdp', 'tp')
- down_grad: float32 [4096, 1536], P('tp', 'fsdp')
Inputs may be any that keep to these rules, and one draw needn't show every extreme that they name: Within each sequence, taken in token order, the positions start at 0 and rise by 1 or 2 from one token to the next, by 2 at exactly 1024 of the steps.
All inputs are finite; a program needn't handle non-finite values.
Results may differ from a plain program's by a relative error of at most 0.023.
Values may be sent and summed in bfloat16 or wider, within the bound.
A program may use at most 192 MiB of HBM per device.

v0:
```python
import math

import jax
import jax.numpy as jnp
from jax import lax
from jax.sharding import PartitionSpec as P

HQ = 16
KVH = 8
HD = 96


EPSILON = 1e-05
ROPE_BASE = 100000.0
NEGATIVE = -1e30


def natural_index(stored, block_len, pair_count):
    device = stored // (2 * block_len)
    second_half = stored // block_len % 2
    within = stored % block_len
    block_id = jnp.where(second_half == 0, device, 2 * pair_count - 1 - device)
    return block_id * block_len + within


def rotate(values, cosine_table, sine_table):
    half_width = values.shape[-1] // 2
    leading = values[..., :half_width]
    trailing = values[..., half_width:]
    return jnp.concatenate(
        [
            leading * cosine_table - trailing * sine_table,
            trailing * cosine_table + leading * sine_table,
        ],
        axis=-1,
    )


def rotate_back(incoming, cosine_table, sine_table):
    half_width = incoming.shape[-1] // 2
    leading = incoming[..., :half_width]
    trailing = incoming[..., half_width:]
    return jnp.concatenate(
        [
            leading * cosine_table + trailing * sine_table,
            trailing * cosine_table - leading * sine_table,
        ],
        axis=-1,
    )


def rms_factor(values):
    return lax.rsqrt(jnp.mean(values * values, axis=-1, keepdims=True) + EPSILON)


def rms_back(values, factor, gain_row, incoming):
    scaled = gain_row * incoming
    return factor * scaled - values * factor**3 * jnp.mean(scaled * values, axis=-1, keepdims=True)


def tensor_sum(term_rows):
    return lax.psum(term_rows.astype(jnp.bfloat16), "tp").astype(jnp.float32)


def body(
    tokens,
    prefix_len,
    positions,
    gain_attend,
    w_query,
    w_key,
    w_value,
    w_project,
    gain_feed,
    w_gate,
    w_up,
    w_down,
    cotangent,
):
    (
        gain_one,
        query_weight_whole,
        key_weight_whole,
        value_weight_whole,
        project_weight_whole,
        gain_two,
        gate_weight_whole,
        up_weight_whole,
        down_weight_whole,
    ) = (
        lax.all_gather(gain_attend, "fsdp", axis=0, tiled=True),
        lax.all_gather(w_query, "fsdp", axis=0, tiled=True),
        lax.all_gather(w_key, "fsdp", axis=0, tiled=True),
        lax.all_gather(w_value, "fsdp", axis=0, tiled=True),
        lax.all_gather(w_project, "fsdp", axis=1, tiled=True),
        lax.all_gather(gain_feed, "fsdp", axis=0, tiled=True),
        lax.all_gather(w_gate, "fsdp", axis=0, tiled=True),
        lax.all_gather(w_up, "fsdp", axis=0, tiled=True),
        lax.all_gather(w_down, "fsdp", axis=1, tiled=True),
    )
    seq_count, rows_local, _ = tokens.shape
    pair_count = lax.axis_size("ctx")
    block_len = rows_local // 2
    query_width = query_weight_whole.shape[1]
    kv_width = key_weight_whole.shape[1]
    query_heads = query_width // HD
    kv_heads = kv_width // HD
    group_size = HQ // KVH
    score_scale = HD ** (-0.5)
    frequency = ROPE_BASE ** (-(jnp.arange(HD // 2, dtype=jnp.float32) * 2.0 / HD))
    angles = positions.astype(jnp.float32)[:, :, None] * frequency
    cosine_table = jnp.cos(angles)[:, :, None, :]
    sine_table = jnp.sin(angles)[:, :, None, :]
    stored_rows = lax.axis_index("ctx") * rows_local + jnp.arange(rows_local, dtype=jnp.int32)
    query_order = natural_index(stored_rows, block_len, pair_count)

    def visible_mask(key_order):
        causal = key_order[None, None, :] <= query_order[None, :, None]
        opened = key_order[None, None, :] < prefix_len[:, None, None]
        return (causal | opened)[:, :, None, None, :]

    inputs = tokens.astype(jnp.float32)
    factor_one = rms_factor(inputs)
    normed_hidden = (inputs * factor_one * gain_one.astype(jnp.float32)).astype(jnp.bfloat16)
    query_projected = jnp.einsum(
        "rxc,cf->rxf", normed_hidden, query_weight_whole, preferred_element_type=jnp.float32
    )
    key_projected = jnp.einsum(
        "rxc,cf->rxf", normed_hidden, key_weight_whole, preferred_element_type=jnp.float32
    )
    value_projected = jnp.einsum(
        "rxc,cf->rxf", normed_hidden, value_weight_whole, preferred_element_type=jnp.float32
    )
    queries = (
        rotate(
            query_projected.reshape(seq_count, rows_local, query_heads, HD),
            cosine_table,
            sine_table,
        )
        .astype(jnp.bfloat16)
        .reshape(seq_count, rows_local, kv_heads, group_size, HD)
    )
    keys_rot = (
        rotate(key_projected.reshape(seq_count, rows_local, kv_heads, HD), cosine_table, sine_table)
        .astype(jnp.bfloat16)
        .reshape(seq_count, rows_local, kv_width)
    )
    values_low = value_projected.astype(jnp.bfloat16)
    stat_shape = (seq_count, rows_local, kv_heads, group_size)
    initial = (
        jnp.full(stat_shape, NEGATIVE, jnp.float32),
        jnp.zeros(stat_shape, jnp.float32),
        jnp.zeros(stat_shape + (HD,), jnp.float32),
    )
    key_piece = lax.all_gather(keys_rot, "ctx", axis=1, tiled=True)
    value_piece = lax.all_gather(values_low, "ctx", axis=1, tiled=True)
    key_total = key_piece.shape[1]
    span_rows = math.gcd(key_total, rows_local)

    def one_span(span_index, running):
        run_max, run_sum, run_acc = running
        span_start = span_index * span_rows
        key_rows = lax.dynamic_slice_in_dim(key_piece, span_start, span_rows, 1).reshape(
            seq_count, span_rows, kv_heads, HD
        )
        value_rows = lax.dynamic_slice_in_dim(value_piece, span_start, span_rows, 1).reshape(
            seq_count, span_rows, kv_heads, HD
        )
        key_order = natural_index(
            span_start + jnp.arange(span_rows, dtype=jnp.int32), block_len, pair_count
        )
        visible = visible_mask(key_order)
        scores = (
            jnp.einsum("slhgd,skhd->slhgk", queries, key_rows, preferred_element_type=jnp.float32)
            * score_scale
        )
        new_max = jnp.maximum(run_max, jnp.max(jnp.where(visible, scores, NEGATIVE), axis=-1))
        weights_raw = jnp.where(visible, jnp.exp(scores - new_max[..., None]), 0.0)
        rescale = jnp.exp(run_max - new_max)
        run_sum = run_sum * rescale + jnp.sum(weights_raw, axis=-1)
        run_acc = run_acc * rescale[..., None] + jnp.einsum(
            "slhgk,skhd->slhgd",
            weights_raw.astype(jnp.bfloat16),
            value_rows,
            preferred_element_type=jnp.float32,
        )
        return (new_max, run_sum, run_acc)

    run_max, run_sum, run_acc = lax.fori_loop(0, key_total // span_rows, one_span, initial)
    attended = run_acc / run_sum[..., None]
    log_total = run_max + jnp.log(run_sum)
    attended_reduced = attended.reshape(seq_count, rows_local, query_width).astype(jnp.bfloat16)
    project_rows = jnp.einsum(
        "hxz,zm->hxm", attended_reduced, project_weight_whole, preferred_element_type=jnp.float32
    )
    middle = inputs + tensor_sum(project_rows)
    factor_two = rms_factor(middle)
    normed_feed_input = (middle * factor_two * gain_two.astype(jnp.float32)).astype(jnp.bfloat16)
    gate_activation = jnp.einsum(
        "qeh,hj->qej", normed_feed_input, gate_weight_whole, preferred_element_type=jnp.float32
    )
    up_activation = jnp.einsum(
        "qeh,hj->qej", normed_feed_input, up_weight_whole, preferred_element_type=jnp.float32
    )
    sigmoid_gate = jax.nn.sigmoid(gate_activation)
    silu_gate = gate_activation * sigmoid_gate
    hidden_state = (silu_gate * up_activation).astype(jnp.bfloat16)
    down_output_rows = jnp.einsum(
        "nct,tm->ncm", hidden_state, down_weight_whole, preferred_element_type=jnp.float32
    )
    layer_output = (middle + tensor_sum(down_output_rows)).astype(jnp.bfloat16)
    (
        gain_one,
        query_weight_whole,
        key_weight_whole,
        value_weight_whole,
        project_weight_whole,
        gain_two,
        gate_weight_whole,
        up_weight_whole,
        down_weight_whole,
    ) = (
        lax.all_gather(gain_attend, "fsdp", axis=0, tiled=True),
        lax.all_gather(w_query, "fsdp", axis=0, tiled=True),
        lax.all_gather(w_key, "fsdp", axis=0, tiled=True),
        lax.all_gather(w_value, "fsdp", axis=0, tiled=True),
        lax.all_gather(w_project, "fsdp", axis=1, tiled=True),
        lax.all_gather(gain_feed, "fsdp", axis=0, tiled=True),
        lax.all_gather(w_gate, "fsdp", axis=0, tiled=True),
        lax.all_gather(w_up, "fsdp", axis=0, tiled=True),
        lax.all_gather(w_down, "fsdp", axis=1, tiled=True),
    )
    hidden_grad = jnp.einsum(
        "ehv,iv->ehi", cotangent, down_weight_whole, preferred_element_type=jnp.float32
    )
    down_weight_part = jnp.einsum(
        "gqa,gqz->az", hidden_state, cotangent, preferred_element_type=jnp.float32
    )
    gate_reduced = (
        hidden_grad * up_activation * sigmoid_gate * (1.0 + gate_activation * (1.0 - sigmoid_gate))
    ).astype(jnp.bfloat16)
    up_reduced = (hidden_grad * silu_gate).astype(jnp.bfloat16)
    gate_weight_part = jnp.einsum(
        "bic,big->cg", normed_feed_input, gate_reduced, preferred_element_type=jnp.float32
    )
    up_weight_part = jnp.einsum(
        "bic,big->cg", normed_feed_input, up_reduced, preferred_element_type=jnp.float32
    )
    feed_rows = jnp.einsum(
        "vte,ce->vtc", gate_reduced, gate_weight_whole, preferred_element_type=jnp.float32
    ) + jnp.einsum("vte,ce->vtc", up_reduced, up_weight_whole, preferred_element_type=jnp.float32)
    feed_in = tensor_sum(feed_rows)
    gain_two_term = jnp.sum(feed_in * middle * factor_two, axis=(0, 1))
    middle_grad = cotangent.astype(jnp.float32) + rms_back(
        middle, factor_two, gain_two.astype(jnp.float32), feed_in
    )
    middle_reduced = middle_grad.astype(jnp.bfloat16)
    project_term = jnp.einsum(
        "xeh,xec->hc", attended_reduced, middle_reduced, preferred_element_type=jnp.float32
    )
    attended_grad = (
        jnp.einsum(
            "vhk,nk->vhn", middle_reduced, project_weight_whole, preferred_element_type=jnp.float32
        )
        .astype(jnp.bfloat16)
        .reshape(seq_count, rows_local, kv_heads, group_size, HD)
    )
    row_delta = jnp.sum(attended_grad.astype(jnp.float32) * attended, axis=-1)
    whole_keys, whole_values = (
        lax.all_gather(keys_rot[None], "ctx", axis=0, tiled=True),
        lax.all_gather(values_low[None], "ctx", axis=0, tiled=True),
    )

    def key_block(grad_acc, block_items):
        key_rows, value_rows, block_index = block_items
        key_rows = key_rows.reshape(seq_count, rows_local, kv_heads, HD)
        value_rows = value_rows.reshape(seq_count, rows_local, kv_heads, HD)
        key_order = natural_index(
            block_index * rows_local + jnp.arange(rows_local, dtype=jnp.int32),
            block_len,
            pair_count,
        )
        visible = visible_mask(key_order)
        scores = (
            jnp.einsum("slhgd,skhd->slhgk", queries, key_rows, preferred_element_type=jnp.float32)
            * score_scale
        )
        weights_norm = jnp.where(visible, jnp.exp(scores - log_total[..., None]), 0.0)
        prob_grad = jnp.einsum(
            "slhgd,skhd->slhgk", attended_grad, value_rows, preferred_element_type=jnp.float32
        )
        score_grad = (weights_norm * (prob_grad - row_delta[..., None])).astype(jnp.bfloat16)
        grad_acc = (
            grad_acc
            + jnp.einsum(
                "slhgk,skhd->slhgd", score_grad, key_rows, preferred_element_type=jnp.float32
            )
            * score_scale
        )
        key_grad = (
            jnp.einsum("slhgk,slhgd->skhd", score_grad, queries, preferred_element_type=jnp.float32)
            * score_scale
        )
        value_grad = jnp.einsum(
            "slhgk,slhgd->skhd",
            weights_norm.astype(jnp.bfloat16),
            attended_grad,
            preferred_element_type=jnp.float32,
        )
        return (
            grad_acc,
            (
                key_grad.reshape(seq_count, rows_local, kv_width),
                value_grad.reshape(seq_count, rows_local, kv_width),
            ),
        )

    block_ids = jnp.arange(pair_count, dtype=jnp.int32)
    query_grad, (key_terms, value_terms) = lax.scan(
        key_block, jnp.zeros(stat_shape + (HD,), jnp.float32), (whole_keys, whole_values, block_ids)
    )
    key_sum, value_sum = (
        lax.psum_scatter(
            key_terms.astype(jnp.bfloat16), "ctx", scatter_dimension=0, tiled=True
        ).astype(jnp.float32),
        lax.psum_scatter(
            value_terms.astype(jnp.bfloat16), "ctx", scatter_dimension=0, tiled=True
        ).astype(jnp.float32),
    )
    key_reduced = (
        rotate_back(
            key_sum[0].reshape(seq_count, rows_local, kv_heads, HD), cosine_table, sine_table
        )
        .astype(jnp.bfloat16)
        .reshape(seq_count, rows_local, kv_width)
    )
    value_backward = value_sum[0].astype(jnp.bfloat16)
    query_reduced = (
        rotate_back(
            query_grad.reshape(seq_count, rows_local, query_heads, HD), cosine_table, sine_table
        )
        .astype(jnp.bfloat16)
        .reshape(seq_count, rows_local, query_width)
    )
    query_weight_part = jnp.einsum(
        "prb,pro->bo", normed_hidden, query_reduced, preferred_element_type=jnp.float32
    )
    key_weight_part = jnp.einsum(
        "prb,pro->bo", normed_hidden, key_reduced, preferred_element_type=jnp.float32
    )
    value_weight_part = jnp.einsum(
        "prb,pro->bo", normed_hidden, value_backward, preferred_element_type=jnp.float32
    )
    normed_rows = (
        jnp.einsum(
            "kjw,iw->kji", query_reduced, query_weight_whole, preferred_element_type=jnp.float32
        )
        + jnp.einsum(
            "kjw,iw->kji", key_reduced, key_weight_whole, preferred_element_type=jnp.float32
        )
        + jnp.einsum(
            "kjw,iw->kji", value_backward, value_weight_whole, preferred_element_type=jnp.float32
        )
    )
    normed_grad = tensor_sum(normed_rows)
    gain_one_term = jnp.sum(normed_grad * inputs * factor_one, axis=(0, 1))
    tokens_grad = (
        middle_grad + rms_back(inputs, factor_one, gain_one.astype(jnp.float32), normed_grad)
    ).astype(jnp.bfloat16)
    (
        part_one,
        part_query,
        part_key,
        part_value,
        part_project,
        part_two,
        part_gate,
        part_up,
        part_down,
    ) = (
        lax.psum_scatter(gain_one_term, ("fsdp", "ctx"), scatter_dimension=0, tiled=True),
        lax.psum_scatter(query_weight_part, ("fsdp", "ctx"), scatter_dimension=0, tiled=True),
        lax.psum_scatter(key_weight_part, ("fsdp", "ctx"), scatter_dimension=0, tiled=True),
        lax.psum_scatter(value_weight_part, ("fsdp", "ctx"), scatter_dimension=0, tiled=True),
        lax.psum_scatter(project_term, ("fsdp", "ctx"), scatter_dimension=1, tiled=True),
        lax.psum_scatter(gain_two_term, ("fsdp", "ctx"), scatter_dimension=0, tiled=True),
        lax.psum_scatter(gate_weight_part, ("fsdp", "ctx"), scatter_dimension=0, tiled=True),
        lax.psum_scatter(up_weight_part, ("fsdp", "ctx"), scatter_dimension=0, tiled=True),
        lax.psum_scatter(down_weight_part, ("fsdp", "ctx"), scatter_dimension=1, tiled=True),
    )
    reduced = (
        lax.all_gather(part_one.astype(jnp.bfloat16), "ctx", axis=0, tiled=True).astype(
            part_one.dtype
        ),
        lax.all_gather(part_query.astype(jnp.bfloat16), "ctx", axis=0, tiled=True).astype(
            part_query.dtype
        ),
        lax.all_gather(part_key.astype(jnp.bfloat16), "ctx", axis=0, tiled=True).astype(
            part_key.dtype
        ),
        lax.all_gather(part_value.astype(jnp.bfloat16), "ctx", axis=0, tiled=True).astype(
            part_value.dtype
        ),
        lax.all_gather(part_project.astype(jnp.bfloat16), "ctx", axis=1, tiled=True).astype(
            part_project.dtype
        ),
        lax.all_gather(part_two.astype(jnp.bfloat16), "ctx", axis=0, tiled=True).astype(
            part_two.dtype
        ),
        lax.all_gather(part_gate.astype(jnp.bfloat16), "ctx", axis=0, tiled=True).astype(
            part_gate.dtype
        ),
        lax.all_gather(part_up.astype(jnp.bfloat16), "ctx", axis=0, tiled=True).astype(
            part_up.dtype
        ),
        lax.all_gather(part_down.astype(jnp.bfloat16), "ctx", axis=1, tiled=True).astype(
            part_down.dtype
        ),
    )
    return (layer_output, tokens_grad) + tuple(reduced)


def solution(mesh):
    return jax.shard_map(
        body,
        mesh=mesh,
        in_specs=(
            P("fsdp", "ctx", None),
            P("fsdp"),
            P("fsdp", "ctx"),
            P("fsdp"),
            P("fsdp", "tp"),
            P("fsdp", "tp"),
            P("fsdp", "tp"),
            P("tp", "fsdp"),
            P("fsdp"),
            P("fsdp", "tp"),
            P("fsdp", "tp"),
            P("tp", "fsdp"),
            P("fsdp", "ctx", None),
        ),
        out_specs=(
            P("fsdp", "ctx", None),
            P("fsdp", "ctx", None),
            P("fsdp"),
            P("fsdp", "tp"),
            P("fsdp", "tp"),
            P("fsdp", "tp"),
            P("tp", "fsdp"),
            P("fsdp"),
            P("fsdp", "tp"),
            P("fsdp", "tp"),
            P("tp", "fsdp"),
        ),
        check_vma=False,
    )
```

profile of v0, /device:TPU:0, one launch (start us, length us, event | category | flops | bytes accessed | tf_op | source)
XLA Modules:
  0.0 1445.3 jit_solution(7575975650537424681)
XLA Ops:
  13.1 13.6 all-gather.2
  28.1 24.4 %all_gather.76 = bf16[1536,192]{0,1:T(8,128)(2,1)S(1)} all-gather(bf16[384,192]{0,1:T(8,128)(2,1)} %param.22), channel_id=1, replica_groups=mesh['fsdp'=4,'ctx'=2,'tp'=4] {'fsdp'}, dimensions={0}, use_global_device_ids=true | all-gather | bytes 737280 | tf_op jit(solution)/shard_map/all_gather | solution.py:93
  57.0 8.5 all_gather.77
  65.6 25.2 %all_gather.79 = bf16[1536,192]{0,1:T(8,128)(2,1)S(1)} all-gather(bf16[384,192]{0,1:T(8,128)(2,1)S(1)} %copy-done.32), channel_id=1, replica_groups=mesh['fsdp'=4,'ctx'=2,'tp'=4] {'fsdp'}, dimensions={0}, use_global_device_ids=true | all-gather | bytes 737280 | tf_op jit(solution)/shard_map/all_gather | solution.py:94
  92.1 9.1 all-gather
  107.6 60.0 %while.39 = (s32[]{:T(128)}, f32[1,1024,2,2]{1,3,2,0:T(2,128)S(1)}, f32[1,1024,2,2]{1,3,2,0:T(2,128)}, f32[1,1024,2,2,96]{1,4,3,2,0:T(8,128)}, s32[1]{0:T(128)},...) while((s32[]{:T(128)}, f32[1,1024,2,2]{1,3,2,0:T(2,128)S(1)}, ...), condition=%wide.region_4.5_spmd.clone, body=%wide.region_1.4_spmd.clone.sunk | while | flops 1660193792 | bytes 132532552 | solution.py:189
  111.2 9.4 fusion.216
  121.4 9.4 bitcast_add_fusion.7
  133.1 3.6 fusion.218
  141.0 9.4 fusion.216
  151.2 9.8 bitcast_add_fusion.7
  163.3 3.6 fusion.218
  170.1 5.0 fusion.100
  176.9 12.6 all-gather.3
  189.5 56.2 %all-reduce.11.cloned.1.call-done = bf16[1,1024,1536]{2,1,0:T(8,128)(2,1)} async-done(((bf16[1,1024,1536]{2,1,0:T(8,128)(2,1)}), bf16[1,1024,1536]{2,1,0:T(8,128)(2,1)}) %all-reduce.11.cloned.1.call-update) | async-done | bytes 3145744 | tf_op jit(solution)/shard_map/psum | solution.py:62
  252.3 58.5 %all-gather.14.cloned.1.call-done = bf16[1536,1024]{1,0:T(8,128)(2,1)} async-done(((bf16[384,1024]{1,0:T(8,128)(2,1)}), bf16[1536,1024]{1,0:T(8,128)(2,1)}) %all-gather.14.cloned.1.call-update) | async-done | bytes 3145744 | tf_op jit(solution)/shard_map/all_gather | solution.py:97
  310.8 8.2 fusion.145
  319.0 55.4 %all-gather.16.cloned.1.call-done = bf16[1536,1024]{1,0:T(8,128)(2,1)} async-done(((bf16[384,1024]{1,0:T(8,128)(2,1)}), bf16[1536,1024]{1,0:T(8,128)(2,1)}) %all-gather.16.cloned.1.call-update) | async-done | bytes 3145744 | tf_op jit(solution)/shard_map/all_gather | solution.py:98
  374.4 8.3 fusion.146
  382.6 55.2 %all-gather.18.cloned.1.call-done = bf16[1024,1536]{1,0:T(8,128)(2,1)} async-done(((bf16[1024,384]{1,0:T(8,128)(2,1)}), bf16[1024,1536]{1,0:T(8,128)(2,1)}) %all-gather.18.cloned.1.call-update) | async-done | bytes 3145744 | tf_op jit(solution)/shard_map/all_gather | solution.py:99
  437.8 11.6 multiply_convert_fusion.1
  449.4 3.7 fusion.147
  453.1 4.9 fusion.97
  458.1 3.3 reshape.911
  463.9 11.4 all_gather.86
  476.6 48.6 %all-reduce.13.cloned.1.call-done = bf16[1,1024,1536]{2,1,0:T(8,128)(2,1)} async-done(((bf16[1,1024,1536]{2,1,0:T(8,128)(2,1)}), bf16[1,1024,1536]{2,1,0:T(8,128)(2,1)}) %all-reduce.13.cloned.1.call-update) | async-done | bytes 3145744 | tf_op jit(solution)/shard_map/psum | solution.py:62
  525.3 5.7 fusion.88
  537.7 85.3 %while.40 = (s32[]{:T(128)}, f32[1,1024,2,2,96]{1,4,3,2,0:T(8,128)}, bf16[2,1,1024,192]{2,3,1,0:T(8,128)(2,1)}, bf16[2,1,1024,192]{2,3,1,0:T(8,128)(2,1)}, bf16[...) while((s32[]{:T(128)}, ...), condition=%wide.region_12.13_spmd.clone, body=%wide.region_11.12_spmd.clone.sunk | while | flops 4072287232 | bytes 126814984 | solution.py:319
  542.1 8.1 fusion.229
  551.3 9.1 fusion.232
  563.7 9.5 fusion.233
  574.2 6.1 bitcast_add_fusion.8
  584.3 8.1 fusion.229
  593.5 9.1 fusion.232
  605.9 9.5 fusion.233
  616.4 6.5 bitcast_add_fusion.8
  623.8 16.9 %reduce-scatter.10.cloned.1.call-done = bf16[1,1,1024,192]{2,3,1,0:T(8,128)(2,1)} async-done(((bf16[2,1,1024,192]{2,3,1,0:T(8,128)(2,1)}), bf16[1,1,1024,192]{2,3,1,0:T(8,128)(2,1)}) %reduce-scatter.10.cloned.1.call-update) | async-done | bytes 393232 | tf_op jit(solution)/shard_map/reduce_scatter | solution.py:323
  645.3 15.3 %reduce-scatter.12.cloned.1.call-done = bf16[1,1,1024,192]{2,3,1,0:T(8,128)(2,1)} async-done(((bf16[2,1,1024,192]{2,3,1,0:T(8,128)(2,1)}), bf16[1,1,1024,192]{2,3,1,0:T(8,128)(2,1)}) %reduce-scatter.12.cloned.1.call-update) | async-done | bytes 393232 | tf_op jit(solution)/shard_map/reduce_scatter | solution.py:326
  660.6 3.4 fusion.118
  664.1 7.6 fusion.99
  679.4 4.7 fusion.114
  684.3 6.4 fusion.102
  690.8 8.7 fusion.150
  699.7 8.7 fusion.151
  708.5 8.6 fusion.106
  720.2 9.1 reduce-scatter.16.cloned.1.call-done
  730.3 5.3 all_gather.90
  736.4 61.1 %reduce-scatter.18.cloned.1.call-done = f32[192,192]{1,0:T(8,128)} async-done(((f32[1536,192]{1,0:T(8,128)}), f32[192,192]{1,0:T(8,128)}) %reduce-scatter.18.cloned.1.call-update) | async-done | bytes 147472 | tf_op jit(solution)/shard_map/reduce_scatter | solution.py:384
  798.5 5.5 all_gather.91
  804.9 114.2 %all-reduce.15.cloned.1.call-done = (bf16[1,1024,1536]{2,1,0:T(8,128)(2,1)}, bf16[1,1024,1536]{2,1,0:T(8,128)(2,1)}) async-done(((bf16[1,1024,1536]{2,1,0:T(8,128)(2,1)}, bf16[1,1024,1536]{2,1,0:T(8,128)(2,1)}), (bf16[1,1024,1536]{2,1,0:T(8,128)(2,1)}, bf16[1,1024,1536]{2,1,0:T(8,128)(2,1)})) %all-reduce.15.cloned.1.call-update) | async-done | bytes 6291472 | tf_op jit(solution)/shard_map/psum | solution.py:62
  919.1 4.2 fusion.95
  923.2 37.2 %all-reduce.4 = (bf16[1536]{0:T(1024)(128)(2,1)S(1)}, bf16[1536]{0:T(1024)(128)(2,1)S(1)}) all-reduce(f32[1536]{0:T(1024)S(1)} %get-tuple-element.622, f32[1536]{0:T(1024)S(1)} %copy-done.41), channel_id=5, replica_groups=mesh['fsdp'=4,'ctx'=2,'tp'=4] {'fsdp','ctx'}, use_global_device_ids=true, to_apply=%region_18.19.clone | all-reduce | flops 3072 | bytes 18432
  961.0 4.9 all-reduce.6
  967.1 25.2 %reduce-scatter.14.cloned.1.call-done = f32[192,384]{1,0:T(8,128)} async-done(((f32[1536,384]{1,0:T(8,128)}), f32[192,384]{1,0:T(8,128)}) %reduce-scatter.14.cloned.1.call-update) | async-done | bytes 294928 | tf_op jit(solution)/shard_map/reduce_scatter | solution.py:382
  993.3 5.8 all_gather.89
  999.9 63.7 %reduce-scatter.20.cloned.1.call-done = f32[384,192]{0,1:T(8,128)} async-done(((f32[384,1536]{0,1:T(8,128)}), f32[384,192]{0,1:T(8,128)}) %reduce-scatter.20.cloned.1.call-update) | async-done | bytes 294928 | tf_op jit(solution)/shard_map/reduce_scatter | solution.py:385
  1064.7 5.8 all_gather.92
  1071.5 9.2 fusion.83
  1080.7 103.4 %reduce-scatter.22.cloned.1.call-done = f32[192,1024]{1,0:T(8,128)} async-done(((f32[1536,1024]{1,0:T(8,128)}), f32[192,1024]{1,0:T(8,128)}) %reduce-scatter.22.cloned.1.call-update) | async-done | bytes 786448 | tf_op jit(solution)/shard_map/reduce_scatter | solution.py:387
  1185.3 12.2 all_gather.94
  1198.8 105.8 %reduce-scatter.24.cloned.1.call-done = f32[192,1024]{1,0:T(8,128)} async-done(((f32[1536,1024]{1,0:T(8,128)}), f32[192,1024]{1,0:T(8,128)}) %reduce-scatter.24.cloned.1.call-update) | async-done | bytes 786448 | tf_op jit(solution)/shard_map/reduce_scatter | solution.py:388
  1305.8 12.3 all_gather.95
  1319.5 105.7 %reduce-scatter.26.cloned.1.call-done = f32[1024,192]{0,1:T(8,128)} async-done(((f32[1024,1536]{0,1:T(8,128)}), f32[1024,192]{0,1:T(8,128)}) %reduce-scatter.26.cloned.1.call-update) | async-done | bytes 786448 | tf_op jit(solution)/shard_map/reduce_scatter | solution.py:389
  1426.4 10.7 all_gather.96
  (256 shorter events, 104.2 us)
Async XLA Ops:
  7.2 46.7 %copy-start.2 = (bf16[1,1024,1536]{2,1,0:T(8,128)(2,1)S(1)}, bf16[1,1024,1536]{2,1,0:T(8,128)(2,1)}, u32[]{:S(2)}) copy-start(bf16[1,1024,1536]{2,1,0:T(8,128)(2,1)} %param.17) | copy-start | bytes 9437188
  7.2 94.0 %all-gather.10.cloned.1.call-start = ((), (), s32[]{:S(2)}) async-start(), calls=%async_computation.9 | async-start | bytes 1474560 | tf_op jit(solution)/shard_map/all_gather | solution.py:92
  7.9 162.1 %all-gather.12.cloned.1.call-start = ((), (), s32[]{:S(2)}) async-start(), calls=%async_computation.10 | async-start | bytes 1474560 | tf_op jit(solution)/shard_map/all_gather | solution.py:95
  8.7 237.0 %all-reduce.11.cloned.1.call-start = ((), (), s32[]{:S(2)}) async-start(), calls=%async_computation.11 | async-start | bytes 6291456 | tf_op jit(solution)/shard_map/psum | solution.py:62
  52.5 3.6 copy-start.24
  53.9 52.5 %copy-start.11 = (f32[1024,48]{0,1:T(8,128)}, f32[1024,48]{0,1:T(8,128)S(1)}, u32[]{:S(2)}) copy-start(f32[1024,48]{0,1:T(8,128)S(1)} %get-tuple-element.697) | copy-start | bytes 589828
  53.9 52.5 %copy-start.13 = (f32[1024,48]{0,1:T(8,128)}, f32[1024,48]{0,1:T(8,128)S(1)}, u32[]{:S(2)}) copy-start(f32[1024,48]{0,1:T(8,128)S(1)} %get-tuple-element.698) | copy-start | bytes 589828
  53.9 11.7 copy-start.32
  56.1 34.7 %copy-start.35 = (f32[1536]{0:T(1024)S(1)}, f32[1536]{0:T(1024)}, u32[]{:S(2)}) copy-start(f32[1536]{0:T(1024)} %reshape.922) | copy-start | bytes 18436
  56.1 34.7 %copy-start.39 = (f32[1024]{0:T(1024)S(1)}, f32[1024]{0:T(1024)}, u32[]{:S(2)}) copy-start(f32[1024]{0:T(1024)} %get-tuple-element.700) | copy-start | bytes 12292
  121.4 11.4 copy-start.1
  121.4 11.6 copy-start.4
  133.1 3.7 copy-start.26
  151.2 11.9 copy-start.1
  151.2 12.1 copy-start.4
  163.3 3.7 copy-start.26
  175.1 135.7 %all-gather.14.cloned.1.call-start = ((), (), s32[]{:S(2)}) async-start(), calls=%async_computation.12 | async-start | bytes 3932160 | tf_op jit(solution)/shard_map/all_gather | solution.py:97
  175.7 198.7 %all-gather.16.cloned.1.call-start = ((), (), s32[]{:S(2)}) async-start(), calls=%async_computation.13 | async-start | bytes 3932160 | tf_op jit(solution)/shard_map/all_gather | solution.py:98
  176.3 261.6 %all-gather.18.cloned.1.call-start = ((), (), s32[]{:S(2)}) async-start(), calls=%async_computation.14 | async-start | bytes 3932160 | tf_op jit(solution)/shard_map/all_gather | solution.py:99
  176.8 348.4 %all-reduce.13.cloned.1.call-start = ((), (), s32[]{:S(2)}) async-start(), calls=%async_computation.15 | async-start | bytes 6291456 | tf_op jit(solution)/shard_map/psum | solution.py:62
  189.5 62.8 %copy-start.33 = (f32[1536]{0:T(1024)}, f32[1536]{0:T(1024)S(1)}, u32[]{:S(2)}) copy-start(f32[1536]{0:T(1024)S(1)} %reshape.923) | copy-start | bytes 18436
  245.7 3.7 copy-start.6
  249.4 2.8 copy-start.37
  437.8 11.6 copy-start.46
  449.4 3.7 copy-start.52
  449.4 3.7 copy-start.51
  449.4 3.7 copy-start.47
  458.0 5.8 copy-start.18
  458.1 182.7 %reduce-scatter.10.cloned.1.call-start = ((), (), s32[]{:S(2)}) async-start(), calls=%async_computation.16 | async-start | bytes 1179648 | tf_op jit(solution)/shard_map/reduce_scatter | solution.py:323
  476.6 54.4 %copy-start.34 = (f32[1536]{0:T(1024)S(1)}, f32[1536]{0:T(1024)}, u32[]{:S(2)}) copy-start(f32[1536]{0:T(1024)} %copy-done.33) | copy-start | bytes 18436
  476.6 54.4 %copy-start.38 = (f32[1024]{0:T(1024)S(1)}, f32[1024]{0:T(1024)}, u32[]{:S(2)}) copy-start(f32[1024]{0:T(1024)} %copy-done.37) | copy-start | bytes 12292
  476.6 54.4 %copy-start.43 = (f32[1024]{0:T(1024)S(1)}, f32[1024]{0:T(1024)}, u32[]{:S(2)}) copy-start(f32[1024]{0:T(1024)} %get-tuple-element.701) | copy-start | bytes 12292
  525.3 5.8 copy-start.7
  525.3 5.8 copy-start.9
  525.3 5.8 copy-start.19
  531.0 2.7 copy-start.48
  533.8 3.0 copy-start.8
  533.8 3.0 copy-start.10
  533.8 3.0 copy-start.28
  533.8 3.8 copy-start.5
  533.8 3.8 copy-start.44
  537.7 104.2 %copy-start.12 = (f32[1024,48]{0,1:T(8,128)S(1)}, f32[1024,48]{0,1:T(8,128)}, u32[]{:S(2)}) copy-start(f32[1024,48]{0,1:T(8,128)} %copy-done.11) | copy-start | bytes 589828
  537.7 104.2 %copy-start.14 = (f32[1024,48]{0,1:T(8,128)S(1)}, f32[1024,48]{0,1:T(8,128)}, u32[]{:S(2)}) copy-start(f32[1024,48]{0,1:T(8,128)} %copy-done.13) | copy-start | bytes 589828
  542.1 9.2 copy-start.30
  560.4 3.3 copy-start
  584.3 9.2 copy-start.30
  602.6 3.3 copy-start
  623.0 19.8 %copy-start.3 = (bf16[1,1024,1536]{2,1,0:T(8,128)(2,1)S(1)}, bf16[1,1024,1536]{2,1,0:T(8,128)(2,1)}, u32[]{:S(2)}) copy-start(bf16[1,1024,1536]{2,1,0:T(8,128)(2,1)} %param.17) | copy-start | bytes 9437188
  623.0 19.8 %copy-start.36 = (f32[1536]{0:T(1024)S(1)}, f32[1536]{0:T(1024)}, u32[]{:S(2)}) copy-start(f32[1536]{0:T(1024)} %reshape.922) | copy-start | bytes 18436
  623.0 19.8 %copy-start.40 = (f32[1024]{0:T(1024)S(1)}, f32[1024]{0:T(1024)}, u32[]{:S(2)}) copy-start(f32[1024]{0:T(1024)} %get-tuple-element.700) | copy-start | bytes 12292
  623.1 37.5 %reduce-scatter.12.cloned.1.call-start = ((), (), s32[]{:S(2)}) async-start(), calls=%async_computation.17 | async-start | bytes 1179648 | tf_op jit(solution)/shard_map/reduce_scatter | solution.py:326
  623.8 105.5 %reduce-scatter.16.cloned.1.call-start = ((), (), s32[]{:S(2)}) async-start(), calls=%async_computation.19 | async-start | bytes 1769472 | tf_op jit(solution)/shard_map/reduce_scatter | solution.py:383
  645.2 152.3 %reduce-scatter.18.cloned.1.call-start = ((), (), s32[]{:S(2)}) async-start(), calls=%async_computation.20 | async-start | bytes 1769472 | tf_op jit(solution)/shard_map/reduce_scatter | solution.py:384
  664.0 255.1 %all-reduce.15.cloned.1.call-start = ((), (), s32[]{:S(2)}) async-start(), calls=%async_computation.25 | async-start | bytes 12582912 | tf_op jit(solution)/shard_map/psum | solution.py:62
  673.4 1.9 copy-start.16
  673.5 1.9 copy-start.21
  679.3 312.9 %reduce-scatter.14.cloned.1.call-start = ((), (), s32[]{:S(2)}) async-start(), calls=%async_computation.18 | async-start | bytes 2654208 | tf_op jit(solution)/shard_map/reduce_scatter | solution.py:382
  684.1 379.6 %reduce-scatter.20.cloned.1.call-start = ((), (), s32[]{:S(2)}) async-start(), calls=%async_computation.21 | async-start | bytes 2654208 | tf_op jit(solution)/shard_map/reduce_scatter | solution.py:385
  690.8 493.3 %reduce-scatter.22.cloned.1.call-start = ((), (), s32[]{:S(2)}) async-start(), calls=%async_computation.22 | async-start | bytes 7077888 | tf_op jit(solution)/shard_map/reduce_scatter | solution.py:387
  699.6 605.1 %reduce-scatter.24.cloned.1.call-start = ((), (), s32[]{:S(2)}) async-start(), calls=%async_computation.23 | async-start | bytes 7077888 | tf_op jit(solution)/shard_map/reduce_scatter | solution.py:388
  708.4 716.8 %reduce-scatter.26.cloned.1.call-start = ((), (), s32[]{:S(2)}) async-start(), calls=%async_computation.24 | async-start | bytes 7077888 | tf_op jit(solution)/shard_map/reduce_scatter | solution.py:389
  717.0 1.9 copy-start.49
  720.2 203.0 %copy-start.41 = (f32[1536]{0:T(1024)S(1)}, f32[1536]{0:T(1024)}, u32[]{:S(2)}) copy-start(f32[1536]{0:T(1024)} %get-tuple-element.620) | copy-start | bytes 18436
  919.1 152.4 %copy-start.42 = (f32[1024]{0:T(1024)S(1)}, f32[1024]{0:T(1024)}, u32[]{:S(2)}) copy-start(f32[1024]{0:T(1024)} %get-tuple-element.699) | copy-start | bytes 12292
  (12 other events, 13.3 us)
Sparse Core Ops, SparseCore 0:
  9.6 42.5 all-gather.9
  53.8 38.7 all-gather.11
  175.2 70.4 all-reduce.10
  247.1 63.5 all-gather.13
  312.2 62.1 all-gather.15
  375.8 61.9 all-gather.17
  458.2 67.0 all-reduce.12
  623.2 17.5 reduce-scatter.9
  643.1 17.4 reduce-scatter.11
  664.4 64.8 reduce-scatter.15
  733.7 63.7 reduce-scatter.17
  800.4 118.6 all-reduce.14
  922.6 69.6 reduce-scatter.13
  995.6 67.9 reduce-scatter.19
  1067.1 116.9 reduce-scatter.21
  1187.5 117.0 reduce-scatter.23
  1308.1 117.0 reduce-scatter.25
where the time goes:
time: 1450 us
  waiting for transfers between devices  898 us (62%)
  matrix products  215 us (15%)
  blocking collectives  205 us (14%)
  other arithmetic  72 us (5%)
  local copies, waits for them, and re-layouts  36 us (2%)
  between operations  16.2 us (1%)
    psum x3, waiting for transfers between devices, tensor_sum(): return lax.psum(term_rows.astype(jnp.bfloat16), 'tp').astype(jnp.float32)  219 us
    reduce_scatter x1, waiting for transfers between devices, body(): lax.psum_scatter(up_weight_part, ('fsdp', 'ctx'), scatter_dimension=0, ti...  106 us
    reduce_scatter x1, waiting for transfers between devices, body(): lax.psum_scatter(down_weight_part, ('fsdp', 'ctx'), scatter_dimension=1,...  106 us
    reduce_scatter x1, waiting for transfers between devices, body(): lax.psum_scatter(gate_weight_part, ('fsdp', 'ctx'), scatter_dimension=0,...  103 us
    reduce_scatter x1, waiting for transfers between devices, body(): lax.psum_scatter(project_term, ('fsdp', 'ctx'), scatter_dimension=1, tile...  63.7 us
    reduce_scatter x1, waiting for transfers between devices, body(): lax.psum_scatter(value_weight_part, ('fsdp', 'ctx'), scatter_dimension=0,...  61.1 us
    all_gather x1, waiting for transfers between devices, body(): lax.all_gather(w_gate, 'fsdp', axis=0, tiled=True)  58.5 us
    all_gather x1, waiting for transfers between devices, body(): lax.all_gather(w_up, 'fsdp', axis=0, tiled=True)  55.4 us
  transfers between devices with their start and end apart: 17, of which 15 were waited for; matrix products, arithmetic and copies ran while one was open for 13% of the time, Pallas kernels for 0%

commit v1 on v0

--- a/solution.py
+++ b/solution.py
@@ -3,6 +3,8 @@
 import jax
 import jax.numpy as jnp
 from jax import lax
+from jax.experimental import pallas as pl
+from jax.experimental.pallas import tpu as pltpu
 from jax.sharding import PartitionSpec as P
 
 HQ = 16
@@ -62,7 +64,7 @@
     return lax.psum(term_rows.astype(jnp.bfloat16), "tp").astype(jnp.float32)
 
 
-def body(
+def general_body(
     tokens,
     prefix_len,
     positions,
@@ -420,9 +422,562 @@
     return (layer_output, tokens_grad) + tuple(reduced)
 
 
+LANES = 128
+HALF = HD // 2
+SPAN = LANES // 2
+LOG2E = math.log2(math.e)
+VMEM_BYTES = 56 * 1024 * 1024
+
+
+def swap_ctx(block):
+    return lax.ppermute(block, "ctx", [(0, 1), (1, 0)])
+
+
+def swap_core(block):
+    return lax.ppermute(block, "tp", [(0, 1), (1, 0), (2, 3), (3, 2)])
+
+
+def swap_chip(block):
+    return lax.ppermute(block, "tp", [(0, 2), (2, 0), (1, 3), (3, 1)])
+
+
+def paired_tensor_sum(term_rows):
+    half = term_rows.shape[0] // 2
+    core = lax.axis_index("tp") % 2
+    low = term_rows.astype(jnp.bfloat16)
+    keep = lax.dynamic_slice_in_dim(low, core * half, half, 0)
+    give = lax.dynamic_slice_in_dim(low, (1 - core) * half, half, 0)
+    chip_part = (keep.astype(jnp.float32) + swap_core(give).astype(jnp.float32)).astype(jnp.bfloat16)
+    total = (chip_part.astype(jnp.float32) + swap_chip(chip_part).astype(jnp.float32)).astype(
+        jnp.bfloat16
+    )
+    other = swap_core(total)
+    return jnp.where(
+        core == 0,
+        jnp.concatenate([total, other], axis=0),
+        jnp.concatenate([other, total], axis=0),
+    ).astype(jnp.float32)
+
+
+def spread_turned(columns):
+    rows, width = columns.shape
+    parts = columns.reshape(rows, width // HD, 2, HALF)
+    return jnp.pad(parts, ((0, 0), (0, 0), (0, 0), (0, SPAN - HALF))).reshape(
+        rows, width // HD * LANES
+    )
+
+
+def spread_plain(columns):
+    rows, width = columns.shape
+    parts = columns.reshape(rows, width // HD, HD)
+    return jnp.pad(parts, ((0, 0), (0, 0), (0, LANES - HD))).reshape(rows, width // HD * LANES)
+
+
+def close_turned(columns):
+    rows, width = columns.shape
+    return columns.reshape(rows, width // SPAN, SPAN)[..., :HALF].reshape(
+        rows, width // SPAN * HALF
+    )
+
+
+def close_plain(columns):
+    rows, width = columns.shape
+    return columns.reshape(rows, width // LANES, LANES)[..., :HD].reshape(
+        rows, width // LANES * HD
+    )
+
+
+def dot(a, b, contract):
+    return lax.dot_general(a, b, (contract, ((), ())), preferred_element_type=jnp.float32)
+
+
+def project_kernel(x_ref, gain_ref, w_ref, cos_ref, sin_ref, normed_ref, q_ref, kv_ref):
+    x = x_ref[...].astype(jnp.float32)
+    factor = lax.rsqrt(jnp.mean(x * x, axis=-1, keepdims=True) + EPSILON)
+    normed = (x * factor * gain_ref[...].astype(jnp.float32)).astype(jnp.bfloat16)
+    normed_ref[...] = normed
+    cosine = cos_ref[...]
+    sine = sin_ref[...]
+    q_tiles = q_ref.shape[1] // LANES
+    tiles = w_ref.shape[1] // LANES
+    turned = q_tiles + (tiles - q_tiles) // 2
+    scale = HD ** (-0.5) * LOG2E
+    for pair in range(tiles // 2):
+        wide = dot(normed, w_ref[:, pair * 2 * LANES : (pair + 1) * 2 * LANES], ((1,), (0,)))
+        for side in range(2):
+            tile = 2 * pair + side
+            part = wide[:, side * LANES : (side + 1) * LANES]
+            if tile < turned:
+                part = part * cosine + pltpu.roll(part, SPAN, 1) * sine
+            if tile < q_tiles:
+                q_ref[:, tile * LANES : (tile + 1) * LANES] = (part * scale).astype(jnp.bfloat16)
+            else:
+                lane = (tile - q_tiles) * LANES
+                kv_ref[:, lane : lane + LANES] = part.astype(jnp.bfloat16)
+
+
+def project_tokens(x, gain, weights, cosine, sine, q_width):
+    rows, width = x.shape
+    out_width = weights.shape[1]
+    tile = min(256, rows)
+    return pl.pallas_call(
+        project_kernel,
+        grid=(rows // tile,),
+        in_specs=[
+            pl.BlockSpec((tile, width), lambda i: (i, 0)),
+            pl.BlockSpec((1, width), lambda i: (0, 0)),
+            pl.BlockSpec((width, out_width), lambda i: (0, 0)),
+            pl.BlockSpec((tile, LANES), lambda i: (i, 0)),
+            pl.BlockSpec((tile, LANES), lambda i: (i, 0)),
+        ],
+        out_specs=[
+            pl.BlockSpec((tile, width), lambda i: (i, 0)),
+            pl.BlockSpec((tile, q_width), lambda i: (i, 0)),
+            pl.BlockSpec((tile, out_width - q_width), lambda i: (i, 0)),
+        ],
+        out_shape=[
+            jax.ShapeDtypeStruct((rows, width), jnp.bfloat16),
+            jax.ShapeDtypeStruct((rows, q_width), jnp.bfloat16),
+            jax.ShapeDtypeStruct((rows, out_width - q_width), jnp.bfloat16),
+        ],
+        compiler_params=pltpu.CompilerParams(vmem_limit_bytes=VMEM_BYTES),
+        name="project_tokens",
+    )(x, gain, weights, cosine, sine)
+
+
+def block_kinds(meta_ref, query_tile, key_tile, q_start, k_start):
+    prefix = meta_ref[0]
+    whole = (k_start + (key_tile - 1) <= q_start) | (k_start + key_tile <= prefix)
+    nothing = (k_start > q_start + (query_tile - 1)) & (k_start >= prefix)
+    return prefix, whole, nothing
+
+
+def mask_scores(scores, prefix, q_start, k_start, query_tile):
+    key_ids = k_start + lax.broadcasted_iota(jnp.int32, scores.shape, 0)
+    column = lax.broadcasted_iota(jnp.int32, scores.shape, 1)
+    query_ids = q_start + jnp.bitwise_and(column, query_tile - 1)
+    return jnp.where((key_ids <= query_ids) | (key_ids < prefix), scores, NEGATIVE)
+
+
+def attend_kernel(meta_ref, q_ref, k_ref, v_ref, o_ref, lse_ref, max_ref, sum_ref, acc_ref):
+    tile = q_ref.shape[0]
+    key_tile = tile
+    query_tiles = pl.num_programs(1)
+    step = pl.program_id(1)
+    q_start = meta_ref[1 + step]
+    queries = jnp.concatenate([q_ref[:, :LANES], q_ref[:, LANES:]], axis=0)
+    max_ref[...] = jnp.full_like(max_ref, NEGATIVE)
+    sum_ref[...] = jnp.zeros_like(sum_ref)
+    acc_ref[...] = jnp.zeros_like(acc_ref)
+
+    def absorb(scores, values):
+        old = max_ref[...]
+        new = jnp.maximum(old, jnp.max(scores, axis=0, keepdims=True))
+        weights = jnp.exp2(scores - new)
+        rescale = jnp.exp2(old - new)
+        max_ref[...] = new
+        sum_ref[...] = sum_ref[...] * rescale + jnp.sum(weights, axis=0, keepdims=True)
+        acc_ref[...] = acc_ref[...] * rescale + dot(
+            values, weights.astype(jnp.bfloat16), ((0,), (0,))
+        )
+
+    def one(j, carry):
+        k_start = meta_ref[1 + query_tiles + j]
+        prefix, whole, nothing = block_kinds(meta_ref, tile, key_tile, q_start, k_start)
+        rows = pl.ds(pl.multiple_of(j * key_tile, key_tile), key_tile)
+
+        @pl.when(whole)
+        def _():
+            absorb(dot(k_ref[rows, :], queries, ((1,), (1,))), v_ref[rows, :])
+
+        @pl.when(jnp.logical_not(whole | nothing))
+        def _():
+            scores = dot(k_ref[rows, :], queries, ((1,), (1,)))
+            absorb(mask_scores(scores, prefix, q_start, k_start, tile), v_ref[rows, :])
+
+        return carry
+
+    lax.fori_loop(0, k_ref.shape[0] // key_tile, one, 0)
+    total = sum_ref[...]
+    lse_ref[0, 0] = max_ref[...] + jnp.log2(total)
+    out = (acc_ref[...] / total).T.astype(jnp.bfloat16)
+    o_ref[:, :LANES] = out[:tile]
+    o_ref[:, LANES:] = out[tile:]
+
+
+def attend(meta, q, kv, tile):
+    rows, q_width = q.shape
+    keys = kv.shape[0]
+    groups = q_width // (2 * LANES)
+    steps = rows // tile
+    return pl.pallas_call(
+        attend_kernel,
+        grid_spec=pltpu.PrefetchScalarGridSpec(
+            num_scalar_prefetch=1,
+            grid=(groups, steps),
+            in_specs=[
+                pl.BlockSpec((tile, 2 * LANES), lambda g, i, m: (i, g)),
+                pl.BlockSpec((keys, LANES), lambda g, i, m: (0, g)),
+                pl.BlockSpec((keys, LANES), lambda g, i, m: (0, groups + g)),
+            ],
+            out_specs=[
+                pl.BlockSpec((tile, 2 * LANES), lambda g, i, m: (i, g)),
+                pl.BlockSpec((1, 1, 1, 2 * tile), lambda g, i, m: (g, i, 0, 0)),
+            ],
+            scratch_shapes=[
+                pltpu.VMEM((1, 2 * tile), jnp.float32),
+                pltpu.VMEM((1, 2 * tile), jnp.float32),
+                pltpu.VMEM((LANES, 2 * tile), jnp.float32),
+            ],
+        ),
+        out_shape=[
+            jax.ShapeDtypeStruct((rows, q_width), jnp.bfloat16),
+            jax.ShapeDtypeStruct((groups, steps, 1, 2 * tile), jnp.float32),
+        ],
+        compiler_params=pltpu.CompilerParams(vmem_limit_bytes=VMEM_BYTES),
+        cost_estimate=pl.CostEstimate(
+            flops=8 * rows * keys * LANES * groups, bytes_accessed=6_000_000, transcendentals=0
+        ),
+        name="attend",
+    )(meta, q, kv, kv)
+
+
+def attend_back_kernel(
+    meta_ref,
+    q_ref,
+    k_ref,
+    v_ref,
+    o_ref,
+    do_ref,
+    lse_ref,
+    cos_ref,
+    sin_ref,
+    dq_ref,
+    dk_ref,
+    dv_ref,
+    delta_ref,
+    acc_ref,
+):
+    query_tiles = lse_ref.shape[1]
+    tile = q_ref.shape[0] // query_tiles
+    key_tile = k_ref.shape[0]
+    j = pl.program_id(1)
+
+    def stacked(ref, i):
+        rows = pl.ds(pl.multiple_of(i * tile, tile), tile)
+        return jnp.concatenate([ref[rows, :LANES], ref[rows, LANES:]], axis=0)
+
+    @pl.when(j == 0)
+    def _():
+        acc_ref[...] = jnp.zeros_like(acc_ref)
+
+        def one_delta(i, carry):
+            product = stacked(o_ref, i).astype(jnp.float32) * stacked(do_ref, i).astype(jnp.float32)
+            delta_ref[i] = jnp.sum(product.T, axis=0, keepdims=True)
+            return carry
+
+        lax.fori_loop(0, query_tiles, one_delta, 0)
+
+    k_start = meta_ref[1 + query_tiles + j]
+    keys = k_ref[...]
+    values = v_ref[...]
+
+    def one(i, carry):
+        q_start = meta_ref[1 + i]
+        prefix, whole, nothing = block_kinds(meta_ref, tile, key_tile, q_start, k_start)
+
+        def some(state):
+            dk, dv = state
+            queries = stacked(q_ref, i)
+            d_out = stacked(do_ref, i)
+            scores = dot(keys, queries, ((1,), (1,)))
+            scores = lax.cond(
+                whole,
+                lambda s: s,
+                lambda s: mask_scores(s, prefix, q_start, k_start, tile),
+                scores,
+            )
+            weights = jnp.exp2(scores - lse_ref[0, i])
+            d_weights = dot(values, d_out, ((1,), (1,)))
+            d_scores = (weights * (d_weights - delta_ref[i])).astype(jnp.bfloat16)
+            dv = dv + dot(weights.astype(jnp.bfloat16), d_out, ((1,), (0,)))
+            dk = dk + dot(d_scores, queries, ((1,), (0,)))
+            acc_ref[i] += dot(keys, d_scores, ((0,), (0,)))
+            return dk, dv
+
+        return lax.cond(nothing, lambda state: state, some, carry)
+
+    zero = jnp.zeros((key_tile, LANES), jnp.float32)
+    dk, dv = lax.fori_loop(0, query_tiles, one, (zero, zero))
+    dk_ref[...] = (dk * (1.0 / LOG2E)).astype(jnp.bfloat16)
+    dv_ref[...] = dv.astype(jnp.bfloat16)
+
+    @pl.when(j == pl.num_programs(1) - 1)
+    def _():
+        scale = HD ** (-0.5)
+
+        def one_out(i, carry):
+            rows = pl.ds(pl.multiple_of(i * tile, tile), tile)
+            turned = acc_ref[i].T * scale
+            for head in range(2):
+                part = turned[head * tile : (head + 1) * tile]
+                part = part * cos_ref[rows, :] - pltpu.roll(part, SPAN, 1) * sin_ref[rows, :]
+                dq_ref[rows, head * LANES : (head + 1) * LANES] = part.astype(jnp.bfloat16)
+            return carry
+
+        lax.fori_loop(0, query_tiles, one_out, 0)
+
+
+def attend_back(meta, q, kv, o, d_out, lse, cosine, sine, tile):
+    rows, q_width = q.shape
+    keys = kv.shape[0]
+    groups = q_width // (2 * LANES)
+    query_tiles = rows // tile
+    key_tiles = keys // tile
+    whole_q = pl.BlockSpec((rows, 2 * LANES), lambda g, j, m: (0, g))
+    return pl.pallas_call(
+        attend_back_kernel,
+        grid_spec=pltpu.PrefetchScalarGridSpec(
+            num_scalar_prefetch=1,
+            grid=(groups, key_tiles),
+            in_specs=[
+                whole_q,
+                pl.BlockSpec((tile, LANES), lambda g, j, m: (j, g)),
+                pl.BlockSpec((tile, LANES), lambda g, j, m: (j, groups + g)),
+                whole_q,
+                whole_q,
+                pl.BlockSpec((1, query_tiles, 1, 2 * tile), lambda g, j, m: (g, 0, 0, 0)),
+                pl.BlockSpec((rows, LANES), lambda g, j, m: (0, 0)),
+                pl.BlockSpec((rows, LANES), lambda g, j, m: (0, 0)),
+            ],
+            out_specs=[
+                whole_q,
+                pl.BlockSpec((tile, LANES), lambda g, j, m: (j, g)),
+                pl.BlockSpec((tile, LANES), lambda g, j, m: (j, g)),
+            ],
+            scratch_shapes=[
+                pltpu.VMEM((query_tiles, 1, 2 * tile), jnp.float32),
+                pltpu.VMEM((query_tiles, LANES, 2 * tile), jnp.float32),
+            ],
+        ),
+        out_shape=[
+            jax.ShapeDtypeStruct((rows, q_width), jnp.bfloat16),
+            jax.ShapeDtypeStruct((keys, groups * LANES), jnp.bfloat16),
+            jax.ShapeDtypeStruct((keys, groups * LANES), jnp.bfloat16),
+        ],
+        compiler_params=pltpu.CompilerParams(vmem_limit_bytes=VMEM_BYTES),
+        cost_estimate=pl.CostEstimate(
+            flops=20 * rows * keys * LANES * groups, bytes_accessed=8_000_000, transcendentals=0
+        ),
+        name="attend_back",
+    )(meta, q, kv, kv, o, d_out, lse, cosine, sine)
+
+
+def paired_body(
+    tokens,
+    prefix_len,
+    positions,
+    gain_attend,
+    w_query,
+    w_key,
+    w_value,
+    w_project,
+    gain_feed,
+    w_gate,
+    w_up,
+    w_down,
+    cotangent,
+):
+    seqs, rows, width = tokens.shape
+    assert seqs == 1
+    c = lax.axis_index("ctx")
+    bf16, f32 = jnp.bfloat16, jnp.float32
+
+    def half(array, axis, which=None):
+        size = array.shape[axis] // 2
+        which = c if which is None else which
+        return lax.dynamic_slice_in_dim(array, which * size, size, axis)
+
+    def ordered(mine, other, axis):
+        return jnp.where(
+            c == 0,
+            jnp.concatenate([mine, other], axis=axis),
+            jnp.concatenate([other, mine], axis=axis),
+        )
+
+    def gathered(mine, axis):
+        whole = lax.all_gather(mine, "fsdp", axis=axis, tiled=True)
+        return whole, swap_ctx(whole)
+
+    gains = lax.all_gather(jnp.stack([gain_attend, gain_feed]), "fsdp", axis=1, tiled=True)
+    gain_one, gain_two = gains[:1].astype(f32), gains[1:].astype(f32)
+    qkv_mine, qkv_other = gathered(
+        jnp.concatenate([half(w_query, 1), half(w_key, 1), half(w_value, 1)], axis=1), 0
+    )
+    wp_mine, wp_other = gathered(half(w_project, 0), 1)
+    wg_mine, wg_other = gathered(half(w_gate, 1), 0)
+    wu_mine, wu_other = gathered(half(w_up, 1), 0)
+    wd_mine, wd_other = gathered(half(w_down, 0), 1)
+
+    kv_half = w_key.shape[1] // 2
+    q_half = w_query.shape[1] // 2
+
+    def parts(block):
+        return (
+            block[:, :q_half],
+            block[:, q_half : q_half + kv_half],
+            block[:, q_half + kv_half :],
+        )
+
+    mine, other = parts(qkv_mine), parts(qkv_other)
+    w_qkv = jnp.concatenate(
+        [spread_turned(jnp.concatenate([mine[0], other[0], mine[1], other[1]], axis=1)),
+         spread_plain(jnp.concatenate([mine[2], other[2]], axis=1))],
+        axis=1,
+    )
+    q_width = 2 * q_half // HD * LANES
+    kv_width = 2 * kv_half // HD * LANES
+
+    frequency = ROPE_BASE ** (-(jnp.arange(HALF, dtype=f32) * 2.0 / HD))
+    frequency = jnp.pad(frequency, (0, SPAN - HALF))
+    angles = positions[0].astype(f32)[:, None] * frequency
+    cosine = jnp.cos(angles)
+    sine = jnp.sin(angles)
+    cosine = jnp.concatenate([cosine, cosine], axis=1)
+    sine = jnp.concatenate([-sine, sine], axis=1)
+
+    block_len = rows // 2
+    tile = min(256, block_len)
+    query_tiles = rows // tile
+    own = c * rows + tile * jnp.arange(query_tiles, dtype=jnp.int32)
+    opposite = (1 - c) * rows + tile * jnp.arange(query_tiles, dtype=jnp.int32)
+    own, opposite = natural_index(own, block_len, 2), natural_index(opposite, block_len, 2)
+    meta = jnp.concatenate([prefix_len.astype(jnp.int32), own, own, opposite])
+
+    x = tokens[0]
+    cot = cotangent[0]
+    normed, q, kv = project_tokens(x, gain_one, w_qkv, cosine, sine, q_width)
+    kv_away = swap_ctx(kv)
+    kv_away = kv_away.reshape(rows, 2, 2, kv_width // 2)[:, :, ::-1].reshape(rows, 2 * kv_width)
+    kv_all = jnp.concatenate([kv, kv_away], axis=0)
+    o, lse = attend(meta, q, kv_all, tile)
+    o_low = close_plain(o)
+    w_p = jnp.concatenate([wp_mine, wp_other], axis=0)
+    middle = x.astype(f32) + paired_tensor_sum(dot(o_low, w_p, ((1,), (0,))))
+    factor_two = rms_factor(middle)
+    normed_feed = (middle * factor_two * gain_two).astype(bf16)
+
+    def feed(wg, wu, wd):
+        gate = dot(normed_feed, wg, ((1,), (0,)))
+        up = dot(normed_feed, wu, ((1,), (0,)))
+        sigmoid = jax.nn.sigmoid(gate)
+        silu = gate * sigmoid
+        hidden = (silu * up).astype(bf16)
+        hidden_in = dot(cot, wd, ((1,), (1,)))
+        gate_back = (hidden_in * up * sigmoid * (1.0 + gate * (1.0 - sigmoid))).astype(bf16)
+        up_back = (hidden_in * silu).astype(bf16)
+        feed_rows = dot(gate_back, wg, ((1,), (1,))) + dot(up_back, wu, ((1,), (1,)))
+        return hidden, gate_back, up_back, feed_rows
+
+    hidden_m, gate_back_m, up_back_m, feed_m = feed(wg_mine, wu_mine, wd_mine)
+    hidden_o, gate_back_o, up_back_o, feed_o = feed(wg_other, wu_other, wd_other)
+    feed_in = paired_tensor_sum(feed_m + feed_o)
+
+    def summed(give, keep, axis):
+        both = (keep + swap_ctx(give.astype(bf16)).astype(f32)).astype(bf16)
+        share = lax.psum_scatter(both, "fsdp", scatter_dimension=axis, tiled=True)
+        return share
+
+    def whole_again(share, axis):
+        return ordered(share, swap_ctx(share), axis).astype(f32)
+
+    contract_rows = ((0,), (0,))
+    gate_share = summed(
+        dot(normed_feed, gate_back_o, contract_rows), dot(normed_feed, gate_back_m, contract_rows), 0
+    )
+    up_share = summed(
+        dot(normed_feed, up_back_o, contract_rows), dot(normed_feed, up_back_m, contract_rows), 0
+    )
+    down_part = jnp.concatenate(
+        [dot(hidden_m, cot, contract_rows), dot(hidden_o, cot, contract_rows)], axis=0
+    ).astype(bf16)
+    down_share = lax.psum_scatter(down_part, "fsdp", scatter_dimension=1, tiled=True)
+    down_away = swap_ctx(down_share)
+    size = down_share.shape[0] // 2
+    down_mine = down_share[:size].astype(f32) + down_away[size:].astype(f32)
+    down_other = down_share[size:].astype(f32) + down_away[:size].astype(f32)
+    down_grad = ordered(down_mine, down_other, 0)
+
+    layer_output = (
+        middle
+        + paired_tensor_sum(
+            dot(hidden_m, wd_mine, ((1,), (0,))) + dot(hidden_o, wd_other, ((1,), (0,)))
+        )
+    ).astype(bf16)
+
+    gain_two_term = jnp.sum(feed_in * middle * factor_two, axis=0)
+    middle_grad = cot.astype(f32) + rms_back(middle, factor_two, gain_two, feed_in)
+    middle_low = middle_grad.astype(bf16)
+    project_part = dot(o_low, middle_low, contract_rows)
+    rows_half = project_part.shape[0] // 2
+    project_share = summed(project_part[rows_half:], project_part[:rows_half], 1)
+    d_out = spread_plain(dot(middle_low, w_p, ((1,), (1,))).astype(bf16))
+    q_low, dk, dv = attend_back(meta, q, kv_all, o, d_out, lse, cosine, sine, tile)
+    d_kv = jnp.concatenate([dk, dv], axis=1)
+    d_kv_away = swap_ctx(d_kv[rows:])
+    d_kv_away = d_kv_away.reshape(rows, 2, 2, kv_width // 2)[:, :, ::-1].reshape(rows, 2 * kv_width)
+    d_kv = d_kv[:rows].astype(f32) + d_kv_away.astype(f32)
+    key_turned = d_kv[:, :kv_width].reshape(rows, 2, 2, SPAN)
+    sine_half, cosine_half = sine[:, None, SPAN:], cosine[:, None, SPAN:]
+    k_low = jnp.stack(
+        [
+            key_turned[:, :, 0] * cosine_half + key_turned[:, :, 1] * sine_half,
+            key_turned[:, :, 1] * cosine_half - key_turned[:, :, 0] * sine_half,
+        ],
+        axis=2,
+    )
+    k_low = k_low.reshape(rows, kv_width).astype(bf16)
+    v_low = d_kv[:, kv_width:].astype(bf16)
+    low = jnp.concatenate([q_low, k_low, v_low], axis=1)
+    normed_in = paired_tensor_sum(dot(low, w_qkv, ((1,), (1,))))
+    qc, kc, vc = close_turned(q_low), close_turned(k_low), close_plain(v_low)
+    low_mine = jnp.concatenate([qc[:, :q_half], kc[:, :kv_half], vc[:, :kv_half]], axis=1)
+    low_other = jnp.concatenate([qc[:, q_half:], kc[:, kv_half:], vc[:, kv_half:]], axis=1)
+    qkv_share = summed(
+        dot(normed, low_other, contract_rows), dot(normed, low_mine, contract_rows), 0
+    )
+    qkv_away = swap_ctx(qkv_share)
+    shares = [
+        ordered(a, b, 1).astype(f32) for a, b in zip(parts(qkv_share), parts(qkv_away))
+    ]
+
+    inputs = x.astype(f32)
+    factor_one = rms_factor(inputs)
+    gain_one_term = jnp.sum(normed_in * inputs * factor_one, axis=0)
+    tokens_grad = (middle_grad + rms_back(inputs, factor_one, gain_one, normed_in)).astype(bf16)
+    gain_terms = jnp.stack([gain_one_term, gain_two_term])
+    gain_terms = lax.psum_scatter(
+        gain_terms + swap_ctx(gain_terms), "fsdp", scatter_dimension=1, tiled=True
+    )
+    return (
+        layer_output[None],
+        tokens_grad[None],
+        gain_terms[0],
+        shares[0],
+        shares[1],
+        shares[2],
+        whole_again(project_share, 0),
+        gain_terms[1],
+        whole_again(gate_share, 1),
+        whole_again(up_share, 1),
+        down_grad,
+    )
+
+
 def solution(mesh):
+    paired = mesh.shape["ctx"] == 2 and mesh.shape["tp"] == 4
     return jax.shard_map(
-        body,
+        paired_body if paired else general_body,
         mesh=mesh,
         in_specs=(
             P("fsdp", "ctx", None),

time: 1450 us -> 710 us (0.49)
  waiting for transfers between devices: 898 us -> 260 us
  blocking collectives: 205 us -> 29.6 us
  matrix products: 215 us -> 92.6 us
  Pallas kernels: 0 us -> 79.6 us
  local copies, waits for them, and re-layouts: 36 us -> 101 us
  other arithmetic: 72 us -> 97.7 us
  starting transfers between devices: 0.9 us -> 22 us
    reduce_scatter x9 -> x3, waiting for transfers between devices: 506 us -> 0.01 us  [summed(): share = lax.psum_scatter(both, 'fsdp', scatter_dimension=axis, tiled=True)]
    psum x3 -> x0, waiting for transfers between devices: 219 us -> none  [tensor_sum(): return lax.psum(term_rows.astype(jnp.bfloat16), 'tp').astype(jnp.float32)]
    ppermute x0 -> x29, waiting for transfers between devices: none -> 181 us  [the longest x17 135 us: swap_ctx(): return lax.ppermute(block, 'ctx', [(0, 1), (1, 0)])]
    all_gather x14 -> x2, blocking collectives: 163 us -> 29.6 us  [the longest x1 15.9 us: gathered(): whole = lax.all_gather(mine, 'fsdp', axis=axis, tiled=True)]
    all_gather x5 -> x4, waiting for transfers between devices: 169 us -> 46.1 us  [gathered(): whole = lax.all_gather(mine, 'fsdp', axis=axis, tiled=True)]
    dot_general x35 -> x24, matrix products: 215 us -> 92.6 us  [dot(): lax.dot_general(a, b, (contract, ((), ())), preferred_element_type=jnp.fl...]
    pallas_call x0 -> x3, Pallas kernels: none -> 79.6 us  [the longest x1 43.8 us: attend_back(): pl.pallas_call(attend_back_kernel, grid_spec=pltpu.PrefetchScalarGridSpec...]
    unnamed x2 -> x0, blocking collectives: 42.1 us -> none
  transfers between devices with their start and end apart: 17 -> 39, of which waited for: 15 -> 19; matrix products, arithmetic and copies ran while one was open for 13% -> 37% of each run, Pallas kernels for 0% -> 11%
where the time goes in v1:
time: 710 us; the launch traced here: 699 us
  waiting for transfers between devices  260 us (37%)
  local copies, waits for them, and re-layouts  101 us (14%)
  other arithmetic  97.7 us (14%)
  matrix products  92.6 us (13%)
  Pallas kernels  79.6 us (11%)
  blocking collectives  29.6 us (4%)
  starting transfers between devices  22 us (3%)
  between operations  16.4 us (2%)
    ppermute x17, waiting for transfers between devices, swap_ctx(): return lax.ppermute(block, 'ctx', [(0, 1), (1, 0)])  135 us
    dot_general x24, matrix products, dot(): lax.dot_general(a, b, (contract, ((), ())), preferred_element_type=jnp.fl...  92.6 us
    all_gather x4, waiting for transfers between devices, gathered(): whole = lax.all_gather(mine, 'fsdp', axis=axis, tiled=True)  46.1 us
    ppermute x4, waiting for transfers between devices, swap_chip(): return lax.ppermute(block, 'tp', [(0, 2), (2, 0), (1, 3), (3, 1)])  44.1 us
    pallas_call x1, Pallas kernels, attend_back(): pl.pallas_call(attend_back_kernel, grid_spec=pltpu.PrefetchScalarGridSpec...  43.8 us
    unnamed x13, waiting for transfers between devices  32.7 us
    unnamed x132, local copies, waits for them, and re-layouts  28.6 us
    pallas_call x1, Pallas kernels, attend(): pl.pallas_call(attend_kernel, grid_spec=pltpu.PrefetchScalarGridSpec(num_...  27.3 us
  transfers between devices with their start and end apart: 39, of which 19 were waited for; matrix products, arithmetic and copies ran while one was open for 37% of the time, Pallas kernels for 11%

profile of v1, /device:TPU:0, one launch (start us, length us, event | category | flops | bytes accessed | tf_op | source)
XLA Modules:
  0.0 698.7 jit_solution(13415320702416320599)
XLA Ops:
  12.0 13.6 %all_gather.18 = bf16[2,1536]{1,0:T(2,128)(2,1)S(1)} all-gather(bf16[2,384]{1,0:T(2,128)(2,1)S(1)} %pad_maximum_fusion.8), channel_id=1, replica_groups=mesh['fsdp'=4,'ctx'=2,'tp'=4] {'fsdp'}, dimensions={1}, use_global_device_ids=true | all-gather | bytes 7680 | tf_op jit(solution)/shard_map/all_gather | solution.py:812
  27.6 15.7 %all-gather.5.cloned.1.call-done = bf16[1536,384]{0,1:T(8,128)(2,1)} async-done(((bf16[384,384]{0,1:T(8,128)(2,1)}), bf16[1536,384]{0,1:T(8,128)(2,1)}) %all-gather.5.cloned.1.call-update) | async-done | bytes 1179664 | tf_op jit(solution)/shard_map/all_gather | solution.py:809
  47.4 23.5 %collective-permute-done = bf16[1536,384]{0,1:T(8,128)(2,1)S(1)} collective-permute-done((bf16[1536,384]{0,1:T(8,128)(2,1)}, bf16[1536,384]{0,1:T(8,128)(2,1)S(1)}, u32[]{:S(2)}, u32[]{:S(2)}) %collective-permute-start) | collective-permute-done | bytes 1179680 | tf_op jit(solution)/shard_map/ppermute | solution.py:433
  75.7 2.8 copy.63
  78.6 2.4 pad_maximum_fusion.w_ref
  81.0 8.5 %project_tokens.1 = (bf16[1024,1536]{1,0:T(8,128)(2,1)}, bf16[1024,512]{1,0:T(8,128)(2,1)}, bf16[1024,512]{1,0:T(8,128)(2,1)}) custom-call(bf16[1024,1536]{1,0:T(8,128)(2,1)} %bitcast.126, f32[1,1536]{1,0:T(1,128)} %slice_convert_fusion.3.gain_ref, bf16[1536,1024]{1,0:T(8,128)(2,1)} %pad_maximum_fusion.w_ref, f32[1024,128]{1,0:T(8,128)} %get-tuple-element.114.cos_ref, ...), custom_call_target="tpu_custom_call" | custom-call | tf_op jit(solution)/shard_map/project_tokens/pallas_call | solution.py:523
  91.0 15.9 %all_gather.20 = bf16[192,1536]{1,0:T(8,128)(2,1)S(1)} all-gather(bf16[192,384]{1,0:T(8,128)(2,1)S(1)} %copy-done.26), channel_id=1, replica_groups=mesh['fsdp'=4,'ctx'=2,'tp'=4] {'fsdp'}, dimensions={1}, use_global_device_ids=true | all-gather | bytes 737280 | tf_op jit(solution)/shard_map/all_gather | solution.py:809
  109.7 16.5 %collective-permute-done.2 = bf16[192,1536]{1,0:T(8,128)(2,1)S(1)} collective-permute-done((bf16[192,1536]{1,0:T(8,128)(2,1)S(1)}, bf16[192,1536]{1,0:T(8,128)(2,1)S(1)}, u32[]{:S(2)}, u32[]{:S(2)}) %collective-permute-start.2) | collective-permute-done | bytes 589856 | tf_op jit(solution)/shard_map/ppermute | solution.py:433
  127.1 2.3 constant_dynamic-update-slice_fusion.1
  130.7 5.5 rev.6
  137.6 27.3 %attend.1 = (bf16[1024,512]{1,0:T(8,128)(2,1)}, f32[2,4,1,512]{3,2,1,0:T(1,128)}) custom-call(s32[13]{0:T(128)} %pad_add_fusion.meta_ref, bf16[1024,512]{1,0:T(8,128)(2,1)} %get-tuple-element.19.q_ref, bf16[2048,512]{1,0:T(8,128)(2,1)} %constant_dynamic-update-slice_fusion.k_ref.v_ref, bf16[2048,512]{1,0:T(8,128)(2,1)} %constant_dynamic-update-slice_fusion.k_ref.v_ref), custom_call_target="tpu_custom_call" | custom-call | flops 4294967296 | bytes 6000000 | tf_op jit(solution)/shard_map/attend/pallas_call | solution.py:613
  166.5 3.4 convolution_convert_fusion
  179.7 33.8 %collective-permute-done.4 = bf16[512,1536]{1,0:T(8,128)(2,1)S(1)} collective-permute-done((bf16[512,1536]{1,0:T(8,128)(2,1)S(1)}, bf16[512,1536]{1,0:T(8,128)(2,1)S(1)}, u32[]{:S(2)}, u32[]{:S(2)}) %collective-permute-start.4) | collective-permute-done | bytes 1572896 | tf_op jit(solution)/shard_map/ppermute | solution.py:441
  215.6 30.4 %all-gather.7.cloned.1.call-done = bf16[1536,512]{1,0:T(8,128)(2,1)} async-done(((bf16[384,512]{1,0:T(8,128)(2,1)}), bf16[1536,512]{1,0:T(8,128)(2,1)}) %all-gather.7.cloned.1.call-update) | async-done | bytes 1572880 | tf_op jit(solution)/shard_map/all_gather | solution.py:809
  247.4 4.2 fusion.24
  251.6 4.3 fusion.22
  256.0 3.8 multiply_reduce_fusion
  259.9 3.8 multiply_convert_fusion
  266.3 3.8 fusion.47
  273.7 12.6 %collective-permute-done.6 = bf16[1536,512]{1,0:T(8,128)(2,1)S(1)} collective-permute-done((bf16[1536,512]{1,0:T(8,128)(2,1)}, bf16[1536,512]{1,0:T(8,128)(2,1)S(1)}, u32[]{:S(2)}, u32[]{:S(2)}) %collective-permute-start.6) | collective-permute-done | bytes 1572896 | tf_op jit(solution)/shard_map/ppermute | solution.py:433
  288.1 5.4 fusion.42
  293.5 6.2 fusion.99
  299.8 6.0 add_convert_fusion
  312.9 32.1 %collective-permute-done.26 = bf16[1536,512]{1,0:T(8,128)(2,1)S(1)} collective-permute-done((bf16[1536,512]{1,0:T(8,128)(2,1)S(1)}, bf16[1536,512]{1,0:T(8,128)(2,1)S(1)}, u32[]{:S(2)}, u32[]{:S(2)}) %collective-permute-start.26) | collective-permute-done | bytes 1572896 | tf_op jit(solution)/shard_map/ppermute | solution.py:433
  345.0 3.0 add_convert_fusion.3
  351.2 4.0 convolution_convert_fusion.3
  356.1 3.4 add_convert_fusion.7
  361.3 3.3 add_convert_fusion.2
  368.0 22.8 %collective-permute-done.24 = bf16[1536,512]{1,0:T(8,128)(2,1)S(1)} collective-permute-done((bf16[1536,512]{1,0:T(8,128)(2,1)S(1)}, bf16[1536,512]{1,0:T(8,128)(2,1)S(1)}, u32[]{:S(2)}, u32[]{:S(2)}) %collective-permute-start.24) | collective-permute-done | bytes 1572896 | tf_op jit(solution)/shard_map/ppermute | solution.py:433
  390.8 3.0 add_convert_fusion.4
  393.9 6.5 fusion.2
  400.4 11.6 %fusion.50 = bf16[1024,384]{0,1:T(8,128)(2,1)} fusion(bf16[384,1536]{1,0:T(8,128)(2,1)} %constant_dynamic-update-slice_fusion.2, bf16[1,1024,1536]{2,1,0:T(8,128)(2,1)S(1)} %copy-done.16, f32[1024]{0:T(1024)S(1)} %broadcast_multiply_fusion.1, f32[1024]{0:T(1024)S(1)} %get-tuple-element.110, f32[1536]{0:T(1024)S(1)} %get-tuple-element.78, ...), kind=kOutput, calls=%fused_computation.96 | convolution fusion | flops 1255538688 | bytes 14567425 | tf_op jit(solution)/shard_map/dot_general | solution.py:491
  412.0 2.4 copy.68
  417.3 43.8 %attend_back.1 = (bf16[1024,512]{1,0:T(8,128)(2,1)}, bf16[2048,256]{1,0:T(8,128)(2,1)}, bf16[2048,256]{1,0:T(8,128)(2,1)}) custom-call(s32[13]{0:T(128)} %pad_add_fusion.meta_ref, bf16[1024,512]{1,0:T(8,128)(2,1)} %get-tuple-element.19.q_ref, bf16[2048,512]{1,0:T(8,128)(2,1)} %constant_dynamic-update-slice_fusion.k_ref.v_ref, ...), custom_call_target="tpu_custom_call" | custom-call | flops 10737418240 | bytes 8000000 | tf_op jit(solution)/shard_map/attend_back/pallas_call | solution.py:738
  465.5 3.0 fusion.32
  468.4 3.0 fusion.29
  471.4 2.9 add_convert_fusion.10
  475.8 13.0 %collective-permute-done.15 = bf16[1024,512]{1,0:T(8,128)(2,1)} collective-permute-done((bf16[1024,512]{1,0:T(8,128)(2,1)S(1)}, bf16[1024,512]{1,0:T(8,128)(2,1)}, u32[]{:S(2)}, u32[]{:S(2)}) %collective-permute-start.15) | collective-permute-done | bytes 1048608 | tf_op jit(solution)/shard_map/ppermute | solution.py:433
  490.9 10.3 %rev.7 = bf16[1024,2,2,128]{3,2,1,0:T(2,128)(2,1)} reverse(bf16[1024,2,2,128]{3,2,1,0:T(2,128)(2,1)} %reshape.575), dimensions={2} | reverse | bytes 2097152 | tf_op jit(solution)/shard_map/rev | solution.py:928
  501.2 2.7 reshape.583
  503.9 2.2 convert_add_fusion.2
  508.0 2.5 copy.69
  514.8 6.0 convolution_convert_fusion.1
  526.8 4.6 copy.86
  531.6 3.6 add_convert_fusion.9
  535.1 3.0 add_convert_fusion.6
  539.6 7.1 %fusion.11 = (f32[1536]{0:T(1024)S(1)}, f32[1024]{0:T(1024)}) fusion(f32[1024]{0:T(1024)S(1)} %get-tuple-element.111, bf16[1,1024,1536]{2,1,0:T(8,128)(2,1)S(1)} %copy-done.2, bf16[512,1536]{1,0:T(8,128)(2,1)} %add_convert_fusion.7, bf16[512,1536]{1,0:T(8,128)(2,1)} %collective-permute-done.14, pred[]{:T(512)S(6)} %eq.31, ...), kind=kLoop, calls=%fused_computation.20 | loop fusion | flops 42464768 | bytes 9451521 | tf_op jit(solution)/shard_map/reduce_sum | solution.py:918
  546.7 2.3 copy.73
  559.8 4.8 convolution_convert_fusion.4
  564.8 10.4 %collective-permute-done.17 = bf16[512,1536]{1,0:T(8,128)(2,1)} collective-permute-done((bf16[512,1536]{1,0:T(8,128)(2,1)}, bf16[512,1536]{1,0:T(8,128)(2,1)}, u32[]{:S(2)}, u32[]{:S(2)}) %collective-permute-start.17) | collective-permute-done | bytes 1572896 | tf_op jit(solution)/shard_map/ppermute | solution.py:441
  575.2 3.5 add_convert_fusion.5
  578.7 7.1 %add_convert_fusion.1 = bf16[1,1024,1536]{2,1,0:T(8,128)(2,1)} fusion(bf16[1,1024,1536]{2,1,0:T(8,128)(2,1)S(1)} %copy-done.2, bf16[1,512,1536]{2,1,0:T(8,128)(2,1)} %bitcast.11, bf16[1,512,1536]{2,1,0:T(8,128)(2,1)} %bitcast.10, pred[]{:T(512)S(6)} %eq.31, bf16[1,512,1536]{2,1,0:T(8,128)(2,1)} %bitcast.8, bf16[1,512,1536]{2,1,0:T(8,128)(2,1)} %bitcast.9), kind=kLoop, calls=%fused_computation.27 | loop fusion | flops 37748736 | bytes 12582913 | tf_op jit(solution)/shard_map/convert_element_type | solution.py:916
  585.8 3.2 reduce-scatter.23.cloned.1.call-done
  589.0 2.3 copy.87
  592.8 5.4 collective-permute-done.20
  598.2 5.3 add_convert_fusion.13
  603.6 5.7 fusion.15
  609.4 15.7 %fusion.9 = (bf16[1,1024,1536]{2,1,0:T(8,128)(2,1)}, bf16[1,1024,1536]{2,1,0:T(8,128)(2,1)S(1)}) fusion(bf16[1,1024,1536]{2,1,0:T(8,128)(2,1)S(1)} %copy-done.2, bf16[1,512,1536]{2,1,0:T(8,128)(2,1)} %bitcast.21, bf16[1,512,1536]{2,1,0:T(8,128)(2,1)} %bitcast.20, f32[1024]{0:T(1024)S(1)} %broadcast_multiply_fusion, f32[1024]{0:T(1024)S(1)} %copy-done.41, ...), kind=kLoop, calls=%fused_computation.18 | loop fusion | flops 73924608 | bytes 22056960 | tf_op jit(solution)/shard_map/convert_element_type | solution.py:957
  626.9 2.5 fusion.67
  629.4 2.5 fusion.68
  636.3 6.7 collective-permute-done.22
  651.2 2.4 collective-permute-done.19
  654.9 9.1 %reduce-scatter.21.cloned.1.call-done = bf16[384,192]{1,0:T(8,128)(2,1)} async-done(((bf16[1536,192]{1,0:T(8,128)(2,1)}), bf16[384,192]{1,0:T(8,128)(2,1)}) %reduce-scatter.21.cloned.1.call-update) | async-done | bytes 147472
  668.5 20.2 %reduce-scatter.19.cloned.1.call-done = f32[384,2]{1,0:T(8,128)} async-done(((f32[1536,2]{1,0:T(8,128)}), f32[384,2]{1,0:T(8,128)}) %reduce-scatter.19.cloned.1.call-update) | async-done | bytes 3088
  (291 shorter events, 121.9 us)
Async XLA Ops:
  7.2 37.5 %copy-start.33 = (bf16[384,384]{1,0:T(8,128)(2,1)S(1)}, bf16[384,384]{1,0:T(8,128)(2,1)}, u32[]{:S(2)}) copy-start(bf16[384,384]{1,0:T(8,128)(2,1)} %param.20) | copy-start | bytes 884740
  7.2 36.0 %all-gather.5.cloned.1.call-start = ((), (), s32[]{:S(2)}) async-start(), calls=%async_computation.6 | async-start | bytes 1474560 | tf_op jit(solution)/shard_map/all_gather | solution.py:809
  10.3 169.3 %all-gather.11.cloned.1.call-start = ((), (), s32[]{:S(2)}) async-start(), calls=%async_computation.9 | async-start | bytes 1966080 | tf_op jit(solution)/shard_map/all_gather | solution.py:809
  11.2 204.4 %all-gather.9.cloned.1.call-start = ((), (), s32[]{:S(2)}) async-start(), calls=%async_computation.8 | async-start | bytes 1966080 | tf_op jit(solution)/shard_map/all_gather | solution.py:809
  27.5 44.1 %copy-start.5 = (f32[1024,64]{1,0:T(8,128)}, f32[1024,64]{1,0:T(8,128)S(1)}, u32[]{:S(2)}) copy-start(f32[1024,64]{1,0:T(8,128)S(1)} %get-tuple-element.107) | copy-start | bytes 786436
  27.6 44.1 %copy-start.6 = (f32[1024,64]{1,0:T(8,128)}, f32[1024,64]{1,0:T(8,128)S(1)}, u32[]{:S(2)}) copy-start(f32[1024,64]{1,0:T(8,128)S(1)} %get-tuple-element.106) | copy-start | bytes 786436
  43.3 27.6 %collective-permute-start = (bf16[1536,384]{0,1:T(8,128)(2,1)}, bf16[1536,384]{0,1:T(8,128)(2,1)S(1)}, u32[]{:S(2)}, u32[]{:S(2)}) collective-permute-start(bf16[1536,384]{0,1:T(8,128)(2,1)} %all-gather.5.cloned.1.call-done), channel_id=1, source_target_pairs={{0,4},{4,0},{1,5},{5,1},{2,6},{6,2},{3,7},{7,3},{8,12},{12,8},{9,1... | collective-permute-start | bytes 3538952 | tf_op jit(solution)/shard_map/ppermute | solution.py:433
  72.3 6.3 copy-start.9
  78.6 50.7 %copy-start.3 = (bf16[1536,768]{1,0:T(8,128)(2,1)}, bf16[1536,768]{1,0:T(8,128)(2,1)S(1)}, u32[]{:S(2)}) copy-start(bf16[1536,768]{1,0:T(8,128)(2,1)S(1)} %copy.63) | copy-start | bytes 7077892
  81.0 10.0 %copy-start.26 = (bf16[192,384]{1,0:T(8,128)(2,1)S(1)}, bf16[192,384]{1,0:T(8,128)(2,1)}, u32[]{:S(2)}) copy-start(bf16[192,384]{1,0:T(8,128)(2,1)} %constant_dynamic-slice_fusion.7) | copy-start | bytes 442372
  89.6 39.8 %collective-permute-start.1 = (bf16[1024,512]{1,0:T(8,128)(2,1)}, bf16[1024,512]{1,0:T(8,128)(2,1)}, u32[]{:S(2)}, u32[]{:S(2)}) collective-permute-start(bf16[1024,512]{1,0:T(8,128)(2,1)} %get-tuple-element.20), channel_id=1, source_target_pairs={{0,4},{4,0},{1,5},{5,1},{2,6},{6,2},{3,7},{7,3},{8,12},{12,8},{9,1... | collective-permute-start | bytes 3145736 | tf_op jit(solution)/shard_map/ppermute | solution.py:433
  106.9 19.3 %collective-permute-start.2 = (bf16[192,1536]{1,0:T(8,128)(2,1)S(1)}, bf16[192,1536]{1,0:T(8,128)(2,1)S(1)}, u32[]{:S(2)}, u32[]{:S(2)}) collective-permute-start(bf16[192,1536]{1,0:T(8,128)(2,1)S(1)} %all_gather.20), channel_id=1, source_target_pairs={{0,4},{4,0},{1,5},{5,1},{2,6},{6,2},{3,7},{7,3},{8,12},{12,8},{9,1... | collective-permute-start | bytes 1769480 | tf_op jit(solution)/shard_map/ppermute | solution.py:433
  171.7 3.5 collective-permute-start.3
  173.5 72.5 %all-gather.7.cloned.1.call-start = ((), (), s32[]{:S(2)}) async-start(), calls=%async_computation.7 | async-start | bytes 1966080 | tf_op jit(solution)/shard_map/all_gather | solution.py:809
  176.9 36.5 %collective-permute-start.4 = (bf16[512,1536]{1,0:T(8,128)(2,1)S(1)}, bf16[512,1536]{1,0:T(8,128)(2,1)S(1)}, u32[]{:S(2)}, u32[]{:S(2)}) collective-permute-start(bf16[512,1536]{1,0:T(8,128)(2,1)S(1)} %add_convert_fusion.12), channel_id=1, source_target_pairs={{0,2},{2,0},{1,3},{3,1},{4,6},{6,4},{5,7},{7,5},{8,10},{10,8},{9,1... | collective-permute-start | bytes 4718600 | tf_op jit(solution)/shard_map/ppermute | solution.py:441
  179.3 372.9 %reduce-scatter.17.cloned.1.call-start = ((), (), s32[]{:S(2)}) async-start(), calls=%async_computation.12 | async-start | bytes 1966080 | tf_op jit(solution)/shard_map/reduce_scatter | solution.py:888
  179.6 72.1 %collective-permute-start.8 = (bf16[512,1536]{1,0:T(8,128)(2,1)}, bf16[512,1536]{1,0:T(8,128)(2,1)}, u32[]{:S(2)}, u32[]{:S(2)}) collective-permute-start(bf16[512,1536]{1,0:T(8,128)(2,1)} %all-gather.11.cloned.1.call-done), channel_id=1, source_target_pairs={{0,4},{4,0},{1,5},{5,1},{2,6},{6,2},{3,7},{7,3},{8,12},{12,8},{9,1... | collective-permute-start | bytes 4718600 | tf_op jit(solution)/shard_map/ppermute | solution.py:433
  215.0 41.0 %collective-permute-start.5 = (bf16[512,1536]{1,0:T(8,128)(2,1)}, bf16[512,1536]{1,0:T(8,128)(2,1)}, u32[]{:S(2)}, u32[]{:S(2)}) collective-permute-start(bf16[512,1536]{1,0:T(8,128)(2,1)} %add_convert_fusion.11), channel_id=1, source_target_pairs={{0,1},{1,0},{2,3},{3,2},{4,5},{5,4},{6,7},{7,6},{8,9},{9,8},{10,11... | collective-permute-start | bytes 4718600 | tf_op jit(solution)/shard_map/ppermute | solution.py:437
  215.6 72.5 %collective-permute-start.7 = (bf16[1536,512]{1,0:T(8,128)(2,1)}, bf16[1536,512]{1,0:T(8,128)(2,1)}, u32[]{:S(2)}, u32[]{:S(2)}) collective-permute-start(bf16[1536,512]{1,0:T(8,128)(2,1)} %all-gather.9.cloned.1.call-done), channel_id=1, source_target_pairs={{0,4},{4,0},{1,5},{5,1},{2,6},{6,2},{3,7},{7,3},{8,12},{12,8},{9,1... | collective-permute-start | bytes 4718600 | tf_op jit(solution)/shard_map/ppermute | solution.py:433
  246.0 40.3 %collective-permute-start.6 = (bf16[1536,512]{1,0:T(8,128)(2,1)}, bf16[1536,512]{1,0:T(8,128)(2,1)S(1)}, u32[]{:S(2)}, u32[]{:S(2)}) collective-permute-start(bf16[1536,512]{1,0:T(8,128)(2,1)} %all-gather.7.cloned.1.call-done), channel_id=1, source_target_pairs={{0,4},{4,0},{1,5},{5,1},{2,6},{6,2},{3,7},{7,3},{8,12},{12,8},{9,1... | collective-permute-start | bytes 4718600 | tf_op jit(solution)/shard_map/ppermute | solution.py:433
  259.8 140.6 %copy-start.39 = (f32[1024]{0:T(1024)}, f32[1024]{0:T(1024)S(1)}, u32[]{:S(2)}) copy-start(f32[1024]{0:T(1024)S(1)} %get-tuple-element.110) | copy-start | bytes 12292
  259.8 279.8 %copy-start.34 = (f32[1024]{0:T(1024)}, f32[1024]{0:T(1024)S(1)}, u32[]{:S(2)}) copy-start(f32[1024]{0:T(1024)S(1)} %get-tuple-element.111) | copy-start | bytes 12292
  263.7 81.3 %copy-start.7 = (bf16[1024,1536]{1,0:T(8,128)(2,1)}, bf16[1024,1536]{1,0:T(8,128)(2,1)S(1)}, u32[]{:S(2)}) copy-start(bf16[1024,1536]{1,0:T(8,128)(2,1)S(1)} %multiply_convert_fusion) | copy-start | bytes 9437188
  293.5 6.2 copy-start.58
  305.9 3.5 collective-permute-start.12
  308.9 36.1 %copy-start.57 = (bf16[1024,512]{1,0:T(8,128)(2,1)S(1)}, bf16[1024,512]{1,0:T(8,128)(2,1)}, u32[]{:S(2)}) copy-start(bf16[1024,512]{1,0:T(8,128)(2,1)} %copy-done.56) | copy-start | bytes 3145732
  308.9 36.1 %collective-permute-start.26 = (bf16[1536,512]{1,0:T(8,128)(2,1)S(1)}, bf16[1536,512]{1,0:T(8,128)(2,1)S(1)}, u32[]{:S(2)}, u32[]{:S(2)}) collective-permute-start(bf16[1536,512]{1,0:T(8,128)(2,1)S(1)} %convolution_convert_fusion.2), channel_id=1, source_target_pairs={{0,4},{4,0},{1,5},{5,1},{2,6},{6,2},{3,7},{7,3},{8,12},{12,8},{9,1... | collective-permute-start | bytes 4718600 | tf_op jit(solution)/shard_map/ppermute | solution.py:433
  311.4 44.7 %collective-permute-start.13 = (bf16[512,1536]{1,0:T(8,128)(2,1)}, bf16[512,1536]{1,0:T(8,128)(2,1)}, u32[]{:S(2)}, u32[]{:S(2)}) collective-permute-start(bf16[512,1536]{1,0:T(8,128)(2,1)} %add_convert_fusion.8), channel_id=1, source_target_pairs={{0,2},{2,0},{1,3},{3,1},{4,6},{6,4},{5,7},{7,5},{8,10},{10,8},{9,1... | collective-permute-start | bytes 4718600 | tf_op jit(solution)/shard_map/ppermute | solution.py:441
  348.0 204.5 %reduce-scatter.15.cloned.1.call-start = ((), (), s32[]{:S(2)}) async-start(), calls=%async_computation.11 | async-start | bytes 1966080 | tf_op jit(solution)/shard_map/reduce_scatter | solution.py:888
  355.3 35.5 %collective-permute-start.24 = (bf16[1536,512]{1,0:T(8,128)(2,1)S(1)}, bf16[1536,512]{1,0:T(8,128)(2,1)S(1)}, u32[]{:S(2)}, u32[]{:S(2)}) collective-permute-start(bf16[1536,512]{1,0:T(8,128)(2,1)S(1)} %convolution_convert_fusion.3), channel_id=1, source_target_pairs={{0,4},{4,0},{1,5},{5,1},{2,6},{6,2},{3,7},{7,3},{8,12},{12,8},{9,1... | collective-permute-start | bytes 4718600 | tf_op jit(solution)/shard_map/ppermute | solution.py:433
  359.5 34.4 %collective-permute-start.14 = (bf16[512,1536]{1,0:T(8,128)(2,1)}, bf16[512,1536]{1,0:T(8,128)(2,1)}, u32[]{:S(2)}, u32[]{:S(2)}) collective-permute-start(bf16[512,1536]{1,0:T(8,128)(2,1)} %add_convert_fusion.7), channel_id=1, source_target_pairs={{0,1},{1,0},{2,3},{3,2},{4,5},{5,4},{6,7},{7,6},{8,9},{9,8},{10,11... | collective-permute-start | bytes 4718600 | tf_op jit(solution)/shard_map/ppermute | solution.py:437
  361.3 29.5 %copy-start.55 = (bf16[1024,512]{1,0:T(8,128)(2,1)S(1)}, bf16[1024,512]{1,0:T(8,128)(2,1)}, u32[]{:S(2)}) copy-start(bf16[1024,512]{1,0:T(8,128)(2,1)} %copy-done.54) | copy-start | bytes 3145732
  366.3 24.5 %copy-start.8 = (bf16[1024,1536]{1,0:T(8,128)(2,1)S(1)}, bf16[1024,1536]{1,0:T(8,128)(2,1)}, u32[]{:S(2)}) copy-start(bf16[1024,1536]{1,0:T(8,128)(2,1)} %copy-done.7) | copy-start | bytes 9437188
  367.6 103.8 %collective-permute-start.9 = (bf16[512,1536]{1,0:T(8,128)(2,1)}, bf16[512,1536]{1,0:T(8,128)(2,1)}, u32[]{:S(2)}, u32[]{:S(2)}) collective-permute-start(bf16[512,1536]{1,0:T(8,128)(2,1)} %constant_dynamic-slice_fusion.2), channel_id=1, source_target_pairs={{0,1},{1,0},{2,3},{3,2},{4,5},{5,4},{6,7},{7,6},{8,9},{9,8},{10,11... | collective-permute-start | bytes 4718600 | tf_op jit(solution)/shard_map/ppermute | solution.py:437
  393.9 195.1 %reduce-scatter.23.cloned.1.call-start = ((), (), s32[]{:S(2)}) async-start(), calls=%async_computation.15 | async-start | bytes 3932160
  393.9 6.5 copy-start.16
  400.4 11.6 %copy-start.43 = (f32[1024]{0:T(1024)}, f32[1024]{0:T(1024)S(1)}, u32[]{:S(2)}) copy-start(f32[1024]{0:T(1024)S(1)} %broadcast_multiply_fusion.1) | copy-start | bytes 12292
  465.4 23.4 %collective-permute-start.15 = (bf16[1024,512]{1,0:T(8,128)(2,1)S(1)}, bf16[1024,512]{1,0:T(8,128)(2,1)}, u32[]{:S(2)}, u32[]{:S(2)}) collective-permute-start(bf16[1024,512]{1,0:T(8,128)(2,1)S(1)} %slice.166), channel_id=1, source_target_pairs={{0,4},{4,0},{1,5},{5,1},{2,6},{6,2},{3,7},{7,3},{8,12},{12,8},{9,1... | collective-permute-start | bytes 3145736 | tf_op jit(solution)/shard_map/ppermute | solution.py:433
  474.4 57.2 %collective-permute-start.10 = (bf16[512,1536]{1,0:T(8,128)(2,1)}, bf16[512,1536]{1,0:T(8,128)(2,1)}, u32[]{:S(2)}, u32[]{:S(2)}) collective-permute-start(bf16[512,1536]{1,0:T(8,128)(2,1)} %add_convert_fusion.10), channel_id=1, source_target_pairs={{0,2},{2,0},{1,3},{3,1},{4,6},{6,4},{5,7},{7,5},{8,10},{10,8},{9,1... | collective-permute-start | bytes 4718600 | tf_op jit(solution)/shard_map/ppermute | solution.py:441
  523.7 11.4 %collective-permute-start.16 = (bf16[512,1536]{1,0:T(8,128)(2,1)}, bf16[512,1536]{1,0:T(8,128)(2,1)}, u32[]{:S(2)}, u32[]{:S(2)}) collective-permute-start(bf16[512,1536]{1,0:T(8,128)(2,1)} %constant_dynamic-slice_fusion), channel_id=1, source_target_pairs={{0,1},{1,0},{2,3},{3,2},{4,5},{5,4},{6,7},{7,6},{8,9},{9,8},{10,11... | collective-permute-start | bytes 4718600 | tf_op jit(solution)/shard_map/ppermute | solution.py:437
  531.5 103.0 %reduce-scatter.13.cloned.1.call-start = ((), (), s32[]{:S(2)}) async-start(), calls=%async_computation.10 | async-start | bytes 1474560 | tf_op jit(solution)/shard_map/reduce_scatter | solution.py:888
  535.1 43.6 %collective-permute-start.11 = (bf16[512,1536]{1,0:T(8,128)(2,1)}, bf16[512,1536]{1,0:T(8,128)(2,1)}, u32[]{:S(2)}, u32[]{:S(2)}) collective-permute-start(bf16[512,1536]{1,0:T(8,128)(2,1)} %add_convert_fusion.9), channel_id=1, source_target_pairs={{0,1},{1,0},{2,3},{3,2},{4,5},{5,4},{6,7},{7,6},{8,9},{9,8},{10,11... | collective-permute-start | bytes 4718600 | tf_op jit(solution)/shard_map/ppermute | solution.py:437
  538.1 37.1 %collective-permute-start.17 = (bf16[512,1536]{1,0:T(8,128)(2,1)}, bf16[512,1536]{1,0:T(8,128)(2,1)}, u32[]{:S(2)}, u32[]{:S(2)}) collective-permute-start(bf16[512,1536]{1,0:T(8,128)(2,1)} %add_convert_fusion.6), channel_id=1, source_target_pairs={{0,2},{2,0},{1,3},{3,1},{4,6},{6,4},{5,7},{7,5},{8,10},{10,8},{9,1... | collective-permute-start | bytes 4718600 | tf_op jit(solution)/shard_map/ppermute | solution.py:441
  552.2 77.2 %collective-permute-start.27 = (bf16[384,512]{1,0:T(8,128)(2,1)}, bf16[384,512]{1,0:T(8,128)(2,1)}, u32[]{:S(2)}, u32[]{:S(2)}) collective-permute-start(bf16[384,512]{1,0:T(8,128)(2,1)} %reduce-scatter.17.cloned.1.call-done), channel_id=1, source_target_pairs={{0,4},{4,0},{1,5},{5,1},{2,6},{6,2},{3,7},{7,3},{8,12},{12,8},{9,1... | collective-permute-start | bytes 1179656 | tf_op jit(solution)/shard_map/ppermute | solution.py:433
  552.5 74.4 %collective-permute-start.25 = (bf16[384,512]{1,0:T(8,128)(2,1)}, bf16[384,512]{1,0:T(8,128)(2,1)}, u32[]{:S(2)}, u32[]{:S(2)}) collective-permute-start(bf16[384,512]{1,0:T(8,128)(2,1)} %reduce-scatter.15.cloned.1.call-done), channel_id=1, source_target_pairs={{0,4},{4,0},{1,5},{5,1},{2,6},{6,2},{3,7},{7,3},{8,12},{12,8},{9,1... | collective-permute-start | bytes 1179656 | tf_op jit(solution)/shard_map/ppermute | solution.py:433
  564.6 33.6 %collective-permute-start.20 = (bf16[1536,384]{1,0:T(8,128)(2,1)}, bf16[1536,384]{1,0:T(8,128)(2,1)}, u32[]{:S(2)}, u32[]{:S(2)}) collective-permute-start(bf16[1536,384]{1,0:T(8,128)(2,1)} %convolution_convert_fusion.4), channel_id=1, source_target_pairs={{0,4},{4,0},{1,5},{5,1},{2,6},{6,2},{3,7},{7,3},{8,12},{12,8},{9,1... | collective-permute-start | bytes 3538952 | tf_op jit(solution)/shard_map/ppermute | solution.py:433
  578.7 24.9 %collective-permute-start.18 = (bf16[512,1536]{1,0:T(8,128)(2,1)}, bf16[512,1536]{1,0:T(8,128)(2,1)}, u32[]{:S(2)}, u32[]{:S(2)}) collective-permute-start(bf16[512,1536]{1,0:T(8,128)(2,1)} %add_convert_fusion.5), channel_id=1, source_target_pairs={{0,1},{1,0},{2,3},{3,2},{4,5},{5,4},{6,7},{7,6},{8,9},{9,8},{10,11... | collective-permute-start | bytes 4718600 | tf_op jit(solution)/shard_map/ppermute | solution.py:437
  591.3 40.7 %collective-permute-start.28 = (bf16[1024,384]{1,0:T(8,128)(2,1)}, bf16[1024,384]{1,0:T(8,128)(2,1)}, u32[]{:S(2)}, u32[]{:S(2)}) collective-permute-start(bf16[1024,384]{1,0:T(8,128)(2,1)} %copy.87), channel_id=1, source_target_pairs={{0,4},{4,0},{1,5},{5,1},{2,6},{6,2},{3,7},{7,3},{8,12},{12,8},{9,1... | collective-permute-start | bytes 2359304 | tf_op jit(solution)/shard_map/ppermute | solution.py:433
  603.5 60.5 %reduce-scatter.21.cloned.1.call-start = ((), (), s32[]{:S(2)}) async-start(), calls=%async_computation.14 | async-start | bytes 983040
  603.6 5.8 copy-start.18
  603.6 5.8 copy-start.35
  603.6 5.8 copy-start.37
  603.6 5.8 copy-start.40
  603.6 5.8 copy-start.41
  603.6 5.8 copy-start.44
  609.4 15.7 %copy-start.25 = (bf16[1024,4,96]{0,2,1:T(8,128)(2,1)S(1)}, bf16[1024,4,96]{0,2,1:T(8,128)(2,1)}, u32[]{:S(2)}) copy-start(bf16[1024,4,96]{0,2,1:T(8,128)(2,1)} %copy-done.24) | copy-start | bytes 2359300
  626.6 16.3 %collective-permute-start.22 = (bf16[192,1536]{1,0:T(8,128)(2,1)S(1)}, bf16[192,1536]{1,0:T(8,128)(2,1)S(1)}, u32[]{:S(2)}, u32[]{:S(2)}) collective-permute-start(bf16[192,1536]{1,0:T(8,128)(2,1)S(1)} %slice.216), channel_id=1, source_target_pairs={{0,4},{4,0},{1,5},{5,1},{2,6},{6,2},{3,7},{7,3},{8,12},{12,8},{9,1... | collective-permute-start | bytes 1769480 | tf_op jit(solution)/shard_map/ppermute | solution.py:433
  634.5 15.4 %copy-start.38 = (f32[1536]{0:T(1024)S(1)}, f32[1536]{0:T(1024)}, u32[]{:S(2)}) copy-start(f32[1536]{0:T(1024)} %get-tuple-element.71) | copy-start | bytes 18436
  634.5 15.4 %copy-start.36 = (f32[1,1536]{1,0:T(1,128)S(1)}, f32[1,1536]{1,0:T(1,128)}, u32[]{:S(2)}) copy-start(f32[1,1536]{1,0:T(1,128)} %stack.28) | copy-start | bytes 18436
  634.5 12.2 %collective-permute-start.21 = (bf16[384,384]{1,0:T(8,128)(2,1)}, bf16[384,384]{1,0:T(8,128)(2,1)}, u32[]{:S(2)}, u32[]{:S(2)}) collective-permute-start(bf16[384,384]{1,0:T(8,128)(2,1)} %reduce-scatter.13.cloned.1.call-done), channel_id=1, source_target_pairs={{0,4},{4,0},{1,5},{5,1},{2,6},{6,2},{3,7},{7,3},{8,12},{12,8},{9,1... | collective-permute-start | bytes 884744 | tf_op jit(solution)/shard_map/ppermute | solution.py:433
  644.2 44.5 %reduce-scatter.19.cloned.1.call-start = ((), (), s32[]{:S(2)}) async-start(), calls=%async_computation.13 | async-start | bytes 983040
  647.6 43.8 %copy-start.1 = (bf16[1024,384]{1,0:T(8,128)(2,1)S(1)}, bf16[1024,384]{1,0:T(8,128)(2,1)}, u32[]{:S(2)}) copy-start(bf16[1024,384]{1,0:T(8,128)(2,1)} %param.24) | copy-start | bytes 2359300
  649.9 3.8 collective-permute-start.19
  665.1 25.5 %collective-permute-start.23 = (bf16[192,384]{1,0:T(8,128)(2,1)S(1)}, bf16[192,384]{1,0:T(8,128)(2,1)S(1)}, u32[]{:S(2)}, u32[]{:S(2)}) collective-permute-start(bf16[192,384]{1,0:T(8,128)(2,1)S(1)} %copy.85), channel_id=1, source_target_pairs={{0,4},{4,0},{1,5},{5,1},{2,6},{6,2},{3,7},{7,3},{8,12},{12,8},{9,1... | collective-permute-start | bytes 442376 | tf_op jit(solution)/shard_map/ppermute | solution.py:433
  (36 other events, 106.2 us)
Sparse Core Ops, SparseCore 0:
  10.4 32.7 all-gather.4
  45.4 36.5 all-gather.10
  173.6 34.3 all-gather.8
  210.0 35.9 all-gather.6
  348.1 32.5 reduce-scatter.16
  394.0 32.5 reduce-scatter.14
  531.6 57.3 reduce-scatter.22
  603.6 25.4 reduce-scatter.12
  644.4 19.5 reduce-scatter.20
  666.2 22.5 reduce-scatter.18

commit v2 on v1

--- a/solution.py
+++ b/solution.py
@@ -2,6 +2,7 @@
 
 import jax
 import jax.numpy as jnp
+import numpy as np
 from jax import lax
 from jax.experimental import pallas as pl
 from jax.experimental.pallas import tpu as pltpu
@@ -459,90 +460,324 @@
     ).astype(jnp.float32)
 
 
-def spread_turned(columns):
-    rows, width = columns.shape
-    parts = columns.reshape(rows, width // HD, 2, HALF)
-    return jnp.pad(parts, ((0, 0), (0, 0), (0, 0), (0, SPAN - HALF))).reshape(
-        rows, width // HD * LANES
-    )
-
-
-def spread_plain(columns):
-    rows, width = columns.shape
-    parts = columns.reshape(rows, width // HD, HD)
-    return jnp.pad(parts, ((0, 0), (0, 0), (0, LANES - HD))).reshape(rows, width // HD * LANES)
-
-
-def close_turned(columns):
-    rows, width = columns.shape
-    return columns.reshape(rows, width // SPAN, SPAN)[..., :HALF].reshape(
-        rows, width // SPAN * HALF
-    )
-
-
-def close_plain(columns):
-    rows, width = columns.shape
-    return columns.reshape(rows, width // LANES, LANES)[..., :HD].reshape(
-        rows, width // LANES * HD
-    )
-
-
 def dot(a, b, contract):
     return lax.dot_general(a, b, (contract, ((), ())), preferred_element_type=jnp.float32)
 
 
-def project_kernel(x_ref, gain_ref, w_ref, cos_ref, sin_ref, normed_ref, q_ref, kv_ref):
-    x = x_ref[...].astype(jnp.float32)
-    factor = lax.rsqrt(jnp.mean(x * x, axis=-1, keepdims=True) + EPSILON)
-    normed = (x * factor * gain_ref[...].astype(jnp.float32)).astype(jnp.bfloat16)
-    normed_ref[...] = normed
-    cosine = cos_ref[...]
-    sine = sin_ref[...]
-    q_tiles = q_ref.shape[1] // LANES
-    tiles = w_ref.shape[1] // LANES
-    turned = q_tiles + (tiles - q_tiles) // 2
+MESH = pl.DeviceIdType.MESH
+GAIN_ROWS = 16
+
+
+def gather_kernel(
+    x_ref,
+    pack_ref,
+    rest_ref,
+    spread_ref,
+    cos_ref,
+    sin_ref,
+    normed_ref,
+    q_ref,
+    kv_ref,
+    wide_ref,
+    project_ref,
+    gain_ref,
+    buf_ref,
+    up_send,
+    up_recv,
+    down_send,
+    down_recv,
+    x_send,
+    x_recv,
+    kv_send,
+    kv_recv,
+):
+    planes = buf_ref.shape[0]
+    depth = wide_ref.shape[0] // planes
+    half_width = wide_ref.shape[1] // 2
+    matrix_rows = pack_ref.shape[0] - GAIN_ROWS
+    project_rows = matrix_rows - depth
+    rows = x_ref.shape[0]
+    z = lax.axis_index("fsdp")
+    c = lax.axis_index("ctx")
+    across = {"ctx": 1 - c}
+    has_above = z < planes - 1
+    has_below = z > 0
+
+    barrier = pltpu.get_barrier_semaphore()
+
+    @pl.when(has_above)
+    def _():
+        pl.semaphore_signal(barrier, inc=1, device_id={"fsdp": z + 1}, device_id_type=MESH)
+
+    @pl.when(has_below)
+    def _():
+        pl.semaphore_signal(barrier, inc=1, device_id={"fsdp": z - 1}, device_id_type=MESH)
+
+    pl.semaphore_signal(barrier, inc=1, device_id=across, device_id_type=MESH)
+
+    @pl.when(has_above & has_below)
+    def _():
+        pl.semaphore_wait(barrier, 3)
+
+    @pl.when(jnp.logical_not(has_above & has_below))
+    def _():
+        pl.semaphore_wait(barrier, 2)
+
+    def up(k):
+        piece = z - k
+        return pltpu.make_async_remote_copy(
+            src_ref=pack_ref if k == 0 else buf_ref.at[piece, 0],
+            dst_ref=buf_ref.at[piece, 0],
+            send_sem=up_send.at[k],
+            recv_sem=up_recv.at[k],
+            device_id={"fsdp": z + 1},
+            device_id_type=MESH,
+        )
+
+    def down(k):
+        piece = z + k
+        return pltpu.make_async_remote_copy(
+            src_ref=pack_ref if k == 0 else buf_ref.at[piece, 0],
+            dst_ref=buf_ref.at[piece, 0],
+            send_sem=down_send.at[k],
+            recv_sem=down_recv.at[k],
+            device_id={"fsdp": z - 1},
+            device_id_type=MESH,
+        )
+
+    def from_below(k):
+        piece = z - 1 - k
+        return pltpu.make_async_remote_copy(
+            src_ref=buf_ref.at[piece, 0],
+            dst_ref=buf_ref.at[piece, 0],
+            send_sem=up_send.at[k],
+            recv_sem=up_recv.at[k],
+            device_id={"fsdp": z - 1},
+            device_id_type=MESH,
+        )
+
+    def from_above(k):
+        piece = z + 1 + k
+        return pltpu.make_async_remote_copy(
+            src_ref=buf_ref.at[piece, 0],
+            dst_ref=buf_ref.at[piece, 0],
+            send_sem=down_send.at[k],
+            recv_sem=down_recv.at[k],
+            device_id={"fsdp": z + 1},
+            device_id_type=MESH,
+        )
+
+    def sideways(side, k):
+        piece = z - k if side == 0 else z + k
+        return pltpu.make_async_remote_copy(
+            src_ref=buf_ref.at[piece, 0, pl.ds(0, matrix_rows)],
+            dst_ref=buf_ref.at[piece, 1, pl.ds(0, matrix_rows)],
+            send_sem=x_send.at[side, k],
+            recv_sem=x_recv.at[side, k],
+            device_id=across,
+            device_id_type=MESH,
+        )
+
+    spread = spread_ref[...]
+
+    def place(block, piece, which):
+        at = pl.ds(pl.multiple_of(piece * depth, depth), depth)
+        wide_ref[at, which * half_width : (which + 1) * half_width] = dot(
+            block[:depth], spread, ((1,), (0,))
+        ).astype(jnp.bfloat16)
+        for head in range(project_rows // HD):
+            row = (which * (project_rows // HD) + head) * LANES
+            project_ref[row : row + HD, at] = block[depth + head * HD : depth + (head + 1) * HD]
+
+    def place_gain(block, piece):
+        at = pl.ds(pl.multiple_of(piece * depth, depth), depth)
+        gain_ref[:, at] = block[matrix_rows:]
+
+    @pl.when(has_above)
+    def _():
+        up(0).start()
+
+    @pl.when(has_below)
+    def _():
+        down(0).start()
+
+    for head in range(project_ref.shape[0] // LANES):
+        row = head * LANES + HD
+        project_ref[row : row + LANES - HD, :] = jnp.zeros(
+            (LANES - HD, project_ref.shape[1]), jnp.bfloat16
+        )
+    place(pack_ref, z, 0)
+    place_gain(pack_ref, z)
+    place(rest_ref, z, 1)
+
+    for k in range(1, planes):
+        below = z - k >= 0
+        above = z + k <= planes - 1
+
+        @pl.when(below)
+        def _():
+            from_below(k - 1).wait_recv()
+            if k < planes - 1:
+
+                @pl.when(has_above)
+                def _():
+                    up(k).start()
+
+            sideways(0, k).start()
+
+        @pl.when(above)
+        def _():
+            from_above(k - 1).wait_recv()
+            if k < planes - 1:
+
+                @pl.when(has_below)
+                def _():
+                    down(k).start()
+
+            sideways(1, k).start()
+
+        @pl.when(below)
+        def _():
+            place(buf_ref.at[z - k, 0], z - k, 0)
+            place_gain(buf_ref.at[z - k, 0], z - k)
+
+        @pl.when(above)
+        def _():
+            place(buf_ref.at[z + k, 0], z + k, 0)
+            place_gain(buf_ref.at[z + k, 0], z + k)
+
+    tile = 128
+    gain = gain_ref[0:1, :].astype(jnp.float32)
+
+    def norm_rows(i, carry):
+        at = pl.ds(pl.multiple_of(i * tile, tile), tile)
+        x = x_ref[at, :].astype(jnp.float32)
+        factor = lax.rsqrt(jnp.mean(x * x, axis=-1, keepdims=True) + EPSILON)
+        normed_ref[at, :] = (x * factor * gain).astype(jnp.bfloat16)
+        return carry
+
+    lax.fori_loop(0, rows // tile, norm_rows, 0)
+
+    for k in range(1, planes):
+
+        @pl.when(z - k >= 0)
+        def _():
+            sideways(0, k).wait_recv()
+            place(buf_ref.at[z - k, 1], z - k, 1)
+
+        @pl.when(z + k <= planes - 1)
+        def _():
+            sideways(1, k).wait_recv()
+            place(buf_ref.at[z + k, 1], z + k, 1)
+
+    block = 256
+
+    def turn(part, at):
+        return part * cos_ref[at, :] + pltpu.roll(part, SPAN, 1) * sin_ref[at, :]
+
+    def key_rows(i, carry):
+        at = pl.ds(pl.multiple_of(i * block, block), block)
+        for which in range(2):
+            lane = which * half_width + 2 * LANES
+            both = dot(normed_ref[at, :], wide_ref[:, lane : lane + 2 * LANES], ((1,), (0,)))
+            kv_ref[which, at, :] = turn(both[:, :LANES], at).astype(jnp.bfloat16)
+            kv_ref[2 + which, at, :] = both[:, LANES:].astype(jnp.bfloat16)
+        return carry
+
+    lax.fori_loop(0, rows // block, key_rows, 0)
+
+    def exchange(slab):
+        return pltpu.make_async_remote_copy(
+            src_ref=kv_ref.at[slab, pl.ds(0, rows)],
+            dst_ref=kv_ref.at[slab ^ 1, pl.ds(rows, rows)],
+            send_sem=kv_send.at[slab],
+            recv_sem=kv_recv.at[slab ^ 1],
+            device_id=across,
+            device_id_type=MESH,
+        )
+
+    for slab in range(4):
+        exchange(slab).start()
     scale = HD ** (-0.5) * LOG2E
-    for pair in range(tiles // 2):
-        wide = dot(normed, w_ref[:, pair * 2 * LANES : (pair + 1) * 2 * LANES], ((1,), (0,)))
-        for side in range(2):
-            tile = 2 * pair + side
-            part = wide[:, side * LANES : (side + 1) * LANES]
-            if tile < turned:
-                part = part * cosine + pltpu.roll(part, SPAN, 1) * sine
-            if tile < q_tiles:
-                q_ref[:, tile * LANES : (tile + 1) * LANES] = (part * scale).astype(jnp.bfloat16)
-            else:
-                lane = (tile - q_tiles) * LANES
-                kv_ref[:, lane : lane + LANES] = part.astype(jnp.bfloat16)
-
-
-def project_tokens(x, gain, weights, cosine, sine, q_width):
+
+    def query_rows(i, carry):
+        at = pl.ds(pl.multiple_of(i * block, block), block)
+        for which in range(2):
+            lane = which * half_width
+            both = dot(normed_ref[at, :], wide_ref[:, lane : lane + 2 * LANES], ((1,), (0,)))
+            for head in range(2):
+                part = turn(both[:, head * LANES : (head + 1) * LANES], at)
+                lane = (2 * which + head) * LANES
+                q_ref[at, lane : lane + LANES] = (part * scale).astype(jnp.bfloat16)
+        return carry
+
+    lax.fori_loop(0, rows // block, query_rows, 0)
+
+    for k in range(planes - 1):
+
+        @pl.when((z - k >= 0) & has_above)
+        def _():
+            up(k).wait_send()
+
+        @pl.when((z + k <= planes - 1) & has_below)
+        def _():
+            down(k).wait_send()
+
+    for k in range(1, planes):
+
+        @pl.when(z - k >= 0)
+        def _():
+            sideways(0, k).wait_send()
+
+        @pl.when(z + k <= planes - 1)
+        def _():
+            sideways(1, k).wait_send()
+
+    for slab in range(4):
+        exchange(slab).wait_send()
+    for slab in range(4):
+        exchange(slab).wait_recv()
+
+
+def gather_project(x, pack, rest, spread, cosine, sine, planes):
     rows, width = x.shape
-    out_width = weights.shape[1]
-    tile = min(256, rows)
+    depth = width // planes
+    half_width = spread.shape[1]
+    project_rows = pack.shape[0] - GAIN_ROWS - depth
+    vmem = pl.BlockSpec(memory_space=pltpu.VMEM)
+    bf16 = jnp.bfloat16
+    dma = pltpu.SemaphoreType.DMA
     return pl.pallas_call(
-        project_kernel,
-        grid=(rows // tile,),
-        in_specs=[
-            pl.BlockSpec((tile, width), lambda i: (i, 0)),
-            pl.BlockSpec((1, width), lambda i: (0, 0)),
-            pl.BlockSpec((width, out_width), lambda i: (0, 0)),
-            pl.BlockSpec((tile, LANES), lambda i: (i, 0)),
-            pl.BlockSpec((tile, LANES), lambda i: (i, 0)),
+        gather_kernel,
+        in_specs=[vmem] * 6,
+        out_specs=[vmem] * 6,
+        out_shape=[
+            jax.ShapeDtypeStruct((rows, width), bf16),
+            jax.ShapeDtypeStruct((rows, half_width), bf16),
+            jax.ShapeDtypeStruct((4, 2 * rows, LANES), bf16),
+            jax.ShapeDtypeStruct((width, 2 * half_width), bf16),
+            jax.ShapeDtypeStruct((2 * project_rows // HD * LANES, width), bf16),
+            jax.ShapeDtypeStruct((GAIN_ROWS, width), bf16),
         ],
-        out_specs=[
-            pl.BlockSpec((tile, width), lambda i: (i, 0)),
-            pl.BlockSpec((tile, q_width), lambda i: (i, 0)),
-            pl.BlockSpec((tile, out_width - q_width), lambda i: (i, 0)),
+        scratch_shapes=[
+            pltpu.VMEM((planes, 2, pack.shape[0], pack.shape[1]), bf16),
+            dma((planes - 1,)),
+            dma((planes - 1,)),
+            dma((planes - 1,)),
+            dma((planes - 1,)),
+            dma((2, planes)),
+            dma((2, planes)),
+            dma((4,)),
+            dma((4,)),
         ],
-        out_shape=[
-            jax.ShapeDtypeStruct((rows, width), jnp.bfloat16),
-            jax.ShapeDtypeStruct((rows, q_width), jnp.bfloat16),
-            jax.ShapeDtypeStruct((rows, out_width - q_width), jnp.bfloat16),
-        ],
-        compiler_params=pltpu.CompilerParams(vmem_limit_bytes=VMEM_BYTES),
-        name="project_tokens",
-    )(x, gain, weights, cosine, sine)
+        compiler_params=pltpu.CompilerParams(
+            collective_id=1, has_side_effects=True, vmem_limit_bytes=VMEM_BYTES
+        ),
+        cost_estimate=pl.CostEstimate(
+            flops=40_000_000_000, bytes_accessed=16_000_000, transcendentals=0
+        ),
+        name="gather_project",
+    )(x, pack, rest, spread, cosine, sine)
 
 
 def block_kinds(meta_ref, query_tile, key_tile, q_start, k_start):
@@ -588,16 +823,16 @@
 
         @pl.when(whole)
         def _():
-            absorb(dot(k_ref[rows, :], queries, ((1,), (1,))), v_ref[rows, :])
+            absorb(dot(k_ref[0, rows, :], queries, ((1,), (1,))), v_ref[0, rows, :])
 
         @pl.when(jnp.logical_not(whole | nothing))
         def _():
-            scores = dot(k_ref[rows, :], queries, ((1,), (1,)))
-            absorb(mask_scores(scores, prefix, q_start, k_start, tile), v_ref[rows, :])
+            scores = dot(k_ref[0, rows, :], queries, ((1,), (1,)))
+            absorb(mask_scores(scores, prefix, q_start, k_start, tile), v_ref[0, rows, :])
 
         return carry
 
-    lax.fori_loop(0, k_ref.shape[0] // key_tile, one, 0)
+    lax.fori_loop(0, k_ref.shape[1] // key_tile, one, 0)
     total = sum_ref[...]
     lse_ref[0, 0] = max_ref[...] + jnp.log2(total)
     out = (acc_ref[...] / total).T.astype(jnp.bfloat16)
@@ -607,7 +842,7 @@
 
 def attend(meta, q, kv, tile):
     rows, q_width = q.shape
-    keys = kv.shape[0]
+    keys = kv.shape[1]
     groups = q_width // (2 * LANES)
     steps = rows // tile
     return pl.pallas_call(
@@ -617,8 +852,8 @@
             grid=(groups, steps),
             in_specs=[
                 pl.BlockSpec((tile, 2 * LANES), lambda g, i, m: (i, g)),
-                pl.BlockSpec((keys, LANES), lambda g, i, m: (0, g)),
-                pl.BlockSpec((keys, LANES), lambda g, i, m: (0, groups + g)),
+                pl.BlockSpec((1, keys, LANES), lambda g, i, m: (g, 0, 0)),
+                pl.BlockSpec((1, keys, LANES), lambda g, i, m: (groups + g, 0, 0)),
             ],
             out_specs=[
                 pl.BlockSpec((tile, 2 * LANES), lambda g, i, m: (i, g)),
@@ -660,7 +895,7 @@
 ):
     query_tiles = lse_ref.shape[1]
     tile = q_ref.shape[0] // query_tiles
-    key_tile = k_ref.shape[0]
+    key_tile = k_ref.shape[1]
     j = pl.program_id(1)
 
     def stacked(ref, i):
@@ -679,8 +914,8 @@
         lax.fori_loop(0, query_tiles, one_delta, 0)
 
     k_start = meta_ref[1 + query_tiles + j]
-    keys = k_ref[...]
-    values = v_ref[...]
+    keys = k_ref[0]
+    values = v_ref[0]
 
     def one(i, carry):
         q_start = meta_ref[1 + i]
@@ -709,8 +944,8 @@
 
     zero = jnp.zeros((key_tile, LANES), jnp.float32)
     dk, dv = lax.fori_loop(0, query_tiles, one, (zero, zero))
-    dk_ref[...] = (dk * (1.0 / LOG2E)).astype(jnp.bfloat16)
-    dv_ref[...] = dv.astype(jnp.bfloat16)
+    dk_ref[0] = (dk * (1.0 / LOG2E)).astype(jnp.bfloat16)
+    dv_ref[0] = dv.astype(jnp.bfloat16)
 
     @pl.when(j == pl.num_programs(1) - 1)
     def _():
@@ -730,7 +965,7 @@
 
 def attend_back(meta, q, kv, o, d_out, lse, cosine, sine, tile):
     rows, q_width = q.shape
-    keys = kv.shape[0]
+    keys = kv.shape[1]
     groups = q_width // (2 * LANES)
     query_tiles = rows // tile
     key_tiles = keys // tile
@@ -742,8 +977,8 @@
             grid=(groups, key_tiles),
             in_specs=[
                 whole_q,
-                pl.BlockSpec((tile, LANES), lambda g, j, m: (j, g)),
-                pl.BlockSpec((tile, LANES), lambda g, j, m: (j, groups + g)),
+                pl.BlockSpec((1, tile, LANES), lambda g, j, m: (g, j, 0)),
+                pl.BlockSpec((1, tile, LANES), lambda g, j, m: (groups + g, j, 0)),
                 whole_q,
                 whole_q,
                 pl.BlockSpec((1, query_tiles, 1, 2 * tile), lambda g, j, m: (g, 0, 0, 0)),
@@ -752,8 +987,8 @@
             ],
             out_specs=[
                 whole_q,
-                pl.BlockSpec((tile, LANES), lambda g, j, m: (j, g)),
-                pl.BlockSpec((tile, LANES), lambda g, j, m: (j, g)),
+                pl.BlockSpec((1, tile, LANES), lambda g, j, m: (g, j, 0)),
+                pl.BlockSpec((1, tile, LANES), lambda g, j, m: (g, j, 0)),
             ],
             scratch_shapes=[
                 pltpu.VMEM((query_tiles, 1, 2 * tile), jnp.float32),
@@ -762,8 +997,8 @@
         ),
         out_shape=[
             jax.ShapeDtypeStruct((rows, q_width), jnp.bfloat16),
-            jax.ShapeDtypeStruct((keys, groups * LANES), jnp.bfloat16),
-            jax.ShapeDtypeStruct((keys, groups * LANES), jnp.bfloat16),
+            jax.ShapeDtypeStruct((groups, keys, LANES), jnp.bfloat16),
+            jax.ShapeDtypeStruct((groups, keys, LANES), jnp.bfloat16),
         ],
         compiler_params=pltpu.CompilerParams(vmem_limit_bytes=VMEM_BYTES),
         cost_estimate=pl.CostEstimate(
@@ -809,18 +1044,23 @@
         whole = lax.all_gather(mine, "fsdp", axis=axis, tiled=True)
         return whole, swap_ctx(whole)
 
-    gains = lax.all_gather(jnp.stack([gain_attend, gain_feed]), "fsdp", axis=1, tiled=True)
-    gain_one, gain_two = gains[:1].astype(f32), gains[1:].astype(f32)
-    qkv_mine, qkv_other = gathered(
-        jnp.concatenate([half(w_query, 1), half(w_key, 1), half(w_value, 1)], axis=1), 0
-    )
-    wp_mine, wp_other = gathered(half(w_project, 0), 1)
+    planes = lax.axis_size("fsdp")
+    kv_half = w_key.shape[1] // 2
+    q_half = w_query.shape[1] // 2
+
+    def packed(which):
+        return jnp.concatenate(
+            [
+                jnp.concatenate([half(w_query, 1, which), half(w_key, 1, which), half(w_value, 1, which)], axis=1),
+                half(w_project, 0, which),
+                jnp.pad(jnp.stack([gain_attend, gain_feed]), ((0, GAIN_ROWS - 2), (0, 0))),
+            ],
+            axis=0,
+        )
+
     wg_mine, wg_other = gathered(half(w_gate, 1), 0)
     wu_mine, wu_other = gathered(half(w_up, 1), 0)
     wd_mine, wd_other = gathered(half(w_down, 0), 1)
-
-    kv_half = w_key.shape[1] // 2
-    q_half = w_query.shape[1] // 2
 
     def parts(block):
         return (
@@ -829,14 +1069,13 @@
             block[:, q_half + kv_half :],
         )
 
-    mine, other = parts(qkv_mine), parts(qkv_other)
-    w_qkv = jnp.concatenate(
-        [spread_turned(jnp.concatenate([mine[0], other[0], mine[1], other[1]], axis=1)),
-         spread_plain(jnp.concatenate([mine[2], other[2]], axis=1))],
-        axis=1,
-    )
-    q_width = 2 * q_half // HD * LANES
-    kv_width = 2 * kv_half // HD * LANES
+    half_heads = (q_half + 2 * kv_half) // HD
+    spread = np.zeros((half_heads * HD, half_heads * LANES), np.float32)
+    for head in range(half_heads):
+        for lane in range(HD):
+            turned = lane if lane < HALF or head == half_heads - 1 else lane - HALF + SPAN
+            spread[head * HD + lane, head * LANES + turned] = 1.0
+    spread = jnp.asarray(spread, bf16)
 
     frequency = ROPE_BASE ** (-(jnp.arange(HALF, dtype=f32) * 2.0 / HD))
     frequency = jnp.pad(frequency, (0, SPAN - HALF))
@@ -856,14 +1095,12 @@
 
     x = tokens[0]
     cot = cotangent[0]
-    normed, q, kv = project_tokens(x, gain_one, w_qkv, cosine, sine, q_width)
-    kv_away = swap_ctx(kv)
-    kv_away = kv_away.reshape(rows, 2, 2, kv_width // 2)[:, :, ::-1].reshape(rows, 2 * kv_width)
-    kv_all = jnp.concatenate([kv, kv_away], axis=0)
+    normed, q, kv_all, w_qkv, w_p, gains = gather_project(
+        x, packed(c), packed(1 - c), spread, cosine, sine, planes
+    )
+    gain_one, gain_two = gains[0:1].astype(f32), gains[1:2].astype(f32)
     o, lse = attend(meta, q, kv_all, tile)
-    o_low = close_plain(o)
-    w_p = jnp.concatenate([wp_mine, wp_other], axis=0)
-    middle = x.astype(f32) + paired_tensor_sum(dot(o_low, w_p, ((1,), (0,))))
+    middle = x.astype(f32) + paired_tensor_sum(dot(o, w_p, ((1,), (0,))))
     factor_two = rms_factor(middle)
     normed_feed = (middle * factor_two * gain_two).astype(bf16)
 
@@ -918,33 +1155,36 @@
     gain_two_term = jnp.sum(feed_in * middle * factor_two, axis=0)
     middle_grad = cot.astype(f32) + rms_back(middle, factor_two, gain_two, feed_in)
     middle_low = middle_grad.astype(bf16)
-    project_part = dot(o_low, middle_low, contract_rows)
+    project_part = dot(o, middle_low, contract_rows)
+    project_part = project_part.reshape(-1, LANES, width)[:, :HD].reshape(-1, width)
     rows_half = project_part.shape[0] // 2
     project_share = summed(project_part[rows_half:], project_part[:rows_half], 1)
-    d_out = spread_plain(dot(middle_low, w_p, ((1,), (1,))).astype(bf16))
+    d_out = dot(middle_low, w_p, ((1,), (1,))).astype(bf16)
     q_low, dk, dv = attend_back(meta, q, kv_all, o, d_out, lse, cosine, sine, tile)
-    d_kv = jnp.concatenate([dk, dv], axis=1)
-    d_kv_away = swap_ctx(d_kv[rows:])
-    d_kv_away = d_kv_away.reshape(rows, 2, 2, kv_width // 2)[:, :, ::-1].reshape(rows, 2 * kv_width)
-    d_kv = d_kv[:rows].astype(f32) + d_kv_away.astype(f32)
-    key_turned = d_kv[:, :kv_width].reshape(rows, 2, 2, SPAN)
-    sine_half, cosine_half = sine[:, None, SPAN:], cosine[:, None, SPAN:]
-    k_low = jnp.stack(
-        [
-            key_turned[:, :, 0] * cosine_half + key_turned[:, :, 1] * sine_half,
-            key_turned[:, :, 1] * cosine_half - key_turned[:, :, 0] * sine_half,
-        ],
-        axis=2,
-    )
-    k_low = k_low.reshape(rows, kv_width).astype(bf16)
-    v_low = d_kv[:, kv_width:].astype(bf16)
-    low = jnp.concatenate([q_low, k_low, v_low], axis=1)
-    normed_in = paired_tensor_sum(dot(low, w_qkv, ((1,), (1,))))
-    qc, kc, vc = close_turned(q_low), close_turned(k_low), close_plain(v_low)
-    low_mine = jnp.concatenate([qc[:, :q_half], kc[:, :kv_half], vc[:, :kv_half]], axis=1)
-    low_other = jnp.concatenate([qc[:, q_half:], kc[:, kv_half:], vc[:, kv_half:]], axis=1)
+    d_kv = jnp.concatenate([dk, dv], axis=0)
+    d_kv_away = swap_ctx(d_kv[:, rows:])
+    d_kv = [
+        d_kv[slab, :rows].astype(f32) + d_kv_away[slab ^ 1].astype(f32) for slab in range(4)
+    ]
+
+    def turn_back(part):
+        return part * cosine - jnp.concatenate([part[:, SPAN:], part[:, :SPAN]], axis=1) * sine
+
+    low_mine = jnp.concatenate(
+        [q_low[:, : 2 * LANES], turn_back(d_kv[0]).astype(bf16), d_kv[2].astype(bf16)], axis=1
+    )
+    low_other = jnp.concatenate(
+        [q_low[:, 2 * LANES :], turn_back(d_kv[1]).astype(bf16), d_kv[3].astype(bf16)], axis=1
+    )
+    half_width = low_mine.shape[1]
+    normed_in = paired_tensor_sum(
+        dot(low_mine, w_qkv[:, :half_width], ((1,), (1,)))
+        + dot(low_other, w_qkv[:, half_width:], ((1,), (1,)))
+    )
+    close_mine = dot(low_mine, spread, ((1,), (1,))).astype(bf16)
+    close_other = dot(low_other, spread, ((1,), (1,))).astype(bf16)
     qkv_share = summed(
-        dot(normed, low_other, contract_rows), dot(normed, low_mine, contract_rows), 0
+        dot(normed, close_other, contract_rows), dot(normed, close_mine, contract_rows), 0
     )
     qkv_away = swap_ctx(qkv_share)
     shares = [
@@ -975,7 +1215,7 @@
 
 
 def solution(mesh):
-    paired = mesh.shape["ctx"] == 2 and mesh.shape["tp"] == 4
+    paired = mesh.shape["ctx"] == 2 and mesh.shape["tp"] == 4 and mesh.shape["fsdp"] == 4
     return jax.shard_map(
         paired_body if paired else general_body,
         mesh=mesh,

time: 710 us -> 657 us (0.925)
  Pallas kernels: 79.6 us -> 169 us
  waiting for transfers between devices: 260 us -> 198 us
  local copies, waits for them, and re-layouts: 101 us -> 46.1 us
  blocking collectives: 29.6 us -> 0 us
  matrix products: 92.6 us -> 105 us
    pallas_call x1, Pallas kernels: 8.53 us -> 102 us  [gather_project(): pl.pallas_call(gather_kernel, in_specs=[vmem] * 6, out_specs=[vmem] * 6,...]
    ppermute x17 -> x14, waiting for transfers between devices: 135 us -> 55 us  [swap_ctx(): return lax.ppermute(block, 'ctx', [(0, 1), (1, 0)])]
    all_gather x2 -> x0, blocking collectives: 29.6 us -> none  [the longest x1 15.9 us: gathered(): whole = lax.all_gather(mine, 'fsdp', axis=axis, tiled=True)]
    ppermute x4, waiting for transfers between devices: 44.1 us -> 73.6 us  [swap_chip(): return lax.ppermute(block, 'tp', [(0, 2), (2, 0), (1, 3), (3, 1)])]
    rev x2 -> x0, local copies, waits for them, and re-layouts: 15.7 us -> none  [the longest x1 10.3 us: paired_body(): d_kv_away.reshape(rows, 2, 2, kv_width // 2)[:, :, ::-1]]
    all_gather x4 -> x3, waiting for transfers between devices: 46.1 us -> 32.6 us  [gathered(): whole = lax.all_gather(mine, 'fsdp', axis=axis, tiled=True)]
    reshape x8 -> x0, local copies, waits for them, and re-layouts: 12.9 us -> none  [the longest x2 3.52 us: close_plain(): columns.reshape(rows, width // LANES, LANES)[..., :HD]]
    dot_general x24 -> x29, matrix products: 92.6 us -> 105 us  [dot(): lax.dot_general(a, b, (contract, ((), ())), preferred_element_type=jnp.fl...]
  transfers between devices with their start and end apart: 39 -> 35, of which waited for: 19 -> 15; matrix products, arithmetic and copies ran while one was open for 37% -> 34% of each run, Pallas kernels for 11% -> 26%
where the time goes in v2:
time: 657 us; the launch traced here: 649 us
  waiting for transfers between devices  198 us (30%)
  Pallas kernels  169 us (26%)
  matrix products  105 us (16%)
  other arithmetic  95.3 us (15%)
  local copies, waits for them, and re-layouts  46.1 us (7%)
  starting transfers between devices  20.1 us (3%)
  between operations  15.6 us (2%)
    dot_general x29, matrix products, dot(): lax.dot_general(a, b, (contract, ((), ())), preferred_element_type=jnp.fl...  105 us
    pallas_call x1, Pallas kernels, gather_project(): pl.pallas_call(gather_kernel, in_specs=[vmem] * 6, out_specs=[vmem] * 6,...  102 us
    ppermute x4, waiting for transfers between devices, swap_chip(): return lax.ppermute(block, 'tp', [(0, 2), (2, 0), (1, 3), (3, 1)])  73.6 us
    ppermute x14, waiting for transfers between devices, swap_ctx(): return lax.ppermute(block, 'ctx', [(0, 1), (1, 0)])  55 us
    pallas_call x1, Pallas kernels, attend_back(): pl.pallas_call(attend_back_kernel, grid_spec=pltpu.PrefetchScalarGridSpec...  41.9 us
    unnamed x12, waiting for transfers between devices  35.1 us
    all_gather x3, waiting for transfers between devices, gathered(): whole = lax.all_gather(mine, 'fsdp', axis=axis, tiled=True)  32.6 us
    pallas_call x1, Pallas kernels, attend(): pl.pallas_call(attend_kernel, grid_spec=pltpu.PrefetchScalarGridSpec(num_...  25.6 us
  transfers between devices with their start and end apart: 35, of which 15 were waited for; matrix products, arithmetic and copies ran while one was open for 34% of the time, Pallas kernels for 26%

profile of v2, /device:TPU:0, one launch (start us, length us, event | category | flops | bytes accessed | tf_op | source)
XLA Modules:
  0.0 649.2 jit_solution(5957705101888833044)
XLA Ops:
  14.1 1.9 fusion.75
  19.3 101.5 %gather_project.1 = (bf16[1024,1536]{1,0:T(8,128)(2,1)}, bf16[1024,512]{1,0:T(8,128)(2,1)}, bf16[4,2048,128]{2,1,0:T(8,128)(2,1)}, bf16[1536,1024]{1,0:T(8,128)(...) custom-call(bf16[1024,1536]{1,0:T(8,128)(2,1)} %bitcast.137, bf16[592,384]{1,0:T(8,128)(2,1)} %get-tuple-element.100.pack_ref, ...), custom_call_target="tpu_custom_call" | custom-call | flops 40000000000 | bytes 16000000 | tf_op jit(solution)/shard_map/gather_project/pallas_call | solution.py:750
  122.1 25.6 %attend.1 = (bf16[1024,512]{1,0:T(8,128)(2,1)}, f32[2,4,1,512]{3,2,1,0:T(1,128)}) custom-call(s32[13]{0:T(128)} %pad_add_fusion.meta_ref, bf16[1024,512]{1,0:T(8,128)(2,1)} %get-tuple-element.22.q_ref, bf16[4,2048,128]{2,1,0:T(8,128)(2,1)} %get-tuple-element.23.k_ref.v_ref, bf16[4,2048,128]{2,1,0:T(8,128)(2,1)} %get-tuple-element.23.k_ref.v_ref), custom_call_target="tpu_custom_call" | custom-call | flops 4294967296 | bytes 6000000 | tf_op jit(solution)/shard_map/attend/pallas_call | solution.py:848
  147.7 3.0 convolution_convert_fusion
  156.0 1.8 add_convert_fusion.13
  160.5 33.8 %collective-permute-done.1 = bf16[512,1536]{1,0:T(8,128)(2,1)S(1)} collective-permute-done((bf16[512,1536]{1,0:T(8,128)(2,1)S(1)}, bf16[512,1536]{1,0:T(8,128)(2,1)S(1)}, u32[]{:S(2)}, u32[]{:S(2)}) %collective-permute-start.1) | collective-permute-done | bytes 1572896 | tf_op jit(solution)/shard_map/ppermute | solution.py:442
  197.3 32.6 %all-gather.4.cloned.1.call-done = bf16[1536,512]{1,0:T(8,128)(2,1)} async-done(((bf16[384,512]{1,0:T(8,128)(2,1)}), bf16[1536,512]{1,0:T(8,128)(2,1)}) %all-gather.4.cloned.1.call-update) | async-done | bytes 1572880 | tf_op jit(solution)/shard_map/all_gather | solution.py:1044
  231.3 4.2 fusion.24
  235.6 4.3 fusion.22
  239.9 3.8 multiply_reduce_fusion
  243.7 3.8 multiply_convert_fusion
  247.6 1.8 fusion.98
  250.1 3.7 fusion.42
  253.8 1.8 fusion.101
  255.6 1.8 fusion.102
  257.5 10.5 %collective-permute-done.3 = bf16[1536,512]{1,0:T(8,128)(2,1)S(1)} collective-permute-done((bf16[1536,512]{1,0:T(8,128)(2,1)}, bf16[1536,512]{1,0:T(8,128)(2,1)S(1)}, u32[]{:S(2)}, u32[]{:S(2)}) %collective-permute-start.3) | collective-permute-done | bytes 1572896 | tf_op jit(solution)/shard_map/ppermute | solution.py:434
  269.8 5.4 fusion.37
  275.2 6.3 fusion.103
  281.5 6.0 add_convert_fusion.1
  289.5 3.0 convolution_convert_fusion.1
  292.8 10.3 %copy.45 = bf16[512,1024]{1,0:T(8,128)(2,1)} copy(bf16[512,1024]{0,1:T(8,128)(2,1)} %bitcast.142) | data formatting | bytes 2097152 | tf_op jit(solution)/shard_map/dot_general | solution.py:464
  303.1 5.3 convolution_convert_fusion.2
  310.1 2.9 add_convert_fusion.9
  314.5 15.6 %collective-permute-done.23 = bf16[1536,512]{1,0:T(8,128)(2,1)} collective-permute-done((bf16[1536,512]{1,0:T(8,128)(2,1)}, bf16[1536,512]{1,0:T(8,128)(2,1)}, u32[]{:S(2)}, u32[]{:S(2)}) %collective-permute-start.23) | collective-permute-done | bytes 1572896 | tf_op jit(solution)/shard_map/ppermute | solution.py:434
  330.1 4.4 add_convert_fusion.4
  334.6 3.6 fusion.99
  338.2 3.2 add_convert_fusion.3
  341.5 7.5 %collective-permute-done.10 = bf16[512,1536]{1,0:T(8,128)(2,1)} collective-permute-done((bf16[512,1536]{1,0:T(8,128)(2,1)}, bf16[512,1536]{1,0:T(8,128)(2,1)}, u32[]{:S(2)}, u32[]{:S(2)}) %collective-permute-start.10) | collective-permute-done | bytes 1572896 | tf_op jit(solution)/shard_map/ppermute | solution.py:442
  348.9 3.4 add_convert_fusion.8
  354.1 3.0 fusion.32
  357.1 3.0 fusion.29
  360.2 2.4 collective-permute-done.21
  362.6 4.4 add_convert_fusion.5
  367.1 6.4 fusion.2
  373.5 11.0 %fusion.48.do_ref = bf16[1024,512]{1,0:T(8,128)(2,1)} fusion(bf16[512,1536]{1,0:T(8,128)(2,1)S(1)} %copy-done.52, bf16[1,1024,1536]{2,1,0:T(8,128)(2,1)S(1)} %copy-done.18, f32[1024]{0:T(1024)S(1)} %broadcast_multiply_fusion.1, f32[1024]{0:T(1024)S(1)} %get-tuple-element.106, f32[1536]{0:T(1024)S(1)} %get-tuple-element.62, ...), kind=kOutput, calls=%fused_computation.93 | convolution fusion | flops 1658322944 | bytes 15222785 | tf_op jit(solution)/shard_map/dot_general | solution.py:464
  384.6 41.9 %attend_back.1 = (bf16[1024,512]{1,0:T(8,128)(2,1)}, bf16[2,2048,128]{2,1,0:T(8,128)(2,1)}, bf16[2,2048,128]{2,1,0:T(8,128)(2,1)}) custom-call(s32[13]{0:T(128)} %pad_add_fusion.meta_ref, bf16[1024,512]{1,0:T(8,128)(2,1)} %get-tuple-element.22.q_ref, bf16[4,2048,128]{2,1,0:T(8,128)(2,1)} %get-tuple-element.23.k_ref.v_ref, ...), custom_call_target="tpu_custom_call" | custom-call | flops 10737418240 | bytes 8000000 | tf_op jit(solution)/shard_map/attend_back/pallas_call | solution.py:973
  426.4 2.4 pad_maximum_fusion.1
  428.9 1.9 pad_maximum_fusion
  430.7 4.7 copy.50
  435.5 2.4 add_convert_fusion.11
  439.5 13.6 %collective-permute-done.12 = bf16[4,1024,128]{2,1,0:T(8,128)(2,1)} collective-permute-done((bf16[4,1024,128]{2,1,0:T(8,128)(2,1)}, bf16[4,1024,128]{2,1,0:T(8,128)(2,1)}, u32[]{:S(2)}, u32[]{:S(2)}) %collective-permute-start.12) | collective-permute-done | bytes 1048608 | tf_op jit(solution)/shard_map/ppermute | solution.py:434
  456.9 1.8 fusion.46
  458.7 1.8 add_convert_fusion
  463.5 9.7 %collective-permute-done.7 = bf16[512,1536]{1,0:T(8,128)(2,1)S(1)} collective-permute-done((bf16[512,1536]{1,0:T(8,128)(2,1)S(1)}, bf16[512,1536]{1,0:T(8,128)(2,1)S(1)}, u32[]{:S(2)}, u32[]{:S(2)}) %collective-permute-start.7) | collective-permute-done | bytes 1572896 | tf_op jit(solution)/shard_map/ppermute | solution.py:442
  474.7 7.2 %fusion.11 = (f32[1536]{0:T(1024)S(1)}, f32[1024]{0:T(1024)S(1)}) fusion(f32[1024]{0:T(1024)S(1)} %get-tuple-element.107, bf16[1,1024,1536]{2,1,0:T(8,128)(2,1)S(1)} %copy-done.2, bf16[512,1536]{1,0:T(8,128)(2,1)} %add_convert_fusion.8, bf16[512,1536]{1,0:T(8,128)(2,1)} %collective-permute-done.11, pred[]{:T(512)S(6)} %eq.31, ...), kind=kLoop, calls=%fused_computation.20 | loop fusion | flops 42464768 | bytes 9451521 | tf_op jit(solution)/shard_map/reduce_sum | solution.py:1155
  482.0 1.8 collective-permute-start.24
  484.1 3.5 add_convert_fusion.7
  493.9 6.1 convolution_convert_fusion.3
  501.6 22.6 %collective-permute-done.14 = bf16[512,1536]{1,0:T(8,128)(2,1)} collective-permute-done((bf16[512,1536]{1,0:T(8,128)(2,1)}, bf16[512,1536]{1,0:T(8,128)(2,1)}, u32[]{:S(2)}, u32[]{:S(2)}) %collective-permute-start.14) | collective-permute-done | bytes 1572896 | tf_op jit(solution)/shard_map/ppermute | solution.py:442
  524.2 3.4 add_convert_fusion.6
  527.7 7.1 %add_convert_fusion.2 = bf16[1,1024,1536]{2,1,0:T(8,128)(2,1)} fusion(bf16[1,1024,1536]{2,1,0:T(8,128)(2,1)S(1)} %copy-done.2, bf16[1,512,1536]{2,1,0:T(8,128)(2,1)} %bitcast.5, bf16[1,512,1536]{2,1,0:T(8,128)(2,1)} %bitcast.4, pred[]{:T(512)S(6)} %eq.31, bf16[1,512,1536]{2,1,0:T(8,128)(2,1)} %bitcast.2, bf16[1,512,1536]{2,1,0:T(8,128)(2,1)} %bitcast.3), kind=kLoop, calls=%fused_computation.28 | loop fusion | flops 37748736 | bytes 12582913 | tf_op jit(solution)/shard_map/convert_element_type | solution.py:1153
  536.4 2.3 copy.51
  540.2 6.2 add_convert_fusion.14
  546.6 5.0 fusion.15
  551.6 15.7 %fusion.9 = (bf16[1,1024,1536]{2,1,0:T(8,128)(2,1)}, bf16[1,1024,1536]{2,1,0:T(8,128)(2,1)S(1)}) fusion(bf16[1,1024,1536]{2,1,0:T(8,128)(2,1)S(1)} %copy-done.2, bf16[1,512,1536]{2,1,0:T(8,128)(2,1)} %bitcast.16, bf16[1,512,1536]{2,1,0:T(8,128)(2,1)} %bitcast.15, f32[1024]{0:T(1024)S(1)} %broadcast_multiply_fusion, f32[1024]{0:T(1024)S(1)} %get-tuple-element.104, ...), kind=kLoop, calls=%fused_computation.18 | loop fusion | flops 73924608 | bytes 22056960 | tf_op jit(solution)/shard_map/convert_element_type | solution.py:1197
  567.3 1.8 fusion.16
  570.5 2.5 fusion.63
  573.0 2.5 fusion.64
  579.6 6.8 %collective-permute-done.19 = bf16[192,1536]{1,0:T(8,128)(2,1)} collective-permute-done((bf16[192,1536]{1,0:T(8,128)(2,1)}, bf16[192,1536]{1,0:T(8,128)(2,1)}, u32[]{:S(2)}, u32[]{:S(2)}) %collective-permute-start.19) | collective-permute-done | bytes 589856 | tf_op jit(solution)/shard_map/ppermute | solution.py:434
  589.1 3.0 collective-permute-done.18
  596.0 3.0 collective-permute-done.16
  600.2 14.5 %reduce-scatter.21.cloned.1.call-done = bf16[384,192]{1,0:T(8,128)(2,1)} async-done(((bf16[1536,192]{1,0:T(8,128)(2,1)}), bf16[384,192]{1,0:T(8,128)(2,1)}) %reduce-scatter.21.cloned.1.call-update) | async-done | bytes 147472
  619.3 20.4 %reduce-scatter.19.cloned.1.call-done = f32[384,2]{1,0:T(8,128)} async-done(((f32[1536,2]{1,0:T(8,128)}), f32[384,2]{1,0:T(8,128)}) %reduce-scatter.19.cloned.1.call-update) | async-done | bytes 3088
  639.7 1.9 slice_reduce_fusion
  (233 shorter events, 72.8 us)
Async XLA Ops:
  7.2 6.6 %copy-start.31 = (bf16[384,384]{1,0:T(8,128)(2,1)S(1)}, bf16[384,384]{1,0:T(8,128)(2,1)}, u32[]{:S(2)}) copy-start(bf16[384,384]{1,0:T(8,128)(2,1)} %param.18) | copy-start | bytes 884740
  7.2 153.2 %all-gather.8.cloned.1.call-start = ((), (), s32[]{:S(2)}) async-start(), calls=%async_computation.8 | async-start | bytes 1966080 | tf_op jit(solution)/shard_map/all_gather | solution.py:1044
  9.1 188.1 %all-gather.6.cloned.1.call-start = ((), (), s32[]{:S(2)}) async-start(), calls=%async_computation.7 | async-start | bytes 1966080 | tf_op jit(solution)/shard_map/all_gather | solution.py:1044
  122.1 25.6 %copy-start.51 = (bf16[512,1536]{1,0:T(8,128)(2,1)S(1)}, bf16[512,1536]{1,0:T(8,128)(2,1)}, u32[]{:S(2)}) copy-start(bf16[512,1536]{1,0:T(8,128)(2,1)} %get-tuple-element.25) | copy-start | bytes 4718596
  152.5 3.5 collective-permute-start
  154.3 75.5 %all-gather.4.cloned.1.call-start = ((), (), s32[]{:S(2)}) async-start(), calls=%async_computation.6 | async-start | bytes 1966080 | tf_op jit(solution)/shard_map/all_gather | solution.py:1044
  154.4 4.9 copy-start.39
  157.8 36.5 %collective-permute-start.1 = (bf16[512,1536]{1,0:T(8,128)(2,1)S(1)}, bf16[512,1536]{1,0:T(8,128)(2,1)S(1)}, u32[]{:S(2)}, u32[]{:S(2)}) collective-permute-start(bf16[512,1536]{1,0:T(8,128)(2,1)S(1)} %add_convert_fusion.13), channel_id=1, source_target_pairs={{0,2},{2,0},{1,3},{3,1},{4,6},{6,4},{5,7},{7,5},{8,10},{10,8},{9,1... | collective-permute-start | bytes 4718600 | tf_op jit(solution)/shard_map/ppermute | solution.py:442
  160.1 321.9 %reduce-scatter.17.cloned.1.call-start = ((), (), s32[]{:S(2)}) async-start(), calls=%async_computation.11 | async-start | bytes 1966080 | tf_op jit(solution)/shard_map/reduce_scatter | solution.py:1125
  160.4 75.1 %collective-permute-start.5 = (bf16[512,1536]{1,0:T(8,128)(2,1)}, bf16[512,1536]{1,0:T(8,128)(2,1)}, u32[]{:S(2)}, u32[]{:S(2)}) collective-permute-start(bf16[512,1536]{1,0:T(8,128)(2,1)} %all-gather.8.cloned.1.call-done), channel_id=1, source_target_pairs={{0,4},{4,0},{1,5},{5,1},{2,6},{6,2},{3,7},{7,3},{8,12},{12,8},{9,1... | collective-permute-start | bytes 4718600 | tf_op jit(solution)/shard_map/ppermute | solution.py:434
  195.8 44.1 %collective-permute-start.2 = (bf16[512,1536]{1,0:T(8,128)(2,1)}, bf16[512,1536]{1,0:T(8,128)(2,1)}, u32[]{:S(2)}, u32[]{:S(2)}) collective-permute-start(bf16[512,1536]{1,0:T(8,128)(2,1)} %add_convert_fusion.12), channel_id=1, source_target_pairs={{0,1},{1,0},{2,3},{3,2},{4,5},{5,4},{6,7},{7,6},{8,9},{9,8},{10,11... | collective-permute-start | bytes 4718600 | tf_op jit(solution)/shard_map/ppermute | solution.py:438
  197.3 72.5 %collective-permute-start.4 = (bf16[1536,512]{1,0:T(8,128)(2,1)}, bf16[1536,512]{1,0:T(8,128)(2,1)}, u32[]{:S(2)}, u32[]{:S(2)}) collective-permute-start(bf16[1536,512]{1,0:T(8,128)(2,1)} %all-gather.6.cloned.1.call-done), channel_id=1, source_target_pairs={{0,4},{4,0},{1,5},{5,1},{2,6},{6,2},{3,7},{7,3},{8,12},{12,8},{9,1... | collective-permute-start | bytes 4718600 | tf_op jit(solution)/shard_map/ppermute | solution.py:434
  229.9 38.1 %collective-permute-start.3 = (bf16[1536,512]{1,0:T(8,128)(2,1)}, bf16[1536,512]{1,0:T(8,128)(2,1)S(1)}, u32[]{:S(2)}, u32[]{:S(2)}) collective-permute-start(bf16[1536,512]{1,0:T(8,128)(2,1)} %all-gather.4.cloned.1.call-done), channel_id=1, source_target_pairs={{0,4},{4,0},{1,5},{5,1},{2,6},{6,2},{3,7},{7,3},{8,12},{12,8},{9,1... | collective-permute-start | bytes 4718600 | tf_op jit(solution)/shard_map/ppermute | solution.py:434
  247.5 41.2 %copy-start.11 = (bf16[1024,1536]{1,0:T(8,128)(2,1)}, bf16[1024,1536]{1,0:T(8,128)(2,1)S(1)}, u32[]{:S(2)}) copy-start(bf16[1024,1536]{1,0:T(8,128)(2,1)S(1)} %multiply_convert_fusion) | copy-start | bytes 9437188
  275.2 6.3 copy-start.49
  287.5 5.0 copy-start.3
  288.7 21.4 %collective-permute-start.9 = (bf16[512,1536]{1,0:T(8,128)(2,1)}, bf16[512,1536]{1,0:T(8,128)(2,1)}, u32[]{:S(2)}, u32[]{:S(2)}) collective-permute-start(bf16[512,1536]{1,0:T(8,128)(2,1)} %constant_dynamic-slice_fusion.1), channel_id=1, source_target_pairs={{0,1},{1,0},{2,3},{3,2},{4,5},{5,4},{6,7},{7,6},{8,9},{9,8},{10,11... | collective-permute-start | bytes 4718600 | tf_op jit(solution)/shard_map/ppermute | solution.py:438
  292.5 37.6 %collective-permute-start.23 = (bf16[1536,512]{1,0:T(8,128)(2,1)}, bf16[1536,512]{1,0:T(8,128)(2,1)}, u32[]{:S(2)}, u32[]{:S(2)}) collective-permute-start(bf16[1536,512]{1,0:T(8,128)(2,1)} %convolution_convert_fusion.1), channel_id=1, source_target_pairs={{0,4},{4,0},{1,5},{5,1},{2,6},{6,2},{3,7},{7,3},{8,12},{12,8},{9,1... | collective-permute-start | bytes 4718600 | tf_op jit(solution)/shard_map/ppermute | solution.py:434
  303.1 7.1 %copy-start.4 = (bf16[1024,1536]{1,0:T(8,128)(2,1)S(1)}, bf16[1024,1536]{1,0:T(8,128)(2,1)}, u32[]{:S(2)}) copy-start(bf16[1024,1536]{1,0:T(8,128)(2,1)} %copy-done.3) | copy-start | bytes 9437188
  308.4 21.7 %copy-start.12 = (bf16[1024,1536]{1,0:T(8,128)(2,1)S(1)}, bf16[1024,1536]{1,0:T(8,128)(2,1)}, u32[]{:S(2)}) copy-start(bf16[1024,1536]{1,0:T(8,128)(2,1)} %copy-done.11) | copy-start | bytes 9437188
  308.4 21.7 %copy-start.48 = (bf16[1024,512]{1,0:T(8,128)(2,1)S(1)}, bf16[1024,512]{1,0:T(8,128)(2,1)}, u32[]{:S(2)}) copy-start(bf16[1024,512]{1,0:T(8,128)(2,1)} %copy-done.47) | copy-start | bytes 3145732
  308.4 54.2 %collective-permute-start.21 = (bf16[1536,512]{1,0:T(8,128)(2,1)}, bf16[1536,512]{1,0:T(8,128)(2,1)}, u32[]{:S(2)}, u32[]{:S(2)}) collective-permute-start(bf16[1536,512]{1,0:T(8,128)(2,1)} %convolution_convert_fusion.2), channel_id=1, source_target_pairs={{0,4},{4,0},{1,5},{5,1},{2,6},{6,2},{3,7},{7,3},{8,12},{12,8},{9,1... | collective-permute-start | bytes 4718600 | tf_op jit(solution)/shard_map/ppermute | solution.py:434
  313.1 35.9 %collective-permute-start.10 = (bf16[512,1536]{1,0:T(8,128)(2,1)}, bf16[512,1536]{1,0:T(8,128)(2,1)}, u32[]{:S(2)}, u32[]{:S(2)}) collective-permute-start(bf16[512,1536]{1,0:T(8,128)(2,1)} %add_convert_fusion.9), channel_id=1, source_target_pairs={{0,2},{2,0},{1,3},{3,1},{4,6},{6,4},{5,7},{7,5},{8,10},{10,8},{9,1... | collective-permute-start | bytes 4718600 | tf_op jit(solution)/shard_map/ppermute | solution.py:442
  334.6 149.2 %reduce-scatter.15.cloned.1.call-start = ((), (), s32[]{:S(2)}) async-start(), calls=%async_computation.10 | async-start | bytes 1966080 | tf_op jit(solution)/shard_map/reduce_scatter | solution.py:1125
  341.4 12.2 %copy-start.14 = (bf16[1024,1536]{1,0:T(8,128)(2,1)}, bf16[1024,1536]{1,0:T(8,128)(2,1)S(1)}, u32[]{:S(2)}) copy-start(bf16[1024,1536]{1,0:T(8,128)(2,1)S(1)} %add_convert_fusion.3) | copy-start | bytes 9437188
  341.4 12.7 %copy-start.17 = (bf16[1,1024,1536]{2,1,0:T(8,128)(2,1)S(1)}, bf16[1,1024,1536]{2,1,0:T(8,128)(2,1)}, u32[]{:S(2)}) copy-start(bf16[1,1024,1536]{2,1,0:T(8,128)(2,1)} %param.26) | copy-start | bytes 9437188
  352.4 14.7 %collective-permute-start.11 = (bf16[512,1536]{1,0:T(8,128)(2,1)}, bf16[512,1536]{1,0:T(8,128)(2,1)}, u32[]{:S(2)}, u32[]{:S(2)}) collective-permute-start(bf16[512,1536]{1,0:T(8,128)(2,1)} %add_convert_fusion.8), channel_id=1, source_target_pairs={{0,1},{1,0},{2,3},{3,2},{4,5},{5,4},{6,7},{7,6},{8,9},{9,8},{10,11... | collective-permute-start | bytes 4718600 | tf_op jit(solution)/shard_map/ppermute | solution.py:438
  353.6 81.9 %collective-permute-start.6 = (bf16[512,1536]{1,0:T(8,128)(2,1)}, bf16[512,1536]{1,0:T(8,128)(2,1)}, u32[]{:S(2)}, u32[]{:S(2)}) collective-permute-start(bf16[512,1536]{1,0:T(8,128)(2,1)} %constant_dynamic-slice_fusion.2), channel_id=1, source_target_pairs={{0,1},{1,0},{2,3},{3,2},{4,5},{5,4},{6,7},{7,6},{8,9},{9,8},{10,11... | collective-permute-start | bytes 4718600 | tf_op jit(solution)/shard_map/ppermute | solution.py:438
  357.1 5.5 copy-start.13
  357.1 5.5 copy-start.46
  367.0 169.4 %reduce-scatter.23.cloned.1.call-start = ((), (), s32[]{:S(2)}) async-start(), calls=%async_computation.14 | async-start | bytes 3932160
  367.0 6.5 copy-start.18
  367.1 6.5 copy-start.52
  428.9 24.3 %collective-permute-start.12 = (bf16[4,1024,128]{2,1,0:T(8,128)(2,1)}, bf16[4,1024,128]{2,1,0:T(8,128)(2,1)}, u32[]{:S(2)}, u32[]{:S(2)}) collective-permute-start(bf16[4,1024,128]{2,1,0:T(8,128)(2,1)} %pad_maximum_fusion.1), channel_id=1, source_target_pairs={{0,4},{4,0},{1,5},{5,1},{2,6},{6,2},{3,7},{7,3},{8,12},{12,8},{9,1... | collective-permute-start | bytes 3145736 | tf_op jit(solution)/shard_map/ppermute | solution.py:434
  435.4 142.6 %reduce-scatter.13.cloned.1.call-start = ((), (), s32[]{:S(2)}) async-start(), calls=%async_computation.9 | async-start | bytes 1474560 | tf_op jit(solution)/shard_map/reduce_scatter | solution.py:1125
  435.5 17.7 %copy-start.8 = (bf16[2,2048,128]{2,1,0:T(8,128)(2,1)S(1)}, bf16[2,2048,128]{2,1,0:T(8,128)(2,1)}, u32[]{:S(2)}) copy-start(bf16[2,2048,128]{2,1,0:T(8,128)(2,1)} %get-tuple-element.29) | copy-start | bytes 3145732
  435.5 17.6 %copy-start.20 = (bf16[2,2048,128]{2,1,0:T(8,128)(2,1)S(1)}, bf16[2,2048,128]{2,1,0:T(8,128)(2,1)}, u32[]{:S(2)}) copy-start(bf16[2,2048,128]{2,1,0:T(8,128)(2,1)} %get-tuple-element.30) | copy-start | bytes 3145732
  437.9 35.3 %collective-permute-start.7 = (bf16[512,1536]{1,0:T(8,128)(2,1)S(1)}, bf16[512,1536]{1,0:T(8,128)(2,1)S(1)}, u32[]{:S(2)}, u32[]{:S(2)}) collective-permute-start(bf16[512,1536]{1,0:T(8,128)(2,1)S(1)} %add_convert_fusion.11), channel_id=1, source_target_pairs={{0,2},{2,0},{1,3},{3,1},{4,6},{6,4},{5,7},{7,5},{8,10},{10,8},{9,1... | collective-permute-start | bytes 4718600 | tf_op jit(solution)/shard_map/ppermute | solution.py:442
  439.5 15.5 %copy-start.7 = (f32[1024,64]{1,0:T(8,128)S(1)}, f32[1024,64]{1,0:T(8,128)}, u32[]{:S(2)}) copy-start(f32[1024,64]{1,0:T(8,128)} %copy-done.6) | copy-start | bytes 786436
  439.5 15.5 %copy-start.21 = (f32[1024,128]{1,0:T(8,128)S(1)}, f32[1024,128]{1,0:T(8,128)}, u32[]{:S(2)}) copy-start(f32[1024,128]{1,0:T(8,128)} %get-tuple-element.113.sin_ref) | copy-start | bytes 1572868
  463.5 20.6 %collective-permute-start.13 = (bf16[512,1536]{1,0:T(8,128)(2,1)}, bf16[512,1536]{1,0:T(8,128)(2,1)}, u32[]{:S(2)}, u32[]{:S(2)}) collective-permute-start(bf16[512,1536]{1,0:T(8,128)(2,1)} %constant_dynamic-slice_fusion), channel_id=1, source_target_pairs={{0,1},{1,0},{2,3},{3,2},{4,5},{5,4},{6,7},{7,6},{8,9},{9,8},{10,11... | collective-permute-start | bytes 4718600 | tf_op jit(solution)/shard_map/ppermute | solution.py:438
  474.7 53.0 %collective-permute-start.8 = (bf16[512,1536]{1,0:T(8,128)(2,1)}, bf16[512,1536]{1,0:T(8,128)(2,1)}, u32[]{:S(2)}, u32[]{:S(2)}) collective-permute-start(bf16[512,1536]{1,0:T(8,128)(2,1)} %add_convert_fusion.10), channel_id=1, source_target_pairs={{0,1},{1,0},{2,3},{3,2},{4,5},{5,4},{6,7},{7,6},{8,9},{9,8},{10,11... | collective-permute-start | bytes 4718600 | tf_op jit(solution)/shard_map/ppermute | solution.py:438
  482.0 91.0 %collective-permute-start.24 = (bf16[384,512]{1,0:T(8,128)(2,1)}, bf16[384,512]{1,0:T(8,128)(2,1)}, u32[]{:S(2)}, u32[]{:S(2)}) collective-permute-start(bf16[384,512]{1,0:T(8,128)(2,1)} %reduce-scatter.17.cloned.1.call-done), channel_id=1, source_target_pairs={{0,4},{4,0},{1,5},{5,1},{2,6},{6,2},{3,7},{7,3},{8,12},{12,8},{9,1... | collective-permute-start | bytes 1179656 | tf_op jit(solution)/shard_map/ppermute | solution.py:434
  483.8 5.2 copy-start.10
  483.8 5.2 copy-start.29
  483.8 86.7 %collective-permute-start.22 = (bf16[384,512]{1,0:T(8,128)(2,1)}, bf16[384,512]{1,0:T(8,128)(2,1)}, u32[]{:S(2)}, u32[]{:S(2)}) collective-permute-start(bf16[384,512]{1,0:T(8,128)(2,1)} %reduce-scatter.15.cloned.1.call-done), channel_id=1, source_target_pairs={{0,4},{4,0},{1,5},{5,1},{2,6},{6,2},{3,7},{7,3},{8,12},{12,8},{9,1... | collective-permute-start | bytes 1179656 | tf_op jit(solution)/shard_map/ppermute | solution.py:434
  487.6 36.7 %collective-permute-start.14 = (bf16[512,1536]{1,0:T(8,128)(2,1)}, bf16[512,1536]{1,0:T(8,128)(2,1)}, u32[]{:S(2)}, u32[]{:S(2)}) collective-permute-start(bf16[512,1536]{1,0:T(8,128)(2,1)} %add_convert_fusion.7), channel_id=1, source_target_pairs={{0,2},{2,0},{1,3},{3,1},{4,6},{6,4},{5,7},{7,5},{8,10},{10,8},{9,1... | collective-permute-start | bytes 4718600 | tf_op jit(solution)/shard_map/ppermute | solution.py:442
  499.9 40.3 %collective-permute-start.17 = (bf16[1536,384]{1,0:T(8,128)(2,1)}, bf16[1536,384]{1,0:T(8,128)(2,1)}, u32[]{:S(2)}, u32[]{:S(2)}) collective-permute-start(bf16[1536,384]{1,0:T(8,128)(2,1)} %convolution_convert_fusion.3), channel_id=1, source_target_pairs={{0,4},{4,0},{1,5},{5,1},{2,6},{6,2},{3,7},{7,3},{8,12},{12,8},{9,1... | collective-permute-start | bytes 3538952 | tf_op jit(solution)/shard_map/ppermute | solution.py:434
  527.7 18.9 %collective-permute-start.15 = (bf16[512,1536]{1,0:T(8,128)(2,1)}, bf16[512,1536]{1,0:T(8,128)(2,1)}, u32[]{:S(2)}, u32[]{:S(2)}) collective-permute-start(bf16[512,1536]{1,0:T(8,128)(2,1)} %add_convert_fusion.6), channel_id=1, source_target_pairs={{0,1},{1,0},{2,3},{3,2},{4,5},{5,4},{6,7},{7,6},{8,9},{9,8},{10,11... | collective-permute-start | bytes 4718600 | tf_op jit(solution)/shard_map/ppermute | solution.py:438
  527.7 7.1 %copy-start.28 = (bf16[1024,128]{1,0:T(8,128)(2,1)S(1)}, bf16[1024,128]{1,0:T(8,128)(2,1)}, u32[]{:S(2)}) copy-start(bf16[1024,128]{1,0:T(8,128)(2,1)} %copy-done.27) | copy-start | bytes 786436
  534.8 5.4 copy-start.37
  538.7 7.9 %copy-start.40 = (f32[1536]{0:T(1024)S(1)}, f32[1536]{0:T(1024)}, u32[]{:S(2)}) copy-start(f32[1536]{0:T(1024)} %get-tuple-element.61) | copy-start | bytes 18436
  538.7 36.8 %collective-permute-start.25 = (bf16[1024,384]{1,0:T(8,128)(2,1)}, bf16[1024,384]{1,0:T(8,128)(2,1)}, u32[]{:S(2)}, u32[]{:S(2)}) collective-permute-start(bf16[1024,384]{1,0:T(8,128)(2,1)} %copy.51), channel_id=1, source_target_pairs={{0,4},{4,0},{1,5},{5,1},{2,6},{6,2},{3,7},{7,3},{8,12},{12,8},{9,1... | collective-permute-start | bytes 2359304 | tf_op jit(solution)/shard_map/ppermute | solution.py:434
  546.5 68.3 %reduce-scatter.21.cloned.1.call-start = ((), (), s32[]{:S(2)}) async-start(), calls=%async_computation.13 | async-start | bytes 983040
  546.5 5.0 copy-start.19
  551.6 15.7 %copy-start.26 = (bf16[512,1024]{1,0:T(8,128)(2,1)S(1)}, bf16[512,1024]{1,0:T(8,128)(2,1)}, u32[]{:S(2)}) copy-start(bf16[512,1024]{1,0:T(8,128)(2,1)} %copy.45) | copy-start | bytes 3145732
  569.1 6.4 copy-start.16
  570.0 16.5 %collective-permute-start.19 = (bf16[192,1536]{1,0:T(8,128)(2,1)}, bf16[192,1536]{1,0:T(8,128)(2,1)}, u32[]{:S(2)}, u32[]{:S(2)}) collective-permute-start(bf16[192,1536]{1,0:T(8,128)(2,1)} %bitcast.22), channel_id=1, source_target_pairs={{0,4},{4,0},{1,5},{5,1},{2,6},{6,2},{3,7},{7,3},{8,12},{12,8},{9,1... | collective-permute-start | bytes 1769480 | tf_op jit(solution)/shard_map/ppermute | solution.py:434
  578.0 11.0 %copy-start.32 = (bf16[384,384]{1,0:T(8,128)(2,1)S(1)}, bf16[384,384]{1,0:T(8,128)(2,1)}, u32[]{:S(2)}) copy-start(bf16[384,384]{1,0:T(8,128)(2,1)} %reduce-scatter.13.cloned.1.call-done) | copy-start | bytes 884740
  578.0 14.1 %collective-permute-start.18 = (bf16[384,384]{1,0:T(8,128)(2,1)}, bf16[384,384]{1,0:T(8,128)(2,1)}, u32[]{:S(2)}, u32[]{:S(2)}) collective-permute-start(bf16[384,384]{1,0:T(8,128)(2,1)} %reduce-scatter.13.cloned.1.call-done), channel_id=1, source_target_pairs={{0,4},{4,0},{1,5},{5,1},{2,6},{6,2},{3,7},{7,3},{8,12},{12,8},{9,1... | collective-permute-start | bytes 884744 | tf_op jit(solution)/shard_map/ppermute | solution.py:434
  588.9 50.8 %reduce-scatter.19.cloned.1.call-start = ((), (), s32[]{:S(2)}) async-start(), calls=%async_computation.12 | async-start | bytes 983040
  593.0 49.5 %copy-start.1 = (bf16[1024,384]{1,0:T(8,128)(2,1)S(1)}, bf16[1024,384]{1,0:T(8,128)(2,1)}, u32[]{:S(2)}) copy-start(bf16[1024,384]{1,0:T(8,128)(2,1)} %param.25) | copy-start | bytes 2359300
  595.3 3.8 collective-permute-start.16
  615.8 25.8 %collective-permute-start.20 = (bf16[192,384]{1,0:T(8,128)(2,1)S(1)}, bf16[192,384]{1,0:T(8,128)(2,1)S(1)}, u32[]{:S(2)}, u32[]{:S(2)}) collective-permute-start(bf16[192,384]{1,0:T(8,128)(2,1)S(1)} %copy.49), channel_id=1, source_target_pairs={{0,4},{4,0},{1,5},{5,1},{2,6},{6,2},{3,7},{7,3},{8,12},{12,8},{9,1... | collective-permute-start | bytes 442376 | tf_op jit(solution)/shard_map/ppermute | solution.py:434
  (24 other events, 62.7 us)
Sparse Core Ops, SparseCore 0:
  10.2 50.0 all-gather.7
  154.5 37.2 all-gather.5
  193.9 35.9 all-gather.3
  334.7 35.4 reduce-scatter.16
  372.3 34.2 reduce-scatter.14
  435.5 63.9 reduce-scatter.22
  546.6 31.3 reduce-scatter.12
  589.0 25.6 reduce-scatter.20
  617.1 22.6 reduce-scatter.18

commit v3 on v2

--- a/solution.py
+++ b/solution.py
@@ -1,3 +1,4 @@
+import functools
 import math
 
 import jax
@@ -457,31 +458,64 @@
         core == 0,
         jnp.concatenate([total, other], axis=0),
         jnp.concatenate([other, total], axis=0),
-    ).astype(jnp.float32)
+    )
 
 
 def dot(a, b, contract):
     return lax.dot_general(a, b, (contract, ((), ())), preferred_element_type=jnp.float32)
 
 
+def block_kinds(meta_ref, query_tile, key_tile, q_start, k_start):
+    prefix = meta_ref[0]
+    whole = (k_start + (key_tile - 1) <= q_start) | (k_start + key_tile <= prefix)
+    nothing = (k_start > q_start + (query_tile - 1)) & (k_start >= prefix)
+    return prefix, whole, nothing
+
+
+def mask_scores(scores, prefix, q_start, k_start, query_tile):
+    key_ids = k_start + lax.broadcasted_iota(jnp.int32, scores.shape, 0)
+    column = lax.broadcasted_iota(jnp.int32, scores.shape, 1)
+    query_ids = q_start + jnp.bitwise_and(column, query_tile - 1)
+    return jnp.where((key_ids <= query_ids) | (key_ids < prefix), scores, NEGATIVE)
+
+
 MESH = pl.DeviceIdType.MESH
 GAIN_ROWS = 16
-
-
-def gather_kernel(
+PREFIX_MOST = 1024
+
+
+def front_kernel(
+    prefix_ref,
     x_ref,
     pack_ref,
     rest_ref,
     spread_ref,
     cos_ref,
     sin_ref,
+    w_project_ref,
+    w_gate_ref,
+    w_up_ref,
+    w_down_ref,
     normed_ref,
     q_ref,
     kv_ref,
     wide_ref,
     project_ref,
     gain_ref,
+    o_ref,
+    lse_ref,
+    total_ref,
+    gate_ref,
+    up_ref,
+    down_ref,
     buf_ref,
+    max_ref,
+    sum_ref,
+    acc_ref,
+    give_ref,
+    core_in_ref,
+    keep_ref,
+    chip_in_ref,
     up_send,
     up_recv,
     down_send,
@@ -490,18 +524,51 @@
     x_recv,
     kv_send,
     kv_recv,
+    m_up_send,
+    m_up_recv,
+    m_down_send,
+    m_down_recv,
+    m_x_send,
+    m_x_recv,
+    local_sem,
+    core_send,
+    core_recv,
+    chip_send,
+    chip_recv,
+    back_send,
+    back_recv,
 ):
+    bf16, f32 = jnp.bfloat16, jnp.float32
     planes = buf_ref.shape[0]
-    depth = wide_ref.shape[0] // planes
+    rows, width = x_ref.shape
+    depth = width // planes
     half_width = wide_ref.shape[1] // 2
-    matrix_rows = pack_ref.shape[0] - GAIN_ROWS
-    project_rows = matrix_rows - depth
-    rows = x_ref.shape[0]
+    matrix_rows = rest_ref.shape[0]
+    heads_half = project_ref.shape[0] // 2
+    units = gate_ref.shape[2]
     z = lax.axis_index("fsdp")
     c = lax.axis_index("ctx")
+    t = lax.axis_index("tp")
+    core = lax.rem(t, 2)
     across = {"ctx": 1 - c}
+    sibling = {"tp": t + 1 - 2 * core}
+    partner = {"tp": lax.rem(t + 2, 4)}
     has_above = z < planes - 1
     has_below = z > 0
+
+    def remote(src, dst, send, recv, device):
+        return pltpu.make_async_remote_copy(
+            src_ref=src,
+            dst_ref=dst,
+            send_sem=send,
+            recv_sem=recv,
+            device_id=device,
+            device_id_type=MESH,
+        )
+
+    project_ref[:, HD:, :] = jnp.zeros(
+        (project_ref.shape[0], LANES - HD, project_ref.shape[2]), bf16
+    )
 
     barrier = pltpu.get_barrier_semaphore()
 
@@ -513,70 +580,143 @@
     def _():
         pl.semaphore_signal(barrier, inc=1, device_id={"fsdp": z - 1}, device_id_type=MESH)
 
-    pl.semaphore_signal(barrier, inc=1, device_id=across, device_id_type=MESH)
+    for device in (across, sibling, partner):
+        pl.semaphore_signal(barrier, inc=1, device_id=device, device_id_type=MESH)
 
     @pl.when(has_above & has_below)
     def _():
-        pl.semaphore_wait(barrier, 3)
+        pl.semaphore_wait(barrier, 5)
 
     @pl.when(jnp.logical_not(has_above & has_below))
     def _():
-        pl.semaphore_wait(barrier, 2)
+        pl.semaphore_wait(barrier, 4)
 
     def up(k):
         piece = z - k
-        return pltpu.make_async_remote_copy(
-            src_ref=pack_ref if k == 0 else buf_ref.at[piece, 0],
-            dst_ref=buf_ref.at[piece, 0],
-            send_sem=up_send.at[k],
-            recv_sem=up_recv.at[k],
-            device_id={"fsdp": z + 1},
-            device_id_type=MESH,
-        )
+        src = pack_ref if k == 0 else buf_ref.at[piece, 0]
+        return remote(src, buf_ref.at[piece, 0], up_send.at[k], up_recv.at[k], {"fsdp": z + 1})
 
     def down(k):
         piece = z + k
-        return pltpu.make_async_remote_copy(
-            src_ref=pack_ref if k == 0 else buf_ref.at[piece, 0],
-            dst_ref=buf_ref.at[piece, 0],
-            send_sem=down_send.at[k],
-            recv_sem=down_recv.at[k],
-            device_id={"fsdp": z - 1},
-            device_id_type=MESH,
-        )
+        src = pack_ref if k == 0 else buf_ref.at[piece, 0]
+        return remote(src, buf_ref.at[piece, 0], down_send.at[k], down_recv.at[k], {"fsdp": z - 1})
 
     def from_below(k):
-        piece = z - 1 - k
-        return pltpu.make_async_remote_copy(
-            src_ref=buf_ref.at[piece, 0],
-            dst_ref=buf_ref.at[piece, 0],
-            send_sem=up_send.at[k],
-            recv_sem=up_recv.at[k],
-            device_id={"fsdp": z - 1},
-            device_id_type=MESH,
-        )
+        slot = buf_ref.at[z - 1 - k, 0]
+        return remote(slot, slot, up_send.at[k], up_recv.at[k], {"fsdp": z - 1})
 
     def from_above(k):
-        piece = z + 1 + k
-        return pltpu.make_async_remote_copy(
-            src_ref=buf_ref.at[piece, 0],
-            dst_ref=buf_ref.at[piece, 0],
-            send_sem=down_send.at[k],
-            recv_sem=down_recv.at[k],
-            device_id={"fsdp": z + 1},
-            device_id_type=MESH,
-        )
+        slot = buf_ref.at[z + 1 + k, 0]
+        return remote(slot, slot, down_send.at[k], down_recv.at[k], {"fsdp": z + 1})
 
     def sideways(side, k):
         piece = z - k if side == 0 else z + k
-        return pltpu.make_async_remote_copy(
-            src_ref=buf_ref.at[piece, 0, pl.ds(0, matrix_rows)],
-            dst_ref=buf_ref.at[piece, 1, pl.ds(0, matrix_rows)],
-            send_sem=x_send.at[side, k],
-            recv_sem=x_recv.at[side, k],
-            device_id=across,
-            device_id_type=MESH,
-        )
+        matrix = pl.ds(0, matrix_rows)
+        return remote(
+            buf_ref.at[piece, 0, matrix],
+            buf_ref.at[piece, 1, matrix],
+            x_send.at[side, k],
+            x_recv.at[side, k],
+            across,
+        )
+
+    def own_half(m, half):
+        if m == 0:
+            return w_gate_ref.at[:, pl.ds(pl.multiple_of(half * units, units), units)]
+        if m == 1:
+            return w_up_ref.at[:, pl.ds(pl.multiple_of(half * units, units), units)]
+        if m == 2:
+            return w_down_ref.at[pl.ds(pl.multiple_of(half * units, units), units), :]
+        return w_project_ref.at[pl.ds(half * heads_half, heads_half)]
+
+    def slot(m, which, piece):
+        at = pl.ds(pl.multiple_of(piece * depth, depth), depth)
+        if m == 0:
+            return gate_ref.at[which, at]
+        if m == 1:
+            return up_ref.at[which, at]
+        if m == 2:
+            return down_ref.at[which, :, at]
+        return project_ref.at[pl.ds(which * heads_half, heads_half), pl.ds(0, HD), at]
+
+    def m_up(m, k):
+        piece = z - k
+        src = own_half(m, c) if k == 0 else slot(m, 0, piece)
+        return remote(
+            src, slot(m, 0, piece), m_up_send.at[m, k], m_up_recv.at[m, k], {"fsdp": z + 1}
+        )
+
+    def m_down(m, k):
+        piece = z + k
+        src = own_half(m, c) if k == 0 else slot(m, 0, piece)
+        return remote(
+            src, slot(m, 0, piece), m_down_send.at[m, k], m_down_recv.at[m, k], {"fsdp": z - 1}
+        )
+
+    def m_below(m, k):
+        at = slot(m, 0, z - 1 - k)
+        return remote(at, at, m_up_send.at[m, k], m_up_recv.at[m, k], {"fsdp": z - 1})
+
+    def m_above(m, k):
+        at = slot(m, 0, z + 1 + k)
+        return remote(at, at, m_down_send.at[m, k], m_down_recv.at[m, k], {"fsdp": z + 1})
+
+    def m_side(m, side, k):
+        piece = z - k if side == 0 else z + k
+        return remote(
+            slot(m, 0, piece),
+            slot(m, 1, piece),
+            m_x_send.at[m, side, k],
+            m_x_recv.at[m, side, k],
+            across,
+        )
+
+    groups = ((3, 0), (1,), (2,))
+
+    def relay(group, k):
+        for m in groups[group]:
+
+            @pl.when(z - k >= 0)
+            def _():
+                m_below(m, k - 1).wait_recv()
+                if k < planes - 1:
+
+                    @pl.when(has_above)
+                    def _():
+                        m_up(m, k).start()
+
+            @pl.when(z + k <= planes - 1)
+            def _():
+                m_above(m, k - 1).wait_recv()
+                if k < planes - 1:
+
+                    @pl.when(has_below)
+                    def _():
+                        m_down(m, k).start()
+
+    def cross(group, k):
+        for m in groups[group]:
+
+            @pl.when(z - k >= 0)
+            def _():
+                m_side(m, 0, k).start()
+
+            @pl.when(z + k <= planes - 1)
+            def _():
+                m_side(m, 1, k).start()
+
+    def crossed(m, k):
+        @pl.when(z - k >= 0)
+        def _():
+            m_side(m, 0, k).wait_recv()
+
+        @pl.when(z + k <= planes - 1)
+        def _():
+            m_side(m, 1, k).wait_recv()
+
+    def local(m, which):
+        half = c if which == 0 else 1 - c
+        return pltpu.make_async_copy(own_half(m, half), slot(m, which, z), local_sem.at[m, which])
 
     spread = spread_ref[...]
 
@@ -584,10 +724,7 @@
         at = pl.ds(pl.multiple_of(piece * depth, depth), depth)
         wide_ref[at, which * half_width : (which + 1) * half_width] = dot(
             block[:depth], spread, ((1,), (0,))
-        ).astype(jnp.bfloat16)
-        for head in range(project_rows // HD):
-            row = (which * (project_rows // HD) + head) * LANES
-            project_ref[row : row + HD, at] = block[depth + head * HD : depth + (head + 1) * HD]
+        ).astype(bf16)
 
     def place_gain(block, piece):
         at = pl.ds(pl.multiple_of(piece * depth, depth), depth)
@@ -601,11 +738,9 @@
     def _():
         down(0).start()
 
-    for head in range(project_ref.shape[0] // LANES):
-        row = head * LANES + HD
-        project_ref[row : row + LANES - HD, :] = jnp.zeros(
-            (LANES - HD, project_ref.shape[1]), jnp.bfloat16
-        )
+    for m in (3, 0, 1, 2):
+        for which in range(2):
+            local(m, which).start()
     place(pack_ref, z, 0)
     place_gain(pack_ref, z)
     place(rest_ref, z, 1)
@@ -636,6 +771,17 @@
 
             sideways(1, k).start()
 
+        if k == max(1, planes - 2):
+            for m in (3, 0, 1, 2):
+
+                @pl.when(has_above)
+                def _():
+                    m_up(m, 0).start()
+
+                @pl.when(has_below)
+                def _():
+                    m_down(m, 0).start()
+
         @pl.when(below)
         def _():
             place(buf_ref.at[z - k, 0], z - k, 0)
@@ -647,13 +793,13 @@
             place_gain(buf_ref.at[z + k, 0], z + k)
 
     tile = 128
-    gain = gain_ref[0:1, :].astype(jnp.float32)
+    gain = gain_ref[0:1, :].astype(f32)
 
     def norm_rows(i, carry):
         at = pl.ds(pl.multiple_of(i * tile, tile), tile)
-        x = x_ref[at, :].astype(jnp.float32)
+        x = x_ref[at, :].astype(f32)
         factor = lax.rsqrt(jnp.mean(x * x, axis=-1, keepdims=True) + EPSILON)
-        normed_ref[at, :] = (x * factor * gain).astype(jnp.bfloat16)
+        normed_ref[at, :] = (x * factor * gain).astype(bf16)
         return carry
 
     lax.fori_loop(0, rows // tile, norm_rows, 0)
@@ -680,24 +826,24 @@
         for which in range(2):
             lane = which * half_width + 2 * LANES
             both = dot(normed_ref[at, :], wide_ref[:, lane : lane + 2 * LANES], ((1,), (0,)))
-            kv_ref[which, at, :] = turn(both[:, :LANES], at).astype(jnp.bfloat16)
-            kv_ref[2 + which, at, :] = both[:, LANES:].astype(jnp.bfloat16)
+            kv_ref[which, at, :] = turn(both[:, :LANES], at).astype(bf16)
+            kv_ref[2 + which, at, :] = both[:, LANES:].astype(bf16)
         return carry
 
     lax.fori_loop(0, rows // block, key_rows, 0)
 
     def exchange(slab):
-        return pltpu.make_async_remote_copy(
-            src_ref=kv_ref.at[slab, pl.ds(0, rows)],
-            dst_ref=kv_ref.at[slab ^ 1, pl.ds(rows, rows)],
-            send_sem=kv_send.at[slab],
-            recv_sem=kv_recv.at[slab ^ 1],
-            device_id=across,
-            device_id_type=MESH,
+        return remote(
+            kv_ref.at[slab, pl.ds(0, rows)],
+            kv_ref.at[slab ^ 1, pl.ds(rows, rows)],
+            kv_send.at[slab],
+            kv_recv.at[slab ^ 1],
+            across,
         )
 
     for slab in range(4):
         exchange(slab).start()
+    relay(0, 1)
     scale = HD ** (-0.5) * LOG2E
 
     def query_rows(i, carry):
@@ -708,177 +854,253 @@
             for head in range(2):
                 part = turn(both[:, head * LANES : (head + 1) * LANES], at)
                 lane = (2 * which + head) * LANES
-                q_ref[at, lane : lane + LANES] = (part * scale).astype(jnp.bfloat16)
+                q_ref[at, lane : lane + LANES] = (part * scale).astype(bf16)
         return carry
 
     lax.fori_loop(0, rows // block, query_rows, 0)
+    relay(1, 1)
+
+    tiles = rows // block
+    tiles_of_block = tiles // 2
+    prefix = prefix_ref[0]
+    max_ref[...] = jnp.full_like(max_ref, NEGATIVE)
+    sum_ref[...] = jnp.zeros_like(sum_ref)
+    acc_ref[...] = jnp.zeros_like(acc_ref)
+
+    def start_of(device, tile_index):
+        second = tile_index // tiles_of_block
+        block_id = device + second * (3 - 2 * device)
+        return (block_id * tiles_of_block + tile_index % tiles_of_block) * block
+
+    def attend_group(g, away):
+        key_device = 1 - c if away else c
+
+        def one_tile(i, carry):
+            at = pl.ds(pl.multiple_of(i * block, block), block)
+            lane = 2 * g * LANES
+            queries = jnp.concatenate(
+                [q_ref[at, lane : lane + LANES], q_ref[at, lane + LANES : lane + 2 * LANES]],
+                axis=0,
+            )
+            q_start = start_of(c, i)
+            u = g * tiles + i
+
+            def absorb(scores, values):
+                old = max_ref[u]
+                new = jnp.maximum(old, jnp.max(scores, axis=0, keepdims=True))
+                weights = jnp.exp2(scores - new)
+                rescale = jnp.exp2(old - new)
+                max_ref[u] = new
+                sum_ref[u] = sum_ref[u] * rescale + jnp.sum(weights, axis=0, keepdims=True)
+                acc_ref[u] = acc_ref[u] * rescale + dot(values, weights.astype(bf16), ((0,), (0,)))
+
+            def one(j, carry):
+                k_start = start_of(key_device, j)
+                first = (tiles if away else 0) + j
+                keys_at = pl.ds(pl.multiple_of(first * block, block), block)
+                whole = k_start + (block - 1) <= q_start
+                nothing = (k_start > q_start + (block - 1)) & (k_start >= PREFIX_MOST)
+
+                @pl.when(whole)
+                def _():
+                    absorb(dot(kv_ref[g, keys_at, :], queries, ((1,), (1,))), kv_ref[2 + g, keys_at, :])
+
+                @pl.when(jnp.logical_not(whole | nothing))
+                def _():
+                    scores = dot(kv_ref[g, keys_at, :], queries, ((1,), (1,)))
+                    absorb(
+                        mask_scores(scores, prefix, q_start, k_start, block),
+                        kv_ref[2 + g, keys_at, :],
+                    )
+
+                return carry
+
+            lax.fori_loop(0, tiles, one, 0)
+            if away:
+                total = sum_ref[u]
+                lse_ref[g, i] = max_ref[u] + jnp.log2(total)
+                out = (acc_ref[u] / total).T.astype(bf16)
+                o_ref[at, lane : lane + LANES] = out[:block]
+                o_ref[at, lane + LANES : lane + 2 * LANES] = out[block:]
+            return carry
+
+        lax.fori_loop(0, tiles, one_tile, 0)
+
+    attend_group(0, False)
+    relay(2, 1)
+    attend_group(1, False)
+    relay(0, 2)
+    for slab in range(4):
+        exchange(slab).wait_recv()
+    cross(0, 1)
+    cross(1, 1)
+    cross(2, 1)
+    attend_group(0, True)
+    relay(1, 2)
+    cross(0, 2)
+    cross(1, 2)
+    attend_group(1, True)
+    relay(2, 2)
+    cross(2, 2)
+
+    chunks, chunk, _ = give_ref.shape
+    half_rows = rows // 2
+    give_start = (1 - core) * half_rows
+    keep_start = core * half_rows
+    relay(0, 3)
+    cross(0, 3)
+    for which in range(2):
+        local(3, which).wait()
+    for k in range(1, planes):
+        crossed(3, k)
+    w_project = project_ref[...].reshape(project_ref.shape[0] * LANES, width)
+
+    def feature_rows(start):
+        at = pl.ds(pl.multiple_of(start, chunk), chunk)
+        return dot(o_ref[at, :], w_project, ((1,), (0,)))
+
+    def to_core(i):
+        return remote(give_ref.at[i], core_in_ref.at[i], core_send.at[i], core_recv.at[i], sibling)
+
+    def to_chip(i):
+        return remote(keep_ref.at[i], chip_in_ref.at[i], chip_send.at[i], chip_recv.at[i], partner)
+
+    def back(i, start):
+        at = pl.ds(pl.multiple_of(start + i * chunk, chunk), chunk)
+        return remote(
+            total_ref.at[at], total_ref.at[at], back_send.at[i], back_recv.at[i], sibling
+        )
+
+    for i in range(chunks):
+        give_ref[i] = feature_rows(give_start + i * chunk).astype(bf16)
+        to_core(i).start()
+    for i in range(chunks):
+        kept = feature_rows(keep_start + i * chunk)
+        to_core(i).wait_recv()
+        keep_ref[i] = (kept + core_in_ref[i].astype(f32)).astype(bf16)
+        to_chip(i).start()
+
+    def finish_chunk(i):
+        to_chip(i).wait_recv()
+        at = pl.ds(pl.multiple_of(keep_start + i * chunk, chunk), chunk)
+        total_ref[at, :] = (keep_ref[i].astype(f32) + chip_in_ref[i].astype(f32)).astype(bf16)
+        back(i, keep_start).start()
+
+    relay(1, 3)
+    cross(1, 3)
+    finish_chunk(0)
+    relay(2, 3)
+    cross(2, 3)
+    for i in range(1, chunks):
+        finish_chunk(i)
 
     for k in range(planes - 1):
 
         @pl.when((z - k >= 0) & has_above)
         def _():
             up(k).wait_send()
+            for m in range(4):
+                m_up(m, k).wait_send()
 
         @pl.when((z + k <= planes - 1) & has_below)
         def _():
             down(k).wait_send()
+            for m in range(4):
+                m_down(m, k).wait_send()
 
     for k in range(1, planes):
 
         @pl.when(z - k >= 0)
         def _():
             sideways(0, k).wait_send()
+            for m in range(4):
+                m_side(m, 0, k).wait_send()
 
         @pl.when(z + k <= planes - 1)
         def _():
             sideways(1, k).wait_send()
-
+            for m in range(4):
+                m_side(m, 1, k).wait_send()
+
+        for m in range(3):
+            crossed(m, k)
+
+    for m in range(3):
+        for which in range(2):
+            local(m, which).wait()
     for slab in range(4):
         exchange(slab).wait_send()
-    for slab in range(4):
-        exchange(slab).wait_recv()
-
-
-def gather_project(x, pack, rest, spread, cosine, sine, planes):
+    for i in range(chunks):
+        to_core(i).wait_send()
+        to_chip(i).wait_send()
+        back(i, keep_start).wait_send()
+        back(i, give_start).wait_recv()
+
+
+def front(prefix, x, pack, rest, spread, cosine, sine, w_project, w_gate, w_up, w_down, planes):
     rows, width = x.shape
-    depth = width // planes
     half_width = spread.shape[1]
-    project_rows = pack.shape[0] - GAIN_ROWS - depth
+    units = w_gate.shape[1] // 2
+    heads = w_project.shape[0]
+    block = 256
+    tiles = rows // block
+    chunks = 4
+    chunk = rows // 2 // chunks
     vmem = pl.BlockSpec(memory_space=pltpu.VMEM)
-    bf16 = jnp.bfloat16
+    anywhere = pl.BlockSpec(memory_space=pl.ANY)
+    smem = pl.BlockSpec(memory_space=pltpu.SMEM)
+    bf16, f32 = jnp.bfloat16, jnp.float32
     dma = pltpu.SemaphoreType.DMA
+    piece = pltpu.VMEM((chunks, chunk, width), bf16)
     return pl.pallas_call(
-        gather_kernel,
-        in_specs=[vmem] * 6,
-        out_specs=[vmem] * 6,
+        front_kernel,
+        in_specs=[smem] + [vmem] * 6 + [anywhere] * 4,
+        out_specs=[vmem] * 9 + [anywhere] * 3,
         out_shape=[
             jax.ShapeDtypeStruct((rows, width), bf16),
             jax.ShapeDtypeStruct((rows, half_width), bf16),
             jax.ShapeDtypeStruct((4, 2 * rows, LANES), bf16),
             jax.ShapeDtypeStruct((width, 2 * half_width), bf16),
-            jax.ShapeDtypeStruct((2 * project_rows // HD * LANES, width), bf16),
+            jax.ShapeDtypeStruct((heads, LANES, width), bf16),
             jax.ShapeDtypeStruct((GAIN_ROWS, width), bf16),
+            jax.ShapeDtypeStruct((rows, half_width), bf16),
+            jax.ShapeDtypeStruct((2, tiles, 1, 2 * block), f32),
+            jax.ShapeDtypeStruct((rows, width), bf16),
+            jax.ShapeDtypeStruct((2, width, units), bf16),
+            jax.ShapeDtypeStruct((2, width, units), bf16),
+            jax.ShapeDtypeStruct((2, units, width), bf16),
         ],
         scratch_shapes=[
             pltpu.VMEM((planes, 2, pack.shape[0], pack.shape[1]), bf16),
-            dma((planes - 1,)),
-            dma((planes - 1,)),
-            dma((planes - 1,)),
-            dma((planes - 1,)),
-            dma((2, planes)),
-            dma((2, planes)),
-            dma((4,)),
-            dma((4,)),
-        ],
+            pltpu.VMEM((2 * tiles, 1, 2 * block), f32),
+            pltpu.VMEM((2 * tiles, 1, 2 * block), f32),
+            pltpu.VMEM((2 * tiles, LANES, 2 * block), f32),
+            piece,
+            piece,
+            piece,
+            piece,
+        ]
+        + [dma((planes - 1,))] * 4
+        + [dma((2, planes))] * 2
+        + [dma((4,))] * 2
+        + [dma((4, planes - 1))] * 4
+        + [dma((4, 2, planes))] * 2
+        + [dma((4, 2))]
+        + [dma((chunks,))] * 6,
         compiler_params=pltpu.CompilerParams(
             collective_id=1, has_side_effects=True, vmem_limit_bytes=VMEM_BYTES
         ),
         cost_estimate=pl.CostEstimate(
-            flops=40_000_000_000, bytes_accessed=16_000_000, transcendentals=0
+            flops=120_000_000_000, bytes_accessed=60_000_000, transcendentals=0
         ),
-        name="gather_project",
-    )(x, pack, rest, spread, cosine, sine)
-
-
-def block_kinds(meta_ref, query_tile, key_tile, q_start, k_start):
-    prefix = meta_ref[0]
-    whole = (k_start + (key_tile - 1) <= q_start) | (k_start + key_tile <= prefix)
-    nothing = (k_start > q_start + (query_tile - 1)) & (k_start >= prefix)
-    return prefix, whole, nothing
-
-
-def mask_scores(scores, prefix, q_start, k_start, query_tile):
-    key_ids = k_start + lax.broadcasted_iota(jnp.int32, scores.shape, 0)
-    column = lax.broadcasted_iota(jnp.int32, scores.shape, 1)
-    query_ids = q_start + jnp.bitwise_and(column, query_tile - 1)
-    return jnp.where((key_ids <= query_ids) | (key_ids < prefix), scores, NEGATIVE)
-
-
-def attend_kernel(meta_ref, q_ref, k_ref, v_ref, o_ref, lse_ref, max_ref, sum_ref, acc_ref):
-    tile = q_ref.shape[0]
-    key_tile = tile
-    query_tiles = pl.num_programs(1)
-    step = pl.program_id(1)
-    q_start = meta_ref[1 + step]
-    queries = jnp.concatenate([q_ref[:, :LANES], q_ref[:, LANES:]], axis=0)
-    max_ref[...] = jnp.full_like(max_ref, NEGATIVE)
-    sum_ref[...] = jnp.zeros_like(sum_ref)
-    acc_ref[...] = jnp.zeros_like(acc_ref)
-
-    def absorb(scores, values):
-        old = max_ref[...]
-        new = jnp.maximum(old, jnp.max(scores, axis=0, keepdims=True))
-        weights = jnp.exp2(scores - new)
-        rescale = jnp.exp2(old - new)
-        max_ref[...] = new
-        sum_ref[...] = sum_ref[...] * rescale + jnp.sum(weights, axis=0, keepdims=True)
-        acc_ref[...] = acc_ref[...] * rescale + dot(
-            values, weights.astype(jnp.bfloat16), ((0,), (0,))
-        )
-
-    def one(j, carry):
-        k_start = meta_ref[1 + query_tiles + j]
-        prefix, whole, nothing = block_kinds(meta_ref, tile, key_tile, q_start, k_start)
-        rows = pl.ds(pl.multiple_of(j * key_tile, key_tile), key_tile)
-
-        @pl.when(whole)
-        def _():
-            absorb(dot(k_ref[0, rows, :], queries, ((1,), (1,))), v_ref[0, rows, :])
-
-        @pl.when(jnp.logical_not(whole | nothing))
-        def _():
-            scores = dot(k_ref[0, rows, :], queries, ((1,), (1,)))
-            absorb(mask_scores(scores, prefix, q_start, k_start, tile), v_ref[0, rows, :])
-
-        return carry
-
-    lax.fori_loop(0, k_ref.shape[1] // key_tile, one, 0)
-    total = sum_ref[...]
-    lse_ref[0, 0] = max_ref[...] + jnp.log2(total)
-    out = (acc_ref[...] / total).T.astype(jnp.bfloat16)
-    o_ref[:, :LANES] = out[:tile]
-    o_ref[:, LANES:] = out[tile:]
-
-
-def attend(meta, q, kv, tile):
-    rows, q_width = q.shape
-    keys = kv.shape[1]
-    groups = q_width // (2 * LANES)
-    steps = rows // tile
-    return pl.pallas_call(
-        attend_kernel,
-        grid_spec=pltpu.PrefetchScalarGridSpec(
-            num_scalar_prefetch=1,
-            grid=(groups, steps),
-            in_specs=[
-                pl.BlockSpec((tile, 2 * LANES), lambda g, i, m: (i, g)),
-                pl.BlockSpec((1, keys, LANES), lambda g, i, m: (g, 0, 0)),
-                pl.BlockSpec((1, keys, LANES), lambda g, i, m: (groups + g, 0, 0)),
-            ],
-            out_specs=[
-                pl.BlockSpec((tile, 2 * LANES), lambda g, i, m: (i, g)),
-                pl.BlockSpec((1, 1, 1, 2 * tile), lambda g, i, m: (g, i, 0, 0)),
-            ],
-            scratch_shapes=[
-                pltpu.VMEM((1, 2 * tile), jnp.float32),
-                pltpu.VMEM((1, 2 * tile), jnp.float32),
-                pltpu.VMEM((LANES, 2 * tile), jnp.float32),
-            ],
-        ),
-        out_shape=[
-            jax.ShapeDtypeStruct((rows, q_width), jnp.bfloat16),
-            jax.ShapeDtypeStruct((groups, steps, 1, 2 * tile), jnp.float32),
-        ],
-        compiler_params=pltpu.CompilerParams(vmem_limit_bytes=VMEM_BYTES),
-        cost_estimate=pl.CostEstimate(
-            flops=8 * rows * keys * LANES * groups, bytes_accessed=6_000_000, transcendentals=0
-        ),
-        name="attend",
-    )(meta, q, kv, kv)
+        name="front",
+    )(prefix, x, pack, rest, spread, cosine, sine, w_project, w_gate, w_up, w_down)
 
 
 def attend_back_kernel(
+    final,
     meta_ref,
+    carry_ref,
     q_ref,
     k_ref,
     v_ref,
@@ -904,7 +1126,7 @@
 
     @pl.when(j == 0)
     def _():
-        acc_ref[...] = jnp.zeros_like(acc_ref)
+        acc_ref[...] = carry_ref[0] if final else jnp.zeros_like(acc_ref)
 
         def one_delta(i, carry):
             product = stacked(o_ref, i).astype(jnp.float32) * stacked(do_ref, i).astype(jnp.float32)
@@ -913,7 +1135,7 @@
 
         lax.fori_loop(0, query_tiles, one_delta, 0)
 
-    k_start = meta_ref[1 + query_tiles + j]
+    k_start = meta_ref[1 + query_tiles + (0 if final else pl.num_programs(1)) + j]
     keys = k_ref[0]
     values = v_ref[0]
 
@@ -950,6 +1172,9 @@
     @pl.when(j == pl.num_programs(1) - 1)
     def _():
         scale = HD ** (-0.5)
+        if not final:
+            dq_ref[0] = acc_ref[...]
+            return
 
         def one_out(i, carry):
             rows = pl.ds(pl.multiple_of(i * tile, tile), tile)
@@ -963,22 +1188,31 @@
         lax.fori_loop(0, query_tiles, one_out, 0)
 
 
-def attend_back(meta, q, kv, o, d_out, lse, cosine, sine, tile):
+def attend_back(meta, carry, q, kv, away, o, d_out, lse, cosine, sine, tile):
     rows, q_width = q.shape
-    keys = kv.shape[1]
+    keys = kv.shape[1] // 2
     groups = q_width // (2 * LANES)
     query_tiles = rows // tile
     key_tiles = keys // tile
+    skip = key_tiles if away else 0
+    acc_block = pl.BlockSpec((1, query_tiles, LANES, 2 * tile), lambda g, j, m: (g, 0, 0, 0))
+    acc_shape = jax.ShapeDtypeStruct((groups, query_tiles, LANES, 2 * tile), jnp.float32)
+    if away:
+        carry = jnp.zeros((1, 1, 8, LANES), jnp.float32)
+        carry_block = pl.BlockSpec((1, 1, 8, LANES), lambda g, j, m: (0, 0, 0, 0))
+    else:
+        carry_block = acc_block
     whole_q = pl.BlockSpec((rows, 2 * LANES), lambda g, j, m: (0, g))
     return pl.pallas_call(
-        attend_back_kernel,
+        functools.partial(attend_back_kernel, not away),
         grid_spec=pltpu.PrefetchScalarGridSpec(
             num_scalar_prefetch=1,
             grid=(groups, key_tiles),
             in_specs=[
+                carry_block,
                 whole_q,
-                pl.BlockSpec((1, tile, LANES), lambda g, j, m: (g, j, 0)),
-                pl.BlockSpec((1, tile, LANES), lambda g, j, m: (groups + g, j, 0)),
+                pl.BlockSpec((1, tile, LANES), lambda g, j, m: (g, skip + j, 0)),
+                pl.BlockSpec((1, tile, LANES), lambda g, j, m: (groups + g, skip + j, 0)),
                 whole_q,
                 whole_q,
                 pl.BlockSpec((1, query_tiles, 1, 2 * tile), lambda g, j, m: (g, 0, 0, 0)),
@@ -986,7 +1220,7 @@
                 pl.BlockSpec((rows, LANES), lambda g, j, m: (0, 0)),
             ],
             out_specs=[
-                whole_q,
+                acc_block if away else whole_q,
                 pl.BlockSpec((1, tile, LANES), lambda g, j, m: (g, j, 0)),
                 pl.BlockSpec((1, tile, LANES), lambda g, j, m: (g, j, 0)),
             ],
@@ -996,16 +1230,701 @@
             ],
         ),
         out_shape=[
-            jax.ShapeDtypeStruct((rows, q_width), jnp.bfloat16),
+            acc_shape if away else jax.ShapeDtypeStruct((rows, q_width), jnp.bfloat16),
             jax.ShapeDtypeStruct((groups, keys, LANES), jnp.bfloat16),
             jax.ShapeDtypeStruct((groups, keys, LANES), jnp.bfloat16),
         ],
         compiler_params=pltpu.CompilerParams(vmem_limit_bytes=VMEM_BYTES),
         cost_estimate=pl.CostEstimate(
-            flops=20 * rows * keys * LANES * groups, bytes_accessed=8_000_000, transcendentals=0
+            flops=20 * rows * keys * LANES * groups * 2, bytes_accessed=8_000_000, transcendentals=0
         ),
-        name="attend_back",
-    )(meta, q, kv, kv, o, d_out, lse, cosine, sine)
+        name="attend_back_away" if away else "attend_back_own",
+    )(meta, carry, q, kv, kv, o, d_out, lse, cosine, sine)
+
+
+def middle_back_kernel(
+    x_ref,
+    project_ref,
+    feed_ref,
+    cot_ref,
+    gain_ref,
+    hidden_ref,
+    down_w_ref,
+    o_ref,
+    wp_ref,
+    grad_ref,
+    d_out_ref,
+    down_ref,
+    wp_grad_ref,
+    gain_grad_ref,
+    acc_ref,
+):
+    step = pl.program_id(0)
+    last = pl.num_programs(0) - 1
+    bf16, f32 = jnp.bfloat16, jnp.float32
+
+    @pl.when(step == 0)
+    def _():
+        acc_ref[...] = jnp.zeros_like(acc_ref)
+        gain_grad_ref[...] = jnp.zeros_like(gain_grad_ref)
+
+    middle = x_ref[...].astype(f32) + project_ref[...].astype(f32)
+    factor = lax.rsqrt(jnp.mean(middle * middle, axis=-1, keepdims=True) + EPSILON)
+    feed_in = feed_ref[...].astype(f32)
+    gain_grad_ref[...] += jnp.sum(feed_in * middle * factor, axis=0, keepdims=True)
+    scaled = gain_ref[1:2, :].astype(f32) * feed_in
+    grad = (
+        cot_ref[...].astype(f32)
+        + factor * scaled
+        - middle * (factor * factor * factor * jnp.mean(scaled * middle, axis=-1, keepdims=True))
+    )
+    grad_ref[...] = grad
+    low = grad.astype(bf16)
+    d_out_ref[...] = dot(low, wp_ref[...], ((1,), (1,))).astype(bf16)
+    acc_ref[...] += dot(o_ref[...], low, ((0,), (0,)))
+    half = hidden_ref.shape[1] // 2
+    down_ref[...] = (
+        dot(hidden_ref[:, :half], down_w_ref[0], ((1,), (0,)))
+        + dot(hidden_ref[:, half:], down_w_ref[1], ((1,), (0,)))
+    ).astype(bf16)
+
+    @pl.when(step == last)
+    def _():
+        for head in range(acc_ref.shape[0] // LANES):
+            wp_grad_ref[head * HD : (head + 1) * HD, :] = acc_ref[
+                head * LANES : head * LANES + HD, :
+            ].astype(bf16)
+
+
+def middle_back(x, project_sum, feed_sum, cot, gains, hidden, down_w, o, w_p):
+    rows, width = x.shape
+    tile = 256
+    units = hidden.shape[1]
+    heads = o.shape[1] // LANES
+    bf16, f32 = jnp.bfloat16, jnp.float32
+
+    def rows_of(columns):
+        return pl.BlockSpec((tile, columns), lambda i: (i, 0))
+
+    def whole(array):
+        return pl.BlockSpec(array.shape, lambda i: (0, 0))
+
+    return pl.pallas_call(
+        middle_back_kernel,
+        grid=(rows // tile,),
+        in_specs=[
+            rows_of(width),
+            rows_of(width),
+            rows_of(width),
+            rows_of(width),
+            whole(gains),
+            rows_of(units),
+            pl.BlockSpec(down_w.shape, lambda i: (0, 0, 0)),
+            rows_of(o.shape[1]),
+            whole(w_p),
+        ],
+        out_specs=[
+            rows_of(width),
+            rows_of(o.shape[1]),
+            rows_of(width),
+            pl.BlockSpec((heads * HD, width), lambda i: (0, 0)),
+            pl.BlockSpec((1, width), lambda i: (0, 0)),
+        ],
+        out_shape=[
+            jax.ShapeDtypeStruct((rows, width), f32),
+            jax.ShapeDtypeStruct(o.shape, bf16),
+            jax.ShapeDtypeStruct((rows, width), bf16),
+            jax.ShapeDtypeStruct((heads * HD, width), bf16),
+            jax.ShapeDtypeStruct((1, width), f32),
+        ],
+        scratch_shapes=[pltpu.VMEM((o.shape[1], width), f32)],
+        compiler_params=pltpu.CompilerParams(vmem_limit_bytes=VMEM_BYTES),
+        cost_estimate=pl.CostEstimate(
+            flops=8_000_000_000, bytes_accessed=30_000_000, transcendentals=0
+        ),
+        name="middle_back",
+    )(x, project_sum, feed_sum, cot, gains, hidden, down_w, o, w_p)
+
+
+def tail_kernel(
+    first_ref,
+    second_ref,
+    q_low_ref,
+    own_ref,
+    away_ref,
+    normed_ref,
+    wide_ref,
+    x_ref,
+    grad_ref,
+    gain_term_ref,
+    gain_ref,
+    project_ref,
+    spread_ref,
+    cos_ref,
+    sin_ref,
+    out_ref,
+    share_ref,
+    gain_share_ref,
+    low_ref,
+    close_ref,
+    part_ref,
+    x_in_ref,
+    up_ref,
+    down_ref,
+    give_ref,
+    core_in_ref,
+    keep_ref,
+    chip_in_ref,
+    total_ref,
+    gain_sum_ref,
+    gain_x_ref,
+    gain_z_ref,
+    x_send,
+    x_recv,
+    up_send,
+    up_recv,
+    down_send,
+    down_recv,
+    core_send,
+    core_recv,
+    chip_send,
+    chip_recv,
+    back_send,
+    back_recv,
+    last_send,
+    last_recv,
+    gain_send,
+    gain_recv,
+):
+    bf16, f32 = jnp.bfloat16, jnp.float32
+    planes = part_ref.shape[1]
+    rows, width = x_ref.shape
+    depth = width // planes
+    project_rows = project_ref.shape[0] // 2
+    half_rows = rows // 2
+    chunks = give_ref.shape[0]
+    chunk = half_rows // chunks
+    half_width = low_ref.shape[2]
+    z = lax.axis_index("fsdp")
+    c = lax.axis_index("ctx")
+    t = lax.axis_index("tp")
+    core = lax.rem(t, 2)
+    across = {"ctx": 1 - c}
+    sibling = {"tp": t + 1 - 2 * core}
+    partner = {"tp": lax.rem(t + 2, 4)}
+    has_above = z < planes - 1
+    has_below = z > 0
+
+    barrier = pltpu.get_barrier_semaphore()
+    for device in (across, sibling, partner):
+        pl.semaphore_signal(barrier, inc=1, device_id=device, device_id_type=MESH)
+    for k in range(1, planes):
+        pl.semaphore_signal(
+            barrier, inc=1, device_id={"fsdp": lax.rem(z + k, planes)}, device_id_type=MESH
+        )
+    pl.semaphore_wait(barrier, 3 + planes - 1)
+
+    def remote(src, dst, send, recv, device):
+        return pltpu.make_async_remote_copy(
+            src_ref=src,
+            dst_ref=dst,
+            send_sem=send,
+            recv_sem=recv,
+            device_id=device,
+            device_id_type=MESH,
+        )
+
+    block = 256
+
+    def lower(i, carry):
+        at = pl.ds(pl.multiple_of(i * block, block), block)
+        for which in range(2):
+            low_ref[which, at, : 2 * LANES] = q_low_ref[
+                at, which * 2 * LANES : (which + 1) * 2 * LANES
+            ]
+            key = own_ref[which, at, :].astype(f32) + away_ref[1 - which, at, :].astype(f32)
+            key = key * cos_ref[at, :] - pltpu.roll(key, SPAN, 1) * sin_ref[at, :]
+            low_ref[which, at, 2 * LANES : 3 * LANES] = key.astype(bf16)
+            value = own_ref[2 + which, at, :].astype(f32) + away_ref[3 - which, at, :].astype(f32)
+            low_ref[which, at, 3 * LANES :] = value.astype(bf16)
+            close_ref[which, at, :] = dot(
+                low_ref[which, at, :], spread_ref[...], ((1,), (1,))
+            ).astype(bf16)
+        return carry
+
+    lax.fori_loop(0, rows // block, lower, 0)
+
+    order = []
+    for k in range((planes + 1) // 2):
+        order += [planes - 1 - k, k]
+    order = order[:planes]
+
+    def weight_part(which, d):
+        at = slice(d * depth, (d + 1) * depth)
+        part_ref[which, d, :depth] = dot(
+            normed_ref[:, at], close_ref[which], ((0,), (0,))
+        ).astype(bf16)
+        part_ref[which, d, depth:] = project_ref[
+            which * project_rows : (which + 1) * project_rows, at
+        ]
+
+    def to_neighbour(d):
+        return remote(part_ref.at[1, d], x_in_ref.at[d], x_send.at[d], x_recv.at[d], across)
+
+    for d in order:
+        weight_part(1, d)
+        to_neighbour(d).start()
+
+    def feature_rows(start):
+        at = pl.ds(pl.multiple_of(start, chunk), chunk)
+        return dot(low_ref[0, at, :], wide_ref[:, :half_width], ((1,), (1,))) + dot(
+            low_ref[1, at, :], wide_ref[:, half_width:], ((1,), (1,))
+        )
+
+    give_start = (1 - core) * half_rows
+    keep_start = core * half_rows
+
+    def to_core(i):
+        return remote(give_ref.at[i], core_in_ref.at[i], core_send.at[i], core_recv.at[i], sibling)
+
+    def to_chip(i):
+        return remote(keep_ref.at[i], chip_in_ref.at[i], chip_send.at[i], chip_recv.at[i], partner)
+
+    def keep_at(i):
+        return pl.ds(pl.multiple_of(keep_start + i * chunk, chunk), chunk)
+
+    def give_at(i):
+        return pl.ds(pl.multiple_of(give_start + i * chunk, chunk), chunk)
+
+    def back(i):
+        return remote(
+            total_ref.at[keep_at(i)],
+            total_ref.at[keep_at(i)],
+            back_send.at[i],
+            back_recv.at[i],
+            sibling,
+        )
+
+    def from_core(i):
+        return remote(
+            total_ref.at[give_at(i)],
+            total_ref.at[give_at(i)],
+            back_send.at[i],
+            back_recv.at[i],
+            sibling,
+        )
+
+    for i in range(chunks):
+        give_ref[i] = feature_rows(give_start + i * chunk).astype(bf16)
+        to_core(i).start()
+    for i in range(chunks):
+        kept = feature_rows(keep_start + i * chunk)
+        to_core(i).wait_recv()
+        keep_ref[i] = (kept + core_in_ref[i].astype(f32)).astype(bf16)
+        to_chip(i).start()
+
+    for d in order:
+        weight_part(0, d)
+
+    def add_neighbour(d):
+        to_neighbour(d).wait_recv()
+        part_ref[0, d] = (part_ref[0, d].astype(f32) + x_in_ref[d].astype(f32)).astype(bf16)
+
+    def up(d):
+        return remote(up_ref.at[d], up_ref.at[d], up_send.at[d], up_recv.at[d], {"fsdp": z + 1})
+
+    def down(d):
+        return remote(
+            down_ref.at[d], down_ref.at[d], down_send.at[d], down_recv.at[d], {"fsdp": z - 1}
+        )
+
+    def upward(d):
+        @pl.when(z == 0)
+        def _():
+            up_ref[d] = part_ref[0, d]
+
+        @pl.when((z > 0) & (z < d))
+        def _():
+            up(d).wait_recv()
+            up_ref[d] = (up_ref[d].astype(f32) + part_ref[0, d].astype(f32)).astype(bf16)
+
+        @pl.when(z < d)
+        def _():
+            up(d).start()
+
+    def downward(d):
+        @pl.when(z == planes - 1)
+        def _():
+            down_ref[d] = part_ref[0, d]
+
+        @pl.when((z < planes - 1) & (z > d))
+        def _():
+            down(d).wait_recv()
+            down_ref[d] = (down_ref[d].astype(f32) + part_ref[0, d].astype(f32)).astype(bf16)
+
+        @pl.when(z > d)
+        def _():
+            down(d).start()
+
+    def finish_chunk(i):
+        to_chip(i).wait_recv()
+        total_ref[keep_at(i)] = (keep_ref[i].astype(f32) + chip_in_ref[i].astype(f32)).astype(bf16)
+        back(i).start()
+
+    def last_share():
+        return remote(
+            share_ref.at[0], share_ref.at[1], last_send.at[0], last_recv.at[0], across
+        )
+
+    added = set()
+
+    def line_step(k):
+        for d in (planes - 1 - k, k):
+            if d not in added:
+                added.add(d)
+                add_neighbour(d)
+        upward(planes - 1 - k)
+        downward(k)
+
+    per_step = -(-chunks // planes)
+    done = 0
+    for k in range(planes - 1):
+        line_step(k)
+        for i in range(done, min(chunks, done + per_step)):
+            finish_chunk(i)
+        done = min(chunks, done + per_step)
+
+    own = part_ref[0, pl.ds(z, 1)][0].astype(f32)
+    share_ref[0] = own.astype(bf16)
+
+    @pl.when(has_below)
+    def _():
+        up(z).wait_recv()
+        share_ref[0] = (share_ref[0].astype(f32) + up_ref[pl.ds(z, 1)][0].astype(f32)).astype(bf16)
+
+    @pl.when(has_above)
+    def _():
+        down(z).wait_recv()
+        share_ref[0] = (share_ref[0].astype(f32) + down_ref[pl.ds(z, 1)][0].astype(f32)).astype(bf16)
+
+    last_share().start()
+    for i in range(done, chunks):
+        finish_chunk(i)
+
+    gain_sum_ref[...] = jnp.zeros_like(gain_sum_ref)
+    gain_sum_ref[1:2, :] = gain_term_ref[...]
+    gain = gain_ref[0:1, :].astype(f32)
+
+    def finish_rows(start):
+        at = pl.ds(pl.multiple_of(start, chunk), chunk)
+        x = x_ref[at, :].astype(f32)
+        factor = lax.rsqrt(jnp.mean(x * x, axis=-1, keepdims=True) + EPSILON)
+        normed_in = total_ref[at, :].astype(f32)
+        gain_sum_ref[0:1, :] += jnp.sum(normed_in * x * factor, axis=0, keepdims=True)
+        scaled = gain * normed_in
+        out_ref[at, :] = (
+            grad_ref[at, :]
+            + factor * scaled
+            - x * (factor * factor * factor * jnp.mean(scaled * x, axis=-1, keepdims=True))
+        ).astype(bf16)
+
+    for i in range(chunks):
+        finish_rows(keep_start + i * chunk)
+    for i in range(chunks):
+        from_core(i).wait_recv()
+        finish_rows(give_start + i * chunk)
+
+    gain_over = remote(gain_sum_ref, gain_x_ref, gain_send.at[0], gain_recv.at[0], across)
+    gain_over.start()
+    gain_over.wait()
+    gain_sum_ref[...] = gain_sum_ref[...] + gain_x_ref[...]
+
+    def gain_to(k):
+        plane = lax.rem(z + k, planes)
+        return remote(
+            gain_sum_ref.at[:, pl.ds(pl.multiple_of(plane * depth, depth), depth)],
+            gain_z_ref.at[k],
+            gain_send.at[k],
+            gain_recv.at[k],
+            {"fsdp": plane},
+        )
+
+    for k in range(1, planes):
+        gain_to(k).start()
+    gain_share_ref[...] = gain_sum_ref[:, pl.ds(pl.multiple_of(z * depth, depth), depth)]
+    for k in range(1, planes):
+        gain_to(k).wait_recv()
+        gain_share_ref[...] += gain_z_ref[k]
+
+    last_share().wait()
+    for k in range(1, planes):
+        gain_to(k).wait_send()
+    for i in range(chunks):
+        to_core(i).wait_send()
+        to_chip(i).wait_send()
+        back(i).wait_send()
+    for d in range(planes):
+        to_neighbour(d).wait_send()
+
+        @pl.when(z < d)
+        def _():
+            up(d).wait_send()
+
+        @pl.when(z > d)
+        def _():
+            down(d).wait_send()
+
+
+def tail(
+    first, second, q_low, own, away, normed, wide, x, grad, gain_term, gains, project,
+    spread, cosine, sine, planes,
+):
+    rows, width = x.shape
+    depth = width // planes
+    half_width = wide.shape[1] // 2
+    close_width = spread.shape[0]
+    chunks = 4
+    chunk = rows // 2 // chunks
+    bf16, f32 = jnp.bfloat16, jnp.float32
+    vmem = pl.BlockSpec(memory_space=pltpu.VMEM)
+    dma = pltpu.SemaphoreType.DMA
+    operands = (
+        first, second, q_low, own, away, normed, wide, x, grad, gain_term, gains, project,
+        spread, cosine, sine,
+    )
+    anywhere = pl.BlockSpec(memory_space=pl.ANY)
+    piece_rows = depth + project.shape[0] // 2
+    return pl.pallas_call(
+        tail_kernel,
+        in_specs=[anywhere] * 2 + [vmem] * (len(operands) - 2),
+        out_specs=[vmem] * 3,
+        out_shape=[
+            jax.ShapeDtypeStruct((rows, width), bf16),
+            jax.ShapeDtypeStruct((2, piece_rows, close_width), bf16),
+            jax.ShapeDtypeStruct((8, depth), f32),
+        ],
+        scratch_shapes=[
+            pltpu.VMEM((2, rows, half_width), bf16),
+            pltpu.VMEM((2, rows, close_width), bf16),
+            pltpu.VMEM((2, planes, piece_rows, close_width), bf16),
+            pltpu.VMEM((planes, piece_rows, close_width), bf16),
+            pltpu.VMEM((planes, piece_rows, close_width), bf16),
+            pltpu.VMEM((planes, piece_rows, close_width), bf16),
+            pltpu.VMEM((chunks, chunk, width), bf16),
+            pltpu.VMEM((chunks, chunk, width), bf16),
+            pltpu.VMEM((chunks, chunk, width), bf16),
+            pltpu.VMEM((chunks, chunk, width), bf16),
+            pltpu.VMEM((rows, width), bf16),
+            pltpu.VMEM((8, width), f32),
+            pltpu.VMEM((8, width), f32),
+            pltpu.VMEM((planes, 8, depth), f32),
+            dma((planes,)),
+            dma((planes,)),
+            dma((planes,)),
+            dma((planes,)),
+            dma((planes,)),
+            dma((planes,)),
+            dma((chunks,)),
+            dma((chunks,)),
+            dma((chunks,)),
+            dma((chunks,)),
+            dma((chunks,)),
+            dma((chunks,)),
+            dma((1,)),
+            dma((1,)),
+            dma((planes,)),
+            dma((planes,)),
+        ],
+        compiler_params=pltpu.CompilerParams(
+            collective_id=2, has_side_effects=True, vmem_limit_bytes=VMEM_BYTES
+        ),
+        cost_estimate=pl.CostEstimate(
+            flops=60_000_000_000, bytes_accessed=24_000_000, transcendentals=0
+        ),
+        name="tail",
+    )(*operands)
+
+
+def feed_kernel(
+    x_ref,
+    project_ref,
+    cot_ref,
+    gain_ref,
+    gate_ref,
+    up_ref,
+    down_ref,
+    total_ref,
+    hidden_ref,
+    gate_grad_ref,
+    up_grad_ref,
+    down_grad_ref,
+    normed_ref,
+    gate_back_ref,
+    up_back_ref,
+    give_ref,
+    core_in_ref,
+    keep_ref,
+    chip_in_ref,
+    core_send,
+    core_recv,
+    chip_send,
+    chip_recv,
+    back_send,
+    back_recv,
+):
+    bf16, f32 = jnp.bfloat16, jnp.float32
+    rows, width = x_ref.shape
+    half_rows = rows // 2
+    chunks, chunk, _ = give_ref.shape
+    units = gate_ref.shape[2]
+    t = lax.axis_index("tp")
+    core = lax.rem(t, 2)
+    sibling = {"tp": t + 1 - 2 * core}
+    partner = {"tp": lax.rem(t + 2, 4)}
+
+    barrier = pltpu.get_barrier_semaphore()
+    for device in (sibling, partner):
+        pl.semaphore_signal(barrier, inc=1, device_id=device, device_id_type=MESH)
+    pl.semaphore_wait(barrier, 2)
+
+    def remote(src, dst, send, recv, device):
+        return pltpu.make_async_remote_copy(
+            src_ref=src,
+            dst_ref=dst,
+            send_sem=send,
+            recv_sem=recv,
+            device_id=device,
+            device_id_type=MESH,
+        )
+
+    give_start = (1 - core) * half_rows
+    keep_start = core * half_rows
+    gain = gain_ref[1:2, :].astype(f32)
+    halves = tuple((gate_ref.at[i], up_ref.at[i], down_ref.at[i]) for i in range(2))
+
+    def feature_rows(start):
+        at = pl.ds(pl.multiple_of(start, chunk), chunk)
+        middle = x_ref[at, :].astype(f32) + project_ref[at, :].astype(f32)
+        factor = lax.rsqrt(jnp.mean(middle * middle, axis=-1, keepdims=True) + EPSILON)
+        normed_ref[at, :] = (middle * factor * gain).astype(bf16)
+        for which, (gate_w, up_w, down_w) in enumerate(halves):
+            cols = slice(which * units, (which + 1) * units)
+            gate = dot(normed_ref[at, :], gate_w[...], ((1,), (0,)))
+            up = dot(normed_ref[at, :], up_w[...], ((1,), (0,)))
+            hidden_in = dot(cot_ref[at, :], down_w[...], ((1,), (1,)))
+            sigmoid = jax.nn.sigmoid(gate)
+            silu = gate * sigmoid
+            hidden_ref[at, cols] = (silu * up).astype(bf16)
+            gate_back_ref[at, cols] = (
+                hidden_in * up * sigmoid * (1.0 + gate * (1.0 - sigmoid))
+            ).astype(bf16)
+            up_back_ref[at, cols] = (hidden_in * silu).astype(bf16)
+        return sum(
+            dot(back_ref[at, which * units : (which + 1) * units], weight[...], ((1,), (1,)))
+            for which, (gate_w, up_w, _) in enumerate(halves)
+            for back_ref, weight in ((gate_back_ref, gate_w), (up_back_ref, up_w))
+        )
+
+    def to_core(i):
+        return remote(give_ref.at[i], core_in_ref.at[i], core_send.at[i], core_recv.at[i], sibling)
+
+    def to_chip(i):
+        return remote(keep_ref.at[i], chip_in_ref.at[i], chip_send.at[i], chip_recv.at[i], partner)
+
+    def back(i, start):
+        at = pl.ds(pl.multiple_of(start + i * chunk, chunk), chunk)
+        return remote(
+            total_ref.at[at], total_ref.at[at], back_send.at[i], back_recv.at[i], sibling
+        )
+
+    for i in range(chunks):
+        give_ref[i] = feature_rows(give_start + i * chunk).astype(bf16)
+        to_core(i).start()
+        kept = feature_rows(keep_start + i * chunk)
+        to_core(i).wait_recv()
+        keep_ref[i] = (kept + core_in_ref[i].astype(f32)).astype(bf16)
+        to_chip(i).start()
+
+    block = 256
+
+    def input_grads(back_ref, grad_ref):
+        def some(i, carry):
+            at = pl.ds(pl.multiple_of(i * block, block), block)
+            for which in (1, 0):
+                grad_ref[which, at, :] = dot(
+                    normed_ref[:, at],
+                    back_ref[:, which * units : (which + 1) * units],
+                    ((0,), (0,)),
+                ).astype(bf16)
+            return carry
+
+        lax.fori_loop(0, width // block, some, 0)
+
+    def down_grads(i, carry):
+        at = pl.ds(pl.multiple_of(i * block, block), block)
+        down_grad_ref[at, :] = dot(hidden_ref[:, at], cot_ref[...], ((0,), (0,))).astype(bf16)
+        return carry
+
+    def finish_chunk(i):
+        to_chip(i).wait_recv()
+        at = pl.ds(pl.multiple_of(keep_start + i * chunk, chunk), chunk)
+        total_ref[at, :] = (keep_ref[i].astype(f32) + chip_in_ref[i].astype(f32)).astype(bf16)
+        back(i, keep_start).start()
+
+    input_grads(gate_back_ref, gate_grad_ref)
+    for i in range(chunks // 2):
+        finish_chunk(i)
+    input_grads(up_back_ref, up_grad_ref)
+    lax.fori_loop(0, down_grad_ref.shape[0] // block, down_grads, 0)
+    for i in range(chunks // 2, chunks):
+        finish_chunk(i)
+    for i in range(chunks):
+        to_core(i).wait_send()
+        to_chip(i).wait_send()
+        back(i, keep_start).wait_send()
+    for i in range(chunks):
+        back(i, give_start).wait_recv()
+
+
+def feed(x, project_sum, cot, gains, gate_w, up_w, down_w):
+    rows, width = x.shape
+    units = gate_w.shape[2]
+    chunk = 256
+    chunks = rows // 2 // chunk
+    bf16 = jnp.bfloat16
+    vmem = pl.BlockSpec(memory_space=pltpu.VMEM)
+    dma = pltpu.SemaphoreType.DMA
+    operands = (x, project_sum, cot, gains, gate_w, up_w, down_w)
+    piece = pltpu.VMEM((chunks, chunk, width), bf16)
+    return pl.pallas_call(
+        feed_kernel,
+        in_specs=[vmem] * len(operands),
+        out_specs=[vmem] * 5,
+        out_shape=[
+            jax.ShapeDtypeStruct((rows, width), bf16),
+            jax.ShapeDtypeStruct((rows, 2 * units), bf16),
+            jax.ShapeDtypeStruct((2, width, units), bf16),
+            jax.ShapeDtypeStruct((2, width, units), bf16),
+            jax.ShapeDtypeStruct((2 * units, width), bf16),
+        ],
+        scratch_shapes=[
+            pltpu.VMEM((rows, width), bf16),
+            pltpu.VMEM((rows, 2 * units), bf16),
+            pltpu.VMEM((rows, 2 * units), bf16),
+            piece,
+            piece,
+            piece,
+            piece,
+        ]
+        + [dma((chunks,))] * 6,
+        compiler_params=pltpu.CompilerParams(
+            collective_id=3, has_side_effects=True, vmem_limit_bytes=VMEM_BYTES
+        ),
+        cost_estimate=pl.CostEstimate(
+            flops=50_000_000_000, bytes_accessed=40_000_000, transcendentals=0
+        ),
+        name="feed",
+    )(*operands)
 
 
 def paired_body(
@@ -1040,27 +1959,17 @@
             jnp.concatenate([other, mine], axis=axis),
         )
 
-    def gathered(mine, axis):
-        whole = lax.all_gather(mine, "fsdp", axis=axis, tiled=True)
-        return whole, swap_ctx(whole)
-
     planes = lax.axis_size("fsdp")
     kv_half = w_key.shape[1] // 2
     q_half = w_query.shape[1] // 2
 
     def packed(which):
         return jnp.concatenate(
-            [
-                jnp.concatenate([half(w_query, 1, which), half(w_key, 1, which), half(w_value, 1, which)], axis=1),
-                half(w_project, 0, which),
-                jnp.pad(jnp.stack([gain_attend, gain_feed]), ((0, GAIN_ROWS - 2), (0, 0))),
-            ],
-            axis=0,
-        )
-
-    wg_mine, wg_other = gathered(half(w_gate, 1), 0)
-    wu_mine, wu_other = gathered(half(w_up, 1), 0)
-    wd_mine, wd_other = gathered(half(w_down, 0), 1)
+            [half(w_query, 1, which), half(w_key, 1, which), half(w_value, 1, which)], axis=1
+        )
+
+    gain_rows = jnp.pad(jnp.stack([gain_attend, gain_feed]), ((0, GAIN_ROWS - 2), (0, 0)))
+    pack = jnp.concatenate([packed(c), gain_rows], axis=0)
 
     def parts(block):
         return (
@@ -1095,49 +2004,26 @@
 
     x = tokens[0]
     cot = cotangent[0]
-    normed, q, kv_all, w_qkv, w_p, gains = gather_project(
-        x, packed(c), packed(1 - c), spread, cosine, sine, planes
-    )
-    gain_one, gain_two = gains[0:1].astype(f32), gains[1:2].astype(f32)
-    o, lse = attend(meta, q, kv_all, tile)
-    middle = x.astype(f32) + paired_tensor_sum(dot(o, w_p, ((1,), (0,))))
-    factor_two = rms_factor(middle)
-    normed_feed = (middle * factor_two * gain_two).astype(bf16)
-
-    def feed(wg, wu, wd):
-        gate = dot(normed_feed, wg, ((1,), (0,)))
-        up = dot(normed_feed, wu, ((1,), (0,)))
-        sigmoid = jax.nn.sigmoid(gate)
-        silu = gate * sigmoid
-        hidden = (silu * up).astype(bf16)
-        hidden_in = dot(cot, wd, ((1,), (1,)))
-        gate_back = (hidden_in * up * sigmoid * (1.0 + gate * (1.0 - sigmoid))).astype(bf16)
-        up_back = (hidden_in * silu).astype(bf16)
-        feed_rows = dot(gate_back, wg, ((1,), (1,))) + dot(up_back, wu, ((1,), (1,)))
-        return hidden, gate_back, up_back, feed_rows
-
-    hidden_m, gate_back_m, up_back_m, feed_m = feed(wg_mine, wu_mine, wd_mine)
-    hidden_o, gate_back_o, up_back_o, feed_o = feed(wg_other, wu_other, wd_other)
-    feed_in = paired_tensor_sum(feed_m + feed_o)
-
-    def summed(give, keep, axis):
-        both = (keep + swap_ctx(give.astype(bf16)).astype(f32)).astype(bf16)
-        share = lax.psum_scatter(both, "fsdp", scatter_dimension=axis, tiled=True)
-        return share
-
-    def whole_again(share, axis):
-        return ordered(share, swap_ctx(share), axis).astype(f32)
-
-    contract_rows = ((0,), (0,))
-    gate_share = summed(
-        dot(normed_feed, gate_back_o, contract_rows), dot(normed_feed, gate_back_m, contract_rows), 0
-    )
-    up_share = summed(
-        dot(normed_feed, up_back_o, contract_rows), dot(normed_feed, up_back_m, contract_rows), 0
-    )
-    down_part = jnp.concatenate(
-        [dot(hidden_m, cot, contract_rows), dot(hidden_o, cot, contract_rows)], axis=0
-    ).astype(bf16)
+    (
+        normed, q, kv_all, w_qkv, w_p, gains, o, lse, project_sum, wg, wu, wd,
+    ) = front(
+        prefix_len, x, pack, packed(1 - c), spread, cosine, sine,
+        w_project.reshape(-1, HD, w_project.shape[1]), w_gate, w_up, w_down, planes,
+    )
+    w_p = w_p.reshape(-1, width)
+    feed_sum, hidden, gate_grad, up_grad, down_part = feed(
+        x, project_sum, cot, gains, wg, wu, wd
+    )
+
+    gate_away, up_away = swap_ctx(gate_grad[1]), swap_ctx(up_grad[1])
+
+    def added(a, b):
+        return (a.astype(f32) + b.astype(f32)).astype(bf16)
+
+    both = jnp.concatenate([added(gate_grad[0], gate_away), added(up_grad[0], up_away)], axis=1)
+    both_share = lax.psum_scatter(both, "fsdp", scatter_dimension=0, tiled=True)
+    both_away = swap_ctx(both_share)
+    units_half = gate_grad.shape[2]
     down_share = lax.psum_scatter(down_part, "fsdp", scatter_dimension=1, tiled=True)
     down_away = swap_ctx(down_share)
     size = down_share.shape[0] // 2
@@ -1145,71 +2031,37 @@
     down_other = down_share[size:].astype(f32) + down_away[:size].astype(f32)
     down_grad = ordered(down_mine, down_other, 0)
 
-    layer_output = (
-        middle
-        + paired_tensor_sum(
-            dot(hidden_m, wd_mine, ((1,), (0,))) + dot(hidden_o, wd_other, ((1,), (0,)))
-        )
-    ).astype(bf16)
-
-    gain_two_term = jnp.sum(feed_in * middle * factor_two, axis=0)
-    middle_grad = cot.astype(f32) + rms_back(middle, factor_two, gain_two, feed_in)
-    middle_low = middle_grad.astype(bf16)
-    project_part = dot(o, middle_low, contract_rows)
-    project_part = project_part.reshape(-1, LANES, width)[:, :HD].reshape(-1, width)
-    rows_half = project_part.shape[0] // 2
-    project_share = summed(project_part[rows_half:], project_part[:rows_half], 1)
-    d_out = dot(middle_low, w_p, ((1,), (1,))).astype(bf16)
-    q_low, dk, dv = attend_back(meta, q, kv_all, o, d_out, lse, cosine, sine, tile)
-    d_kv = jnp.concatenate([dk, dv], axis=0)
-    d_kv_away = swap_ctx(d_kv[:, rows:])
-    d_kv = [
-        d_kv[slab, :rows].astype(f32) + d_kv_away[slab ^ 1].astype(f32) for slab in range(4)
+    middle_grad, d_out, down_rows, project_part, gain_two_term = middle_back(
+        x, project_sum, feed_sum, cot, gains, hidden, wd, o, w_p
+    )
+    layer_output = (x.astype(f32) + project_sum.astype(f32)
+                    + paired_tensor_sum(down_rows).astype(f32)).astype(bf16)
+    dq_away, dk_away, dv_away = attend_back(
+        meta, None, q, kv_all, True, o, d_out, lse, cosine, sine, tile
+    )
+    d_kv_away = swap_ctx(jnp.concatenate([dk_away, dv_away], axis=0))
+    q_low, dk_own, dv_own = attend_back(
+        meta, dq_away, q, kv_all, False, o, d_out, lse, cosine, sine, tile
+    )
+    d_kv_own = jnp.concatenate([dk_own, dv_own], axis=0)
+    tokens_grad, share, gain_share = tail(
+        both, down_share, q_low, d_kv_own, d_kv_away, normed, w_qkv, x, middle_grad,
+        gain_two_term, gains, project_part, spread, cosine, sine, planes,
+    )
+    shares = [
+        ordered(a, b, 1).astype(f32) for a, b in zip(parts(share[0, : width // planes]), parts(share[1, : width // planes]))
     ]
-
-    def turn_back(part):
-        return part * cosine - jnp.concatenate([part[:, SPAN:], part[:, :SPAN]], axis=1) * sine
-
-    low_mine = jnp.concatenate(
-        [q_low[:, : 2 * LANES], turn_back(d_kv[0]).astype(bf16), d_kv[2].astype(bf16)], axis=1
-    )
-    low_other = jnp.concatenate(
-        [q_low[:, 2 * LANES :], turn_back(d_kv[1]).astype(bf16), d_kv[3].astype(bf16)], axis=1
-    )
-    half_width = low_mine.shape[1]
-    normed_in = paired_tensor_sum(
-        dot(low_mine, w_qkv[:, :half_width], ((1,), (1,)))
-        + dot(low_other, w_qkv[:, half_width:], ((1,), (1,)))
-    )
-    close_mine = dot(low_mine, spread, ((1,), (1,))).astype(bf16)
-    close_other = dot(low_other, spread, ((1,), (1,))).astype(bf16)
-    qkv_share = summed(
-        dot(normed, close_other, contract_rows), dot(normed, close_mine, contract_rows), 0
-    )
-    qkv_away = swap_ctx(qkv_share)
-    shares = [
-        ordered(a, b, 1).astype(f32) for a, b in zip(parts(qkv_share), parts(qkv_away))
-    ]
-
-    inputs = x.astype(f32)
-    factor_one = rms_factor(inputs)
-    gain_one_term = jnp.sum(normed_in * inputs * factor_one, axis=0)
-    tokens_grad = (middle_grad + rms_back(inputs, factor_one, gain_one, normed_in)).astype(bf16)
-    gain_terms = jnp.stack([gain_one_term, gain_two_term])
-    gain_terms = lax.psum_scatter(
-        gain_terms + swap_ctx(gain_terms), "fsdp", scatter_dimension=1, tiled=True
-    )
     return (
         layer_output[None],
         tokens_grad[None],
-        gain_terms[0],
+        gain_share[0],
         shares[0],
         shares[1],
         shares[2],
-        whole_again(project_share, 0),
-        gain_terms[1],
-        whole_again(gate_share, 1),
-        whole_again(up_share, 1),
+        ordered(share[0, width // planes :], share[1, width // planes :], 0).astype(f32),
+        gain_share[1],
+        ordered(both_share[:, :units_half], both_away[:, :units_half], 1).astype(f32),
+        ordered(both_share[:, units_half:], both_away[:, units_half:], 1).astype(f32),
         down_grad,
     )
 

time: 657 us -> 515 us (0.78)
  Pallas kernels: 169 us -> 395 us
  waiting for transfers between devices: 198 us -> 34.9 us
  matrix products: 105 us -> 0 us
  other arithmetic: 95.3 us -> 30.7 us
  local copies, waits for them, and re-layouts: 46.1 us -> 25.2 us
  starting transfers between devices: 20.1 us -> 5.49 us
    pallas_call x3 -> x6, Pallas kernels: 169 us -> 395 us  [the longest x1 181 us: front(): pl.pallas_call(front_kernel, in_specs=[smem] + [vmem] * 6 + [anywhere] *...]
    dot_general x29 -> x0, matrix products: 105 us -> none  [dot(): lax.dot_general(a, b, (contract, ((), ())), preferred_element_type=jnp.fl...]
    ppermute x4 -> x1, waiting for transfers between devices: 73.6 us -> 0.01 us  [swap_chip(): return lax.ppermute(block, 'tp', [(0, 2), (2, 0), (1, 3), (3, 1)])]
    unnamed x12 -> x3, waiting for transfers between devices: 35.1 us -> 0.03 us
    all_gather x3 -> x0, waiting for transfers between devices: 32.6 us -> none  [gathered(): whole = lax.all_gather(mine, 'fsdp', axis=axis, tiled=True)]
    convert_element_type x8 -> x5, other arithmetic: 35.4 us -> 7.94 us  [the longest x2 4.32 us: added(): return (a.astype(f32) + b.astype(f32)).astype(bf16)]
    reduce_sum x4 -> x0, other arithmetic: 22.4 us -> none  [the longest x1 7.21 us: paired_body(): gain_two_term = jnp.sum(feed_in * middle * factor_two, axis=0)]
    ppermute x14 -> x5, waiting for transfers between devices: 55 us -> 34.9 us  [swap_ctx(): return lax.ppermute(block, 'ctx', [(0, 1), (1, 0)])]
  transfers between devices with their start and end apart: 35 -> 10, of which waited for: 15 -> 3; matrix products, arithmetic and copies ran while one was open for 34% -> 8% of each run, Pallas kernels for 26% -> 27%
where the time goes in v3:
time: 515 us; the launch traced here: 507 us
  Pallas kernels  395 us (77%)
  waiting for transfers between devices  34.9 us (7%)
  other arithmetic  30.7 us (6%)
  local copies, waits for them, and re-layouts  25.2 us (5%)
  between operations  15.2 us (3%)
  starting transfers between devices  5.49 us (1%)
    pallas_call x1, Pallas kernels, front(): pl.pallas_call(front_kernel, in_specs=[smem] + [vmem] * 6 + [anywhere] *...  181 us
    pallas_call x1, Pallas kernels, tail(): pl.pallas_call(tail_kernel, in_specs=[anywhere] * 2 + [vmem] * (len(opera...  94.6 us
    pallas_call x1, Pallas kernels, feed(): pl.pallas_call(feed_kernel, in_specs=[vmem] * len(operands), out_specs=[v...  60.4 us
    pallas_call x2, Pallas kernels, attend_back(): pl.pallas_call(functools.partial(attend_back_kernel, not away), grid_spec...  42.9 us
    ppermute x5, waiting for transfers between devices, swap_ctx(): return lax.ppermute(block, 'ctx', [(0, 1), (1, 0)])  34.9 us
    pallas_call x1, Pallas kernels, middle_back(): pl.pallas_call(middle_back_kernel, grid=(rows // tile,), in_specs=[rows_o...  17 us
  transfers between devices with their start and end apart: 10, of which 3 were waited for; matrix products, arithmetic and copies ran while one was open for 8% of the time, Pallas kernels for 27%

profile of v3, /device:TPU:0, one launch (start us, length us, event | category | flops | bytes accessed | tf_op | source)
XLA Modules:
  0.0 507.0 jit_solution(13878347088727586165)
XLA Ops:
  7.3 1.0 constant_dynamic-slice_fusion.1
  8.3 0.1 copy.41
  8.4 0.1 copy.42
  8.6 0.1 copy.39
  8.7 0.1 copy.40
  8.8 0.7 stack.10
  9.5 0.7 stack.9
  10.2 0.7 convert_element_type.99
  11.6 1.9 fusion.9
  13.5 0.2 constant_dynamic-slice_fusion.3
  13.7 0.9 pad_maximum_fusion.6.rest_ref
  14.6 1.3 pad_maximum_fusion.3
  15.9 0.9 pad_maximum_fusion.5.pack_ref
  16.7 180.6 %front.1 = (bf16[1024,1536]{1,0:T(8,128)(2,1)}, bf16[1024,512]{1,0:T(8,128)(2,1)}, bf16[4,2048,128]{2,1,0:T(8,128)(2,1)}, bf16[1536,1024]{1,0:T(8,128)(2,1)}, bf...) custom-call(s32[1]{0:T(128)S(6)} %copy.44.prefix_ref, ...), custom_call_target="tpu_custom_call" | custom-call | flops 120000004096 | bytes 60000000 | tf_op jit(solution)/shard_map/front/pallas_call | solution.py:1055
  197.3 60.4 %feed.1 = (bf16[1024,1536]{1,0:T(8,128)(2,1)}, bf16[1024,1024]{1,0:T(8,128)(2,1)}, bf16[2,1536,512]{2,1,0:T(8,128)(2,1)}, bf16[2,1536,512]{2,1,0:T(8,128)(2,1)}, bf16[1024,1536]{1,0:T(8,128)(2,1)}) custom-call(bf16[1024,1536]{1,0:T(8,128)(2,1)} %bitcast.32, bf16[1024,1536]{1,0:T(8,128)(2,1)} %get-tuple-element.42.project_ref, bf16[1024,1536]{1,0:T(8,128)(2,1)} %bitcast.37, ...), custom_call_target="tpu_custom_call" | custom-call | flops 49999998976 | bytes 40000000 | tf_op jit(solution)/shard_map/feed/pallas_call | solution.py:1899
  257.7 17.0 %middle_back.1 = (f32[1024,1536]{1,0:T(8,128)}, bf16[1024,512]{1,0:T(8,128)(2,1)}, bf16[1024,1536]{1,0:T(8,128)(2,1)}, bf16[384,1536]{1,0:T(8,128)(2,1)}, f32[1,1536]{1,0:T(1,128)}) custom-call(bf16[1024,1536]{1,0:T(8,128)(2,1)} %bitcast.33, bf16[1024,1536]{1,0:T(8,128)(2,1)} %get-tuple-element.42.project_ref, ...), custom_call_target="tpu_custom_call" | custom-call | flops 8000000000 | bytes 30000000 | tf_op jit(solution)/shard_map/middle_back/pallas_call | solution.py:1312
  274.7 2.8 constant_dynamic-slice_fusion
  277.5 0.3 collective-permute-start
  277.9 3.0 copy.37
  280.8 0.4 reduce-scatter.5.cloned.1.call-start
  281.3 2.8 slice_bitcast_fusion.1
  284.1 2.7 slice_bitcast_fusion
  286.8 2.0 collective-permute-start.4
  288.8 0.6 pad_add_fusion.meta_ref
  289.4 1.8 add_convert_fusion.2
  291.2 0.9 collective-permute-start.1
  292.1 0.6 broadcast_in_dim.12.carry_ref
  292.7 18.6 %attend_back_away.1 = (f32[2,4,128,512]{3,2,1,0:T(8,128)}, bf16[2,1024,128]{2,1,0:T(8,128)(2,1)}, bf16[2,1024,128]{2,1,0:T(8,128)(2,1)}) custom-call(s32[13]{0:T(128)} %pad_add_fusion.meta_ref, f32[1,1,8,128]{3,2,1,0:T(8,128)} %broadcast_in_dim.12.carry_ref, bf16[1024,512]{1,0:T(8,128)(2,1)} %get-tuple-element.55.q_ref, ...), custom_call_target="tpu_custom_call" | custom-call | flops 10737418240 | bytes 8000000 | tf_op jit(solution)/shard_map/attend_back_away/pallas_call | solution.py:1206
  311.3 2.3 pad_maximum_fusion.2
  313.6 1.6 collective-permute-start.5
  315.2 24.3 %attend_back_own.1 = (bf16[1024,512]{1,0:T(8,128)(2,1)}, bf16[2,1024,128]{2,1,0:T(8,128)(2,1)}, bf16[2,1024,128]{2,1,0:T(8,128)(2,1)}) custom-call(s32[13]{0:T(128)} %pad_add_fusion.meta_ref, f32[2,4,128,512]{3,2,1,0:T(8,128)} %get-tuple-element.59.carry_ref, bf16[1024,512]{1,0:T(8,128)(2,1)} %get-tuple-element.55.q_ref, ...), custom_call_target="tpu_custom_call" | custom-call | flops 10737418240 | bytes 8000000 | tf_op jit(solution)/shard_map/attend_back_own/pallas_call | solution.py:1206
  339.6 0.4 add_convert_fusion.1
  340.0 0.1 collective-permute-start.2
  340.1 0.5 copy-done.6
  340.6 0.2 copy-done.7
  340.8 1.1 pad_maximum_fusion.1.own_ref
  341.8 2.5 fusion.2
  344.3 11.0 %collective-permute-done.4 = bf16[1536,512]{1,0:T(8,128)(2,1)} collective-permute-done((bf16[1536,512]{1,0:T(8,128)(2,1)}, bf16[1536,512]{1,0:T(8,128)(2,1)}, u32[]{:S(2)}, u32[]{:S(2)}) %collective-permute-start.4) | collective-permute-done | bytes 1572896 | tf_op jit(solution)/shard_map/ppermute | solution.py:435
  355.4 1.8 fusion.1
  357.2 2.1 pad_maximum_fusion.first_ref
  359.3 4.8 fusion
  364.2 2.3 copy.38.second_ref
  366.5 0.1 collective-permute-start.7
  366.5 11.3 %collective-permute-done.5.away_ref = bf16[4,1024,128]{2,1,0:T(8,128)(2,1)} collective-permute-done((bf16[4,1024,128]{2,1,0:T(8,128)(2,1)}, bf16[4,1024,128]{2,1,0:T(8,128)(2,1)}, u32[]{:S(2)}, u32[]{:S(2)}) %collective-permute-start.5) | collective-permute-done | bytes 1048608 | tf_op jit(solution)/shard_map/ppermute | solution.py:435
  377.8 94.6 %tail.1 = (bf16[1024,1536]{1,0:T(8,128)(2,1)}, bf16[2,576,384]{2,1,0:T(8,128)(2,1)}, f32[8,384]{1,0:T(8,128)}) custom-call(bf16[1536,1024]{1,0:T(8,128)(2,1)} %pad_maximum_fusion.first_ref, bf16[1024,384]{1,0:T(8,128)(2,1)} %copy.38.second_ref, bf16[1024,512]{1,0:T(8,128)(2,1)} %get-tuple-element.60.q_low_ref, ...), custom_call_target="tpu_custom_call" | custom-call | flops 60000002048 | bytes 24000000 | tf_op jit(solution)/shard_map/tail/pallas_call | solution.py:1697
  472.5 1.1 slice_bitcast_fusion.3
  473.6 0.1 fusion.21
  473.8 0.1 fusion.22
  473.9 0.2 fusion.8
  474.1 0.9 copy.36
  474.9 0.2 fusion.7
  475.1 0.9 copy.35
  476.0 1.0 slice_bitcast_fusion.5
  477.0 0.9 fusion.6
  477.9 1.0 fusion.5
  478.9 1.4 slice_reduce_fusion
  480.3 1.3 convert_add_fusion.3
  481.6 1.2 maximum_select_fusion.1
  482.9 0.1 fusion.19
  483.0 12.5 %collective-permute-done.6 = bf16[384,1024]{1,0:T(8,128)(2,1)S(1)} collective-permute-done((bf16[384,1024]{1,0:T(8,128)(2,1)}, bf16[384,1024]{1,0:T(8,128)(2,1)S(1)}, u32[]{:S(2)}, u32[]{:S(2)}) %collective-permute-start.6) | collective-permute-done | bytes 786464 | tf_op jit(solution)/shard_map/ppermute | solution.py:435
  495.5 0.1 fusion.20
  495.6 1.4 fusion.4
  496.9 1.4 fusion.3
  498.3 1.7 copy.45
  (32 shorter events, 0.2 us)
Async XLA Ops:
  7.2 6.3 %copy-start.5 = (bf16[384,384]{1,0:T(8,128)(2,1)S(1)}, bf16[384,384]{1,0:T(8,128)(2,1)}, u32[]{:S(2)}) copy-start(bf16[384,384]{1,0:T(8,128)(2,1)} %param.18) | copy-start | bytes 884740
  7.2 357.0 %reduce-scatter.7.cloned.1.call-start = ((), (), s32[]{:S(2)}) async-start(), calls=%async_computation.3 | async-start | bytes 3932160
  274.7 3.2 copy-start.2
  277.5 11.9 %collective-permute-start = (bf16[512,1536]{1,0:T(8,128)(2,1)}, bf16[512,1536]{1,0:T(8,128)(2,1)}, u32[]{:S(2)}, u32[]{:S(2)}) collective-permute-start(bf16[512,1536]{1,0:T(8,128)(2,1)} %constant_dynamic-slice_fusion), channel_id=1, source_target_pairs={{0,1},{1,0},{2,3},{3,2},{4,5},{5,4},{6,7},{7,6},{8,9},{9,8},{10,11... | collective-permute-start | bytes 4718600 | tf_op jit(solution)/shard_map/ppermute | solution.py:439
  280.8 198.1 %reduce-scatter.5.cloned.1.call-start = ((), (), s32[]{:S(2)}) async-start(), calls=%async_computation.2 | async-start | bytes 3932160 | tf_op jit(solution)/shard_map/reduce_scatter | solution.py:2024
  281.3 8.1 %copy-start.1 = (bf16[1024,1536]{1,0:T(8,128)(2,1)S(1)}, bf16[1024,1536]{1,0:T(8,128)(2,1)}, u32[]{:S(2)}) copy-start(bf16[1024,1536]{1,0:T(8,128)(2,1)} %get-tuple-element.51) | copy-start | bytes 9437188
  284.1 57.7 %collective-permute-start.3 = (bf16[1536,512]{1,0:T(8,128)(2,1)}, bf16[1536,512]{1,0:T(8,128)(2,1)}, u32[]{:S(2)}, u32[]{:S(2)}) collective-permute-start(bf16[1536,512]{1,0:T(8,128)(2,1)} %slice_bitcast_fusion.1), channel_id=1, source_target_pairs={{0,4},{4,0},{1,5},{5,1},{2,6},{6,2},{3,7},{7,3},{8,12},{12,8},{9,1... | collective-permute-start | bytes 4718600 | tf_op jit(solution)/shard_map/ppermute | solution.py:435
  286.8 68.6 %collective-permute-start.4 = (bf16[1536,512]{1,0:T(8,128)(2,1)}, bf16[1536,512]{1,0:T(8,128)(2,1)}, u32[]{:S(2)}, u32[]{:S(2)}) collective-permute-start(bf16[1536,512]{1,0:T(8,128)(2,1)} %slice_bitcast_fusion), channel_id=1, source_target_pairs={{0,4},{4,0},{1,5},{5,1},{2,6},{6,2},{3,7},{7,3},{8,12},{12,8},{9,1... | collective-permute-start | bytes 4718600 | tf_op jit(solution)/shard_map/ppermute | solution.py:435
  291.2 48.4 %collective-permute-start.1 = (bf16[512,1536]{1,0:T(8,128)(2,1)S(1)}, bf16[512,1536]{1,0:T(8,128)(2,1)S(1)}, u32[]{:S(2)}, u32[]{:S(2)}) collective-permute-start(bf16[512,1536]{1,0:T(8,128)(2,1)S(1)} %add_convert_fusion.2), channel_id=1, source_target_pairs={{0,2},{2,0},{1,3},{3,1},{4,6},{6,4},{5,7},{7,5},{8,10},{10,8},{9,1... | collective-permute-start | bytes 4718600 | tf_op jit(solution)/shard_map/ppermute | solution.py:443
  313.6 64.3 %collective-permute-start.5 = (bf16[4,1024,128]{2,1,0:T(8,128)(2,1)}, bf16[4,1024,128]{2,1,0:T(8,128)(2,1)}, u32[]{:S(2)}, u32[]{:S(2)}) collective-permute-start(bf16[4,1024,128]{2,1,0:T(8,128)(2,1)} %pad_maximum_fusion.2), channel_id=1, source_target_pairs={{0,4},{4,0},{1,5},{5,1},{2,6},{6,2},{3,7},{7,3},{8,12},{12,8},{9,1... | collective-permute-start | bytes 3145736 | tf_op jit(solution)/shard_map/ppermute | solution.py:435
  339.6 1.0 copy-start.6
  339.6 1.2 copy-start.7
  340.0 19.3 %collective-permute-start.2 = (bf16[512,1536]{1,0:T(8,128)(2,1)S(1)}, bf16[512,1536]{1,0:T(8,128)(2,1)S(1)}, u32[]{:S(2)}, u32[]{:S(2)}) collective-permute-start(bf16[512,1536]{1,0:T(8,128)(2,1)S(1)} %add_convert_fusion.1), channel_id=1, source_target_pairs={{0,1},{1,0},{2,3},{3,2},{4,5},{5,4},{6,7},{7,6},{8,9},{9,8},{10,11... | collective-permute-start | bytes 4718600 | tf_op jit(solution)/shard_map/ppermute | solution.py:439
  341.8 13.5 %copy-start.3 = (bf16[2,1536,512]{2,1,0:T(8,128)(2,1)S(1)}, bf16[2,1536,512]{2,1,0:T(8,128)(2,1)}, u32[]{:S(2)}) copy-start(bf16[2,1536,512]{2,1,0:T(8,128)(2,1)} %get-tuple-element.53) | copy-start | bytes 9437188
  366.5 113.8 %collective-permute-start.7 = (bf16[1024,384]{1,0:T(8,128)(2,1)}, bf16[1024,384]{1,0:T(8,128)(2,1)S(1)}, u32[]{:S(2)}, u32[]{:S(2)}) collective-permute-start(bf16[1024,384]{1,0:T(8,128)(2,1)} %copy.38.second_ref), channel_id=1, source_target_pairs={{0,4},{4,0},{1,5},{5,1},{2,6},{6,2},{3,7},{7,3},{8,12},{12,8},{9,1... | collective-permute-start | bytes 2359304 | tf_op jit(solution)/shard_map/ppermute | solution.py:435
  478.9 16.6 %collective-permute-start.6 = (bf16[384,1024]{1,0:T(8,128)(2,1)}, bf16[384,1024]{1,0:T(8,128)(2,1)S(1)}, u32[]{:S(2)}, u32[]{:S(2)}) collective-permute-start(bf16[384,1024]{1,0:T(8,128)(2,1)} %reduce-scatter.5.cloned.1.call-done), channel_id=1, source_target_pairs={{0,4},{4,0},{1,5},{5,1},{2,6},{6,2},{3,7},{7,3},{8,12},{12,8},{9,1... | collective-permute-start | bytes 2359304 | tf_op jit(solution)/shard_map/ppermute | solution.py:435
  480.3 2.6 copy-start.4
  483.0 15.4 %copy-start = (bf16[1024,1536]{1,0:T(8,128)(2,1)S(1)}, bf16[1024,1536]{1,0:T(8,128)(2,1)}, u32[]{:S(2)}) copy-start(bf16[1024,1536]{1,0:T(8,128)(2,1)} %get-tuple-element.70) | copy-start | bytes 9437188
Sparse Core Ops, SparseCore 0:
  281.0 57.1 reduce-scatter.6
  359.4 57.5 reduce-scatter.4

commit v4 on v3

--- a/solution.py
+++ b/solution.py
@@ -428,7 +428,7 @@
 HALF = HD // 2
 SPAN = LANES // 2
 LOG2E = math.log2(math.e)
-VMEM_BYTES = 56 * 1024 * 1024
+VMEM_BYTES = 60 * 1024 * 1024
 
 
 def swap_ctx(block):
@@ -443,19 +443,9 @@
     return lax.ppermute(block, "tp", [(0, 2), (2, 0), (1, 3), (3, 1)])
 
 
-def paired_tensor_sum(term_rows):
-    half = term_rows.shape[0] // 2
-    core = lax.axis_index("tp") % 2
-    low = term_rows.astype(jnp.bfloat16)
-    keep = lax.dynamic_slice_in_dim(low, core * half, half, 0)
-    give = lax.dynamic_slice_in_dim(low, (1 - core) * half, half, 0)
-    chip_part = (keep.astype(jnp.float32) + swap_core(give).astype(jnp.float32)).astype(jnp.bfloat16)
-    total = (chip_part.astype(jnp.float32) + swap_chip(chip_part).astype(jnp.float32)).astype(
-        jnp.bfloat16
-    )
-    other = swap_core(total)
+def by_core(total, other):
     return jnp.where(
-        core == 0,
+        lax.axis_index("tp") % 2 == 0,
         jnp.concatenate([total, other], axis=0),
         jnp.concatenate([other, total], axis=0),
     )
@@ -482,6 +472,104 @@
 MESH = pl.DeviceIdType.MESH
 GAIN_ROWS = 16
 PREFIX_MOST = 1024
+
+
+def line_sum(z, planes, source, up_ref, down_ref, up_send, up_recv, down_send, down_recv):
+    f32 = jnp.float32
+
+    def up(d):
+        return pltpu.make_async_remote_copy(
+            src_ref=up_ref.at[d - 1],
+            dst_ref=up_ref.at[d - 1],
+            send_sem=up_send.at[d],
+            recv_sem=up_recv.at[d],
+            device_id={"fsdp": z + 1},
+            device_id_type=MESH,
+        )
+
+    def down(d):
+        return pltpu.make_async_remote_copy(
+            src_ref=down_ref.at[d],
+            dst_ref=down_ref.at[d],
+            send_sem=down_send.at[d],
+            recv_sem=down_recv.at[d],
+            device_id={"fsdp": z - 1},
+            device_id_type=MESH,
+        )
+
+    def begin(k):
+        high, low = planes - 1 - k, k
+
+        @pl.when(z == 0)
+        def _():
+            up_ref[high - 1] = source(high)
+            up(high).start()
+
+        @pl.when(z == planes - 1)
+        def _():
+            down_ref[low] = source(low)
+            down(low).start()
+
+    def relay(k):
+        high, low = planes - 1 - k, k
+
+        def pass_up():
+            @pl.when((z > 0) & (z < high))
+            def _():
+                up(high).wait_recv()
+                up_ref[high - 1] = (
+                    up_ref[high - 1].astype(f32) + source(high).astype(f32)
+                ).astype(up_ref.dtype)
+                up(high).start()
+
+        def pass_down():
+            @pl.when((z < planes - 1) & (z > low))
+            def _():
+                down(low).wait_recv()
+                down_ref[low] = (
+                    down_ref[low].astype(f32) + source(low).astype(f32)
+                ).astype(down_ref.dtype)
+                down(low).start()
+
+        @pl.when(2 * z < planes)
+        def _():
+            pass_up()
+            pass_down()
+
+        @pl.when(2 * z >= planes)
+        def _():
+            pass_down()
+            pass_up()
+
+    def finish(out_ref):
+        out_ref[...] = source(z)
+
+        @pl.when(z > 0)
+        def _():
+            up(z).wait_recv()
+            out_ref[...] = (
+                out_ref[...].astype(f32) + up_ref[pl.ds(z - 1, 1)][0].astype(f32)
+            ).astype(out_ref.dtype)
+
+        @pl.when(z < planes - 1)
+        def _():
+            down(z).wait_recv()
+            out_ref[...] = (
+                out_ref[...].astype(f32) + down_ref[pl.ds(z, 1)][0].astype(f32)
+            ).astype(out_ref.dtype)
+
+    def sent():
+        for d in range(planes):
+
+            @pl.when(z < d)
+            def _():
+                up(d).wait_send()
+
+            @pl.when(z > d)
+            def _():
+                down(d).wait_send()
+
+    return begin, relay, finish, sent
 
 
 def front_kernel(
@@ -546,6 +634,7 @@
     matrix_rows = rest_ref.shape[0]
     heads_half = project_ref.shape[0] // 2
     units = gate_ref.shape[2]
+    direct = units // 2
     z = lax.axis_index("fsdp")
     c = lax.axis_index("ctx")
     t = lax.axis_index("tp")
@@ -627,6 +716,8 @@
             return w_up_ref.at[:, pl.ds(pl.multiple_of(half * units, units), units)]
         if m == 2:
             return w_down_ref.at[pl.ds(pl.multiple_of(half * units, units), units), :]
+        if m == 4:
+            return w_down_ref.at[pl.ds(pl.multiple_of((1 - half) * units, units), direct), :]
         return w_project_ref.at[pl.ds(half * heads_half, heads_half)]
 
     def slot(m, which, piece):
@@ -637,6 +728,8 @@
             return up_ref.at[which, at]
         if m == 2:
             return down_ref.at[which, :, at]
+        if m == 4:
+            return down_ref.at[1, pl.ds(0, direct), at]
         return project_ref.at[pl.ds(which * heads_half, heads_half), pl.ds(0, HD), at]
 
     def m_up(m, k):
@@ -663,15 +756,19 @@
 
     def m_side(m, side, k):
         piece = z - k if side == 0 else z + k
+        src, dst = slot(m, 0, piece), slot(m, 1, piece)
+        if m == 2:
+            left = pl.ds(direct, units - direct)
+            src, dst = src.at[left], dst.at[left]
         return remote(
-            slot(m, 0, piece),
-            slot(m, 1, piece),
+            src,
+            dst,
             m_x_send.at[m, side, k],
             m_x_recv.at[m, side, k],
             across,
         )
 
-    groups = ((3, 0), (1,), (2,))
+    groups = ((3,), (0,), (1,), (2, 4))
 
     def relay(group, k):
         for m in groups[group]:
@@ -694,8 +791,21 @@
                     def _():
                         m_down(m, k).start()
 
+    def launch(group):
+        for m in groups[group]:
+
+            @pl.when(has_above)
+            def _():
+                m_up(m, 0).start()
+
+            @pl.when(has_below)
+            def _():
+                m_down(m, 0).start()
+
     def cross(group, k):
         for m in groups[group]:
+            if m == 4:
+                continue
 
             @pl.when(z - k >= 0)
             def _():
@@ -772,15 +882,8 @@
             sideways(1, k).start()
 
         if k == max(1, planes - 2):
-            for m in (3, 0, 1, 2):
-
-                @pl.when(has_above)
-                def _():
-                    m_up(m, 0).start()
-
-                @pl.when(has_below)
-                def _():
-                    m_down(m, 0).start()
+            launch(0)
+            launch(1)
 
         @pl.when(below)
         def _():
@@ -792,6 +895,8 @@
             place(buf_ref.at[z + k, 0], z + k, 0)
             place_gain(buf_ref.at[z + k, 0], z + k)
 
+    relay(0, 1)
+    cross(0, 1)
     tile = 128
     gain = gain_ref[0:1, :].astype(f32)
 
@@ -803,6 +908,9 @@
         return carry
 
     lax.fori_loop(0, rows // tile, norm_rows, 0)
+    relay(0, 2)
+    cross(0, 2)
+    launch(2)
 
     for k in range(1, planes):
 
@@ -843,7 +951,10 @@
 
     for slab in range(4):
         exchange(slab).start()
-    relay(0, 1)
+    relay(0, 3)
+    cross(0, 3)
+    relay(1, 1)
+    launch(3)
     scale = HD ** (-0.5) * LOG2E
 
     def query_rows(i, carry):
@@ -858,7 +969,6 @@
         return carry
 
     lax.fori_loop(0, rows // block, query_rows, 0)
-    relay(1, 1)
 
     tiles = rows // block
     tiles_of_block = tiles // 2
@@ -929,15 +1039,14 @@
     attend_group(0, False)
     relay(2, 1)
     attend_group(1, False)
-    relay(0, 2)
+    relay(3, 1)
     for slab in range(4):
         exchange(slab).wait_recv()
-    cross(0, 1)
     cross(1, 1)
     cross(2, 1)
+    cross(3, 1)
     attend_group(0, True)
     relay(1, 2)
-    cross(0, 2)
     cross(1, 2)
     attend_group(1, True)
     relay(2, 2)
@@ -947,8 +1056,6 @@
     half_rows = rows // 2
     give_start = (1 - core) * half_rows
     keep_start = core * half_rows
-    relay(0, 3)
-    cross(0, 3)
     for which in range(2):
         local(3, which).wait()
     for k in range(1, planes):
@@ -986,26 +1093,26 @@
         total_ref[at, :] = (keep_ref[i].astype(f32) + chip_in_ref[i].astype(f32)).astype(bf16)
         back(i, keep_start).start()
 
-    relay(1, 3)
-    cross(1, 3)
-    finish_chunk(0)
-    relay(2, 3)
-    cross(2, 3)
-    for i in range(1, chunks):
+    relay(3, 2)
+    cross(3, 2)
+    for i in range(chunks):
         finish_chunk(i)
+        if i < planes - 1:
+            relay(i + 1, planes - 1)
+            cross(i + 1, planes - 1)
 
     for k in range(planes - 1):
 
         @pl.when((z - k >= 0) & has_above)
         def _():
             up(k).wait_send()
-            for m in range(4):
+            for m in range(5):
                 m_up(m, k).wait_send()
 
         @pl.when((z + k <= planes - 1) & has_below)
         def _():
             down(k).wait_send()
-            for m in range(4):
+            for m in range(5):
                 m_down(m, k).wait_send()
 
     for k in range(1, planes):
@@ -1083,7 +1190,7 @@
         + [dma((planes - 1,))] * 4
         + [dma((2, planes))] * 2
         + [dma((4,))] * 2
-        + [dma((4, planes - 1))] * 4
+        + [dma((5, planes - 1))] * 4
         + [dma((4, 2, planes))] * 2
         + [dma((4, 2))]
         + [dma((chunks,))] * 6,
@@ -1101,6 +1208,8 @@
     final,
     meta_ref,
     carry_ref,
+    first_ref,
+    second_ref,
     q_ref,
     k_ref,
     v_ref,
@@ -1110,10 +1219,11 @@
     cos_ref,
     sin_ref,
     dq_ref,
-    dk_ref,
-    dv_ref,
+    dkv_ref,
     delta_ref,
     acc_ref,
+    dk_acc_ref,
+    dv_acc_ref,
 ):
     query_tiles = lse_ref.shape[1]
     tile = q_ref.shape[0] // query_tiles
@@ -1139,35 +1249,39 @@
     keys = k_ref[0]
     values = v_ref[0]
 
+    dk_acc_ref[...] = jnp.zeros_like(dk_acc_ref)
+    dv_acc_ref[...] = jnp.zeros_like(dv_acc_ref)
+
     def one(i, carry):
         q_start = meta_ref[1 + i]
         prefix, whole, nothing = block_kinds(meta_ref, tile, key_tile, q_start, k_start)
 
-        def some(state):
-            dk, dv = state
+        def some(masked):
             queries = stacked(q_ref, i)
             d_out = stacked(do_ref, i)
             scores = dot(keys, queries, ((1,), (1,)))
-            scores = lax.cond(
-                whole,
-                lambda s: s,
-                lambda s: mask_scores(s, prefix, q_start, k_start, tile),
-                scores,
-            )
+            if masked:
+                scores = mask_scores(scores, prefix, q_start, k_start, tile)
             weights = jnp.exp2(scores - lse_ref[0, i])
             d_weights = dot(values, d_out, ((1,), (1,)))
             d_scores = (weights * (d_weights - delta_ref[i])).astype(jnp.bfloat16)
-            dv = dv + dot(weights.astype(jnp.bfloat16), d_out, ((1,), (0,)))
-            dk = dk + dot(d_scores, queries, ((1,), (0,)))
+            dv_acc_ref[...] += dot(weights.astype(jnp.bfloat16), d_out, ((1,), (0,)))
+            dk_acc_ref[...] += dot(d_scores, queries, ((1,), (0,)))
             acc_ref[i] += dot(keys, d_scores, ((0,), (0,)))
-            return dk, dv
-
-        return lax.cond(nothing, lambda state: state, some, carry)
-
-    zero = jnp.zeros((key_tile, LANES), jnp.float32)
-    dk, dv = lax.fori_loop(0, query_tiles, one, (zero, zero))
-    dk_ref[0] = (dk * (1.0 / LOG2E)).astype(jnp.bfloat16)
-    dv_ref[0] = dv.astype(jnp.bfloat16)
+
+        @pl.when(whole)
+        def _():
+            some(False)
+
+        @pl.when(jnp.logical_not(whole | nothing))
+        def _():
+            some(True)
+
+        return carry
+
+    lax.fori_loop(0, query_tiles, one, 0)
+    dkv_ref[0, 0] = (dk_acc_ref[...] * (1.0 / LOG2E)).astype(jnp.bfloat16)
+    dkv_ref[0, 1] = dv_acc_ref[...].astype(jnp.bfloat16)
 
     @pl.when(j == pl.num_programs(1) - 1)
     def _():
@@ -1188,7 +1302,7 @@
         lax.fori_loop(0, query_tiles, one_out, 0)
 
 
-def attend_back(meta, carry, q, kv, away, o, d_out, lse, cosine, sine, tile):
+def attend_back(meta, carry, first, second, q, kv, away, o, d_out, lse, cosine, sine, tile):
     rows, q_width = q.shape
     keys = kv.shape[1] // 2
     groups = q_width // (2 * LANES)
@@ -1210,6 +1324,8 @@
             grid=(groups, key_tiles),
             in_specs=[
                 carry_block,
+                pl.BlockSpec(memory_space=pl.ANY),
+                pl.BlockSpec(memory_space=pl.ANY),
                 whole_q,
                 pl.BlockSpec((1, tile, LANES), lambda g, j, m: (g, skip + j, 0)),
                 pl.BlockSpec((1, tile, LANES), lambda g, j, m: (groups + g, skip + j, 0)),
@@ -1221,25 +1337,25 @@
             ],
             out_specs=[
                 acc_block if away else whole_q,
-                pl.BlockSpec((1, tile, LANES), lambda g, j, m: (g, j, 0)),
-                pl.BlockSpec((1, tile, LANES), lambda g, j, m: (g, j, 0)),
+                pl.BlockSpec((1, 2, tile, LANES), lambda g, j, m: (g, 0, j, 0)),
             ],
             scratch_shapes=[
                 pltpu.VMEM((query_tiles, 1, 2 * tile), jnp.float32),
                 pltpu.VMEM((query_tiles, LANES, 2 * tile), jnp.float32),
+                pltpu.VMEM((tile, LANES), jnp.float32),
+                pltpu.VMEM((tile, LANES), jnp.float32),
             ],
         ),
         out_shape=[
             acc_shape if away else jax.ShapeDtypeStruct((rows, q_width), jnp.bfloat16),
-            jax.ShapeDtypeStruct((groups, keys, LANES), jnp.bfloat16),
-            jax.ShapeDtypeStruct((groups, keys, LANES), jnp.bfloat16),
+            jax.ShapeDtypeStruct((groups, 2, keys, LANES), jnp.bfloat16),
         ],
         compiler_params=pltpu.CompilerParams(vmem_limit_bytes=VMEM_BYTES),
         cost_estimate=pl.CostEstimate(
             flops=20 * rows * keys * LANES * groups * 2, bytes_accessed=8_000_000, transcendentals=0
         ),
         name="attend_back_away" if away else "attend_back_own",
-    )(meta, carry, q, kv, kv, o, d_out, lse, cosine, sine)
+    )(meta, carry, first, second, q, kv, kv, o, d_out, lse, cosine, sine)
 
 
 def middle_back_kernel(
@@ -1248,13 +1364,10 @@
     feed_ref,
     cot_ref,
     gain_ref,
-    hidden_ref,
-    down_w_ref,
     o_ref,
     wp_ref,
     grad_ref,
     d_out_ref,
-    down_ref,
     wp_grad_ref,
     gain_grad_ref,
     acc_ref,
@@ -1282,11 +1395,6 @@
     low = grad.astype(bf16)
     d_out_ref[...] = dot(low, wp_ref[...], ((1,), (1,))).astype(bf16)
     acc_ref[...] += dot(o_ref[...], low, ((0,), (0,)))
-    half = hidden_ref.shape[1] // 2
-    down_ref[...] = (
-        dot(hidden_ref[:, :half], down_w_ref[0], ((1,), (0,)))
-        + dot(hidden_ref[:, half:], down_w_ref[1], ((1,), (0,)))
-    ).astype(bf16)
 
     @pl.when(step == last)
     def _():
@@ -1296,10 +1404,9 @@
             ].astype(bf16)
 
 
-def middle_back(x, project_sum, feed_sum, cot, gains, hidden, down_w, o, w_p):
+def middle_back(x, project_sum, feed_sum, cot, gains, o, w_p):
     rows, width = x.shape
     tile = 256
-    units = hidden.shape[1]
     heads = o.shape[1] // LANES
     bf16, f32 = jnp.bfloat16, jnp.float32
 
@@ -1318,62 +1425,79 @@
             rows_of(width),
             rows_of(width),
             whole(gains),
-            rows_of(units),
-            pl.BlockSpec(down_w.shape, lambda i: (0, 0, 0)),
             rows_of(o.shape[1]),
             whole(w_p),
         ],
         out_specs=[
             rows_of(width),
             rows_of(o.shape[1]),
-            rows_of(width),
             pl.BlockSpec((heads * HD, width), lambda i: (0, 0)),
             pl.BlockSpec((1, width), lambda i: (0, 0)),
         ],
         out_shape=[
             jax.ShapeDtypeStruct((rows, width), f32),
             jax.ShapeDtypeStruct(o.shape, bf16),
-            jax.ShapeDtypeStruct((rows, width), bf16),
             jax.ShapeDtypeStruct((heads * HD, width), bf16),
             jax.ShapeDtypeStruct((1, width), f32),
         ],
         scratch_shapes=[pltpu.VMEM((o.shape[1], width), f32)],
         compiler_params=pltpu.CompilerParams(vmem_limit_bytes=VMEM_BYTES),
         cost_estimate=pl.CostEstimate(
-            flops=8_000_000_000, bytes_accessed=30_000_000, transcendentals=0
+            flops=5_000_000_000, bytes_accessed=26_000_000, transcendentals=0
         ),
         name="middle_back",
-    )(x, project_sum, feed_sum, cot, gains, hidden, down_w, o, w_p)
+    )(x, project_sum, feed_sum, cot, gains, o, w_p)
 
 
 def tail_kernel(
     first_ref,
-    second_ref,
+    gate_hbm,
+    gate_away_hbm,
+    gate_rest_hbm,
+    up_hbm,
+    up_away_hbm,
     q_low_ref,
     own_ref,
     away_ref,
-    normed_ref,
-    wide_ref,
-    x_ref,
-    grad_ref,
+    normed_hbm,
+    wide_hbm,
+    x_hbm,
+    grad_hbm,
     gain_term_ref,
     gain_ref,
     project_ref,
     spread_ref,
     cos_ref,
     sin_ref,
-    out_ref,
+    out_hbm,
     share_ref,
+    project_share_ref,
+    gate_share_ref,
+    up_share_ref,
     gain_share_ref,
+    normed_ref,
+    wide_ref,
+    x_ref,
+    grad_ref,
+    gate_ref,
+    gate_away_ref,
+    upw_ref,
+    upw_away_ref,
     low_ref,
     close_ref,
     part_ref,
     x_in_ref,
     up_ref,
     down_ref,
+    p_in_ref,
+    p_up_ref,
+    p_down_ref,
+    g_up_ref,
+    g_down_ref,
+    u_up_ref,
+    u_down_ref,
     give_ref,
     core_in_ref,
-    keep_ref,
     chip_in_ref,
     total_ref,
     gain_sum_ref,
@@ -1385,6 +1509,18 @@
     up_recv,
     down_send,
     down_recv,
+    p_up_send,
+    p_up_recv,
+    p_down_send,
+    p_down_recv,
+    g_up_send,
+    g_up_recv,
+    g_down_send,
+    g_down_recv,
+    u_up_send,
+    u_up_recv,
+    u_down_send,
+    u_down_recv,
     core_send,
     core_recv,
     chip_send,
@@ -1395,12 +1531,31 @@
     last_recv,
     gain_send,
     gain_recv,
+    load_sem,
 ):
     bf16, f32 = jnp.bfloat16, jnp.float32
     planes = part_ref.shape[1]
     rows, width = x_ref.shape
     depth = width // planes
-    project_rows = project_ref.shape[0] // 2
+    sent_rows = gate_away_hbm.shape[0]
+    loads = [
+        pltpu.make_async_copy(src, dst, load_sem.at[i])
+        for i, (src, dst) in enumerate(
+            (
+                (gate_hbm, gate_ref),
+                (gate_away_hbm, gate_away_ref.at[pl.ds(0, sent_rows)]),
+                (gate_rest_hbm, gate_away_ref.at[pl.ds(sent_rows, width - sent_rows)]),
+                (up_hbm, upw_ref),
+                (up_away_hbm, upw_away_ref),
+                (normed_hbm, normed_ref),
+                (wide_hbm, wide_ref),
+                (x_hbm, x_ref),
+                (grad_hbm, grad_ref),
+            )
+        )
+    ]
+    for load in loads:
+        load.start()
     half_rows = rows // 2
     chunks = give_ref.shape[0]
     chunk = half_rows // chunks
@@ -1412,8 +1567,6 @@
     across = {"ctx": 1 - c}
     sibling = {"tp": t + 1 - 2 * core}
     partner = {"tp": lax.rem(t + 2, 4)}
-    has_above = z < planes - 1
-    has_below = z > 0
 
     barrier = pltpu.get_barrier_semaphore()
     for device in (across, sibling, partner):
@@ -1434,6 +1587,54 @@
             device_id_type=MESH,
         )
 
+    def plane_rows(d):
+        return pl.ds(pl.multiple_of(d * depth, depth), depth)
+
+    def pair_source(mine_ref, away_ref):
+        def source(d):
+            at = plane_rows(d)
+            return (mine_ref[at, :].astype(f32) + away_ref[at, :].astype(f32)).astype(bf16)
+
+        return source
+
+    g_begin, g_relay, g_finish, g_sent = line_sum(
+        z, planes, pair_source(gate_ref, gate_away_ref),
+        g_up_ref, g_down_ref, g_up_send, g_up_recv, g_down_send, g_down_recv,
+    )
+    u_begin, u_relay, u_finish, u_sent = line_sum(
+        z, planes, pair_source(upw_ref, upw_away_ref),
+        u_up_ref, u_down_ref, u_up_send, u_up_recv, u_down_send, u_down_recv,
+    )
+
+    project_half = project_ref.shape[0] // 2
+
+    def project_over():
+        return remote(
+            project_ref.at[pl.ds(project_half, project_half)], p_in_ref,
+            last_send.at[2], last_recv.at[2], across,
+        )
+
+    def project_source(d):
+        at = plane_rows(d)
+        return (
+            project_ref[0:project_half, at].astype(f32) + p_in_ref[:, at].astype(f32)
+        ).astype(bf16)
+
+    p_begin, p_relay, p_finish, p_sent = line_sum(
+        z, planes, project_source, p_up_ref, p_down_ref, p_up_send, p_up_recv, p_down_send, p_down_recv
+    )
+    order = []
+    for step in range((planes + 1) // 2):
+        order += [planes - 1 - step, step]
+    order = order[:planes]
+    project_over().start()
+    for load in loads[:3]:
+        load.wait()
+    g_begin(0)
+    for load in loads[3:5]:
+        load.wait()
+    u_begin(0)
+
     block = 256
 
     def lower(i, carry):
@@ -1442,10 +1643,10 @@
             low_ref[which, at, : 2 * LANES] = q_low_ref[
                 at, which * 2 * LANES : (which + 1) * 2 * LANES
             ]
-            key = own_ref[which, at, :].astype(f32) + away_ref[1 - which, at, :].astype(f32)
+            key = own_ref[which, 0, at, :].astype(f32) + away_ref[1 - which, 0, at, :].astype(f32)
             key = key * cos_ref[at, :] - pltpu.roll(key, SPAN, 1) * sin_ref[at, :]
             low_ref[which, at, 2 * LANES : 3 * LANES] = key.astype(bf16)
-            value = own_ref[2 + which, at, :].astype(f32) + away_ref[3 - which, at, :].astype(f32)
+            value = own_ref[which, 1, at, :].astype(f32) + away_ref[1 - which, 1, at, :].astype(f32)
             low_ref[which, at, 3 * LANES :] = value.astype(bf16)
             close_ref[which, at, :] = dot(
                 low_ref[which, at, :], spread_ref[...], ((1,), (1,))
@@ -1454,23 +1655,15 @@
 
     lax.fori_loop(0, rows // block, lower, 0)
 
-    order = []
-    for k in range((planes + 1) // 2):
-        order += [planes - 1 - k, k]
-    order = order[:planes]
-
     def weight_part(which, d):
-        at = slice(d * depth, (d + 1) * depth)
-        part_ref[which, d, :depth] = dot(
-            normed_ref[:, at], close_ref[which], ((0,), (0,))
+        part_ref[which, d] = dot(
+            normed_ref[:, d * depth : (d + 1) * depth], close_ref[which], ((0,), (0,))
         ).astype(bf16)
-        part_ref[which, d, depth:] = project_ref[
-            which * project_rows : (which + 1) * project_rows, at
-        ]
 
     def to_neighbour(d):
         return remote(part_ref.at[1, d], x_in_ref.at[d], x_send.at[d], x_recv.at[d], across)
 
+    loads[5].wait()
     for d in order:
         weight_part(1, d)
         to_neighbour(d).start()
@@ -1481,6 +1674,7 @@
             low_ref[1, at, :], wide_ref[:, half_width:], ((1,), (1,))
         )
 
+    loads[6].wait()
     give_start = (1 - core) * half_rows
     keep_start = core * half_rows
 
@@ -1488,7 +1682,7 @@
         return remote(give_ref.at[i], core_in_ref.at[i], core_send.at[i], core_recv.at[i], sibling)
 
     def to_chip(i):
-        return remote(keep_ref.at[i], chip_in_ref.at[i], chip_send.at[i], chip_recv.at[i], partner)
+        return remote(total_ref.at[keep_at(i)], chip_in_ref.at[i], chip_send.at[i], chip_recv.at[i], partner)
 
     def keep_at(i):
         return pl.ds(pl.multiple_of(keep_start + i * chunk, chunk), chunk)
@@ -1520,9 +1714,13 @@
     for i in range(chunks):
         kept = feature_rows(keep_start + i * chunk)
         to_core(i).wait_recv()
-        keep_ref[i] = (kept + core_in_ref[i].astype(f32)).astype(bf16)
+        total_ref[keep_at(i)] = (kept + core_in_ref[i].astype(f32)).astype(bf16)
         to_chip(i).start()
 
+    g_begin(1)
+    g_relay(0)
+    u_begin(1)
+    u_relay(0)
     for d in order:
         weight_part(0, d)
 
@@ -1530,45 +1728,15 @@
         to_neighbour(d).wait_recv()
         part_ref[0, d] = (part_ref[0, d].astype(f32) + x_in_ref[d].astype(f32)).astype(bf16)
 
-    def up(d):
-        return remote(up_ref.at[d], up_ref.at[d], up_send.at[d], up_recv.at[d], {"fsdp": z + 1})
-
-    def down(d):
-        return remote(
-            down_ref.at[d], down_ref.at[d], down_send.at[d], down_recv.at[d], {"fsdp": z - 1}
-        )
-
-    def upward(d):
-        @pl.when(z == 0)
-        def _():
-            up_ref[d] = part_ref[0, d]
-
-        @pl.when((z > 0) & (z < d))
-        def _():
-            up(d).wait_recv()
-            up_ref[d] = (up_ref[d].astype(f32) + part_ref[0, d].astype(f32)).astype(bf16)
-
-        @pl.when(z < d)
-        def _():
-            up(d).start()
-
-    def downward(d):
-        @pl.when(z == planes - 1)
-        def _():
-            down_ref[d] = part_ref[0, d]
-
-        @pl.when((z < planes - 1) & (z > d))
-        def _():
-            down(d).wait_recv()
-            down_ref[d] = (down_ref[d].astype(f32) + part_ref[0, d].astype(f32)).astype(bf16)
-
-        @pl.when(z > d)
-        def _():
-            down(d).start()
+    q_begin, q_relay, q_finish, q_sent = line_sum(
+        z, planes, lambda d: part_ref[0, pl.ds(d, 1)][0], up_ref, down_ref, up_send, up_recv, down_send, down_recv
+    )
 
     def finish_chunk(i):
-        to_chip(i).wait_recv()
-        total_ref[keep_at(i)] = (keep_ref[i].astype(f32) + chip_in_ref[i].astype(f32)).astype(bf16)
+        to_chip(i).wait()
+        total_ref[keep_at(i)] = (
+            total_ref[keep_at(i)].astype(f32) + chip_in_ref[i].astype(f32)
+        ).astype(bf16)
         back(i).start()
 
     def last_share():
@@ -1576,40 +1744,36 @@
             share_ref.at[0], share_ref.at[1], last_send.at[0], last_recv.at[0], across
         )
 
-    added = set()
-
-    def line_step(k):
-        for d in (planes - 1 - k, k):
-            if d not in added:
-                added.add(d)
-                add_neighbour(d)
-        upward(planes - 1 - k)
-        downward(k)
-
-    per_step = -(-chunks // planes)
-    done = 0
-    for k in range(planes - 1):
-        line_step(k)
-        for i in range(done, min(chunks, done + per_step)):
-            finish_chunk(i)
-        done = min(chunks, done + per_step)
-
-    own = part_ref[0, pl.ds(z, 1)][0].astype(f32)
-    share_ref[0] = own.astype(bf16)
-
-    @pl.when(has_below)
-    def _():
-        up(z).wait_recv()
-        share_ref[0] = (share_ref[0].astype(f32) + up_ref[pl.ds(z, 1)][0].astype(f32)).astype(bf16)
-
-    @pl.when(has_above)
-    def _():
-        down(z).wait_recv()
-        share_ref[0] = (share_ref[0].astype(f32) + down_ref[pl.ds(z, 1)][0].astype(f32)).astype(bf16)
-
-    last_share().start()
-    for i in range(done, chunks):
+    def last_project():
+        return remote(
+            project_share_ref.at[0], project_share_ref.at[1], last_send.at[1], last_recv.at[1], across
+        )
+
+    def last_of(ref, i):
+        return remote(ref.at[0], ref.at[1], last_send.at[i], last_recv.at[i], across)
+
+    g_begin(2)
+    u_begin(2)
+    g_relay(1)
+    finish_chunk(0)
+    u_relay(1)
+    project_over().wait_recv()
+    for step in range(planes - 1):
+        p_begin(step)
+    for d in order:
+        add_neighbour(d)
+    for step in range(planes - 1):
+        q_begin(step)
+    for i in range(1, chunks):
         finish_chunk(i)
+    g_finish(gate_share_ref.at[0])
+    last_of(gate_share_ref, 3).start()
+    p_relay(0)
+    u_finish(up_share_ref.at[0])
+    last_of(up_share_ref, 4).start()
+    q_relay(0)
+    for load in loads[7:]:
+        load.wait()
 
     gain_sum_ref[...] = jnp.zeros_like(gain_sum_ref)
     gain_sum_ref[1:2, :] = gain_term_ref[...]
@@ -1622,7 +1786,7 @@
         normed_in = total_ref[at, :].astype(f32)
         gain_sum_ref[0:1, :] += jnp.sum(normed_in * x * factor, axis=0, keepdims=True)
         scaled = gain * normed_in
-        out_ref[at, :] = (
+        x_ref[at, :] = (
             grad_ref[at, :]
             + factor * scaled
             - x * (factor * factor * factor * jnp.mean(scaled * x, axis=-1, keepdims=True))
@@ -1630,9 +1794,17 @@
 
     for i in range(chunks):
         finish_rows(keep_start + i * chunk)
+    p_relay(1)
+    q_relay(1)
     for i in range(chunks):
         from_core(i).wait_recv()
         finish_rows(give_start + i * chunk)
+    p_finish(project_share_ref.at[0])
+    last_project().start()
+    q_finish(share_ref.at[0])
+    last_share().start()
+    out_copy = pltpu.make_async_copy(x_ref, out_hbm, load_sem.at[0])
+    out_copy.start()
 
     gain_over = remote(gain_sum_ref, gain_x_ref, gain_send.at[0], gain_recv.at[0], across)
     gain_over.start()
@@ -1657,60 +1829,81 @@
         gain_share_ref[...] += gain_z_ref[k]
 
     last_share().wait()
+    last_project().wait()
+    last_of(gate_share_ref, 3).wait()
+    last_of(up_share_ref, 4).wait()
+    project_over().wait_send()
+    p_sent()
+    g_sent()
+    u_sent()
+    q_sent()
+    out_copy.wait()
     for k in range(1, planes):
         gain_to(k).wait_send()
     for i in range(chunks):
         to_core(i).wait_send()
-        to_chip(i).wait_send()
         back(i).wait_send()
     for d in range(planes):
         to_neighbour(d).wait_send()
 
-        @pl.when(z < d)
-        def _():
-            up(d).wait_send()
-
-        @pl.when(z > d)
-        def _():
-            down(d).wait_send()
-
 
 def tail(
-    first, second, q_low, own, away, normed, wide, x, grad, gain_term, gains, project,
-    spread, cosine, sine, planes,
+    first, gate, gate_away, gate_rest, upw, up_away, q_low, own, away, normed, wide, x, grad,
+    gain_term, gains, project, spread, cosine, sine, planes,
 ):
     rows, width = x.shape
     depth = width // planes
     half_width = wide.shape[1] // 2
     close_width = spread.shape[0]
-    chunks = 4
+    chunks = 2
     chunk = rows // 2 // chunks
     bf16, f32 = jnp.bfloat16, jnp.float32
     vmem = pl.BlockSpec(memory_space=pltpu.VMEM)
     dma = pltpu.SemaphoreType.DMA
     operands = (
-        first, second, q_low, own, away, normed, wide, x, grad, gain_term, gains, project,
-        spread, cosine, sine,
-    )
+        first, gate, gate_away, gate_rest, upw, up_away, q_low, own, away, normed, wide, x, grad,
+        gain_term, gains, project, spread, cosine, sine,
+    )
+    units = gate.shape[1]
+    unit_line = pltpu.VMEM((planes - 1, depth, units), bf16)
     anywhere = pl.BlockSpec(memory_space=pl.ANY)
-    piece_rows = depth + project.shape[0] // 2
+    line = pltpu.VMEM((planes, depth, close_width), bf16)
+    short_line = pltpu.VMEM((planes - 1, depth, close_width), bf16)
+    project_line = pltpu.VMEM((planes - 1, project.shape[0] // 2, depth), bf16)
     return pl.pallas_call(
         tail_kernel,
-        in_specs=[anywhere] * 2 + [vmem] * (len(operands) - 2),
-        out_specs=[vmem] * 3,
+        in_specs=[anywhere] * 6 + [vmem] * 3 + [anywhere] * 4 + [vmem] * (len(operands) - 13),
+        out_specs=[anywhere] + [vmem] * 5,
         out_shape=[
             jax.ShapeDtypeStruct((rows, width), bf16),
-            jax.ShapeDtypeStruct((2, piece_rows, close_width), bf16),
+            jax.ShapeDtypeStruct((2, depth, close_width), bf16),
+            jax.ShapeDtypeStruct((2, project.shape[0] // 2, depth), bf16),
+            jax.ShapeDtypeStruct((2, depth, units), bf16),
+            jax.ShapeDtypeStruct((2, depth, units), bf16),
             jax.ShapeDtypeStruct((8, depth), f32),
         ],
         scratch_shapes=[
+            pltpu.VMEM((rows, width), bf16),
+            pltpu.VMEM(wide.shape, bf16),
+            pltpu.VMEM((rows, width), bf16),
+            pltpu.VMEM((rows, width), f32),
+            pltpu.VMEM((width, units), bf16),
+            pltpu.VMEM((width, units), bf16),
+            pltpu.VMEM((width, units), bf16),
+            pltpu.VMEM((width, units), bf16),
             pltpu.VMEM((2, rows, half_width), bf16),
             pltpu.VMEM((2, rows, close_width), bf16),
-            pltpu.VMEM((2, planes, piece_rows, close_width), bf16),
-            pltpu.VMEM((planes, piece_rows, close_width), bf16),
-            pltpu.VMEM((planes, piece_rows, close_width), bf16),
-            pltpu.VMEM((planes, piece_rows, close_width), bf16),
-            pltpu.VMEM((chunks, chunk, width), bf16),
+            pltpu.VMEM((2, planes, depth, close_width), bf16),
+            line,
+            short_line,
+            short_line,
+            pltpu.VMEM((project.shape[0] // 2, width), bf16),
+            project_line,
+            project_line,
+            unit_line,
+            unit_line,
+            unit_line,
+            unit_line,
             pltpu.VMEM((chunks, chunk, width), bf16),
             pltpu.VMEM((chunks, chunk, width), bf16),
             pltpu.VMEM((chunks, chunk, width), bf16),
@@ -1718,25 +1911,14 @@
             pltpu.VMEM((8, width), f32),
             pltpu.VMEM((8, width), f32),
             pltpu.VMEM((planes, 8, depth), f32),
-            dma((planes,)),
-            dma((planes,)),
-            dma((planes,)),
-            dma((planes,)),
-            dma((planes,)),
-            dma((planes,)),
-            dma((chunks,)),
-            dma((chunks,)),
-            dma((chunks,)),
-            dma((chunks,)),
-            dma((chunks,)),
-            dma((chunks,)),
-            dma((1,)),
-            dma((1,)),
-            dma((planes,)),
-            dma((planes,)),
-        ],
+        ]
+        + [dma((planes,))] * 18
+        + [dma((chunks,))] * 6
+        + [dma((5,))] * 2
+        + [dma((planes,))] * 2
+        + [dma((9,))],
         compiler_params=pltpu.CompilerParams(
-            collective_id=2, has_side_effects=True, vmem_limit_bytes=VMEM_BYTES
+            collective_id=2, has_side_effects=True, vmem_limit_bytes=VMEM_BYTES + (3 << 19)
         ),
         cost_estimate=pl.CostEstimate(
             flops=60_000_000_000, bytes_accessed=24_000_000, transcendentals=0
@@ -1746,46 +1928,86 @@
 
 
 def feed_kernel(
+    x_hbm,
+    project_hbm,
+    cot_hbm,
+    gain_ref,
+    gate_hbm,
+    up_hbm,
+    down_hbm,
+    total_hbm,
+    gate_m_hbm,
+    gate_away_hbm,
+    gate_rest_hbm,
+    up_m_hbm,
+    up_o_hbm,
+    down_grad_hbm,
+    down_rows_hbm,
     x_ref,
     project_ref,
     cot_ref,
-    gain_ref,
     gate_ref,
     up_ref,
     down_ref,
     total_ref,
+    grad_ref,
+    down_grad_ref,
+    down_rows_ref,
+    gate_o_ref,
+    normed_ref,
+    turned_ref,
     hidden_ref,
-    gate_grad_ref,
-    up_grad_ref,
-    down_grad_ref,
-    normed_ref,
     gate_back_ref,
     up_back_ref,
     give_ref,
     core_in_ref,
     keep_ref,
     chip_in_ref,
+    load_sem,
+    store_sem,
     core_send,
     core_recv,
     chip_send,
     chip_recv,
     back_send,
     back_recv,
+    x_send,
+    x_recv,
+    over_send,
+    over_recv,
 ):
     bf16, f32 = jnp.bfloat16, jnp.float32
     rows, width = x_ref.shape
     half_rows = rows // 2
     chunks, chunk, _ = give_ref.shape
     units = gate_ref.shape[2]
+    c = lax.axis_index("ctx")
     t = lax.axis_index("tp")
     core = lax.rem(t, 2)
+    across = {"ctx": 1 - c}
     sibling = {"tp": t + 1 - 2 * core}
     partner = {"tp": lax.rem(t + 2, 4)}
 
+    loads = [
+        pltpu.make_async_copy(src, dst, load_sem.at[i])
+        for i, (src, dst) in enumerate(
+            (
+                (x_hbm, x_ref),
+                (project_hbm, project_ref),
+                (gate_hbm, gate_ref),
+                (up_hbm, up_ref),
+                (cot_hbm, cot_ref),
+                (down_hbm, down_ref),
+            )
+        )
+    ]
+    for load in loads:
+        load.start()
+
     barrier = pltpu.get_barrier_semaphore()
-    for device in (sibling, partner):
+    for device in (across, sibling, partner):
         pl.semaphore_signal(barrier, inc=1, device_id=device, device_id_type=MESH)
-    pl.semaphore_wait(barrier, 2)
+    pl.semaphore_wait(barrier, 3)
 
     def remote(src, dst, send, recv, device):
         return pltpu.make_async_remote_copy(
@@ -1800,18 +2022,25 @@
     give_start = (1 - core) * half_rows
     keep_start = core * half_rows
     gain = gain_ref[1:2, :].astype(f32)
-    halves = tuple((gate_ref.at[i], up_ref.at[i], down_ref.at[i]) for i in range(2))
-
-    def feature_rows(start):
+
+    def feature_rows(start, first):
         at = pl.ds(pl.multiple_of(start, chunk), chunk)
+        if first:
+            loads[0].wait()
+            loads[1].wait()
         middle = x_ref[at, :].astype(f32) + project_ref[at, :].astype(f32)
         factor = lax.rsqrt(jnp.mean(middle * middle, axis=-1, keepdims=True) + EPSILON)
-        normed_ref[at, :] = (middle * factor * gain).astype(bf16)
-        for which, (gate_w, up_w, down_w) in enumerate(halves):
+        normed = (middle * factor * gain).astype(bf16)
+        normed_ref[...] = normed
+        turned_ref[:, at] = normed.T
+        if first:
+            for load in loads[2:]:
+                load.wait()
+        for which in range(2):
             cols = slice(which * units, (which + 1) * units)
-            gate = dot(normed_ref[at, :], gate_w[...], ((1,), (0,)))
-            up = dot(normed_ref[at, :], up_w[...], ((1,), (0,)))
-            hidden_in = dot(cot_ref[at, :], down_w[...], ((1,), (1,)))
+            gate = dot(normed_ref[...], gate_ref[which], ((1,), (0,)))
+            up = dot(normed_ref[...], up_ref[which], ((1,), (0,)))
+            hidden_in = dot(cot_ref[at, :], down_ref[which], ((1,), (1,)))
             sigmoid = jax.nn.sigmoid(gate)
             silu = gate * sigmoid
             hidden_ref[at, cols] = (silu * up).astype(bf16)
@@ -1820,9 +2049,9 @@
             ).astype(bf16)
             up_back_ref[at, cols] = (hidden_in * silu).astype(bf16)
         return sum(
-            dot(back_ref[at, which * units : (which + 1) * units], weight[...], ((1,), (1,)))
-            for which, (gate_w, up_w, _) in enumerate(halves)
-            for back_ref, weight in ((gate_back_ref, gate_w), (up_back_ref, up_w))
+            dot(back_ref[at, which * units : (which + 1) * units], weight[which], ((1,), (1,)))
+            for which in range(2)
+            for back_ref, weight in ((gate_back_ref, gate_ref), (up_back_ref, up_ref))
         )
 
     def to_core(i):
@@ -1838,85 +2067,165 @@
         )
 
     for i in range(chunks):
-        give_ref[i] = feature_rows(give_start + i * chunk).astype(bf16)
+        give_ref[i] = feature_rows(give_start + i * chunk, i == 0).astype(bf16)
         to_core(i).start()
-        kept = feature_rows(keep_start + i * chunk)
+        kept = feature_rows(keep_start + i * chunk, False)
         to_core(i).wait_recv()
         keep_ref[i] = (kept + core_in_ref[i].astype(f32)).astype(bf16)
         to_chip(i).start()
 
     block = 256
 
-    def input_grads(back_ref, grad_ref):
+    def weight_rows(back_ref, which, out_ref, begin, count, block=256):
         def some(i, carry):
             at = pl.ds(pl.multiple_of(i * block, block), block)
-            for which in (1, 0):
-                grad_ref[which, at, :] = dot(
-                    normed_ref[:, at],
-                    back_ref[:, which * units : (which + 1) * units],
-                    ((0,), (0,)),
-                ).astype(bf16)
+            out_ref[at, :] = dot(
+                turned_ref[at, :], back_ref[:, which * units : (which + 1) * units], ((1,), (0,))
+            ).astype(bf16)
             return carry
 
-        lax.fori_loop(0, width // block, some, 0)
-
-    def down_grads(i, carry):
-        at = pl.ds(pl.multiple_of(i * block, block), block)
-        down_grad_ref[at, :] = dot(hidden_ref[:, at], cot_ref[...], ((0,), (0,))).astype(bf16)
-        return carry
+        lax.fori_loop(begin // block, (begin + count) // block, some, 0)
 
     def finish_chunk(i):
-        to_chip(i).wait_recv()
+        to_chip(i).wait()
         at = pl.ds(pl.multiple_of(keep_start + i * chunk, chunk), chunk)
         total_ref[at, :] = (keep_ref[i].astype(f32) + chip_in_ref[i].astype(f32)).astype(bf16)
         back(i, keep_start).start()
 
-    input_grads(gate_back_ref, gate_grad_ref)
+    planes, _, depth = down_grad_ref.shape
+    pieces = gate_away_hbm.shape[0] // depth
+
+    def over(i):
+        at = pl.ds(i * depth, depth)
+        return remote(gate_o_ref.at[at], gate_away_hbm.at[at], x_send.at[i], x_recv.at[i], across)
+
+    def down_over(i):
+        at = pl.ds(pl.multiple_of(give_start + i * chunk, chunk), chunk)
+        return remote(
+            down_rows_ref.at[at], core_in_ref.at[i], over_send.at[i], over_recv.at[i], sibling
+        )
+
+    stores = []
+
+    def store(src, dst):
+        copy = pltpu.make_async_copy(src, dst, store_sem.at[len(stores)])
+        copy.start()
+        stores.append(copy)
+
+    for i in range(pieces):
+        weight_rows(gate_back_ref, 1, gate_o_ref, i * depth, depth, depth)
+        over(i).start()
+    weight_rows(gate_back_ref, 1, gate_o_ref, pieces * depth, width - pieces * depth, depth)
+    store(gate_o_ref.at[pl.ds(pieces * depth, width - pieces * depth)], gate_rest_hbm)
+    weight_rows(up_back_ref, 1, grad_ref.at[0], 0, width)
+    store(grad_ref.at[0], up_o_hbm)
     for i in range(chunks // 2):
         finish_chunk(i)
-    input_grads(up_back_ref, up_grad_ref)
-    lax.fori_loop(0, down_grad_ref.shape[0] // block, down_grads, 0)
+    weight_rows(gate_back_ref, 0, grad_ref.at[1], 0, width)
+    store(grad_ref.at[1], gate_m_hbm)
+    weight_rows(up_back_ref, 0, grad_ref.at[2], 0, width)
+    store(grad_ref.at[2], up_m_hbm)
+
+    def down_grads(i, carry):
+        at = pl.ds(pl.multiple_of(i * block, block), block)
+        part = dot(hidden_ref[:, at], cot_ref[...], ((0,), (0,))).astype(bf16)
+        planes, _, depth = down_grad_ref.shape
+        for d in range(planes):
+            down_grad_ref[d, at, :] = part[:, d * depth : (d + 1) * depth]
+        return carry
+
+    lax.fori_loop(0, 2 * units // block, down_grads, 0)
+    store(down_grad_ref, down_grad_hbm)
+
+    def down_features(i, carry):
+        at = pl.ds(pl.multiple_of(i * block, block), block)
+        down_rows_ref[at, :] = (
+            dot(hidden_ref[at, :units], down_ref[0], ((1,), (0,)))
+            + dot(hidden_ref[at, units:], down_ref[1], ((1,), (0,)))
+        ).astype(bf16)
+        return carry
+
+    lax.fori_loop(0, rows // block, down_features, 0)
+    for i in range(chunks // 2):
+        back(i, give_start).wait_recv()
     for i in range(chunks // 2, chunks):
         finish_chunk(i)
+    for i in range(chunks // 2, chunks):
+        back(i, give_start).wait_recv()
+    store(total_ref, total_hbm)
+    for i in range(chunks):
+        down_over(i).start()
+    for i in range(chunks):
+        down_over(i).wait()
+        at = pl.ds(pl.multiple_of(keep_start + i * chunk, chunk), chunk)
+        keep_ref[i] = (down_rows_ref[at, :].astype(f32) + core_in_ref[i].astype(f32)).astype(bf16)
+    store(keep_ref, down_rows_hbm)
     for i in range(chunks):
         to_core(i).wait_send()
-        to_chip(i).wait_send()
         back(i, keep_start).wait_send()
-    for i in range(chunks):
-        back(i, give_start).wait_recv()
-
-
-def feed(x, project_sum, cot, gains, gate_w, up_w, down_w):
+    for i in range(pieces):
+        over(i).wait()
+    for copy in stores:
+        copy.wait()
+
+
+def feed(x, project_sum, cot, gains, gate_w, up_w, down_w, planes):
     rows, width = x.shape
     units = gate_w.shape[2]
     chunk = 256
     chunks = rows // 2 // chunk
+    depth = width // planes
+    sent = 2 * depth
     bf16 = jnp.bfloat16
     vmem = pl.BlockSpec(memory_space=pltpu.VMEM)
+    anywhere = pl.BlockSpec(memory_space=pl.ANY)
     dma = pltpu.SemaphoreType.DMA
     operands = (x, project_sum, cot, gains, gate_w, up_w, down_w)
     piece = pltpu.VMEM((chunks, chunk, width), bf16)
+    rows_by_width = pltpu.VMEM((rows, width), bf16)
+    rows_by_units = pltpu.VMEM((rows, 2 * units), bf16)
+    weight = jax.ShapeDtypeStruct((width, units), bf16)
     return pl.pallas_call(
         feed_kernel,
-        in_specs=[vmem] * len(operands),
-        out_specs=[vmem] * 5,
+        in_specs=[anywhere] * 3 + [vmem] + [anywhere] * 3,
+        out_specs=[anywhere] * 8,
         out_shape=[
             jax.ShapeDtypeStruct((rows, width), bf16),
-            jax.ShapeDtypeStruct((rows, 2 * units), bf16),
-            jax.ShapeDtypeStruct((2, width, units), bf16),
-            jax.ShapeDtypeStruct((2, width, units), bf16),
-            jax.ShapeDtypeStruct((2 * units, width), bf16),
+            weight,
+            jax.ShapeDtypeStruct((sent, units), bf16),
+            jax.ShapeDtypeStruct((width - sent, units), bf16),
+            weight,
+            weight,
+            jax.ShapeDtypeStruct((planes, 2 * units, width // planes), bf16),
+            jax.ShapeDtypeStruct((chunks, chunk, width), bf16),
         ],
         scratch_shapes=[
-            pltpu.VMEM((rows, width), bf16),
-            pltpu.VMEM((rows, 2 * units), bf16),
-            pltpu.VMEM((rows, 2 * units), bf16),
+            rows_by_width,
+            rows_by_width,
+            rows_by_width,
+            pltpu.VMEM(gate_w.shape, bf16),
+            pltpu.VMEM(up_w.shape, bf16),
+            pltpu.VMEM(down_w.shape, bf16),
+            rows_by_width,
+            pltpu.VMEM((3, width, units), bf16),
+            pltpu.VMEM((planes, 2 * units, width // planes), bf16),
+            rows_by_width,
+            pltpu.VMEM((width, units), bf16),
+            pltpu.VMEM((chunk, width), bf16),
+            pltpu.VMEM((width, rows), bf16),
+            rows_by_units,
+            rows_by_units,
+            rows_by_units,
             piece,
             piece,
             piece,
             piece,
+            dma((6,)),
+            dma((7,)),
         ]
-        + [dma((chunks,))] * 6,
+        + [dma((chunks,))] * 6
+        + [dma((sent // depth,))] * 2
+        + [dma((chunks,))] * 2,
         compiler_params=pltpu.CompilerParams(
             collective_id=3, has_side_effects=True, vmem_limit_bytes=VMEM_BYTES
         ),
@@ -2011,45 +2320,42 @@
         w_project.reshape(-1, HD, w_project.shape[1]), w_gate, w_up, w_down, planes,
     )
     w_p = w_p.reshape(-1, width)
-    feed_sum, hidden, gate_grad, up_grad, down_part = feed(
-        x, project_sum, cot, gains, wg, wu, wd
-    )
-
-    gate_away, up_away = swap_ctx(gate_grad[1]), swap_ctx(up_grad[1])
-
-    def added(a, b):
-        return (a.astype(f32) + b.astype(f32)).astype(bf16)
-
-    both = jnp.concatenate([added(gate_grad[0], gate_away), added(up_grad[0], up_away)], axis=1)
-    both_share = lax.psum_scatter(both, "fsdp", scatter_dimension=0, tiled=True)
-    both_away = swap_ctx(both_share)
-    units_half = gate_grad.shape[2]
-    down_share = lax.psum_scatter(down_part, "fsdp", scatter_dimension=1, tiled=True)
+    (
+        feed_sum, gate_mine, gate_away, gate_rest, up_mine, up_other, down_part, down_rows,
+    ) = feed(x, project_sum, cot, gains, wg, wu, wd, planes)
+
+    gate_rest, up_away = swap_ctx(gate_rest), swap_ctx(up_other)
+    down_share = lax.psum_scatter(down_part, "fsdp", scatter_dimension=0, tiled=False)
     down_away = swap_ctx(down_share)
     size = down_share.shape[0] // 2
     down_mine = down_share[:size].astype(f32) + down_away[size:].astype(f32)
     down_other = down_share[size:].astype(f32) + down_away[:size].astype(f32)
     down_grad = ordered(down_mine, down_other, 0)
 
-    middle_grad, d_out, down_rows, project_part, gain_two_term = middle_back(
-        x, project_sum, feed_sum, cot, gains, hidden, wd, o, w_p
-    )
-    layer_output = (x.astype(f32) + project_sum.astype(f32)
-                    + paired_tensor_sum(down_rows).astype(f32)).astype(bf16)
-    dq_away, dk_away, dv_away = attend_back(
-        meta, None, q, kv_all, True, o, d_out, lse, cosine, sine, tile
-    )
-    d_kv_away = swap_ctx(jnp.concatenate([dk_away, dv_away], axis=0))
-    q_low, dk_own, dv_own = attend_back(
-        meta, dq_away, q, kv_all, False, o, d_out, lse, cosine, sine, tile
-    )
-    d_kv_own = jnp.concatenate([dk_own, dv_own], axis=0)
-    tokens_grad, share, gain_share = tail(
-        both, down_share, q_low, d_kv_own, d_kv_away, normed, w_qkv, x, middle_grad,
+    middle_grad, d_out, project_part, gain_two_term = middle_back(
+        x, project_sum, feed_sum, cot, gains, o, w_p
+    )
+    def added(a, b):
+        return (a.astype(f32) + b.astype(f32)).astype(bf16)
+
+    down_total = added(down_rows, swap_chip(down_rows)).reshape(rows // 2, width)
+    down_sum = by_core(down_total, swap_core(down_total))
+    layer_output = (
+        x.astype(f32) + project_sum.astype(f32) + down_sum.astype(f32)
+    ).astype(bf16)
+    dq_away, d_kv_away = attend_back(
+        meta, None, d_out, d_out, q, kv_all, True, o, d_out, lse, cosine, sine, tile
+    )
+    d_kv_away = swap_ctx(d_kv_away)
+    q_low, d_kv_own = attend_back(
+        meta, dq_away, gate_rest, up_away, q, kv_all, False, o, d_out, lse, cosine, sine, tile
+    )
+    tokens_grad, share, project_share, gate_share, up_share, gain_share = tail(
+        down_share, gate_mine, gate_away, gate_rest, up_mine, up_away, q_low, d_kv_own, d_kv_away, normed, w_qkv, x, middle_grad,
         gain_two_term, gains, project_part, spread, cosine, sine, planes,
     )
     shares = [
-        ordered(a, b, 1).astype(f32) for a, b in zip(parts(share[0, : width // planes]), parts(share[1, : width // planes]))
+        ordered(a, b, 1).astype(f32) for a, b in zip(parts(share[0]), parts(share[1]))
     ]
     return (
         layer_output[None],
@@ -2058,10 +2364,10 @@
         shares[0],
         shares[1],
         shares[2],
-        ordered(share[0, width // planes :], share[1, width // planes :], 0).astype(f32),
+        ordered(project_share[0], project_share[1], 0).astype(f32),
         gain_share[1],
-        ordered(both_share[:, :units_half], both_away[:, :units_half], 1).astype(f32),
-        ordered(both_share[:, units_half:], both_away[:, units_half:], 1).astype(f32),
+        ordered(gate_share[0], gate_share[1], 1).astype(f32),
+        ordered(up_share[0], up_share[1], 1).astype(f32),
         down_grad,
     )
 

time: 515 us -> 444 us (0.86)
  Pallas kernels: 395 us -> 364 us
  waiting for transfers between devices: 34.9 us -> 19.1 us
  local copies, waits for them, and re-layouts: 25.2 us -> 12.6 us
  other arithmetic: 30.7 us -> 19.4 us
    ppermute x5 -> x4, waiting for transfers between devices: 34.9 us -> 0.07 us  [swap_ctx(): return lax.ppermute(block, 'ctx', [(0, 1), (1, 0)])]
    pallas_call x1, Pallas kernels: 181 us -> 147 us  [front(): pl.pallas_call(front_kernel, in_specs=[smem] + [vmem] * 6 + [anywhere] *...]
    ppermute x1, waiting for transfers between devices: 0.01 us -> 19 us  [swap_chip(): return lax.ppermute(block, 'tp', [(0, 2), (2, 0), (1, 3), (3, 1)])]
    pallas_call x2, Pallas kernels: 155 us -> 167 us  [the longest x1 104 us: tail(): pl.pallas_call(tail_kernel, in_specs=[anywhere] * 6 + [vmem] * 3 + [anywh...]
    squeeze x4, local copies, waits for them, and re-layouts: 7.62 us -> 1.29 us  [the longest x1 1.16 us: paired_body(): share[0]]
    pallas_call x2, Pallas kernels: 42.9 us -> 37.1 us  [attend_back(): pl.pallas_call(functools.partial(attend_back_kernel, not away), grid_spec...]
    concatenate x3 -> x0, other arithmetic: 5.43 us -> none  [the longest x1 2.31 us: paired_body(): d_kv_away = swap_ctx(jnp.concatenate([dk_away, dv_away], axis=0))]
  transfers between devices with their start and end apart: 10 -> 7, of which waited for: 3 -> 2; matrix products, arithmetic and copies ran while one was open for 8% -> 4% of each run, Pallas kernels for 27% -> 35%
where the time goes in v4:
time: 444 us; the launch traced here: 437 us
  Pallas kernels  364 us (82%)
  other arithmetic  19.4 us (4%)
  waiting for transfers between devices  19.1 us (4%)
  between operations  15.4 us (3%)
  local copies, waits for them, and re-layouts  12.6 us (3%)
  starting transfers between devices  6.71 us (2%)
    pallas_call x1, Pallas kernels, front(): pl.pallas_call(front_kernel, in_specs=[smem] + [vmem] * 6 + [anywhere] *...  147 us
    pallas_call x1, Pallas kernels, tail(): pl.pallas_call(tail_kernel, in_specs=[anywhere] * 6 + [vmem] * 3 + [anywh...  104 us
    pallas_call x1, Pallas kernels, feed(): pl.pallas_call(feed_kernel, in_specs=[anywhere] * 3 + [vmem] + [anywhere]...  63 us
    pallas_call x2, Pallas kernels, attend_back(): pl.pallas_call(functools.partial(attend_back_kernel, not away), grid_spec...  37.1 us
    ppermute x1, waiting for transfers between devices, swap_chip(): return lax.ppermute(block, 'tp', [(0, 2), (2, 0), (1, 3), (3, 1)])  19 us
    pallas_call x1, Pallas kernels, middle_back(): pl.pallas_call(middle_back_kernel, grid=(rows // tile,), in_specs=[rows_o...  13.1 us
  transfers between devices with their start and end apart: 7, of which 2 were waited for; matrix products, arithmetic and copies ran while one was open for 4% of the time, Pallas kernels for 35%

profile of v4, /device:TPU:0, one launch (start us, length us, event | category | flops | bytes accessed | tf_op | source)
XLA Modules:
  0.0 436.9 jit_solution(12960322018281992477)
XLA Ops:
  7.2 0.0 copy-start.5
  7.2 0.0 reduce-scatter.2.cloned.1.call-start
  7.3 1.0 constant_dynamic-slice_fusion
  8.3 0.1 copy.33
  8.4 0.1 copy.34
  8.5 0.1 copy.31
  8.7 0.1 copy.32
  8.8 0.7 stack.10
  9.5 0.7 stack.9
  10.2 0.7 convert_element_type.72
  11.5 1.9 fusion.7
  13.5 0.0 copy-done.5
  13.5 0.2 constant_dynamic-slice_fusion.2
  13.7 0.9 pad_maximum_fusion.3.rest_ref
  14.5 1.3 pad_maximum_fusion
  15.8 0.9 pad_maximum_fusion.2.pack_ref
  16.7 146.6 %front.1 = (bf16[1024,1536]{1,0:T(8,128)(2,1)}, bf16[1024,512]{1,0:T(8,128)(2,1)}, bf16[4,2048,128]{2,1,0:T(8,128)(2,1)}, bf16[1536,1024]{1,0:T(8,128)(2,1)}, bf...) custom-call(s32[1]{0:T(128)S(6)} %copy.36.prefix_ref, ...), custom_call_target="tpu_custom_call" | custom-call | flops 120000004096 | bytes 60000000 | tf_op jit(solution)/shard_map/front/pallas_call | solution.py:1162
  163.3 63.0 %feed.1 = (bf16[1024,1536]{1,0:T(8,128)(2,1)}, bf16[1536,512]{1,0:T(8,128)(2,1)}, bf16[768,512]{1,0:T(8,128)(2,1)}, bf16[768,512]{1,0:T(8,128)(2,1)}, bf16[1536,...) custom-call(bf16[1024,1536]{1,0:T(8,128)(2,1)} %bitcast.41, ...), custom_call_target="tpu_custom_call" | custom-call | flops 49999998976 | bytes 40000000 | tf_op jit(solution)/shard_map/feed/pallas_call | solution.py:2188
  226.2 0.0 copy-start.1
  226.3 0.0 reduce-scatter.2.cloned.1.call-update
  226.3 1.4 copy-done.1
  227.7 2.6 collective-permute-start
  230.2 0.0 collective-permute-start.3
  230.2 2.0 collective-permute-start.2
  232.3 0.6 pad_add_fusion.meta_ref
  232.9 13.1 %middle_back.1 = (f32[1024,1536]{1,0:T(8,128)}, bf16[1024,512]{1,0:T(8,128)(2,1)}, bf16[384,1536]{1,0:T(8,128)(2,1)}, f32[1,1536]{1,0:T(1,128)}) custom-call(bf16[1024,1536]{1,0:T(8,128)(2,1)} %bitcast.42, bf16[1024,1536]{1,0:T(8,128)(2,1)} %get-tuple-element.45.project_hbm.project_ref, bf16[1024,1536]{1,0:T(8,128)(2,1)} %get-tuple-element.57.feed_ref, ...), custom_call_target="tpu_custom_call" | custom-call | flops 5000000000 | bytes 26000000 | tf_op jit(solution)/shard_map/middle_back/pallas_call | solution.py:1419
  246.0 19.0 %collective-permute-done = bf16[2,256,1536]{2,1,0:T(8,128)(2,1)} collective-permute-done((bf16[2,256,1536]{2,1,0:T(8,128)(2,1)S(1)}, bf16[2,256,1536]{2,1,0:T(8,128)(2,1)}, u32[]{:S(2)}, u32[]{:S(2)}) %collective-permute-start) | collective-permute-done | bytes 1572896 | tf_op jit(solution)/shard_map/ppermute | solution.py:443
  265.0 1.8 add_convert_fusion.1
  266.8 0.1 collective-permute-start.1
  266.9 0.6 broadcast_in_dim.12.carry_ref
  267.5 18.2 %attend_back_away.1 = (f32[2,4,128,512]{3,2,1,0:T(8,128)}, bf16[2,2,1024,128]{3,2,1,0:T(8,128)(2,1)}) custom-call(s32[13]{0:T(128)} %pad_add_fusion.meta_ref, f32[1,1,8,128]{3,2,1,0:T(8,128)} %broadcast_in_dim.12.carry_ref, bf16[1024,512]{1,0:T(8,128)(2,1)} %get-tuple-element.60.first_ref.second_ref.do_ref, ...), custom_call_target="tpu_custom_call" | custom-call | flops 10737418240 | bytes 8000000 | tf_op jit(solution)/shard_map/attend_back_away/pallas_call | solution.py:1320
  285.7 0.1 collective-permute-start.4
  285.7 0.0 collective-permute-done.2.first_ref.gate_rest_hbm
  285.8 0.0 collective-permute-done.3.second_ref.up_away_hbm
  285.8 18.9 %attend_back_own.1 = (bf16[1024,512]{1,0:T(8,128)(2,1)}, bf16[2,2,1024,128]{3,2,1,0:T(8,128)(2,1)}) custom-call(s32[13]{0:T(128)} %pad_add_fusion.meta_ref, f32[2,4,128,512]{3,2,1,0:T(8,128)} %get-tuple-element.64.carry_ref, bf16[768,512]{1,0:T(8,128)(2,1)} %collective-permute-done.2.first_ref.gate_rest_hbm, ...), custom_call_target="tpu_custom_call" | custom-call | flops 10737418240 | bytes 8000000 | tf_op jit(solution)/shard_map/attend_back_own/pallas_call | solution.py:1320
  304.7 0.0 collective-permute-done.1
  304.7 4.8 %fusion = bf16[1,1024,1536]{2,1,0:T(8,128)(2,1)} fusion(bf16[1024,1536]{1,0:T(8,128)(2,1)} %get-tuple-element.45.project_hbm.project_ref, bf16[512,1536]{1,0:T(8,128)(2,1)S(1)} %collective-permute-done.1, bf16[512,1536]{1,0:T(8,128)(2,1)S(1)} %bitcast.38, pred[]{:T(512)S(6)} %eq.25, bf16[1,1024,1536]{2,1,0:T(8,128)(2,1)} %param.14), kind=kLoop, calls=%fused_computation.1 | loop fusion | flops 23592960 | bytes 12582913 | tf_op jit(solution)/shard_map/broadcast_in_dim | solution.py:2361
  309.5 2.0 collective-permute-start.5
  311.5 0.1 collective-permute-done.4.away_ref
  311.6 104.0 %tail.1 = (bf16[1024,1536]{1,0:T(8,128)(2,1)}, bf16[2,384,384]{2,1,0:T(8,128)(2,1)}, bf16[2,192,384]{2,1,0:T(8,128)(2,1)}, bf16[2,384,512]{2,1,0:T(8,128)(2,1)},...) custom-call(bf16[1024,384]{1,0:T(8,128)(2,1)} %bitcast.45, bf16[1536,512]{1,0:T(8,128)(2,1)} %get-tuple-element.52.gate_hbm, ...), custom_call_target="tpu_custom_call" | custom-call | flops 60000002048 | bytes 24000000 | tf_op jit(solution)/shard_map/tail/pallas_call | solution.py:1873
  415.6 0.0 copy-start.6
  415.6 1.2 slice_bitcast_fusion.7
  416.7 0.1 fusion.17
  416.9 0.1 fusion.18
  417.0 0.0 copy-done.6
  417.1 0.0 copy-start.3
  417.1 0.2 fusion.6
  417.3 0.9 copy.30
  418.1 0.2 fusion.5
  418.3 0.9 copy.29
  419.2 1.4 slice_reduce_fusion
  420.6 0.9 fusion.4
  421.4 1.0 fusion.3
  422.5 0.1 slice_bitcast_fusion.3
  422.5 1.4 fusion.2
  423.9 0.0 copy-done.2
  423.9 0.1 slice_bitcast_fusion.5
  424.0 1.4 fusion.1
  425.4 0.0 collective-permute-done.5
  425.4 0.0 copy-done.4
  425.4 0.2 convert_add_fusion.1
  425.5 1.2 maximum_select_fusion.1
  426.8 1.2 copy-done
  428.0 1.7 copy.37
  (12 shorter events, 0.1 us)
Async XLA Ops:
  7.2 6.3 %copy-start.5 = (bf16[384,384]{1,0:T(8,128)(2,1)S(1)}, bf16[384,384]{1,0:T(8,128)(2,1)}, u32[]{:S(2)}) copy-start(bf16[384,384]{1,0:T(8,128)(2,1)} %param.18) | copy-start | bytes 884740
  7.2 302.4 %reduce-scatter.2.cloned.1.call-start = ((), (), s32[]{:S(2)}) async-start(), calls=%async_computation.1 | async-start | bytes 3932160 | tf_op jit(solution)/shard_map/reduce_scatter | solution.py:2328
  226.2 1.4 copy-start.1
  227.7 37.4 %collective-permute-start = (bf16[2,256,1536]{2,1,0:T(8,128)(2,1)S(1)}, bf16[2,256,1536]{2,1,0:T(8,128)(2,1)}, u32[]{:S(2)}, u32[]{:S(2)}) collective-permute-start(bf16[2,256,1536]{2,1,0:T(8,128)(2,1)S(1)} %copy-done.1), channel_id=1, source_target_pairs={{0,2},{2,0},{1,3},{3,1},{4,6},{6,4},{5,7},{7,5},{8,10},{10,8},{9,1... | collective-permute-start | bytes 4718600 | tf_op jit(solution)/shard_map/ppermute | solution.py:443
  230.2 55.5 %collective-permute-start.3 = (bf16[1536,512]{1,0:T(8,128)(2,1)}, bf16[1536,512]{1,0:T(8,128)(2,1)}, u32[]{:S(2)}, u32[]{:S(2)}) collective-permute-start(bf16[1536,512]{1,0:T(8,128)(2,1)} %get-tuple-element.56), channel_id=1, source_target_pairs={{0,4},{4,0},{1,5},{5,1},{2,6},{6,2},{3,7},{7,3},{8,12},{12,8},{9,1... | collective-permute-start | bytes 4718600 | tf_op jit(solution)/shard_map/ppermute | solution.py:435
  230.2 55.5 %collective-permute-start.2 = (bf16[768,512]{1,0:T(8,128)(2,1)}, bf16[768,512]{1,0:T(8,128)(2,1)}, u32[]{:S(2)}, u32[]{:S(2)}) collective-permute-start(bf16[768,512]{1,0:T(8,128)(2,1)} %get-tuple-element.54), channel_id=1, source_target_pairs={{0,4},{4,0},{1,5},{5,1},{2,6},{6,2},{3,7},{7,3},{8,12},{12,8},{9,1... | collective-permute-start | bytes 2359304 | tf_op jit(solution)/shard_map/ppermute | solution.py:435
  266.8 37.9 %collective-permute-start.1 = (bf16[512,1536]{1,0:T(8,128)(2,1)S(1)}, bf16[512,1536]{1,0:T(8,128)(2,1)S(1)}, u32[]{:S(2)}, u32[]{:S(2)}) collective-permute-start(bf16[512,1536]{1,0:T(8,128)(2,1)S(1)} %bitcast.37), channel_id=1, source_target_pairs={{0,1},{1,0},{2,3},{3,2},{4,5},{5,4},{6,7},{7,6},{8,9},{9,8},{10,11... | collective-permute-start | bytes 4718600 | tf_op jit(solution)/shard_map/ppermute | solution.py:439
  285.7 25.9 %collective-permute-start.4 = (bf16[2,2,1024,128]{3,2,1,0:T(8,128)(2,1)}, bf16[2,2,1024,128]{3,2,1,0:T(8,128)(2,1)}, u32[]{:S(2)}, u32[]{:S(2)}) collective-permute-start(bf16[2,2,1024,128]{3,2,1,0:T(8,128)(2,1)} %get-tuple-element.67), channel_id=1, source_target_pairs={{0,4},{4,0},{1,5},{5,1},{2,6},{6,2},{3,7},{7,3},{8,12},{12,8},{9,1... | collective-permute-start | bytes 3145736 | tf_op jit(solution)/shard_map/ppermute | solution.py:435
  309.5 115.8 %collective-permute-start.5 = (bf16[1024,384]{1,0:T(8,128)(2,1)}, bf16[1024,384]{1,0:T(8,128)(2,1)S(1)}, u32[]{:S(2)}, u32[]{:S(2)}) collective-permute-start(bf16[1024,384]{1,0:T(8,128)(2,1)} %bitcast.44), channel_id=1, source_target_pairs={{0,4},{4,0},{1,5},{5,1},{2,6},{6,2},{3,7},{7,3},{8,12},{12,8},{9,1... | collective-permute-start | bytes 2359304 | tf_op jit(solution)/shard_map/ppermute | solution.py:435
  415.6 1.5 copy-start.6
  417.1 5.4 %copy-start.3 = (bf16[2,384,512]{2,1,0:T(8,128)(2,1)S(1)}, bf16[2,384,512]{2,1,0:T(8,128)(2,1)}, u32[]{:S(2)}) copy-start(bf16[2,384,512]{2,1,0:T(8,128)(2,1)} %get-tuple-element.78) | copy-start | bytes 2359300
  422.5 1.4 copy-start.2
  423.9 1.4 copy-start.4
  425.5 2.5 copy-start
Sparse Core Ops, SparseCore 0:
  226.4 59.1 reduce-scatter.1

commit v5 on v4

--- a/solution.py
+++ b/solution.py
@@ -584,10 +584,10 @@
     w_gate_ref,
     w_up_ref,
     w_down_ref,
-    normed_ref,
-    q_ref,
-    kv_ref,
-    wide_ref,
+    normed_hbm,
+    q_hbm,
+    kv_hbm,
+    wide_hbm,
     project_ref,
     gain_ref,
     o_ref,
@@ -596,6 +596,10 @@
     gate_ref,
     up_ref,
     down_ref,
+    normed_ref,
+    q_ref,
+    kv_ref,
+    wide_ref,
     buf_ref,
     max_ref,
     sum_ref,
@@ -625,6 +629,7 @@
     chip_recv,
     back_send,
     back_recv,
+    store_sem,
 ):
     bf16, f32 = jnp.bfloat16, jnp.float32
     planes = buf_ref.shape[0]
@@ -969,6 +974,14 @@
         return carry
 
     lax.fori_loop(0, rows // block, query_rows, 0)
+    stores = [
+        pltpu.make_async_copy(src, dst, store_sem.at[i])
+        for i, (src, dst) in enumerate(
+            ((normed_ref, normed_hbm), (q_ref, q_hbm), (wide_ref, wide_hbm), (kv_ref, kv_hbm))
+        )
+    ]
+    for store in stores[:3]:
+        store.start()
 
     tiles = rows // block
     tiles_of_block = tiles // 2
@@ -1042,6 +1055,7 @@
     relay(3, 1)
     for slab in range(4):
         exchange(slab).wait_recv()
+    stores[3].start()
     cross(1, 1)
     cross(2, 1)
     cross(3, 1)
@@ -1101,6 +1115,8 @@
             relay(i + 1, planes - 1)
             cross(i + 1, planes - 1)
 
+    for store in stores:
+        store.wait()
     for k in range(planes - 1):
 
         @pl.when((z - k >= 0) & has_above)
@@ -1162,7 +1178,7 @@
     return pl.pallas_call(
         front_kernel,
         in_specs=[smem] + [vmem] * 6 + [anywhere] * 4,
-        out_specs=[vmem] * 9 + [anywhere] * 3,
+        out_specs=[anywhere] * 4 + [vmem] * 5 + [anywhere] * 3,
         out_shape=[
             jax.ShapeDtypeStruct((rows, width), bf16),
             jax.ShapeDtypeStruct((rows, half_width), bf16),
@@ -1178,6 +1194,10 @@
             jax.ShapeDtypeStruct((2, units, width), bf16),
         ],
         scratch_shapes=[
+            pltpu.VMEM((rows, width), bf16),
+            pltpu.VMEM((rows, half_width), bf16),
+            pltpu.VMEM((4, 2 * rows, LANES), bf16),
+            pltpu.VMEM((width, 2 * half_width), bf16),
             pltpu.VMEM((planes, 2, pack.shape[0], pack.shape[1]), bf16),
             pltpu.VMEM((2 * tiles, 1, 2 * block), f32),
             pltpu.VMEM((2 * tiles, 1, 2 * block), f32),
@@ -1193,7 +1213,8 @@
         + [dma((5, planes - 1))] * 4
         + [dma((4, 2, planes))] * 2
         + [dma((4, 2))]
-        + [dma((chunks,))] * 6,
+        + [dma((chunks,))] * 6
+        + [dma((4,))],
         compiler_params=pltpu.CompilerParams(
             collective_id=1, has_side_effects=True, vmem_limit_bytes=VMEM_BYTES
         ),
@@ -1450,7 +1471,7 @@
 
 
 def tail_kernel(
-    first_ref,
+    down_hbm,
     gate_hbm,
     gate_away_hbm,
     gate_rest_hbm,
@@ -1475,6 +1496,7 @@
     gate_share_ref,
     up_share_ref,
     gain_share_ref,
+    down_away_hbm,
     normed_ref,
     wide_ref,
     x_ref,
@@ -1749,6 +1771,9 @@
             project_share_ref.at[0], project_share_ref.at[1], last_send.at[1], last_recv.at[1], across
         )
 
+    def down_over():
+        return remote(down_hbm, down_away_hbm, last_send.at[5], last_recv.at[5], across)
+
     def last_of(ref, i):
         return remote(ref.at[0], ref.at[1], last_send.at[i], last_recv.at[i], across)
 
@@ -1764,6 +1789,7 @@
         add_neighbour(d)
     for step in range(planes - 1):
         q_begin(step)
+    down_over().start()
     for i in range(1, chunks):
         finish_chunk(i)
     g_finish(gate_share_ref.at[0])
@@ -1833,6 +1859,7 @@
     last_of(gate_share_ref, 3).wait()
     last_of(up_share_ref, 4).wait()
     project_over().wait_send()
+    down_over().wait()
     p_sent()
     g_sent()
     u_sent()
@@ -1848,7 +1875,7 @@
 
 
 def tail(
-    first, gate, gate_away, gate_rest, upw, up_away, q_low, own, away, normed, wide, x, grad,
+    down_share, gate, gate_away, gate_rest, upw, up_away, q_low, own, away, normed, wide, x, grad,
     gain_term, gains, project, spread, cosine, sine, planes,
 ):
     rows, width = x.shape
@@ -1861,7 +1888,7 @@
     vmem = pl.BlockSpec(memory_space=pltpu.VMEM)
     dma = pltpu.SemaphoreType.DMA
     operands = (
-        first, gate, gate_away, gate_rest, upw, up_away, q_low, own, away, normed, wide, x, grad,
+        down_share, gate, gate_away, gate_rest, upw, up_away, q_low, own, away, normed, wide, x, grad,
         gain_term, gains, project, spread, cosine, sine,
     )
     units = gate.shape[1]
@@ -1873,7 +1900,7 @@
     return pl.pallas_call(
         tail_kernel,
         in_specs=[anywhere] * 6 + [vmem] * 3 + [anywhere] * 4 + [vmem] * (len(operands) - 13),
-        out_specs=[anywhere] + [vmem] * 5,
+        out_specs=[anywhere] + [vmem] * 5 + [anywhere],
         out_shape=[
             jax.ShapeDtypeStruct((rows, width), bf16),
             jax.ShapeDtypeStruct((2, depth, close_width), bf16),
@@ -1881,6 +1908,7 @@
             jax.ShapeDtypeStruct((2, depth, units), bf16),
             jax.ShapeDtypeStruct((2, depth, units), bf16),
             jax.ShapeDtypeStruct((8, depth), f32),
+            jax.ShapeDtypeStruct(down_share.shape, bf16),
         ],
         scratch_shapes=[
             pltpu.VMEM((rows, width), bf16),
@@ -1914,7 +1942,7 @@
         ]
         + [dma((planes,))] * 18
         + [dma((chunks,))] * 6
-        + [dma((5,))] * 2
+        + [dma((6,))] * 2
         + [dma((planes,))] * 2
         + [dma((9,))],
         compiler_params=pltpu.CompilerParams(
@@ -2148,20 +2176,20 @@
     lax.fori_loop(0, rows // block, down_features, 0)
     for i in range(chunks // 2):
         back(i, give_start).wait_recv()
+    for i in range(chunks):
+        down_over(i).start()
+    for i in range(chunks):
+        to_core(i).wait_send()
+        down_over(i).wait()
+        at = pl.ds(pl.multiple_of(keep_start + i * chunk, chunk), chunk)
+        give_ref[i] = (down_rows_ref[at, :].astype(f32) + core_in_ref[i].astype(f32)).astype(bf16)
+    store(give_ref, down_rows_hbm)
     for i in range(chunks // 2, chunks):
         finish_chunk(i)
     for i in range(chunks // 2, chunks):
         back(i, give_start).wait_recv()
     store(total_ref, total_hbm)
     for i in range(chunks):
-        down_over(i).start()
-    for i in range(chunks):
-        down_over(i).wait()
-        at = pl.ds(pl.multiple_of(keep_start + i * chunk, chunk), chunk)
-        keep_ref[i] = (down_rows_ref[at, :].astype(f32) + core_in_ref[i].astype(f32)).astype(bf16)
-    store(keep_ref, down_rows_hbm)
-    for i in range(chunks):
-        to_core(i).wait_send()
         back(i, keep_start).wait_send()
     for i in range(pieces):
         over(i).wait()
@@ -2175,7 +2203,7 @@
     chunk = 256
     chunks = rows // 2 // chunk
     depth = width // planes
-    sent = 2 * depth
+    sent = 3 * depth
     bf16 = jnp.bfloat16
     vmem = pl.BlockSpec(memory_space=pltpu.VMEM)
     anywhere = pl.BlockSpec(memory_space=pl.ANY)
@@ -2236,6 +2264,26 @@
     )(*operands)
 
 
+def add_kernel(first_ref, a_ref, b_ref, out_ref):
+    out_ref[...] = (a_ref[...].astype(jnp.float32) + b_ref[...].astype(jnp.float32)).astype(
+        out_ref.dtype
+    )
+
+
+def add_after(first, a, b):
+    rows, width = a.shape
+    tile = 256
+    spec = pl.BlockSpec((tile, width), lambda i: (i, 0))
+    return pl.pallas_call(
+        add_kernel,
+        grid=(rows // tile,),
+        in_specs=[pl.BlockSpec(memory_space=pl.ANY), spec, spec],
+        out_specs=spec,
+        out_shape=jax.ShapeDtypeStruct(a.shape, a.dtype),
+        name="add_after",
+    )(first, a, b)
+
+
 def paired_body(
     tokens,
     prefix_len,
@@ -2326,34 +2374,31 @@
 
     gate_rest, up_away = swap_ctx(gate_rest), swap_ctx(up_other)
     down_share = lax.psum_scatter(down_part, "fsdp", scatter_dimension=0, tiled=False)
-    down_away = swap_ctx(down_share)
-    size = down_share.shape[0] // 2
-    down_mine = down_share[:size].astype(f32) + down_away[size:].astype(f32)
-    down_other = down_share[size:].astype(f32) + down_away[:size].astype(f32)
-    down_grad = ordered(down_mine, down_other, 0)
-
     middle_grad, d_out, project_part, gain_two_term = middle_back(
         x, project_sum, feed_sum, cot, gains, o, w_p
     )
-    def added(a, b):
-        return (a.astype(f32) + b.astype(f32)).astype(bf16)
-
-    down_total = added(down_rows, swap_chip(down_rows)).reshape(rows // 2, width)
+    down_rows = down_rows.reshape(rows // 2, width)
+    down_away = swap_chip(down_rows)
+    dq_away, d_kv_away = attend_back(
+        meta, None, d_out, d_out, q, kv_all, True, o, d_out, lse, cosine, sine, tile
+    )
+    d_kv_away = swap_ctx(d_kv_away)
+    down_total = add_after(dq_away, down_rows, down_away)
     down_sum = by_core(down_total, swap_core(down_total))
     layer_output = (
         x.astype(f32) + project_sum.astype(f32) + down_sum.astype(f32)
     ).astype(bf16)
-    dq_away, d_kv_away = attend_back(
-        meta, None, d_out, d_out, q, kv_all, True, o, d_out, lse, cosine, sine, tile
-    )
-    d_kv_away = swap_ctx(d_kv_away)
     q_low, d_kv_own = attend_back(
         meta, dq_away, gate_rest, up_away, q, kv_all, False, o, d_out, lse, cosine, sine, tile
     )
-    tokens_grad, share, project_share, gate_share, up_share, gain_share = tail(
+    tokens_grad, share, project_share, gate_share, up_share, gain_share, down_other_share = tail(
         down_share, gate_mine, gate_away, gate_rest, up_mine, up_away, q_low, d_kv_own, d_kv_away, normed, w_qkv, x, middle_grad,
         gain_two_term, gains, project_part, spread, cosine, sine, planes,
     )
+    size = down_share.shape[0] // 2
+    down_mine = down_share[:size].astype(f32) + down_other_share[size:].astype(f32)
+    down_other = down_share[size:].astype(f32) + down_other_share[:size].astype(f32)
+    down_grad = ordered(down_mine, down_other, 0)
     shares = [
         ordered(a, b, 1).astype(f32) for a, b in zip(parts(share[0]), parts(share[1]))
     ]

time: 444 us -> 433 us (0.975)
  Pallas kernels: 364 us -> 357 us
    ppermute x1, waiting for transfers between devices: 19 us -> 5.56 us  [swap_chip(): return lax.ppermute(block, 'tp', [(0, 2), (2, 0), (1, 3), (3, 1)])]
    ppermute x4 -> x3, waiting for transfers between devices: 0.07 us -> 10 us  [swap_ctx(): return lax.ppermute(block, 'ctx', [(0, 1), (1, 0)])]
    pallas_call x2, Pallas kernels: 37.1 us -> 32.4 us  [attend_back(): pl.pallas_call(functools.partial(attend_back_kernel, not away), grid_spec...]
  transfers between devices with their start and end apart: 7 -> 6, of which waited for: 2 -> 2; matrix products, arithmetic and copies ran while one was open for 4% -> 1% of each run, Pallas kernels for 35% -> 11%
where the time goes in v5:
time: 433 us; the launch traced here: 427 us
  Pallas kernels  357 us (82%)
  other arithmetic  19.6 us (5%)
  waiting for transfers between devices  15.6 us (4%)
  between operations  15.4 us (4%)
  local copies, waits for them, and re-layouts  13.4 us (3%)
  starting transfers between devices  5.41 us (1%)
    pallas_call x1, Pallas kernels, front(): pl.pallas_call(front_kernel, in_specs=[smem] + [vmem] * 6 + [anywhere] *...  144 us
    pallas_call x1, Pallas kernels, tail(): pl.pallas_call(tail_kernel, in_specs=[anywhere] * 6 + [vmem] * 3 + [anywh...  101 us
    pallas_call x1, Pallas kernels, feed(): pl.pallas_call(feed_kernel, in_specs=[anywhere] * 3 + [vmem] + [anywhere]...  63.6 us
    pallas_call x2, Pallas kernels, attend_back(): pl.pallas_call(functools.partial(attend_back_kernel, not away), grid_spec...  32.4 us
    pallas_call x1, Pallas kernels, middle_back(): pl.pallas_call(middle_back_kernel, grid=(rows // tile,), in_specs=[rows_o...  13.5 us
    ppermute x3, waiting for transfers between devices, swap_ctx(): return lax.ppermute(block, 'ctx', [(0, 1), (1, 0)])  10 us
  transfers between devices with their start and end apart: 6, of which 2 were waited for; matrix products, arithmetic and copies ran while one was open for 1% of the time, Pallas kernels for 11%

profile of v5, /device:TPU:0, one launch (start us, length us, event | category | flops | bytes accessed | tf_op | source)
XLA Modules:
  0.0 426.5 jit_solution(1020591749501541525)
XLA Ops:
  7.2 0.0 copy-start.7
  7.2 0.0 reduce-scatter.2.cloned.1.call-start
  7.3 1.0 constant_dynamic-slice_fusion
  8.3 0.1 copy.33
  8.4 0.1 copy.34
  8.5 0.1 copy.31
  8.7 0.1 copy.32
  8.8 0.7 stack.10
  9.5 0.7 stack.9
  10.2 0.7 convert_element_type.63
  11.5 1.9 fusion.7
  13.5 0.0 copy-done.7
  13.5 0.2 constant_dynamic-slice_fusion.2
  13.7 0.9 pad_maximum_fusion.3.rest_ref
  14.5 1.3 pad_maximum_fusion
  15.8 0.9 pad_maximum_fusion.2.pack_ref
  16.7 143.8 %front.1 = (bf16[1024,1536]{1,0:T(8,128)(2,1)}, bf16[1024,512]{1,0:T(8,128)(2,1)}, bf16[4,2048,128]{2,1,0:T(8,128)(2,1)}, bf16[1536,1024]{1,0:T(8,128)(2,1)}, bf...) custom-call(s32[1]{0:T(128)S(6)} %copy.36.prefix_ref, ...), custom_call_target="tpu_custom_call" | custom-call | flops 120000004096 | bytes 60000000 | tf_op jit(solution)/shard_map/front/pallas_call | solution.py:1178
  160.5 63.6 %feed.1 = (bf16[1024,1536]{1,0:T(8,128)(2,1)}, bf16[1536,512]{1,0:T(8,128)(2,1)}, bf16[1152,512]{1,0:T(8,128)(2,1)}, bf16[384,512]{1,0:T(8,128)(2,1)}, bf16[1536...) custom-call(bf16[1024,1536]{1,0:T(8,128)(2,1)} %bitcast.39, ...), custom_call_target="tpu_custom_call" | custom-call | flops 49999998976 | bytes 40000000 | tf_op jit(solution)/shard_map/feed/pallas_call | solution.py:2216
  224.1 0.0 copy-start.2
  224.1 0.0 reduce-scatter.2.cloned.1.call-update
  224.1 0.7 collective-permute-start.3
  224.9 0.6 copy-done.2
  225.5 2.6 collective-permute-start
  228.1 0.6 pad_add_fusion.meta_ref
  228.7 13.5 %middle_back.1 = (f32[1024,1536]{1,0:T(8,128)}, bf16[1024,512]{1,0:T(8,128)(2,1)}, bf16[384,1536]{1,0:T(8,128)(2,1)}, f32[1,1536]{1,0:T(1,128)}) custom-call(bf16[1024,1536]{1,0:T(8,128)(2,1)} %bitcast.40, bf16[1024,1536]{1,0:T(8,128)(2,1)} %get-tuple-element.46.project_hbm.project_ref, bf16[1024,1536]{1,0:T(8,128)(2,1)} %get-tuple-element.51.feed_ref, ...), custom_call_target="tpu_custom_call" | custom-call | flops 5000000000 | bytes 26000000 | tf_op jit(solution)/shard_map/middle_back/pallas_call | solution.py:1440
  242.2 0.6 broadcast_in_dim.11.carry_ref
  242.8 14.4 %attend_back_away.1 = (f32[2,4,128,512]{3,2,1,0:T(8,128)}, bf16[2,2,1024,128]{3,2,1,0:T(8,128)(2,1)}) custom-call(s32[13]{0:T(128)} %pad_add_fusion.meta_ref, f32[1,1,8,128]{3,2,1,0:T(8,128)} %broadcast_in_dim.11.carry_ref, bf16[1024,512]{1,0:T(8,128)(2,1)} %get-tuple-element.54.first_ref.second_ref.do_ref, ...), custom_call_target="tpu_custom_call" | custom-call | flops 10737418240 | bytes 8000000 | tf_op jit(solution)/shard_map/attend_back_away/pallas_call | solution.py:1341
  257.2 5.6 %collective-permute-done.b_ref = bf16[512,1536]{1,0:T(8,128)(2,1)S(1)} collective-permute-done((bf16[512,1536]{1,0:T(8,128)(2,1)S(1)}, bf16[512,1536]{1,0:T(8,128)(2,1)S(1)}, u32[]{:S(2)}, u32[]{:S(2)}) %collective-permute-start) | collective-permute-done | bytes 1572896 | tf_op jit(solution)/shard_map/ppermute | solution.py:443
  262.8 1.1 copy-done.3
  263.9 3.0 add_after.1
  266.9 0.0 collective-permute-start.1
  266.9 0.0 copy-done.9
  266.9 0.5 collective-permute-start.2
  267.4 1.6 collective-permute-start.4
  269.0 10.0 %collective-permute-done.2.first_ref.gate_rest_hbm = bf16[384,512]{1,0:T(8,128)(2,1)} collective-permute-done((bf16[384,512]{1,0:T(8,128)(2,1)S(1)}, bf16[384,512]{1,0:T(8,128)(2,1)}, u32[]{:S(2)}, u32[]{:S(2)}) %collective-permute-start.2) | collective-permute-done | bytes 393248 | tf_op jit(solution)/shard_map/ppermute | solution.py:435
  279.0 0.0 collective-permute-done.3.second_ref.up_away_hbm
  279.0 18.0 %attend_back_own.1 = (bf16[1024,512]{1,0:T(8,128)(2,1)}, bf16[2,2,1024,128]{3,2,1,0:T(8,128)(2,1)}) custom-call(s32[13]{0:T(128)} %pad_add_fusion.meta_ref, f32[2,4,128,512]{3,2,1,0:T(8,128)} %get-tuple-element.58.first_ref.carry_ref, bf16[384,512]{1,0:T(8,128)(2,1)} %collective-permute-done.2.first_ref.gate_rest_hbm, ...), custom_call_target="tpu_custom_call" | custom-call | flops 10737418240 | bytes 8000000 | tf_op jit(solution)/shard_map/attend_back_own/pallas_call | solution.py:1341
  297.0 0.0 collective-permute-done.1
  297.0 0.0 copy-done
  297.0 4.8 %fusion = bf16[1,1024,1536]{2,1,0:T(8,128)(2,1)} fusion(bf16[1024,1536]{1,0:T(8,128)(2,1)} %get-tuple-element.46.project_hbm.project_ref, bf16[512,1536]{1,0:T(8,128)(2,1)S(1)} %collective-permute-done.1, bf16[512,1536]{1,0:T(8,128)(2,1)S(1)} %copy-done, pred[]{:T(512)S(6)} %eq.25, bf16[1,1024,1536]{2,1,0:T(8,128)(2,1)} %param.14), kind=kLoop, calls=%fused_computation.1 | loop fusion | flops 23592960 | bytes 12582913 | tf_op jit(solution)/shard_map/broadcast_in_dim | solution.py:2406
  301.8 0.0 collective-permute-done.4.away_ref
  301.8 100.9 %tail.1 = (bf16[1024,1536]{1,0:T(8,128)(2,1)}, bf16[2,384,384]{2,1,0:T(8,128)(2,1)}, bf16[2,192,384]{2,1,0:T(8,128)(2,1)}, bf16[2,384,512]{2,1,0:T(8,128)(2,1)},...) custom-call(bf16[1024,384]{1,0:T(8,128)(2,1)} %bitcast.44, ...), custom_call_target="tpu_custom_call" | custom-call | flops 60000002048 | bytes 24000000 | tf_op jit(solution)/shard_map/tail/pallas_call | solution.py:1900
  402.7 0.0 copy-start.5
  402.8 1.2 slice_bitcast_fusion.7
  403.9 0.0 copy-start.4
  403.9 0.1 fusion.17
  404.1 0.8 fusion.18
  404.9 0.1 slice_bitcast_fusion.3
  405.0 0.1 copy-done.4
  405.1 0.1 slice_bitcast_fusion.5
  405.2 0.7 copy-done.8
  405.9 0.2 fusion.6
  406.1 0.9 copy.30
  407.0 1.1 fusion.5
  408.1 0.9 copy.29
  409.0 1.4 slice_reduce_fusion
  410.4 0.0 copy-done.6
  410.4 1.3 convert_add_fusion.1
  411.7 1.2 maximum_select_fusion.1
  412.9 1.4 fusion.2
  414.3 1.4 fusion.1
  415.7 0.9 fusion.4
  416.5 1.0 fusion.3
  417.6 1.7 copy.37
  (16 shorter events, 0.1 us)
Async XLA Ops:
  7.2 6.3 %copy-start.7 = (bf16[384,384]{1,0:T(8,128)(2,1)S(1)}, bf16[384,384]{1,0:T(8,128)(2,1)}, u32[]{:S(2)}) copy-start(bf16[384,384]{1,0:T(8,128)(2,1)} %param.18) | copy-start | bytes 884740
  7.2 294.6 %reduce-scatter.2.cloned.1.call-start = ((), (), s32[]{:S(2)}) async-start(), calls=%async_computation.1 | async-start | bytes 3932160 | tf_op jit(solution)/shard_map/reduce_scatter | solution.py:2376
  224.1 1.4 copy-start.2
  224.1 54.8 %collective-permute-start.3 = (bf16[1536,512]{1,0:T(8,128)(2,1)}, bf16[1536,512]{1,0:T(8,128)(2,1)}, u32[]{:S(2)}, u32[]{:S(2)}) collective-permute-start(bf16[1536,512]{1,0:T(8,128)(2,1)} %get-tuple-element.65), channel_id=1, source_target_pairs={{0,4},{4,0},{1,5},{5,1},{2,6},{6,2},{3,7},{7,3},{8,12},{12,8},{9,1... | collective-permute-start | bytes 4718600 | tf_op jit(solution)/shard_map/ppermute | solution.py:435
  225.5 37.2 %collective-permute-start = (bf16[512,1536]{1,0:T(8,128)(2,1)S(1)}, bf16[512,1536]{1,0:T(8,128)(2,1)S(1)}, u32[]{:S(2)}, u32[]{:S(2)}) collective-permute-start(bf16[512,1536]{1,0:T(8,128)(2,1)S(1)} %bitcast.43), channel_id=1, source_target_pairs={{0,2},{2,0},{1,3},{3,1},{4,6},{6,4},{5,7},{7,5},{8,10},{10,8},{9,1... | collective-permute-start | bytes 4718600 | tf_op jit(solution)/shard_map/ppermute | solution.py:443
  262.8 1.1 copy-start.3
  263.9 3.0 copy-start.9
  266.9 30.1 %collective-permute-start.1 = (bf16[512,1536]{1,0:T(8,128)(2,1)}, bf16[512,1536]{1,0:T(8,128)(2,1)S(1)}, u32[]{:S(2)}, u32[]{:S(2)}) collective-permute-start(bf16[512,1536]{1,0:T(8,128)(2,1)} %add_after.1), channel_id=1, source_target_pairs={{0,1},{1,0},{2,3},{3,2},{4,5},{5,4},{6,7},{7,6},{8,9},{9,8},{10,11... | collective-permute-start | bytes 4718600 | tf_op jit(solution)/shard_map/ppermute | solution.py:439
  266.9 12.1 %collective-permute-start.2 = (bf16[384,512]{1,0:T(8,128)(2,1)S(1)}, bf16[384,512]{1,0:T(8,128)(2,1)}, u32[]{:S(2)}, u32[]{:S(2)}) collective-permute-start(bf16[384,512]{1,0:T(8,128)(2,1)S(1)} %copy-done.9), channel_id=1, source_target_pairs={{0,4},{4,0},{1,5},{5,1},{2,6},{6,2},{3,7},{7,3},{8,12},{12,8},{9,1... | collective-permute-start | bytes 1179656 | tf_op jit(solution)/shard_map/ppermute | solution.py:435
  267.4 34.4 %collective-permute-start.4 = (bf16[2,2,1024,128]{3,2,1,0:T(8,128)(2,1)}, bf16[2,2,1024,128]{3,2,1,0:T(8,128)(2,1)}, u32[]{:S(2)}, u32[]{:S(2)}) collective-permute-start(bf16[2,2,1024,128]{3,2,1,0:T(8,128)(2,1)} %get-tuple-element.68), channel_id=1, source_target_pairs={{0,4},{4,0},{1,5},{5,1},{2,6},{6,2},{3,7},{7,3},{8,12},{12,8},{9,1... | collective-permute-start | bytes 3145736 | tf_op jit(solution)/shard_map/ppermute | solution.py:435
  269.0 28.0 %copy-start = (bf16[512,1536]{1,0:T(8,128)(2,1)S(1)}, bf16[512,1536]{1,0:T(8,128)(2,1)}, u32[]{:S(2)}) copy-start(bf16[512,1536]{1,0:T(8,128)(2,1)} %add_after.1) | copy-start | bytes 4718596
  402.7 2.1 copy-start.5
  403.9 1.2 copy-start.4
  404.9 1.0 copy-start.8
  405.9 4.5 %copy-start.6 = (bf16[1,1024,384]{2,1,0:T(8,128)(2,1)S(1)}, bf16[1,1024,384]{2,1,0:T(8,128)(2,1)}, u32[]{:S(2)}) copy-start(bf16[1,1024,384]{2,1,0:T(8,128)(2,1)} %reduce-scatter.2.cloned.1.call-done) | copy-start | bytes 2359300
  414.3 3.3 copy-start.1
Sparse Core Ops, SparseCore 0:
  224.3 59.2 reduce-scatter.1

commit v6 on v5

--- a/solution.py
+++ b/solution.py
@@ -1051,12 +1051,12 @@
 
     attend_group(0, False)
     relay(2, 1)
+    cross(1, 1)
     attend_group(1, False)
     relay(3, 1)
     for slab in range(4):
         exchange(slab).wait_recv()
     stores[3].start()
-    cross(1, 1)
     cross(2, 1)
     cross(3, 1)
     attend_group(0, True)
@@ -1790,17 +1790,8 @@
     for step in range(planes - 1):
         q_begin(step)
     down_over().start()
-    for i in range(1, chunks):
-        finish_chunk(i)
-    g_finish(gate_share_ref.at[0])
-    last_of(gate_share_ref, 3).start()
-    p_relay(0)
-    u_finish(up_share_ref.at[0])
-    last_of(up_share_ref, 4).start()
-    q_relay(0)
     for load in loads[7:]:
         load.wait()
-
     gain_sum_ref[...] = jnp.zeros_like(gain_sum_ref)
     gain_sum_ref[1:2, :] = gain_term_ref[...]
     gain = gain_ref[0:1, :].astype(f32)
@@ -1818,22 +1809,31 @@
             - x * (factor * factor * factor * jnp.mean(scaled * x, axis=-1, keepdims=True))
         ).astype(bf16)
 
-    for i in range(chunks):
+    finish_rows(keep_start)
+    for i in range(1, chunks):
+        finish_chunk(i)
+    g_finish(gate_share_ref.at[0])
+    last_of(gate_share_ref, 3).start()
+    p_relay(0)
+    u_finish(up_share_ref.at[0])
+    last_of(up_share_ref, 4).start()
+    q_relay(0)
+    for i in range(1, chunks):
         finish_rows(keep_start + i * chunk)
     p_relay(1)
     q_relay(1)
     for i in range(chunks):
         from_core(i).wait_recv()
         finish_rows(give_start + i * chunk)
+    out_copy = pltpu.make_async_copy(x_ref, out_hbm, load_sem.at[0])
+    out_copy.start()
+
+    gain_over = remote(gain_sum_ref, gain_x_ref, gain_send.at[0], gain_recv.at[0], across)
+    gain_over.start()
     p_finish(project_share_ref.at[0])
     last_project().start()
     q_finish(share_ref.at[0])
     last_share().start()
-    out_copy = pltpu.make_async_copy(x_ref, out_hbm, load_sem.at[0])
-    out_copy.start()
-
-    gain_over = remote(gain_sum_ref, gain_x_ref, gain_send.at[0], gain_recv.at[0], across)
-    gain_over.start()
     gain_over.wait()
     gain_sum_ref[...] = gain_sum_ref[...] + gain_x_ref[...]
 

time: 433 us -> 427 us (0.986)
  Pallas kernels: 357 us -> 350 us
    pallas_call x1, Pallas kernels: 101 us -> 95.2 us  [tail(): pl.pallas_call(tail_kernel, in_specs=[anywhere] * 6 + [vmem] * 3 + [anywh...]
  transfers between devices with their start and end apart: 6 -> 6, of which waited for: 2 -> 2; matrix products, arithmetic and copies ran while one was open for 1% -> 1% of each run, Pallas kernels for 11% -> 12%
where the time goes in v6:
time: 427 us; the launch traced here: 420 us
  Pallas kernels  350 us (82%)
  other arithmetic  19.6 us (5%)
  waiting for transfers between devices  15.6 us (4%)
  between operations  15.4 us (4%)
  local copies, waits for them, and re-layouts  13.4 us (3%)
  starting transfers between devices  5.42 us (1%)
    pallas_call x1, Pallas kernels, front(): pl.pallas_call(front_kernel, in_specs=[smem] + [vmem] * 6 + [anywhere] *...  142 us
    pallas_call x1, Pallas kernels, tail(): pl.pallas_call(tail_kernel, in_specs=[anywhere] * 6 + [vmem] * 3 + [anywh...  95.2 us
    pallas_call x1, Pallas kernels, feed(): pl.pallas_call(feed_kernel, in_specs=[anywhere] * 3 + [vmem] + [anywhere]...  63.6 us
    pallas_call x2, Pallas kernels, attend_back(): pl.pallas_call(functools.partial(attend_back_kernel, not away), grid_spec...  33.3 us
    pallas_call x1, Pallas kernels, middle_back(): pl.pallas_call(middle_back_kernel, grid=(rows // tile,), in_specs=[rows_o...  13.5 us
    ppermute x3, waiting for transfers between devices, swap_ctx(): return lax.ppermute(block, 'ctx', [(0, 1), (1, 0)])  10 us
  transfers between devices with their start and end apart: 6, of which 2 were waited for; matrix products, arithmetic and copies ran while one was open for 1% of the time, Pallas kernels for 12%

profile of v6, /device:TPU:0, one launch (start us, length us, event | category | flops | bytes accessed | tf_op | source)
XLA Modules:
  0.0 419.5 jit_solution(2244524561319561657)
XLA Ops:
  7.2 0.0 copy-start.7
  7.2 0.0 reduce-scatter.2.cloned.1.call-start
  7.3 1.0 constant_dynamic-slice_fusion
  8.3 0.1 copy.33
  8.4 0.1 copy.34
  8.5 0.1 copy.31
  8.7 0.1 copy.32
  8.8 0.7 stack.10
  9.5 0.7 stack.9
  10.2 0.7 convert_element_type.63
  11.5 1.9 fusion.7
  13.5 0.0 copy-done.7
  13.5 0.2 constant_dynamic-slice_fusion.2
  13.7 0.9 pad_maximum_fusion.3.rest_ref
  14.5 1.3 pad_maximum_fusion
  15.8 0.9 pad_maximum_fusion.2.pack_ref
  16.7 141.6 %front.1 = (bf16[1024,1536]{1,0:T(8,128)(2,1)}, bf16[1024,512]{1,0:T(8,128)(2,1)}, bf16[4,2048,128]{2,1,0:T(8,128)(2,1)}, bf16[1536,1024]{1,0:T(8,128)(2,1)}, bf...) custom-call(s32[1]{0:T(128)S(6)} %copy.36.prefix_ref, ...), custom_call_target="tpu_custom_call" | custom-call | flops 120000004096 | bytes 60000000 | tf_op jit(solution)/shard_map/front/pallas_call | solution.py:1178
  158.3 63.6 %feed.1 = (bf16[1024,1536]{1,0:T(8,128)(2,1)}, bf16[1536,512]{1,0:T(8,128)(2,1)}, bf16[1152,512]{1,0:T(8,128)(2,1)}, bf16[384,512]{1,0:T(8,128)(2,1)}, bf16[1536...) custom-call(bf16[1024,1536]{1,0:T(8,128)(2,1)} %bitcast.39, ...), custom_call_target="tpu_custom_call" | custom-call | flops 49999998976 | bytes 40000000 | tf_op jit(solution)/shard_map/feed/pallas_call | solution.py:2216
  221.9 0.0 copy-start.2
  221.9 0.0 reduce-scatter.2.cloned.1.call-update
  221.9 0.7 collective-permute-start.3
  222.7 0.6 copy-done.2
  223.3 2.6 collective-permute-start
  225.9 0.6 pad_add_fusion.meta_ref
  226.5 13.5 %middle_back.1 = (f32[1024,1536]{1,0:T(8,128)}, bf16[1024,512]{1,0:T(8,128)(2,1)}, bf16[384,1536]{1,0:T(8,128)(2,1)}, f32[1,1536]{1,0:T(1,128)}) custom-call(bf16[1024,1536]{1,0:T(8,128)(2,1)} %bitcast.40, bf16[1024,1536]{1,0:T(8,128)(2,1)} %get-tuple-element.46.project_hbm.project_ref, bf16[1024,1536]{1,0:T(8,128)(2,1)} %get-tuple-element.51.feed_ref, ...), custom_call_target="tpu_custom_call" | custom-call | flops 5000000000 | bytes 26000000 | tf_op jit(solution)/shard_map/middle_back/pallas_call | solution.py:1440
  240.0 0.6 broadcast_in_dim.11.carry_ref
  240.6 14.4 %attend_back_away.1 = (f32[2,4,128,512]{3,2,1,0:T(8,128)}, bf16[2,2,1024,128]{3,2,1,0:T(8,128)(2,1)}) custom-call(s32[13]{0:T(128)} %pad_add_fusion.meta_ref, f32[1,1,8,128]{3,2,1,0:T(8,128)} %broadcast_in_dim.11.carry_ref, bf16[1024,512]{1,0:T(8,128)(2,1)} %get-tuple-element.54.first_ref.second_ref.do_ref, ...), custom_call_target="tpu_custom_call" | custom-call | flops 10737418240 | bytes 8000000 | tf_op jit(solution)/shard_map/attend_back_away/pallas_call | solution.py:1341
  255.0 5.5 %collective-permute-done.b_ref = bf16[512,1536]{1,0:T(8,128)(2,1)S(1)} collective-permute-done((bf16[512,1536]{1,0:T(8,128)(2,1)S(1)}, bf16[512,1536]{1,0:T(8,128)(2,1)S(1)}, u32[]{:S(2)}, u32[]{:S(2)}) %collective-permute-start) | collective-permute-done | bytes 1572896 | tf_op jit(solution)/shard_map/ppermute | solution.py:443
  260.6 1.1 copy-done.3
  261.7 3.0 add_after.1
  264.7 0.0 collective-permute-start.1
  264.7 0.0 copy-done.9
  264.7 0.5 collective-permute-start.2
  265.2 1.6 collective-permute-start.4
  266.8 10.0 %collective-permute-done.2.first_ref.gate_rest_hbm = bf16[384,512]{1,0:T(8,128)(2,1)} collective-permute-done((bf16[384,512]{1,0:T(8,128)(2,1)S(1)}, bf16[384,512]{1,0:T(8,128)(2,1)}, u32[]{:S(2)}, u32[]{:S(2)}) %collective-permute-start.2) | collective-permute-done | bytes 393248 | tf_op jit(solution)/shard_map/ppermute | solution.py:435
  276.8 0.0 collective-permute-done.3.second_ref.up_away_hbm
  276.8 18.9 %attend_back_own.1 = (bf16[1024,512]{1,0:T(8,128)(2,1)}, bf16[2,2,1024,128]{3,2,1,0:T(8,128)(2,1)}) custom-call(s32[13]{0:T(128)} %pad_add_fusion.meta_ref, f32[2,4,128,512]{3,2,1,0:T(8,128)} %get-tuple-element.58.first_ref.carry_ref, bf16[384,512]{1,0:T(8,128)(2,1)} %collective-permute-done.2.first_ref.gate_rest_hbm, ...), custom_call_target="tpu_custom_call" | custom-call | flops 10737418240 | bytes 8000000 | tf_op jit(solution)/shard_map/attend_back_own/pallas_call | solution.py:1341
  295.7 0.0 collective-permute-done.1
  295.7 0.0 copy-done
  295.7 4.8 %fusion = bf16[1,1024,1536]{2,1,0:T(8,128)(2,1)} fusion(bf16[1024,1536]{1,0:T(8,128)(2,1)} %get-tuple-element.46.project_hbm.project_ref, bf16[512,1536]{1,0:T(8,128)(2,1)S(1)} %collective-permute-done.1, bf16[512,1536]{1,0:T(8,128)(2,1)S(1)} %copy-done, pred[]{:T(512)S(6)} %eq.25, bf16[1,1024,1536]{2,1,0:T(8,128)(2,1)} %param.14), kind=kLoop, calls=%fused_computation.1 | loop fusion | flops 23592960 | bytes 12582913 | tf_op jit(solution)/shard_map/broadcast_in_dim | solution.py:2406
  300.6 0.0 collective-permute-done.4.away_ref
  300.6 95.2 %tail.1 = (bf16[1024,1536]{1,0:T(8,128)(2,1)}, bf16[2,384,384]{2,1,0:T(8,128)(2,1)}, bf16[2,192,384]{2,1,0:T(8,128)(2,1)}, bf16[2,384,512]{2,1,0:T(8,128)(2,1)},...) custom-call(bf16[1024,384]{1,0:T(8,128)(2,1)} %bitcast.44, ...), custom_call_target="tpu_custom_call" | custom-call | flops 60000002048 | bytes 24000000 | tf_op jit(solution)/shard_map/tail/pallas_call | solution.py:1900
  395.7 0.0 copy-start.5
  395.8 1.2 slice_bitcast_fusion.7
  396.9 0.0 copy-start.4
  397.0 0.1 fusion.17
  397.1 0.8 fusion.18
  397.9 0.0 copy-done.5
  397.9 0.1 slice_bitcast_fusion.3
  398.0 0.1 copy-done.4
  398.1 0.1 slice_bitcast_fusion.5
  398.2 0.7 copy-done.8
  398.9 0.2 fusion.6
  399.1 0.9 copy.30
  400.0 1.1 fusion.5
  401.1 0.9 copy.29
  402.0 1.4 slice_reduce_fusion
  403.4 1.3 convert_add_fusion.1
  404.7 1.2 maximum_select_fusion.1
  405.9 1.4 fusion.2
  407.3 1.4 fusion.1
  408.7 0.9 fusion.4
  409.5 1.0 fusion.3
  410.6 1.7 copy.37
  (16 shorter events, 0.1 us)
Async XLA Ops:
  7.2 6.3 %copy-start.7 = (bf16[384,384]{1,0:T(8,128)(2,1)S(1)}, bf16[384,384]{1,0:T(8,128)(2,1)}, u32[]{:S(2)}) copy-start(bf16[384,384]{1,0:T(8,128)(2,1)} %param.18) | copy-start | bytes 884740
  7.2 293.4 %reduce-scatter.2.cloned.1.call-start = ((), (), s32[]{:S(2)}) async-start(), calls=%async_computation.1 | async-start | bytes 3932160 | tf_op jit(solution)/shard_map/reduce_scatter | solution.py:2376
  221.9 1.4 copy-start.2
  221.9 54.8 %collective-permute-start.3 = (bf16[1536,512]{1,0:T(8,128)(2,1)}, bf16[1536,512]{1,0:T(8,128)(2,1)}, u32[]{:S(2)}, u32[]{:S(2)}) collective-permute-start(bf16[1536,512]{1,0:T(8,128)(2,1)} %get-tuple-element.65), channel_id=1, source_target_pairs={{0,4},{4,0},{1,5},{5,1},{2,6},{6,2},{3,7},{7,3},{8,12},{12,8},{9,1... | collective-permute-start | bytes 4718600 | tf_op jit(solution)/shard_map/ppermute | solution.py:435
  223.3 37.3 %collective-permute-start = (bf16[512,1536]{1,0:T(8,128)(2,1)S(1)}, bf16[512,1536]{1,0:T(8,128)(2,1)S(1)}, u32[]{:S(2)}, u32[]{:S(2)}) collective-permute-start(bf16[512,1536]{1,0:T(8,128)(2,1)S(1)} %bitcast.43), channel_id=1, source_target_pairs={{0,2},{2,0},{1,3},{3,1},{4,6},{6,4},{5,7},{7,5},{8,10},{10,8},{9,1... | collective-permute-start | bytes 4718600 | tf_op jit(solution)/shard_map/ppermute | solution.py:443
  260.6 1.1 copy-start.3
  261.7 3.0 copy-start.9
  264.7 31.0 %collective-permute-start.1 = (bf16[512,1536]{1,0:T(8,128)(2,1)}, bf16[512,1536]{1,0:T(8,128)(2,1)S(1)}, u32[]{:S(2)}, u32[]{:S(2)}) collective-permute-start(bf16[512,1536]{1,0:T(8,128)(2,1)} %add_after.1), channel_id=1, source_target_pairs={{0,1},{1,0},{2,3},{3,2},{4,5},{5,4},{6,7},{7,6},{8,9},{9,8},{10,11... | collective-permute-start | bytes 4718600 | tf_op jit(solution)/shard_map/ppermute | solution.py:439
  264.7 12.1 %collective-permute-start.2 = (bf16[384,512]{1,0:T(8,128)(2,1)S(1)}, bf16[384,512]{1,0:T(8,128)(2,1)}, u32[]{:S(2)}, u32[]{:S(2)}) collective-permute-start(bf16[384,512]{1,0:T(8,128)(2,1)S(1)} %copy-done.9), channel_id=1, source_target_pairs={{0,4},{4,0},{1,5},{5,1},{2,6},{6,2},{3,7},{7,3},{8,12},{12,8},{9,1... | collective-permute-start | bytes 1179656 | tf_op jit(solution)/shard_map/ppermute | solution.py:435
  265.2 35.4 %collective-permute-start.4 = (bf16[2,2,1024,128]{3,2,1,0:T(8,128)(2,1)}, bf16[2,2,1024,128]{3,2,1,0:T(8,128)(2,1)}, u32[]{:S(2)}, u32[]{:S(2)}) collective-permute-start(bf16[2,2,1024,128]{3,2,1,0:T(8,128)(2,1)} %get-tuple-element.68), channel_id=1, source_target_pairs={{0,4},{4,0},{1,5},{5,1},{2,6},{6,2},{3,7},{7,3},{8,12},{12,8},{9,1... | collective-permute-start | bytes 3145736 | tf_op jit(solution)/shard_map/ppermute | solution.py:435
  266.8 28.9 %copy-start = (bf16[512,1536]{1,0:T(8,128)(2,1)S(1)}, bf16[512,1536]{1,0:T(8,128)(2,1)}, u32[]{:S(2)}) copy-start(bf16[512,1536]{1,0:T(8,128)(2,1)} %add_after.1) | copy-start | bytes 4718596
  395.7 2.1 copy-start.5
  396.9 1.2 copy-start.4
  397.9 1.0 copy-start.8
  398.9 4.5 %copy-start.6 = (bf16[1,1024,384]{2,1,0:T(8,128)(2,1)S(1)}, bf16[1,1024,384]{2,1,0:T(8,128)(2,1)}, u32[]{:S(2)}) copy-start(bf16[1,1024,384]{2,1,0:T(8,128)(2,1)} %reduce-scatter.2.cloned.1.call-done) | copy-start | bytes 2359300
  407.3 3.3 copy-start.1
Sparse Core Ops, SparseCore 0:
  222.0 59.2 reduce-scatter.1

commit v7 on v6

--- a/solution.py
+++ b/solution.py
@@ -1649,7 +1649,6 @@
     for step in range((planes + 1) // 2):
         order += [planes - 1 - step, step]
     order = order[:planes]
-    project_over().start()
     for load in loads[:3]:
         load.wait()
     g_begin(0)
@@ -1689,6 +1688,7 @@
     for d in order:
         weight_part(1, d)
         to_neighbour(d).start()
+    project_over().start()
 
     def feature_rows(start):
         at = pl.ds(pl.multiple_of(start, chunk), chunk)
@@ -1782,14 +1782,14 @@
     g_relay(1)
     finish_chunk(0)
     u_relay(1)
-    project_over().wait_recv()
-    for step in range(planes - 1):
-        p_begin(step)
     for d in order:
         add_neighbour(d)
     for step in range(planes - 1):
         q_begin(step)
     down_over().start()
+    project_over().wait_recv()
+    for step in range(planes - 1):
+        p_begin(step)
     for load in loads[7:]:
         load.wait()
     gain_sum_ref[...] = jnp.zeros_like(gain_sum_ref)
@@ -1814,14 +1814,14 @@
         finish_chunk(i)
     g_finish(gate_share_ref.at[0])
     last_of(gate_share_ref, 3).start()
-    p_relay(0)
     u_finish(up_share_ref.at[0])
     last_of(up_share_ref, 4).start()
     q_relay(0)
+    p_relay(0)
     for i in range(1, chunks):
         finish_rows(keep_start + i * chunk)
+    q_relay(1)
     p_relay(1)
-    q_relay(1)
     for i in range(chunks):
         from_core(i).wait_recv()
         finish_rows(give_start + i * chunk)

time: 427 us -> 433 us (1.014)
  the two profiles are of different devices: /device:TPU:0 before, /device:TPU:14 now
where the time goes in v7:
time: 433 us; the launch traced here: 425 us
  Pallas kernels  360 us (83%)
  other arithmetic  19.6 us (5%)
  between operations  15.4 us (4%)
  waiting for transfers between devices  14.1 us (3%)
  local copies, waits for them, and re-layouts  14 us (3%)
    pallas_call x1, Pallas kernels, front(): pl.pallas_call(front_kernel, in_specs=[smem] + [vmem] * 6 + [anywhere] *...  130 us
    pallas_call x1, Pallas kernels, tail(): pl.pallas_call(tail_kernel, in_specs=[anywhere] * 6 + [vmem] * 3 + [anywh...  113 us
    pallas_call x1, Pallas kernels, feed(): pl.pallas_call(feed_kernel, in_specs=[anywhere] * 3 + [vmem] + [anywhere]...  65.2 us
    pallas_call x2, Pallas kernels, attend_back(): pl.pallas_call(functools.partial(attend_back_kernel, not away), grid_spec...  35.3 us
    pallas_call x1, Pallas kernels, middle_back(): pl.pallas_call(middle_back_kernel, grid=(rows // tile,), in_specs=[rows_o...  13.1 us
    ppermute x3, waiting for transfers between devices, swap_ctx(): return lax.ppermute(block, 'ctx', [(0, 1), (1, 0)])  10 us
  transfers between devices with their start and end apart: 6, of which 2 were waited for; matrix products, arithmetic and copies ran while one was open for 1% of the time, Pallas kernels for 12%

profile of v7, /device:TPU:14, one launch (start us, length us, event | category | flops | bytes accessed | tf_op | source)
XLA Modules:
  0.0 425.5 jit_solution(9394295617328747949)
XLA Ops:
  7.2 0.0 copy-start.7
  7.2 0.0 reduce-scatter.2.cloned.1.call-start
  7.3 1.0 constant_dynamic-slice_fusion
  8.3 0.1 copy.33
  8.4 0.1 copy.34
  8.5 0.1 copy.31
  8.7 0.1 copy.32
  8.8 0.7 stack.10
  9.5 0.7 stack.9
  10.2 0.7 convert_element_type.63
  11.5 1.9 fusion.7
  13.5 0.0 copy-done.7
  13.5 0.2 constant_dynamic-slice_fusion.2
  13.7 0.9 pad_maximum_fusion.3.rest_ref
  14.5 1.3 pad_maximum_fusion
  15.8 0.9 pad_maximum_fusion.2.pack_ref
  16.7 130.4 %front.1 = (bf16[1024,1536]{1,0:T(8,128)(2,1)}, bf16[1024,512]{1,0:T(8,128)(2,1)}, bf16[4,2048,128]{2,1,0:T(8,128)(2,1)}, bf16[1536,1024]{1,0:T(8,128)(2,1)}, bf...) custom-call(s32[1]{0:T(128)S(6)} %copy.36.prefix_ref, ...), custom_call_target="tpu_custom_call" | custom-call | flops 120000004096 | bytes 60000000 | tf_op jit(solution)/shard_map/front/pallas_call | solution.py:1178
  147.1 65.2 %feed.1 = (bf16[1024,1536]{1,0:T(8,128)(2,1)}, bf16[1536,512]{1,0:T(8,128)(2,1)}, bf16[1152,512]{1,0:T(8,128)(2,1)}, bf16[384,512]{1,0:T(8,128)(2,1)}, bf16[1536...) custom-call(bf16[1024,1536]{1,0:T(8,128)(2,1)} %bitcast.39, ...), custom_call_target="tpu_custom_call" | custom-call | flops 49999998976 | bytes 40000000 | tf_op jit(solution)/shard_map/feed/pallas_call | solution.py:2216
  212.3 0.0 copy-start.2
  212.3 0.0 reduce-scatter.2.cloned.1.call-update
  212.3 0.1 collective-permute-start.3
  212.4 1.3 copy-done.2
  213.7 0.0 collective-permute-start
  213.8 0.6 pad_add_fusion.meta_ref
  214.3 13.1 %middle_back.1 = (f32[1024,1536]{1,0:T(8,128)}, bf16[1024,512]{1,0:T(8,128)(2,1)}, bf16[384,1536]{1,0:T(8,128)(2,1)}, f32[1,1536]{1,0:T(1,128)}) custom-call(bf16[1024,1536]{1,0:T(8,128)(2,1)} %bitcast.40, bf16[1024,1536]{1,0:T(8,128)(2,1)} %get-tuple-element.46.project_hbm.project_ref, bf16[1024,1536]{1,0:T(8,128)(2,1)} %get-tuple-element.51.feed_ref, ...), custom_call_target="tpu_custom_call" | custom-call | flops 5000000000 | bytes 26000000 | tf_op jit(solution)/shard_map/middle_back/pallas_call | solution.py:1440
  227.5 0.6 broadcast_in_dim.11.carry_ref
  228.0 16.4 %attend_back_away.1 = (f32[2,4,128,512]{3,2,1,0:T(8,128)}, bf16[2,2,1024,128]{3,2,1,0:T(8,128)(2,1)}) custom-call(s32[13]{0:T(128)} %pad_add_fusion.meta_ref, f32[1,1,8,128]{3,2,1,0:T(8,128)} %broadcast_in_dim.11.carry_ref, bf16[1024,512]{1,0:T(8,128)(2,1)} %get-tuple-element.54.first_ref.second_ref.do_ref, ...), custom_call_target="tpu_custom_call" | custom-call | flops 10737418240 | bytes 8000000 | tf_op jit(solution)/shard_map/attend_back_away/pallas_call | solution.py:1341
  244.4 4.1 collective-permute-done.b_ref
  248.5 1.1 copy-done.3
  249.6 3.0 add_after.1
  252.6 0.0 collective-permute-start.1
  252.6 0.0 copy-done.9
  252.6 1.6 collective-permute-start.2
  254.2 0.5 collective-permute-start.4
  254.7 10.0 %collective-permute-done.2.first_ref.gate_rest_hbm = bf16[384,512]{1,0:T(8,128)(2,1)} collective-permute-done((bf16[384,512]{1,0:T(8,128)(2,1)S(1)}, bf16[384,512]{1,0:T(8,128)(2,1)}, u32[]{:S(2)}, u32[]{:S(2)}) %collective-permute-start.2) | collective-permute-done | bytes 393248 | tf_op jit(solution)/shard_map/ppermute | solution.py:435
  264.7 0.0 collective-permute-done.3.second_ref.up_away_hbm
  264.7 18.9 %attend_back_own.1 = (bf16[1024,512]{1,0:T(8,128)(2,1)}, bf16[2,2,1024,128]{3,2,1,0:T(8,128)(2,1)}) custom-call(s32[13]{0:T(128)} %pad_add_fusion.meta_ref, f32[2,4,128,512]{3,2,1,0:T(8,128)} %get-tuple-element.58.first_ref.carry_ref, bf16[384,512]{1,0:T(8,128)(2,1)} %collective-permute-done.2.first_ref.gate_rest_hbm, ...), custom_call_target="tpu_custom_call" | custom-call | flops 10737418240 | bytes 8000000 | tf_op jit(solution)/shard_map/attend_back_own/pallas_call | solution.py:1341
  283.7 0.0 collective-permute-done.1
  283.7 0.0 copy-done
  283.7 4.8 %fusion = bf16[1,1024,1536]{2,1,0:T(8,128)(2,1)} fusion(bf16[1024,1536]{1,0:T(8,128)(2,1)} %get-tuple-element.46.project_hbm.project_ref, bf16[512,1536]{1,0:T(8,128)(2,1)S(1)} %collective-permute-done.1, bf16[512,1536]{1,0:T(8,128)(2,1)S(1)} %copy-done, pred[]{:T(512)S(6)} %eq.25, bf16[1,1024,1536]{2,1,0:T(8,128)(2,1)} %param.14), kind=kLoop, calls=%fused_computation.1 | loop fusion | flops 23592960 | bytes 12582913 | tf_op jit(solution)/shard_map/broadcast_in_dim | solution.py:2406
  288.5 0.0 collective-permute-done.4.away_ref
  288.5 113.2 %tail.1 = (bf16[1024,1536]{1,0:T(8,128)(2,1)}, bf16[2,384,384]{2,1,0:T(8,128)(2,1)}, bf16[2,192,384]{2,1,0:T(8,128)(2,1)}, bf16[2,384,512]{2,1,0:T(8,128)(2,1)},...) custom-call(bf16[1024,384]{1,0:T(8,128)(2,1)} %bitcast.44, ...), custom_call_target="tpu_custom_call" | custom-call | flops 60000002048 | bytes 24000000 | tf_op jit(solution)/shard_map/tail/pallas_call | solution.py:1900
  401.7 0.0 copy-start.5
  401.7 1.2 slice_bitcast_fusion.7
  402.9 0.0 copy-start.4
  402.9 0.1 fusion.17
  403.1 0.8 fusion.18
  403.8 0.1 slice_bitcast_fusion.3
  403.9 0.1 copy-done.4
  404.1 0.1 slice_bitcast_fusion.5
  404.1 0.7 copy-done.8
  404.9 0.2 fusion.6
  405.1 0.9 copy.30
  405.9 1.1 fusion.5
  407.1 0.9 copy.29
  408.0 1.4 slice_reduce_fusion
  409.3 1.3 convert_add_fusion.1
  410.6 1.2 maximum_select_fusion.1
  411.9 1.4 fusion.2
  413.2 1.4 fusion.1
  414.6 0.9 fusion.4
  415.5 1.0 fusion.3
  416.5 0.0 copy-done.1
  416.5 1.7 copy.37
  (16 shorter events, 0.1 us)
Async XLA Ops:
  7.2 6.3 %copy-start.7 = (bf16[384,384]{1,0:T(8,128)(2,1)S(1)}, bf16[384,384]{1,0:T(8,128)(2,1)}, u32[]{:S(2)}) copy-start(bf16[384,384]{1,0:T(8,128)(2,1)} %param.18) | copy-start | bytes 884740
  7.2 281.3 %reduce-scatter.2.cloned.1.call-start = ((), (), s32[]{:S(2)}) async-start(), calls=%async_computation.1 | async-start | bytes 3932160 | tf_op jit(solution)/shard_map/reduce_scatter | solution.py:2376
  212.3 1.4 copy-start.2
  212.3 52.4 %collective-permute-start.3 = (bf16[1536,512]{1,0:T(8,128)(2,1)}, bf16[1536,512]{1,0:T(8,128)(2,1)}, u32[]{:S(2)}, u32[]{:S(2)}) collective-permute-start(bf16[1536,512]{1,0:T(8,128)(2,1)} %get-tuple-element.65), channel_id=1, source_target_pairs={{0,4},{4,0},{1,5},{5,1},{2,6},{6,2},{3,7},{7,3},{8,12},{12,8},{9,1... | collective-permute-start | bytes 4718600 | tf_op jit(solution)/shard_map/ppermute | solution.py:435
  213.7 34.8 %collective-permute-start = (bf16[512,1536]{1,0:T(8,128)(2,1)S(1)}, bf16[512,1536]{1,0:T(8,128)(2,1)S(1)}, u32[]{:S(2)}, u32[]{:S(2)}) collective-permute-start(bf16[512,1536]{1,0:T(8,128)(2,1)S(1)} %bitcast.43), channel_id=1, source_target_pairs={{0,2},{2,0},{1,3},{3,1},{4,6},{6,4},{5,7},{7,5},{8,10},{10,8},{9,1... | collective-permute-start | bytes 4718600 | tf_op jit(solution)/shard_map/ppermute | solution.py:443
  248.5 1.1 copy-start.3
  249.6 3.0 copy-start.9
  252.6 31.0 %collective-permute-start.1 = (bf16[512,1536]{1,0:T(8,128)(2,1)}, bf16[512,1536]{1,0:T(8,128)(2,1)S(1)}, u32[]{:S(2)}, u32[]{:S(2)}) collective-permute-start(bf16[512,1536]{1,0:T(8,128)(2,1)} %add_after.1), channel_id=1, source_target_pairs={{0,1},{1,0},{2,3},{3,2},{4,5},{5,4},{6,7},{7,6},{8,9},{9,8},{10,11... | collective-permute-start | bytes 4718600 | tf_op jit(solution)/shard_map/ppermute | solution.py:439
  252.6 12.1 %collective-permute-start.2 = (bf16[384,512]{1,0:T(8,128)(2,1)S(1)}, bf16[384,512]{1,0:T(8,128)(2,1)}, u32[]{:S(2)}, u32[]{:S(2)}) collective-permute-start(bf16[384,512]{1,0:T(8,128)(2,1)S(1)} %copy-done.9), channel_id=1, source_target_pairs={{0,4},{4,0},{1,5},{5,1},{2,6},{6,2},{3,7},{7,3},{8,12},{12,8},{9,1... | collective-permute-start | bytes 1179656 | tf_op jit(solution)/shard_map/ppermute | solution.py:435
  254.2 34.3 %collective-permute-start.4 = (bf16[2,2,1024,128]{3,2,1,0:T(8,128)(2,1)}, bf16[2,2,1024,128]{3,2,1,0:T(8,128)(2,1)}, u32[]{:S(2)}, u32[]{:S(2)}) collective-permute-start(bf16[2,2,1024,128]{3,2,1,0:T(8,128)(2,1)} %get-tuple-element.68), channel_id=1, source_target_pairs={{0,4},{4,0},{1,5},{5,1},{2,6},{6,2},{3,7},{7,3},{8,12},{12,8},{9,1... | collective-permute-start | bytes 3145736 | tf_op jit(solution)/shard_map/ppermute | solution.py:435
  254.7 28.9 %copy-start = (bf16[512,1536]{1,0:T(8,128)(2,1)S(1)}, bf16[512,1536]{1,0:T(8,128)(2,1)}, u32[]{:S(2)}) copy-start(bf16[512,1536]{1,0:T(8,128)(2,1)} %add_after.1) | copy-start | bytes 4718596
  401.7 2.1 copy-start.5
  402.9 1.2 copy-start.4
  403.8 1.0 copy-start.8
  404.9 4.5 %copy-start.6 = (bf16[1,1024,384]{2,1,0:T(8,128)(2,1)S(1)}, bf16[1,1024,384]{2,1,0:T(8,128)(2,1)}, u32[]{:S(2)}) copy-start(bf16[1,1024,384]{2,1,0:T(8,128)(2,1)} %reduce-scatter.2.cloned.1.call-done) | copy-start | bytes 2359300
  413.2 3.3 copy-start.1
Sparse Core Ops, SparseCore 0:
  212.5 66.7 reduce-scatter.1
